TPU v7x, 32 devices: a whole 2x2x4 slice. The times are simulated.
32 devices in a mesh: seq: 8 (over y, x, core), mp: 4 (over z).
Axes of the slice: x: 2, y: 2, z: 4, core: 2. Of those that a mesh axis runs over, the one named last changes fastest.
Arguments:
- enc_states: bfloat16 [6144, 1280], P(('seq', 'mp')), may hold values from -6 to 6
- dec_states: bfloat16 [6144, 1280], P(('seq', 'mp')), may hold values from -240 to 240
- segments: int32 [6144], P(('seq', 'mp')), may hold values from 0 to 30, as said below
- patch_keys: bfloat16 [992, 1280], P(('seq', 'mp')), may hold values from -7 to 7
- w_in: bfloat16 [1280, 4096], P(None, 'mp'), may hold values from -0.15625 to 0.15625
- w_gate: bfloat16 [4096, 7168], P('seq', 'mp'), may hold values from -0.09375 to 0.09375
- w_up: bfloat16 [4096, 7168], P('seq', 'mp'), may hold values from -0.09375 to 0.09375
- w_down: bfloat16 [7168, 4096], P('mp', 'seq'), may hold values from -0.0625 to 0.0625
- w_out: bfloat16 [4096, 1280], P('mp'), may hold values from -0.09375 to 0.09375
Outputs:
- decoded: bfloat16 [6144, 1280], P(('seq', 'mp'))
Inputs may be any that keep to these rules, and one draw needn't show every extreme that they name: `segments`: within each block of 192 bytes the patch number starts at 0 and rises by 0 or 1 from byte to byte. Block b belongs to device b, counted seq first; the blocks of the devices that share an mp index hold 128 patches together. A block holds at most 31 patches, and in every such set of blocks one holds exactly 31.
All inputs are finite; a program needn't handle non-finite values.
Results may differ from a plain program's by a relative error of at most 0.01.
Values may be sent and summed in bfloat16 or wider, within the bound.
No kernel may reach another device: no remote copies, remote signals or barrier semaphores. Data moves between devices by JAX's collectives and lax.ppermute only.
A program may use at most 128 MiB of HBM per device.

v0:
```python
import math

import jax
import jax.numpy as jnp
from jax import lax
from jax.sharding import PartitionSpec as P

HD = 128
D = 4096
RMEAN = 16


norm_epsilon = 1e-05


def body(enc_states, dec_states, segments, patch_keys, w_in, w_gate, w_up, w_down, w_out):
    byte_rows = segments.shape[0]
    most_patches = patch_keys.shape[0]
    width = enc_states.shape[1]
    seq_size = lax.axis_size("seq")
    slots = -(-most_patches // seq_size)
    local_ids = jnp.arange(most_patches, dtype=jnp.int32)
    member = segments[None, :] == local_ids[:, None]
    pool_sums = jnp.dot(member.astype(jnp.bfloat16), enc_states, preferred_element_type=jnp.float32)
    lengths = jnp.sum(member.astype(jnp.float32), axis=1)
    pooled = (pool_sums / jnp.maximum(lengths, 1.0)[:, None]).astype(jnp.bfloat16)
    patch_total = segments[byte_rows - 1] + 1
    all_counts = lax.all_gather(patch_total.reshape(1), "seq", axis=0, tiled=True)
    my_index = lax.axis_index("seq")
    source_ids = jnp.arange(seq_size, dtype=jnp.int32)
    starts = jnp.cumsum(all_counts) - all_counts
    my_start = jnp.sum(jnp.where(source_ids == my_index, starts, 0))
    owner_ids = jnp.arange(seq_size * slots, dtype=jnp.int32) // slots
    slot_ids = jnp.arange(seq_size * slots, dtype=jnp.int32) % slots
    send_patch = jnp.mod(owner_ids - my_start, seq_size) + slot_ids * seq_size
    send_live = send_patch < patch_total
    picker = ((send_patch[:, None] == local_ids[None, :]) & send_live[:, None]).astype(jnp.bfloat16)
    outgoing = jnp.dot(picker, pooled, preferred_element_type=jnp.float32).astype(jnp.bfloat16)
    incoming = lax.all_to_all(
        outgoing.reshape(seq_size, slots, width), "seq", split_axis=0, concat_axis=0, tiled=True
    )
    source_start = jnp.repeat(starts, slots)
    source_total = jnp.repeat(all_counts, slots)
    recv_patch = jnp.mod(my_index - source_start, seq_size) + slot_ids * seq_size
    recv_live = recv_patch < source_total
    recv_place = (source_start + recv_patch) // seq_size
    owned_ids = jnp.arange(RMEAN, dtype=jnp.int32)
    placer = ((recv_place[None, :] == owned_ids[:, None]) & recv_live[None, :]).astype(jnp.bfloat16)
    owned = jnp.dot(
        placer, incoming.reshape(seq_size * slots, width), preferred_element_type=jnp.float32
    ).astype(jnp.bfloat16)
    x_part = jnp.dot(
        lax.all_gather(owned, "mp", axis=0, tiled=True), w_in, preferred_element_type=jnp.float32
    ).astype(jnp.bfloat16)
    part_wide = x_part.astype(jnp.float32)
    square_sum = lax.psum(jnp.sum(part_wide * part_wide, axis=1, keepdims=True), "mp")
    normed_part = (part_wide * lax.rsqrt(square_sum / D + norm_epsilon)).astype(jnp.bfloat16)
    normed = lax.all_gather(normed_part, "mp", axis=1, tiled=True)
    gate_next = jnp.dot(
        normed,
        lax.all_gather(w_gate, "seq", axis=0, tiled=True),
        preferred_element_type=jnp.float32,
    )
    up_next = jnp.dot(
        normed, lax.all_gather(w_up, "seq", axis=0, tiled=True), preferred_element_type=jnp.float32
    )
    hidden = (jax.nn.silu(gate_next) * up_next).astype(jnp.bfloat16)
    down_terms = jnp.dot(
        hidden,
        lax.all_gather(w_down, "seq", axis=1, tiled=True),
        preferred_element_type=jnp.float32,
    )
    down_part = lax.psum_scatter(
        down_terms.astype(jnp.bfloat16), "mp", scatter_dimension=1, tiled=True
    ).astype(jnp.float32)
    residual = (x_part.astype(jnp.float32) + down_part).astype(jnp.bfloat16)
    outputs = lax.psum_scatter(
        jnp.dot(residual, w_out, preferred_element_type=jnp.float32).astype(jnp.bfloat16),
        "mp",
        scatter_dimension=0,
        tiled=True,
    )
    backward = jnp.dot(jnp.transpose(placer), outputs, preferred_element_type=jnp.float32).astype(
        jnp.bfloat16
    )
    returned = lax.all_to_all(
        backward.reshape(seq_size, slots, width), "seq", split_axis=0, concat_axis=0, tiled=True
    )
    patch_values = jnp.dot(
        jnp.transpose(picker),
        returned.reshape(seq_size * slots, width),
        preferred_element_type=jnp.float32,
    ).astype(jnp.bfloat16)
    heads = width // HD
    queries = dec_states.reshape(byte_rows, heads, HD)
    keys_local = patch_keys.reshape(most_patches, heads, HD)
    values_local = patch_values.reshape(most_patches, heads, HD)
    scores = jnp.einsum(
        "bhd,jhd->hbj", queries, keys_local, preferred_element_type=jnp.float32
    ) / math.sqrt(HD)
    allowed = local_ids[None, :] <= segments[:, None]
    scores = jnp.where(allowed[None, :, :], scores, -1e30)
    peak = jnp.max(scores, axis=2, keepdims=True)
    expon = jnp.exp(scores - peak)
    weights = (expon / jnp.sum(expon, axis=2, keepdims=True)).astype(jnp.bfloat16)
    mixed = jnp.einsum("hbj,jhd->bhd", weights, values_local, preferred_element_type=jnp.float32)
    return (dec_states.astype(jnp.float32) + mixed.reshape(byte_rows, width)).astype(jnp.bfloat16)


def solution(mesh):
    placed = (
        P(("seq", "mp"), None),
        P(("seq", "mp"), None),
        P(("seq", "mp")),
        P(("seq", "mp"), None),
        P(None, "mp"),
        P("seq", "mp"),
        P("seq", "mp"),
        P("mp", "seq"),
        P("mp", None),
    )
    return jax.shard_map(
        body, mesh=mesh, in_specs=placed, out_specs=P(("seq", "mp"), None), check_vma=False
    )
```

profile of v0, /device:TPU:0, one launch (start us, length us, event | category | flops | bytes accessed | tf_op | source)
XLA Modules:
  0.0 346.8 jit_solution(17798250296724276152)
XLA Ops:
  6.5 0.0 copy-start
  6.5 0.0 all-gather.4.cloned.1.call-start
  6.5 0.7 all-gather.4.cloned.1.call-update
  7.3 0.0 all-gather.6.cloned.1.call-start
  7.3 0.7 all-gather.6.cloned.1.call-update
  8.0 0.0 all-gather.8.cloned.1.call-start
  8.1 0.7 all-gather.8.cloned.1.call-update
  8.8 1.2 dynamic-slice
  10.0 2.0 slice_add_fusion
  12.0 9.5 %all-reduce = s32[8]{0:T(128)S(1)} all-reduce(s32[8]{0:T(128)S(1)} %get-tuple-element.10), channel_id=1, replica_groups=mesh['seq'=8,'mp'=4] {'seq'}, use_global_device_ids=true, to_apply=%add | all-reduce | flops 8 | bytes 64
  21.4 0.2 reduce-window.9
  21.6 0.6 fusion.37
  22.3 0.7 fusion.33
  22.9 1.3 broadcast_compare_fusion
  24.2 0.8 convert_reduce_fusion
  25.0 1.4 convolution_convert_fusion.4
  26.4 0.7 reshape.185
  27.1 3.4 all-to-all-start
  30.4 0.0 reduce-scatter.3.cloned.1.call-start
  30.5 0.1 broadcast_in_dim.19
  30.6 0.1 reshape.183
  30.7 0.1 broadcast_in_dim.20
  30.7 0.1 reshape.184
  30.8 5.7 %all-to-all-done = bf16[8,4,1280]{2,1,0:T(4,128)(2,1)S(1)} async-done(((bf16[8,4,1280]{2,1,0:T(4,128)(2,1)}), bf16[8,4,1280]{2,1,0:T(4,128)(2,1)S(1)}, u32[]{:S(2)}, u32[]{:S(2)}) %all-to-all-start) | async-done | bytes 81952 | tf_op jit(solution)/shard_map/all_to_all | solution.py:39
  36.6 0.1 convolution_convert_fusion.5
  36.7 13.7 %all_gather.19 = bf16[64,1280]{1,0:T(8,128)(2,1)S(1)} all-gather(bf16[16,1280]{1,0:T(8,128)(2,1)S(1)} %convolution_convert_fusion.5), channel_id=1, replica_groups=mesh['seq'=8,'mp'=4] {'mp'}, dimensions={0}, use_global_device_ids=true | all-gather | bytes 204800 | tf_op jit(solution)/shard_map/all_gather | solution.py:53
  50.5 3.2 multiply_reduce_fusion
  53.7 11.9 %psum.7 = f32[64,1]{0,1:T(1,128)S(1)} all-reduce(f32[64,1]{0,1:T(1,128)S(1)} %bitcast.31), channel_id=1, replica_groups=mesh['seq'=8,'mp'=4] {'mp'}, use_global_device_ids=true, to_apply=%region_4.5 | all-reduce | flops 64 | bytes 512 | tf_op jit(solution)/shard_map/psum | solution.py:56
  65.5 0.1 multiply_convert_fusion
  65.6 14.7 %all_gather.20 = bf16[64,4096]{1,0:T(8,128)(2,1)S(1)} all-gather(bf16[64,1024]{1,0:T(8,128)(2,1)S(1)} %multiply_convert_fusion), channel_id=1, replica_groups=mesh['seq'=8,'mp'=4] {'mp'}, dimensions={1}, use_global_device_ids=true | all-gather | bytes 655360 | tf_op jit(solution)/shard_map/all_gather | solution.py:58
  80.4 13.5 %all-gather.4.cloned.1.call-done = bf16[4096,1792]{1,0:T(8,128)(2,1)} async-done(((bf16[512,1792]{1,0:T(8,128)(2,1)}), bf16[4096,1792]{1,0:T(8,128)(2,1)}) %all-gather.4.cloned.1.call-update) | async-done | bytes 14680080 | tf_op jit(solution)/shard_map/all_gather | solution.py:61
  93.9 8.6 %fusion.46 = f32[64,1792]{1,0:T(8,128)} fusion(bf16[64,4096]{1,0:T(8,128)(2,1)S(1)} %all_gather.20, bf16[4096,1792]{1,0:T(8,128)(2,1)} %all-gather.4.cloned.1.call-done), kind=kOutput, calls=%fused_computation.82 | convolution fusion | flops 939524096 | bytes 15663104 | tf_op jit(solution)/shard_map/dot_general | solution.py:59
  102.4 0.0 copy-start.2
  102.4 0.0 copy-start.1
  102.4 74.3 %all-gather.6.cloned.1.call-done = bf16[4096,1792]{1,0:T(8,128)(2,1)} async-done(((bf16[512,1792]{1,0:T(8,128)(2,1)}), bf16[4096,1792]{1,0:T(8,128)(2,1)}) %all-gather.6.cloned.1.call-update) | async-done | bytes 14680080 | tf_op jit(solution)/shard_map/all_gather | solution.py:65
  176.8 85.7 %all-gather.8.cloned.1.call-done = bf16[1792,4096]{1,0:T(8,128)(2,1)} async-done(((bf16[1792,512]{1,0:T(8,128)(2,1)}), bf16[1792,4096]{1,0:T(8,128)(2,1)}) %all-gather.8.cloned.1.call-update) | async-done | bytes 14680080 | tf_op jit(solution)/shard_map/all_gather | solution.py:70
  262.5 15.2 %convolution_convert_fusion = bf16[64,4096]{1,0:T(8,128)(2,1)} fusion(bf16[1792,4096]{1,0:T(8,128)(2,1)} %all-gather.8.cloned.1.call-done, bf16[64,4096]{1,0:T(8,128)(2,1)S(1)} %all_gather.20, bf16[4096,1792]{1,0:T(8,128)(2,1)} %all-gather.6.cloned.1.call-done, f32[64,1792]{1,0:T(8,128)} %fusion.46), kind=kOutput, calls=%fused_computation.1 | convolution fusion | flops 1879998464 | bytes 30867456 | tf_op jit(solution)/shard_map/dot_general | solution.py:68
  277.7 0.0 reduce-scatter.3.cloned.1.call-update
  277.7 0.0 reduce-scatter.5.cloned.1.call-start
  277.8 21.7 %reduce-scatter.3.cloned.1.call-done = bf16[64,1024]{1,0:T(8,128)(2,1)} async-done(((bf16[64,4096]{1,0:T(8,128)(2,1)}), bf16[64,1024]{1,0:T(8,128)(2,1)}) %reduce-scatter.3.cloned.1.call-update) | async-done | bytes 131088 | tf_op jit(solution)/shard_map/reduce_scatter | solution.py:73
  299.5 0.0 copy-done
  299.5 2.1 convolution_convert_fusion.1
  301.6 0.0 reduce-scatter.5.cloned.1.call-update
  301.7 0.0 copy-done.2
  301.7 1.3 copy.27
  303.0 0.0 copy-done.1
  303.0 0.1 reshape.191
  303.1 0.9 fusion.5
  304.0 15.4 %reduce-scatter.5.cloned.1.call-done = bf16[16,1280]{1,0:T(8,128)(2,1)} async-done(((bf16[64,1280]{1,0:T(8,128)(2,1)}), bf16[16,1280]{1,0:T(8,128)(2,1)}) %reduce-scatter.5.cloned.1.call-update) | async-done | bytes 40976 | tf_op jit(solution)/shard_map/reduce_scatter | solution.py:77
  319.5 1.0 convolution_convert_fusion.3
  320.4 0.7 reshape.187
  321.1 3.7 %all-to-all-start.1 = ((bf16[8,4,1280]{2,1,0:T(4,128)(2,1)}), bf16[8,4,1280]{2,1,0:T(4,128)(2,1)S(1)}, u32[]{:S(2)}, u32[]{:S(2)}) async-start(bf16[8,4,1280]{2,1,0:T(4,128)(2,1)} %reshape.187), calls=%async_computation.3 | async-start | bytes 163840 | tf_op jit(solution)/shard_map/all_to_all | solution.py:86
  324.8 1.2 fusion.45
  325.9 3.9 %all-to-all-done.1 = bf16[8,4,1280]{2,1,0:T(4,128)(2,1)S(1)} async-done(((bf16[8,4,1280]{2,1,0:T(4,128)(2,1)}), bf16[8,4,1280]{2,1,0:T(4,128)(2,1)S(1)}, u32[]{:S(2)}, u32[]{:S(2)}) %all-to-all-start.1) | async-done | bytes 81952 | tf_op jit(solution)/shard_map/all_to_all | solution.py:86
  329.9 0.3 convolution_convert_fusion.2
  330.2 0.1 reshape.189
  330.3 2.4 convolution_bitcast_fusion
  332.7 2.7 copy.31
  335.4 2.7 copy.32
  338.0 2.2 add_convert_fusion
  (8 shorter events, 0.1 us)
Async XLA Ops:
  6.5 293.0 %copy-start = (bf16[1024,1280]{1,0:T(8,128)(2,1)S(1)}, bf16[1024,1280]{1,0:T(8,128)(2,1)}, u32[]{:S(2)}) copy-start(bf16[1024,1280]{1,0:T(8,128)(2,1)} %param.17) | copy-start | bytes 7864324
  6.5 87.3 %all-gather.4.cloned.1.call-start = ((), (), s32[]{:S(2)}) async-start(), calls=%async_computation.4 | async-start | bytes 16515072 | tf_op jit(solution)/shard_map/all_gather | solution.py:61
  7.3 169.5 %all-gather.6.cloned.1.call-start = ((), (), s32[]{:S(2)}) async-start(), calls=%async_computation.5 | async-start | bytes 16515072 | tf_op jit(solution)/shard_map/all_gather | solution.py:65
  8.0 254.5 %all-gather.8.cloned.1.call-start = ((), (), s32[]{:S(2)}) async-start(), calls=%async_computation.6 | async-start | bytes 16515072 | tf_op jit(solution)/shard_map/all_gather | solution.py:70
  27.1 9.5 %all-to-all-start = ((bf16[8,4,1280]{2,1,0:T(4,128)(2,1)}), bf16[8,4,1280]{2,1,0:T(4,128)(2,1)S(1)}, u32[]{:S(2)}, u32[]{:S(2)}) async-start(bf16[8,4,1280]{2,1,0:T(4,128)(2,1)} %reshape.185), calls=%async_computation | async-start | bytes 163840 | tf_op jit(solution)/shard_map/all_to_all | solution.py:39
  30.4 269.1 %reduce-scatter.3.cloned.1.call-start = ((), (), s32[]{:S(2)}) async-start(), calls=%async_computation.7 | async-start | bytes 655360 | tf_op jit(solution)/shard_map/reduce_scatter | solution.py:73
  102.4 199.2 %copy-start.2 = (s32[192]{0:T(256)S(1)}, s32[192]{0:T(256)}, u32[]{:S(2)}) copy-start(s32[192]{0:T(256)} %param.11) | copy-start | bytes 2308
  102.4 200.5 %copy-start.1 = (bf16[31,1280]{1,0:T(8,128)(2,1)S(1)}, bf16[31,1280]{1,0:T(8,128)(2,1)}, u32[]{:S(2)}) copy-start(bf16[31,1280]{1,0:T(8,128)(2,1)} %param.12) | copy-start | bytes 238084
  277.7 41.7 %reduce-scatter.5.cloned.1.call-start = ((), (), s32[]{:S(2)}) async-start(), calls=%async_computation.8 | async-start | bytes 204800 | tf_op jit(solution)/shard_map/reduce_scatter | solution.py:77
  321.1 8.8 %all-to-all-start.1 = ((bf16[8,4,1280]{2,1,0:T(4,128)(2,1)}), bf16[8,4,1280]{2,1,0:T(4,128)(2,1)S(1)}, u32[]{:S(2)}, u32[]{:S(2)}) async-start(bf16[8,4,1280]{2,1,0:T(4,128)(2,1)} %reshape.187), calls=%async_computation.3 | async-start | bytes 163840 | tf_op jit(solution)/shard_map/all_to_all | solution.py:86
Sparse Core Ops, SparseCore 0:
  9.3 84.5 all-gather.3
  95.7 80.9 all-gather.5
  178.7 83.8 all-gather.7
  277.9 21.6 reduce-scatter.2
  301.8 17.6 reduce-scatter.4
where the time goes:
time: 348 us; the launch traced here: 347 us
  waiting for transfers between devices  223 us (64%)
  blocking collectives  49.8 us (14%)
  matrix products  35.3 us (10%)
  between operations  13.3 us (4%)
  local copies, waits for them, and re-layouts  9.72 us (3%)
  other arithmetic  9.05 us (3%)
  starting transfers between devices  7.17 us (2%)
    all_gather x1, waiting for transfers between devices, body(): lax.all_gather(w_down, 'seq', axis=1, tiled=True)  85.7 us
    all_gather x1, waiting for transfers between devices, body(): lax.all_gather(w_up, 'seq', axis=0, tiled=True)  74.3 us
    reduce_scatter x1, waiting for transfers between devices, body(): lax.psum_scatter(down_terms.astype(jnp.bfloat16), 'mp', scatter_dimension...  21.7 us
    reduce_scatter x1, waiting for transfers between devices, body(): lax.psum_scatter(jnp.dot(residual, w_out, preferred_element_type=jnp.floa...  15.4 us
    dot_general x1, matrix products, body(): jnp.dot(hidden, lax.all_gather(w_down, 'seq', axis=1, tiled=True), prefer...  15.2 us
    all_gather x1, blocking collectives, body(): normed = lax.all_gather(normed_part, 'mp', axis=1, tiled=True)  14.7 us
    all_gather x1, blocking collectives, body(): lax.all_gather(owned, 'mp', axis=0, tiled=True)  13.7 us
    all_gather x1, waiting for transfers between devices, body(): lax.all_gather(w_gate, 'seq', axis=0, tiled=True)  13.5 us
  transfers between devices with their start and end apart: 7, of which 7 were waited for; matrix products, arithmetic and copies ran while one was open for 7% of the time, Pallas kernels for 0%

commit v1 on v0

v1 whole, which is shorter than its diff:
```python
import functools
import math

import jax
import jax.numpy as jnp
from jax import lax
from jax.experimental import pallas as pl
from jax.experimental.pallas import tpu as pltpu
from jax.sharding import PartitionSpec as P

HD = 128
ROWS = 16
norm_epsilon = 1e-05

VMEM = pl.BlockSpec(memory_space=pltpu.VMEM)
SMEM = pl.BlockSpec(memory_space=pltpu.SMEM)
BF16 = jnp.bfloat16
F32 = jnp.float32


def shape(dims, dtype=BF16):
    return jax.ShapeDtypeStruct(tuple(dims), dtype)


def call(kernel, out, ids, *arrays, scratch=(), flops=0, limit=40):
    moved = sum(a.size * a.dtype.itemsize for a in arrays)
    moved += sum(math.prod(o.shape) * o.dtype.itemsize for o in jax.tree.leaves(out))
    return pl.pallas_call(
        kernel,
        out_shape=out,
        in_specs=[SMEM] + [VMEM] * len(arrays),
        out_specs=jax.tree.map(lambda _: VMEM, out),
        scratch_shapes=list(scratch),
        compiler_params=pltpu.CompilerParams(vmem_limit_bytes=limit * 1024 * 1024),
        cost_estimate=pl.CostEstimate(flops=int(flops), bytes_accessed=int(moved), transcendentals=0),
    )(ids, *arrays)


def dot(a, b):
    return jnp.dot(a, b, preferred_element_type=F32)


def pool_kernel(slots, ids, seg, enc, out):
    patch = lax.broadcasted_iota(jnp.int32, (slots, seg.shape[1]), 0)
    member = seg[...] == patch
    lengths = jnp.sum(member.astype(F32), axis=1, keepdims=True)
    sums = dot(member.astype(BF16), enc[...])
    pooled = sums / jnp.maximum(lengths, 1.0)
    total = jnp.max(seg[...].astype(F32)) + 1.0
    row = lax.broadcasted_iota(jnp.int32, pooled.shape, 0)
    out[...] = jnp.where(row == slots - 1, total, pooled).astype(BF16)


def pack_kernel(chips, slots, ids, *refs):
    mine, theirs = refs[:chips], refs[chips]
    out, start_out, packed = refs[chips + 1 :]
    q, c = ids[0], ids[1]
    blocks = 2 * chips
    lanes = blocks * slots
    for k in range(chips):
        packed[k * slots : (k + 1) * slots, :] = mine[k][...]
    packed[chips * slots :, :] = theirs[...]
    lane = lax.broadcasted_iota(jnp.int32, (1, lanes), 1)
    block = lane // slots
    patch = lane - block * slots
    part = block // chips
    place = 2 * ((block - part * chips) ^ q) + (part ^ c)
    start = jnp.zeros((1, lanes), F32)
    total = jnp.zeros((1, lanes), F32)
    own = jnp.zeros((1, lanes), F32)
    for b in range(blocks):
        count = packed[(b + 1) * slots - 1 : (b + 1) * slots, 0:lanes].astype(F32)
        where = 2 * ((b % chips) ^ q) + ((b // chips) ^ c)
        start += jnp.where(place > where, count, 0.0)
        total += jnp.where(block == b, count, 0.0)
        own += jnp.where(2 * q + c > where, count, 0.0)
    wanted = (2 * q + c) * ROWS + lax.broadcasted_iota(jnp.int32, (ROWS, lanes), 0)
    found = (start.astype(jnp.int32) + patch == wanted) & (patch < total.astype(jnp.int32))
    out[...] = dot(found.astype(BF16), packed[...]).astype(BF16)
    start_out[...] = jnp.broadcast_to(own[:, 0:HD].astype(jnp.int32), start_out.shape)


def x_kernel(groups, ids, *refs):
    pieces, w, out, packed = refs[:groups], refs[groups], refs[groups + 1], refs[groups + 2]
    for k in range(groups):
        packed[ids[2] ^ k] = pieces[k][...]
    rows = packed[...].reshape(groups * ROWS, packed.shape[2])
    out[...] = dot(rows, w[...]).astype(BF16)


def norm_kernel(groups, chips, ids, *refs):
    pieces, outs, units = refs[:groups], refs[groups : groups + chips], refs[groups + chips]
    q, c, z = ids[0], ids[1], ids[2]
    unit = units.shape[2]
    per = 2 * chips // groups
    squares = jnp.zeros((units.shape[1], 1), F32)
    for k in range(groups):
        wide = pieces[k][...].astype(F32)
        squares += jnp.sum(wide * wide, axis=1, keepdims=True)
        for u in range(per):
            units[(z ^ k) * per + u] = pieces[k][:, u * unit : (u + 1) * unit]
    scale = lax.rsqrt(squares / (2 * chips * unit) + norm_epsilon)
    for k in range(chips):
        for h in range(2):
            piece = units[2 * (q ^ k) + (c ^ h)].astype(F32)
            outs[k][h] = (piece * scale).astype(BF16)


def gate_kernel(count, ids, *refs):
    pieces = refs[:count]
    gate_a, gate_b, up_a, up_b = refs[count : count + 4]
    outs = refs[count + 4 :]
    rows, wide = pieces[0].shape[1], gate_a.shape[1]
    a = jnp.concatenate([p[0] for p in pieces], axis=0)
    b = jnp.concatenate([p[1] for p in pieces], axis=0)
    gate = (dot(a, gate_a[...]) + dot(b, gate_b[...])).astype(BF16)
    for k in range(count):
        outs[k][:, :wide] = gate[k * rows : (k + 1) * rows]
    up = (dot(a, up_a[...]) + dot(b, up_b[...])).astype(BF16)
    for k in range(count):
        outs[k][:, wide:] = up[k * rows : (k + 1) * rows]


def hidden_kernel(ids, *refs):
    pieces, out = refs[:-1], refs[-1]
    wide = out.shape[1]
    gate = sum(p[:, :wide].astype(F32) for p in pieces)
    up = sum(p[:, wide:].astype(F32) for p in pieces)
    out[...] = (gate / (1.0 + jnp.exp(-gate)) * up).astype(BF16)


def down_kernel(count, ids, *refs):
    pieces, w_a, w_b, outs = refs[:count], refs[count], refs[count + 1], refs[count + 2 :]
    rows = pieces[0].shape[0]
    a = jnp.concatenate([p[...] for p in pieces], axis=0)
    for h, w in enumerate((w_a, w_b)):
        y = dot(a, w[...]).astype(BF16)
        for k in range(count):
            outs[k][h] = y[k * rows : (k + 1) * rows]


def regroup_kernel(chips, groups, ids, *refs):
    pieces, outs, units = refs[:chips], refs[chips : chips + groups], refs[chips + groups]
    q, c, z = ids[0], ids[1], ids[2]
    unit = units.shape[2]
    per = 2 * chips // groups
    for k in range(chips):
        for h in range(2):
            units[2 * (q ^ k) + (c ^ h)] = pieces[k][h]
    for k in range(groups):
        for u in range(per):
            outs[k][:, u * unit : (u + 1) * unit] = units[(z ^ k) * per + u]


def out_kernel(groups, ids, *refs):
    pieces, x, w, outs, rows = refs[:groups], refs[groups], refs[groups + 1], refs[groups + 2 : -1], refs[-1]
    down = sum(p[...].astype(F32) for p in pieces)
    residual = (x[...].astype(F32) + down).astype(BF16)
    y = dot(residual, w[...]).astype(BF16)
    rows[...] = y.reshape(rows.shape)
    for k in range(groups):
        outs[k][...] = rows[ids[2] ^ k]


def add_kernel(ids, *refs):
    refs[-1][...] = sum(p[...].astype(F32) for p in refs[:-1]).astype(BF16)


def weights_kernel(ids, seg, dec, keys, out):
    slots = keys.shape[0]
    patch = lax.broadcasted_iota(jnp.int32, (dec.shape[0], slots), 1)
    allowed = patch <= seg[...]
    for h in range(out.shape[0]):
        part = slice(h * HD, (h + 1) * HD)
        scores = lax.dot_general(dec[:, part], keys[:, part], (((1,), (1,)), ((), ())), preferred_element_type=F32)
        scores = jnp.where(allowed, scores / math.sqrt(HD), -1e30)
        expon = jnp.exp(scores - jnp.max(scores, axis=1, keepdims=True))
        out[h] = (expon / jnp.sum(expon, axis=1, keepdims=True)).astype(BF16)


def mix_kernel(chips, ids, *refs):
    mine, theirs = refs[:chips], refs[chips]
    start, weights, dec, out, rows = refs[chips + 1 :]
    q, c = ids[0], ids[1]
    for k in range(chips):
        rows[2 * (q ^ k) + c] = mine[k][...]
        rows[2 * (q ^ k) + 1 - c] = theirs[k]
    every = rows[...].reshape(2 * chips * ROWS, rows.shape[2])
    slots = weights.shape[2]
    patch = lax.broadcasted_iota(jnp.int32, (slots, every.shape[0]), 0)
    position = lax.broadcasted_iota(jnp.int32, (slots, every.shape[0]), 1)
    found = (position - start[0:1, 0:1] == patch).astype(BF16)
    values = dot(found, every).astype(BF16)
    for h in range(weights.shape[0]):
        part = slice(h * HD, (h + 1) * HD)
        out[:, part] = (dec[:, part].astype(F32) + dot(weights[h], values[:, part])).astype(BF16)


def body(enc_states, dec_states, segments, patch_keys, w_in, w_gate, w_up, w_down, w_out):
    seq, groups = lax.axis_size("seq"), lax.axis_size("mp")
    chips = seq // 2
    bytes_, width = enc_states.shape
    slots = patch_keys.shape[0] + 1
    heads = width // HD
    rows = groups * ROWS
    wide = w_in.shape[1]
    unit = w_gate.shape[0]
    ffw = w_gate.shape[1]
    index = lax.axis_index("seq")
    ids = jnp.stack([index // 2, index % 2, lax.axis_index("mp")]).astype(jnp.int32)

    def sibling(a):
        return lax.ppermute(a, "seq", [(i, i ^ 1) for i in range(seq)])

    def chip(a, k):
        return lax.ppermute(a, "seq", [(i, i ^ (2 * k)) for i in range(seq)])

    def plane(a, k):
        return lax.ppermute(a, "mp", [(i, i ^ k) for i in range(groups)])

    pooled = call(functools.partial(pool_kernel, slots), shape((slots, width)), ids, segments.reshape(1, bytes_), enc_states)
    gathered = [pooled] + [chip(pooled, k) for k in range(1, chips)]
    theirs = sibling(jnp.concatenate(gathered, axis=0))
    packed, start = call(
        functools.partial(pack_kernel, chips, slots),
        (shape((ROWS, width)), shape((8, HD), jnp.int32)),
        ids,
        *gathered,
        theirs,
        scratch=[pltpu.VMEM((seq * slots, width), BF16)],
    )
    gate_b, up_b, down_b = sibling(w_gate), sibling(w_up), sibling(w_down)
    pieces = [packed] + [plane(packed, k) for k in range(1, groups)]
    x = call(
        functools.partial(x_kernel, groups),
        shape((rows, wide)),
        ids,
        *pieces,
        w_in,
        scratch=[pltpu.VMEM((groups, ROWS, width), BF16)],
        flops=2 * rows * width * wide,
    )
    pieces = [x] + [plane(x, k) for k in range(1, groups)]
    normed = call(
        functools.partial(norm_kernel, groups, chips),
        [shape((2, rows, unit)) for _ in range(chips)],
        ids,
        *pieces,
        scratch=[pltpu.VMEM((seq, rows, unit), BF16)],
    )

    def gate(pieces):
        return call(
            functools.partial(gate_kernel, len(pieces)),
            [shape((rows, 2 * ffw)) for _ in pieces],
            ids,
            *pieces,
            w_gate,
            gate_b,
            w_up,
            up_b,
            flops=8 * len(pieces) * rows * unit * ffw,
        )

    arrived = [chip(normed[k], k) for k in range(1, chips)]
    partial = gate([normed[0]]) + gate(arrived)
    partial = [partial[0]] + [chip(partial[k], k) for k in range(1, chips)]
    hidden = call(hidden_kernel, shape((rows, ffw)), ids, *partial)

    def down(pieces):
        return call(
            functools.partial(down_kernel, len(pieces)),
            [shape((2, rows, unit)) for _ in pieces],
            ids,
            *pieces,
            w_down,
            down_b,
            flops=4 * len(pieces) * rows * unit * ffw,
        )

    arrived = [chip(hidden, k) for k in range(1, chips)]
    columns = down([hidden]) + down(arrived)
    columns = [columns[0]] + [chip(columns[k], k) for k in range(1, chips)]
    slices = call(
        functools.partial(regroup_kernel, chips, groups),
        [shape((rows, wide)) for _ in range(groups)],
        ids,
        *columns,
        scratch=[pltpu.VMEM((seq, rows, unit), BF16)],
    )
    slices = [slices[0]] + [plane(slices[k], k) for k in range(1, groups)]
    outs = call(
        functools.partial(out_kernel, groups),
        [shape((ROWS, width)) for _ in range(groups)],
        ids,
        *slices,
        x,
        w_out,
        scratch=[pltpu.VMEM((groups, ROWS, width), BF16)],
        flops=2 * rows * width * wide,
    )
    outs = [outs[0]] + [plane(outs[k], k) for k in range(1, groups)]
    outputs = call(add_kernel, shape((ROWS, width)), ids, *outs)
    outputs = [outputs] + [chip(outputs, k) for k in range(1, chips)]
    theirs = sibling(jnp.stack(outputs))
    keys = jnp.pad(patch_keys, ((0, 1), (0, 0)))
    weights = call(weights_kernel, shape((heads, bytes_, slots)), ids, segments.reshape(bytes_, 1), dec_states, keys)
    return call(
        functools.partial(mix_kernel, chips),
        shape((bytes_, width)),
        ids,
        *outputs,
        theirs,
        start,
        weights,
        dec_states,
        scratch=[pltpu.VMEM((seq, ROWS, width), BF16)],
    )


def solution(mesh):
    placed = (
        P(("seq", "mp"), None),
        P(("seq", "mp"), None),
        P(("seq", "mp")),
        P(("seq", "mp"), None),
        P(None, "mp"),
        P("seq", "mp"),
        P("seq", "mp"),
        P("mp", "seq"),
        P("mp", None),
    )
    return jax.shard_map(
        body, mesh=mesh, in_specs=placed, out_specs=P(("seq", "mp"), None), check_vma=False
    )
```

time: 348 us -> 134 us (0.39)
  waiting for transfers between devices: 223 us -> 61.3 us
  blocking collectives: 49.8 us -> 0 us
  starting transfers between devices: 7.17 us -> 49.7 us
  matrix products: 35.3 us -> 0 us
  Pallas kernels: 0 us -> 18.6 us
  between operations: 13.3 us -> 0.26 us
  other arithmetic: 9.05 us -> 0.12 us
  local copies, waits for them, and re-layouts: 9.72 us -> 3.61 us
    all_gather x3 -> x0, waiting for transfers between devices: 174 us -> none  [the longest x1 85.7 us: body(): lax.all_gather(w_down, 'seq', axis=1, tiled=True)]
    ppermute x0 -> x35, waiting for transfers between devices: none -> 61.3 us  [the longest x18 42.4 us: chip(): return lax.ppermute(a, 'seq', [(i, i ^ 2 * k) for i in range(seq)])]
    ppermute x0 -> x35, starting transfers between devices: none -> 49.7 us  [the longest x12 26.2 us: plane(): return lax.ppermute(a, 'mp', [(i, i ^ k) for i in range(groups)])]
    reduce_scatter x2 -> x0, waiting for transfers between devices: 37.2 us -> none  [the longest x1 21.7 us: body(): lax.psum_scatter(down_terms.astype(jnp.bfloat16), 'mp', scatter_dimension...]
    dot_general x10 -> x0, matrix products: 35.3 us -> none  [the longest x1 15.2 us: body(): jnp.dot(hidden, lax.all_gather(w_down, 'seq', axis=1, tiled=True), prefer...]
    all_gather x2 -> x0, blocking collectives: 28.5 us -> none  [the longest x1 14.7 us: body(): normed = lax.all_gather(normed_part, 'mp', axis=1, tiled=True)]
    pallas_call x0 -> x14, Pallas kernels: none -> 18.6 us  [call(): pl.pallas_call(kernel, out_shape=out, in_specs=[SMEM] + [VMEM] * len(arra...]
    psum x1 -> x0, blocking collectives: 11.9 us -> none  [body(): lax.psum(jnp.sum(part_wide * part_wide, axis=1, keepdims=True), 'mp')]
  transfers between devices with their start and end apart: 7 -> 35, of which waited for: 7 -> 23; matrix products, arithmetic and copies ran while one was open for 7% -> 0% of each run, Pallas kernels for 0% -> 10%
where the time goes in v1:
time: 134 us
  waiting for transfers between devices  61.3 us (46%)
  starting transfers between devices  49.7 us (37%)
  Pallas kernels  18.6 us (14%)
  local copies, waits for them, and re-layouts  3.61 us (3%)
    ppermute x18, waiting for transfers between devices, chip(): return lax.ppermute(a, 'seq', [(i, i ^ 2 * k) for i in range(seq)])  42.4 us
    ppermute x12, starting transfers between devices, plane(): return lax.ppermute(a, 'mp', [(i, i ^ k) for i in range(groups)])  26.2 us
    ppermute x18, starting transfers between devices, chip(): return lax.ppermute(a, 'seq', [(i, i ^ 2 * k) for i in range(seq)])  22.9 us
    pallas_call x14, Pallas kernels, call(): pl.pallas_call(kernel, out_shape=out, in_specs=[SMEM] + [VMEM] * len(arra...  18.6 us
    ppermute x12, waiting for transfers between devices, plane(): return lax.ppermute(a, 'mp', [(i, i ^ k) for i in range(groups)])  17.3 us
    unnamed x20, local copies, waits for them, and re-layouts  3.48 us
  transfers between devices with their start and end apart: 35, of which 23 were waited for; matrix products, arithmetic and copies ran while one was open for 0% of the time, Pallas kernels for 10%

profile of v1, /device:TPU:0, one launch (start us, length us, event | category | flops | bytes accessed | tf_op | source)
XLA Modules:
  0.0 133.6 jit_solution(14487833878195455830)
XLA Ops:
  0.6 1.0 copy-done.6
  1.6 0.7 copy-done.7
  2.3 0.8 shard_map.91.refs_0_
  3.1 3.0 %collective-permute-start = (bf16[32,1280]{1,0:T(8,128)(2,1)S(1)}, bf16[32,1280]{1,0:T(8,128)(2,1)S(1)}, u32[]{:S(2)}, u32[]{:S(2)}) collective-permute-start(bf16[32,1280]{1,0:T(8,128)(2,1)S(1)} %shard_map.91.refs_0_), channel_id=1, source_target_pairs={{0,8},{4,12},{8,0},{12,4},{16,24},{20,28},{24,16},{28,20},{1,9},{5... | collective-permute-start | bytes 245768 | tf_op jit(solution)/shard_map/ppermute | solution.py:216
  6.0 1.5 %collective-permute-start.1 = (bf16[32,1280]{1,0:T(8,128)(2,1)S(1)}, bf16[32,1280]{1,0:T(8,128)(2,1)S(1)}, u32[]{:S(2)}, u32[]{:S(2)}) collective-permute-start(bf16[32,1280]{1,0:T(8,128)(2,1)S(1)} %shard_map.91.refs_0_), channel_id=1, source_target_pairs={{0,16},{4,20},{8,24},{12,28},{16,0},{20,4},{24,8},{28,12},{1,17},{... | collective-permute-start | bytes 245768 | tf_op jit(solution)/shard_map/ppermute | solution.py:216
  7.6 1.1 collective-permute-done.refs_1_
  8.7 1.8 %collective-permute-done.1.refs_2_ = bf16[32,1280]{1,0:T(8,128)(2,1)S(1)} collective-permute-done((bf16[32,1280]{1,0:T(8,128)(2,1)S(1)}, bf16[32,1280]{1,0:T(8,128)(2,1)S(1)}, u32[]{:S(2)}, u32[]{:S(2)}) %collective-permute-start.1) | collective-permute-done | bytes 81952 | tf_op jit(solution)/shard_map/ppermute | solution.py:216
  10.5 2.4 %collective-permute-done.2.refs_3_ = bf16[32,1280]{1,0:T(8,128)(2,1)S(1)} collective-permute-done((bf16[32,1280]{1,0:T(8,128)(2,1)S(1)}, bf16[32,1280]{1,0:T(8,128)(2,1)S(1)}, u32[]{:S(2)}, u32[]{:S(2)}) %collective-permute-start.2) | collective-permute-done | bytes 81952 | tf_op jit(solution)/shard_map/ppermute | solution.py:216
  13.0 1.6 %collective-permute-done.3.refs_4_ = bf16[128,1280]{1,0:T(8,128)(2,1)S(1)} collective-permute-done((bf16[128,1280]{1,0:T(8,128)(2,1)S(1)}, bf16[128,1280]{1,0:T(8,128)(2,1)S(1)}, u32[]{:S(2)}, u32[]{:S(2)}) %collective-permute-start.3) | collective-permute-done | bytes 327712 | tf_op jit(solution)/shard_map/ppermute | solution.py:213
  14.6 0.8 shard_map.92
  15.4 1.6 %collective-permute-start.4 = (bf16[16,1280]{1,0:T(8,128)(2,1)S(1)}, bf16[16,1280]{1,0:T(8,128)(2,1)S(1)}, u32[]{:S(2)}, u32[]{:S(2)}) collective-permute-start(bf16[16,1280]{1,0:T(8,128)(2,1)S(1)} %get-tuple-element.25.refs_0_), channel_id=1, source_target_pairs={{0,1},{1,0},{2,3},{3,2},{4,5},{5,4},{6,7},{7,6},{8,9},{9,8},{10,11... | collective-permute-start | bytes 122888 | tf_op jit(solution)/shard_map/ppermute | solution.py:219
  17.0 2.6 %collective-permute-start.5 = (bf16[16,1280]{1,0:T(8,128)(2,1)S(1)}, bf16[16,1280]{1,0:T(8,128)(2,1)S(1)}, u32[]{:S(2)}, u32[]{:S(2)}) collective-permute-start(bf16[16,1280]{1,0:T(8,128)(2,1)S(1)} %get-tuple-element.25.refs_0_), channel_id=1, source_target_pairs={{0,2},{1,3},{2,0},{3,1},{4,6},{5,7},{6,4},{7,5},{8,10},{9,11},{10,... | collective-permute-start | bytes 122888 | tf_op jit(solution)/shard_map/ppermute | solution.py:219
  19.6 3.9 %collective-permute-start.6 = (bf16[16,1280]{1,0:T(8,128)(2,1)S(1)}, bf16[16,1280]{1,0:T(8,128)(2,1)S(1)}, u32[]{:S(2)}, u32[]{:S(2)}) collective-permute-start(bf16[16,1280]{1,0:T(8,128)(2,1)S(1)} %get-tuple-element.25.refs_0_), channel_id=1, source_target_pairs={{0,3},{1,2},{2,1},{3,0},{4,7},{5,6},{6,5},{7,4},{8,11},{9,10},{10,... | collective-permute-start | bytes 122888 | tf_op jit(solution)/shard_map/ppermute | solution.py:219
  23.5 2.0 %collective-permute-done.6.refs_3_ = bf16[16,1280]{1,0:T(8,128)(2,1)S(1)} collective-permute-done((bf16[16,1280]{1,0:T(8,128)(2,1)S(1)}, bf16[16,1280]{1,0:T(8,128)(2,1)S(1)}, u32[]{:S(2)}, u32[]{:S(2)}) %collective-permute-start.6) | collective-permute-done | bytes 40992 | tf_op jit(solution)/shard_map/ppermute | solution.py:219
  25.5 1.7 %copy-done.3 = bf16[1280,1024]{1,0:T(8,128)(2,1)S(1)} copy-done((bf16[1280,1024]{1,0:T(8,128)(2,1)S(1)}, bf16[1280,1024]{1,0:T(8,128)(2,1)}, u32[]{:S(2)}) %copy-start.3) | copy-done | bytes 2621464
  27.2 1.1 shard_map.93.refs_0_.refs_4_
  28.4 4.4 %collective-permute-start.8 = (bf16[64,1024]{1,0:T(8,128)(2,1)S(1)}, bf16[64,1024]{1,0:T(8,128)(2,1)S(1)}, u32[]{:S(2)}, u32[]{:S(2)}) collective-permute-start(bf16[64,1024]{1,0:T(8,128)(2,1)S(1)} %shard_map.93.refs_0_.refs_4_), channel_id=1, source_target_pairs={{0,2},{1,3},{2,0},{3,1},{4,6},{5,7},{6,4},{7,5},{8,10},{9,11},{10,... | collective-permute-start | bytes 393224 | tf_op jit(solution)/shard_map/ppermute | solution.py:219
  32.8 0.7 collective-permute-done.7.refs_1_
  33.4 4.2 %collective-permute-start.9 = (bf16[64,1024]{1,0:T(8,128)(2,1)S(1)}, bf16[64,1024]{1,0:T(8,128)(2,1)S(1)}, u32[]{:S(2)}, u32[]{:S(2)}) collective-permute-start(bf16[64,1024]{1,0:T(8,128)(2,1)S(1)} %shard_map.93.refs_0_.refs_4_), channel_id=1, source_target_pairs={{0,3},{1,2},{2,1},{3,0},{4,7},{5,6},{6,5},{7,4},{8,11},{9,10},{10,... | collective-permute-start | bytes 393224 | tf_op jit(solution)/shard_map/ppermute | solution.py:219
  37.6 3.3 %collective-permute-done.8.refs_2_ = bf16[64,1024]{1,0:T(8,128)(2,1)S(1)} collective-permute-done((bf16[64,1024]{1,0:T(8,128)(2,1)S(1)}, bf16[64,1024]{1,0:T(8,128)(2,1)S(1)}, u32[]{:S(2)}, u32[]{:S(2)}) %collective-permute-start.8) | collective-permute-done | bytes 131104 | tf_op jit(solution)/shard_map/ppermute | solution.py:219
  40.9 0.8 shard_map.94
  41.7 0.7 collective-permute-start.12
  42.3 1.5 %collective-permute-start.13 = (bf16[2,64,512]{2,1,0:T(8,128)(2,1)S(1)}, bf16[2,64,512]{2,1,0:T(8,128)(2,1)S(1)}, u32[]{:S(2)}, u32[]{:S(2)}) collective-permute-start(bf16[2,64,512]{2,1,0:T(8,128)(2,1)S(1)} %get-tuple-element.28), channel_id=1, source_target_pairs={{0,16},{4,20},{8,24},{12,28},{16,0},{20,4},{24,8},{28,12},{1,17},{... | collective-permute-start | bytes 393224 | tf_op jit(solution)/shard_map/ppermute | solution.py:216
  43.9 4.2 %collective-permute-done.12.refs_0_ = bf16[2,64,512]{2,1,0:T(8,128)(2,1)S(1)} collective-permute-done((bf16[2,64,512]{2,1,0:T(8,128)(2,1)S(1)}, bf16[2,64,512]{2,1,0:T(8,128)(2,1)S(1)}, u32[]{:S(2)}, u32[]{:S(2)}) %collective-permute-start.12) | collective-permute-done | bytes 131104 | tf_op jit(solution)/shard_map/ppermute | solution.py:216
  48.1 1.4 %collective-permute-start.14 = (bf16[2,64,512]{2,1,0:T(8,128)(2,1)S(1)}, bf16[2,64,512]{2,1,0:T(8,128)(2,1)S(1)}, u32[]{:S(2)}, u32[]{:S(2)}) collective-permute-start(bf16[2,64,512]{2,1,0:T(8,128)(2,1)S(1)} %get-tuple-element.29), channel_id=1, source_target_pairs={{0,24},{4,28},{8,16},{12,20},{16,8},{20,12},{24,0},{28,4},{1,25},{... | collective-permute-start | bytes 393224 | tf_op jit(solution)/shard_map/ppermute | solution.py:216
  49.5 4.5 %collective-permute-done.14.refs_2_ = bf16[2,64,512]{2,1,0:T(8,128)(2,1)S(1)} collective-permute-done((bf16[2,64,512]{2,1,0:T(8,128)(2,1)S(1)}, bf16[2,64,512]{2,1,0:T(8,128)(2,1)S(1)}, u32[]{:S(2)}, u32[]{:S(2)}) %collective-permute-start.14) | collective-permute-done | bytes 131104 | tf_op jit(solution)/shard_map/ppermute | solution.py:216
  54.0 3.1 %shard_map.96 = (bf16[64,3584]{1,0:T(8,128)(2,1)S(1)}, bf16[64,3584]{1,0:T(8,128)(2,1)S(1)}, bf16[64,3584]{1,0:T(8,128)(2,1)S(1)}) custom-call(s32[3]{0:T(128)S(1)} %pad_add_fusion.ids, bf16[2,64,512]{2,1,0:T(8,128)(2,1)S(1)} %collective-permute-done.12.refs_0_, bf16[2,64,512]{2,1,0:T(8,128)(2,1)S(1)} %collective-permute-done.13.refs_1_, ...), custom_call_target="tpu_custom_call" | custom-call | flops 1409286144 | bytes 9109504 | tf_op jit(solution)/shard_map/pallas_call | solution.py:28
  57.2 1.9 %collective-permute-start.16 = (bf16[64,3584]{1,0:T(8,128)(2,1)S(1)}, bf16[64,3584]{1,0:T(8,128)(2,1)S(1)}, u32[]{:S(2)}, u32[]{:S(2)}) collective-permute-start(bf16[64,3584]{1,0:T(8,128)(2,1)S(1)} %get-tuple-element.31), channel_id=1, source_target_pairs={{0,16},{4,20},{8,24},{12,28},{16,0},{20,4},{24,8},{28,12},{1,17},{... | collective-permute-start | bytes 1376264 | tf_op jit(solution)/shard_map/ppermute | solution.py:216
  59.1 1.5 %collective-permute-start.17 = (bf16[64,3584]{1,0:T(8,128)(2,1)S(1)}, bf16[64,3584]{1,0:T(8,128)(2,1)S(1)}, u32[]{:S(2)}, u32[]{:S(2)}) collective-permute-start(bf16[64,3584]{1,0:T(8,128)(2,1)S(1)} %get-tuple-element.32), channel_id=1, source_target_pairs={{0,24},{4,28},{8,16},{12,20},{16,8},{20,12},{24,0},{28,4},{1,25},{... | collective-permute-start | bytes 1376264 | tf_op jit(solution)/shard_map/ppermute | solution.py:216
  60.6 2.9 %shard_map.95.refs_0_ = bf16[64,3584]{1,0:T(8,128)(2,1)S(1)} custom-call(s32[3]{0:T(128)S(1)} %pad_add_fusion.ids, bf16[2,64,512]{2,1,0:T(8,128)(2,1)S(1)} %get-tuple-element.26.refs_0_, bf16[512,1792]{1,0:T(8,128)(2,1)S(1)} %copy-done.1, bf16[512,1792]{1,0:T(8,128)(2,1)S(1)} %collective-permute-done.10.refs_2_.refs_4_, bf16[512,1792]{1,0:T(8,128)(2,1)S(1)} %copy-done.2, ...), custom_call_target="tpu_custom_call" | custom-call | flops 469762048 | bytes 7929856 | tf_op jit(solution)/shard_map/pallas_call | solution.py:28
  63.6 5.2 %collective-permute-done.15.refs_1_ = bf16[64,3584]{1,0:T(8,128)(2,1)S(1)} collective-permute-done((bf16[64,3584]{1,0:T(8,128)(2,1)S(1)}, bf16[64,3584]{1,0:T(8,128)(2,1)S(1)}, u32[]{:S(2)}, u32[]{:S(2)}) %collective-permute-start.15) | collective-permute-done | bytes 458784 | tf_op jit(solution)/shard_map/ppermute | solution.py:216
  68.8 2.8 %collective-permute-done.16.refs_2_ = bf16[64,3584]{1,0:T(8,128)(2,1)S(1)} collective-permute-done((bf16[64,3584]{1,0:T(8,128)(2,1)S(1)}, bf16[64,3584]{1,0:T(8,128)(2,1)S(1)}, u32[]{:S(2)}, u32[]{:S(2)}) %collective-permute-start.16) | collective-permute-done | bytes 458784 | tf_op jit(solution)/shard_map/ppermute | solution.py:216
  71.5 6.1 %collective-permute-done.17.refs_3_ = bf16[64,3584]{1,0:T(8,128)(2,1)S(1)} collective-permute-done((bf16[64,3584]{1,0:T(8,128)(2,1)S(1)}, bf16[64,3584]{1,0:T(8,128)(2,1)S(1)}, u32[]{:S(2)}, u32[]{:S(2)}) %collective-permute-start.17) | collective-permute-done | bytes 458784 | tf_op jit(solution)/shard_map/ppermute | solution.py:216
  77.7 0.9 shard_map.97.refs_0_
  78.6 0.7 collective-permute-start.20
  79.3 2.8 %collective-permute-start.21 = (bf16[64,1792]{1,0:T(8,128)(2,1)S(1)}, bf16[64,1792]{1,0:T(8,128)(2,1)S(1)}, u32[]{:S(2)}, u32[]{:S(2)}) collective-permute-start(bf16[64,1792]{1,0:T(8,128)(2,1)S(1)} %shard_map.97.refs_0_), channel_id=1, source_target_pairs={{0,24},{4,28},{8,16},{12,20},{16,8},{20,12},{24,0},{28,4},{1,25},{... | collective-permute-start | bytes 688136 | tf_op jit(solution)/shard_map/ppermute | solution.py:216
  82.1 3.4 %collective-permute-done.19.refs_0_ = bf16[64,1792]{1,0:T(8,128)(2,1)S(1)} collective-permute-done((bf16[64,1792]{1,0:T(8,128)(2,1)S(1)}, bf16[64,1792]{1,0:T(8,128)(2,1)S(1)}, u32[]{:S(2)}, u32[]{:S(2)}) %collective-permute-start.19) | collective-permute-done | bytes 229408 | tf_op jit(solution)/shard_map/ppermute | solution.py:216
  85.5 3.8 %collective-permute-done.20.refs_1_ = bf16[64,1792]{1,0:T(8,128)(2,1)S(1)} collective-permute-done((bf16[64,1792]{1,0:T(8,128)(2,1)S(1)}, bf16[64,1792]{1,0:T(8,128)(2,1)S(1)}, u32[]{:S(2)}, u32[]{:S(2)}) %collective-permute-start.20) | collective-permute-done | bytes 229408 | tf_op jit(solution)/shard_map/ppermute | solution.py:216
  89.3 1.4 %shard_map.99 = (bf16[2,64,512]{2,1,0:T(8,128)(2,1)S(1)}, bf16[2,64,512]{2,1,0:T(8,128)(2,1)S(1)}, bf16[2,64,512]{2,1,0:T(8,128)(2,1)S(1)}) custom-call(s32[3]{0:T(128)S(1)} %pad_add_fusion.ids, bf16[64,1792]{1,0:T(8,128)(2,1)S(1)} %collective-permute-done.19.refs_0_, bf16[64,1792]{1,0:T(8,128)(2,1)S(1)} %collective-permute-done.20.refs_1_, ...), custom_call_target="tpu_custom_call" | custom-call | flops 704643072 | bytes 4751360 | tf_op jit(solution)/shard_map/pallas_call | solution.py:28
  90.7 2.6 %collective-permute-start.22 = (bf16[2,64,512]{2,1,0:T(8,128)(2,1)S(1)}, bf16[2,64,512]{2,1,0:T(8,128)(2,1)S(1)}, u32[]{:S(2)}, u32[]{:S(2)}) collective-permute-start(bf16[2,64,512]{2,1,0:T(8,128)(2,1)S(1)} %get-tuple-element.33), channel_id=1, source_target_pairs={{0,8},{4,12},{8,0},{12,4},{16,24},{20,28},{24,16},{28,20},{1,9},{5... | collective-permute-start | bytes 393224 | tf_op jit(solution)/shard_map/ppermute | solution.py:216
  93.4 1.5 %collective-permute-start.24 = (bf16[2,64,512]{2,1,0:T(8,128)(2,1)S(1)}, bf16[2,64,512]{2,1,0:T(8,128)(2,1)S(1)}, u32[]{:S(2)}, u32[]{:S(2)}) collective-permute-start(bf16[2,64,512]{2,1,0:T(8,128)(2,1)S(1)} %get-tuple-element.35), channel_id=1, source_target_pairs={{0,24},{4,28},{8,16},{12,20},{16,8},{20,12},{24,0},{28,4},{1,25},{... | collective-permute-start | bytes 393224 | tf_op jit(solution)/shard_map/ppermute | solution.py:216
  94.9 1.3 shard_map.98.refs_0_
  96.3 3.4 %collective-permute-done.23.refs_2_ = bf16[2,64,512]{2,1,0:T(8,128)(2,1)S(1)} collective-permute-done((bf16[2,64,512]{2,1,0:T(8,128)(2,1)S(1)}, bf16[2,64,512]{2,1,0:T(8,128)(2,1)S(1)}, u32[]{:S(2)}, u32[]{:S(2)}) %collective-permute-start.23) | collective-permute-done | bytes 131104 | tf_op jit(solution)/shard_map/ppermute | solution.py:216
  99.7 0.6 shard_map.100
  100.4 2.6 %collective-permute-start.25 = (bf16[64,1024]{1,0:T(8,128)(2,1)S(1)}, bf16[64,1024]{1,0:T(8,128)(2,1)S(1)}, u32[]{:S(2)}, u32[]{:S(2)}) collective-permute-start(bf16[64,1024]{1,0:T(8,128)(2,1)S(1)} %get-tuple-element.37), channel_id=1, source_target_pairs={{0,1},{1,0},{2,3},{3,2},{4,5},{5,4},{6,7},{7,6},{8,9},{9,8},{10,11... | collective-permute-start | bytes 393224 | tf_op jit(solution)/shard_map/ppermute | solution.py:219
  103.0 1.5 %collective-permute-start.26 = (bf16[64,1024]{1,0:T(8,128)(2,1)S(1)}, bf16[64,1024]{1,0:T(8,128)(2,1)S(1)}, u32[]{:S(2)}, u32[]{:S(2)}) collective-permute-start(bf16[64,1024]{1,0:T(8,128)(2,1)S(1)} %get-tuple-element.38), channel_id=1, source_target_pairs={{0,2},{1,3},{2,0},{3,1},{4,6},{5,7},{6,4},{7,5},{8,10},{9,11},{10,... | collective-permute-start | bytes 393224 | tf_op jit(solution)/shard_map/ppermute | solution.py:219
  104.5 0.9 collective-permute-start.27
  105.4 0.9 collective-permute-done.25.refs_1_
  106.3 6.5 %collective-permute-done.26.refs_2_ = bf16[64,1024]{1,0:T(8,128)(2,1)S(1)} collective-permute-done((bf16[64,1024]{1,0:T(8,128)(2,1)S(1)}, bf16[64,1024]{1,0:T(8,128)(2,1)S(1)}, u32[]{:S(2)}, u32[]{:S(2)}) %collective-permute-start.26) | collective-permute-done | bytes 131104 | tf_op jit(solution)/shard_map/ppermute | solution.py:219
  112.8 1.1 shard_map.101
  114.0 2.0 %collective-permute-start.28 = (bf16[16,1280]{1,0:T(8,128)(2,1)S(1)}, bf16[16,1280]{1,0:T(8,128)(2,1)S(1)}, u32[]{:S(2)}, u32[]{:S(2)}) collective-permute-start(bf16[16,1280]{1,0:T(8,128)(2,1)S(1)} %get-tuple-element.41), channel_id=1, source_target_pairs={{0,1},{1,0},{2,3},{3,2},{4,5},{5,4},{6,7},{7,6},{8,9},{9,8},{10,11... | collective-permute-start | bytes 122888 | tf_op jit(solution)/shard_map/ppermute | solution.py:219
  116.0 0.6 collective-permute-start.29
  116.6 1.8 %collective-permute-start.30 = (bf16[16,1280]{1,0:T(8,128)(2,1)S(1)}, bf16[16,1280]{1,0:T(8,128)(2,1)S(1)}, u32[]{:S(2)}, u32[]{:S(2)}) collective-permute-start(bf16[16,1280]{1,0:T(8,128)(2,1)S(1)} %get-tuple-element.43), channel_id=1, source_target_pairs={{0,3},{1,2},{2,1},{3,0},{4,7},{5,6},{6,5},{7,4},{8,11},{9,10},{10,... | collective-permute-start | bytes 122888 | tf_op jit(solution)/shard_map/ppermute | solution.py:219
  118.4 2.5 %collective-permute-done.29.refs_2_ = bf16[16,1280]{1,0:T(8,128)(2,1)S(1)} collective-permute-done((bf16[16,1280]{1,0:T(8,128)(2,1)S(1)}, bf16[16,1280]{1,0:T(8,128)(2,1)S(1)}, u32[]{:S(2)}, u32[]{:S(2)}) %collective-permute-start.29) | collective-permute-done | bytes 40992 | tf_op jit(solution)/shard_map/ppermute | solution.py:219
  120.9 1.5 %collective-permute-done.30.refs_3_ = bf16[16,1280]{1,0:T(8,128)(2,1)S(1)} collective-permute-done((bf16[16,1280]{1,0:T(8,128)(2,1)S(1)}, bf16[16,1280]{1,0:T(8,128)(2,1)S(1)}, u32[]{:S(2)}, u32[]{:S(2)}) %collective-permute-start.30) | collective-permute-done | bytes 40992 | tf_op jit(solution)/shard_map/ppermute | solution.py:219
  122.4 0.6 shard_map.102.refs_0_
  123.0 0.9 collective-permute-start.31
  123.9 1.2 collective-permute-start.32
  125.1 1.4 %collective-permute-start.33 = (bf16[16,1280]{1,0:T(8,128)(2,1)S(1)}, bf16[16,1280]{1,0:T(8,128)(2,1)S(1)}, u32[]{:S(2)}, u32[]{:S(2)}) collective-permute-start(bf16[16,1280]{1,0:T(8,128)(2,1)S(1)} %shard_map.102.refs_0_), channel_id=1, source_target_pairs={{0,24},{4,28},{8,16},{12,20},{16,8},{20,12},{24,0},{28,4},{1,25},{... | collective-permute-start | bytes 122888 | tf_op jit(solution)/shard_map/ppermute | solution.py:216
  126.5 0.5 collective-permute-done.31.refs_1_
  127.0 0.9 collective-permute-done.32.refs_2_
  127.9 2.1 %collective-permute-done.33.refs_3_ = bf16[16,1280]{1,0:T(8,128)(2,1)S(1)} collective-permute-done((bf16[16,1280]{1,0:T(8,128)(2,1)S(1)}, bf16[16,1280]{1,0:T(8,128)(2,1)S(1)}, u32[]{:S(2)}, u32[]{:S(2)}) %collective-permute-start.33) | collective-permute-done | bytes 40992 | tf_op jit(solution)/shard_map/ppermute | solution.py:216
  130.3 1.5 %shard_map.103.refs_6_ = bf16[10,192,32]{2,1,0:T(8,128)(2,1)S(1)} custom-call(s32[3]{0:T(128)S(1)} %pad_add_fusion.ids, s32[192,1]{1,0:T(8,128)S(1)} %copy.10.seg, bf16[192,1280]{1,0:T(8,128)(2,1)S(1)} %copy-done.5, bf16[32,1280]{1,0:T(8,128)(2,1)S(1)} %pad.4.keys), custom_call_target="tpu_custom_call" | custom-call | bytes 697088 | tf_op jit(solution)/shard_map/pallas_call | solution.py:28
  131.8 1.8 %shard_map.104 = bf16[192,1280]{1,0:T(8,128)(2,1)} custom-call(s32[3]{0:T(128)S(1)} %pad_add_fusion.ids, bf16[16,1280]{1,0:T(8,128)(2,1)S(1)} %shard_map.102.refs_0_, bf16[16,1280]{1,0:T(8,128)(2,1)S(1)} %collective-permute-done.31.refs_1_, bf16[16,1280]{1,0:T(8,128)(2,1)S(1)} %collective-permute-done.32.refs_2_, ...), custom_call_target="tpu_custom_call" | custom-call | bytes 1437696 | tf_op jit(solution)/shard_map/pallas_call | solution.py:28
  (45 shorter events, 1.3 us)
Async XLA Ops:
  0.0 53.9 %collective-permute-start.10 = (bf16[512,1792]{1,0:T(8,128)(2,1)}, bf16[512,1792]{1,0:T(8,128)(2,1)S(1)}, u32[]{:S(2)}, u32[]{:S(2)}) collective-permute-start(bf16[512,1792]{1,0:T(8,128)(2,1)} %refs_3_.4), channel_id=1, source_target_pairs={{0,4},{4,0},{8,12},{12,8},{16,20},{20,16},{24,28},{28,24},{1,5},{5... | collective-permute-start | bytes 5505032 | tf_op jit(solution)/shard_map/ppermute | solution.py:213
  0.5 53.5 %collective-permute-start.11 = (bf16[512,1792]{1,0:T(8,128)(2,1)}, bf16[512,1792]{1,0:T(8,128)(2,1)}, u32[]{:S(2)}, u32[]{:S(2)}) collective-permute-start(bf16[512,1792]{1,0:T(8,128)(2,1)} %refs_5_.2), channel_id=1, source_target_pairs={{0,4},{4,0},{8,12},{12,8},{16,20},{20,16},{24,28},{28,24},{1,5},{5... | collective-permute-start | bytes 5505032 | tf_op jit(solution)/shard_map/ppermute | solution.py:213
  0.6 1.0 copy-start.6
  1.6 0.7 copy-start.7
  3.1 5.6 %collective-permute-start = (bf16[32,1280]{1,0:T(8,128)(2,1)S(1)}, bf16[32,1280]{1,0:T(8,128)(2,1)S(1)}, u32[]{:S(2)}, u32[]{:S(2)}) collective-permute-start(bf16[32,1280]{1,0:T(8,128)(2,1)S(1)} %shard_map.91.refs_0_), channel_id=1, source_target_pairs={{0,8},{4,12},{8,0},{12,4},{16,24},{20,28},{24,16},{28,20},{1,9},{5... | collective-permute-start | bytes 245768 | tf_op jit(solution)/shard_map/ppermute | solution.py:216
  6.0 4.4 %collective-permute-start.1 = (bf16[32,1280]{1,0:T(8,128)(2,1)S(1)}, bf16[32,1280]{1,0:T(8,128)(2,1)S(1)}, u32[]{:S(2)}, u32[]{:S(2)}) collective-permute-start(bf16[32,1280]{1,0:T(8,128)(2,1)S(1)} %shard_map.91.refs_0_), channel_id=1, source_target_pairs={{0,16},{4,20},{8,24},{12,28},{16,0},{20,4},{24,8},{28,12},{1,17},{... | collective-permute-start | bytes 245768 | tf_op jit(solution)/shard_map/ppermute | solution.py:216
  7.6 5.3 %collective-permute-start.2 = (bf16[32,1280]{1,0:T(8,128)(2,1)S(1)}, bf16[32,1280]{1,0:T(8,128)(2,1)S(1)}, u32[]{:S(2)}, u32[]{:S(2)}) collective-permute-start(bf16[32,1280]{1,0:T(8,128)(2,1)S(1)} %shard_map.91.refs_0_), channel_id=1, source_target_pairs={{0,24},{4,28},{8,16},{12,20},{16,8},{20,12},{24,0},{28,4},{1,25},{... | collective-permute-start | bytes 245768 | tf_op jit(solution)/shard_map/ppermute | solution.py:216
  8.6 73.4 %collective-permute-start.18 = (bf16[1792,512]{1,0:T(8,128)(2,1)}, bf16[1792,512]{1,0:T(8,128)(2,1)S(1)}, u32[]{:S(2)}, u32[]{:S(2)}) collective-permute-start(bf16[1792,512]{1,0:T(8,128)(2,1)} %refs_3_.5), channel_id=1, source_target_pairs={{0,4},{4,0},{8,12},{12,8},{16,20},{20,16},{24,28},{28,24},{1,5},{5... | collective-permute-start | bytes 5505032 | tf_op jit(solution)/shard_map/ppermute | solution.py:213
  12.9 1.7 %collective-permute-start.3 = (bf16[128,1280]{1,0:T(8,128)(2,1)S(1)}, bf16[128,1280]{1,0:T(8,128)(2,1)S(1)}, u32[]{:S(2)}, u32[]{:S(2)}) collective-permute-start(bf16[128,1280]{1,0:T(8,128)(2,1)S(1)} %pad_maximum_fusion), channel_id=1, source_target_pairs={{0,4},{4,0},{8,12},{12,8},{16,20},{20,16},{24,28},{28,24},{1,5},{5... | collective-permute-start | bytes 983048 | tf_op jit(solution)/shard_map/ppermute | solution.py:213
  14.6 39.3 %copy-start.2 = (bf16[512,1792]{1,0:T(8,128)(2,1)S(1)}, bf16[512,1792]{1,0:T(8,128)(2,1)}, u32[]{:S(2)}) copy-start(bf16[512,1792]{1,0:T(8,128)(2,1)} %refs_5_.2) | copy-start | bytes 5505028
  15.4 38.6 %copy-start.1 = (bf16[512,1792]{1,0:T(8,128)(2,1)S(1)}, bf16[512,1792]{1,0:T(8,128)(2,1)}, u32[]{:S(2)}) copy-start(bf16[512,1792]{1,0:T(8,128)(2,1)} %refs_3_.4) | copy-start | bytes 5505028
  15.4 4.2 %collective-permute-start.4 = (bf16[16,1280]{1,0:T(8,128)(2,1)S(1)}, bf16[16,1280]{1,0:T(8,128)(2,1)S(1)}, u32[]{:S(2)}, u32[]{:S(2)}) collective-permute-start(bf16[16,1280]{1,0:T(8,128)(2,1)S(1)} %get-tuple-element.25.refs_0_), channel_id=1, source_target_pairs={{0,1},{1,0},{2,3},{3,2},{4,5},{5,4},{6,7},{7,6},{8,9},{9,8},{10,11... | collective-permute-start | bytes 122888 | tf_op jit(solution)/shard_map/ppermute | solution.py:219
  17.0 6.5 %collective-permute-start.5 = (bf16[16,1280]{1,0:T(8,128)(2,1)S(1)}, bf16[16,1280]{1,0:T(8,128)(2,1)S(1)}, u32[]{:S(2)}, u32[]{:S(2)}) collective-permute-start(bf16[16,1280]{1,0:T(8,128)(2,1)S(1)} %get-tuple-element.25.refs_0_), channel_id=1, source_target_pairs={{0,2},{1,3},{2,0},{3,1},{4,6},{5,7},{6,4},{7,5},{8,10},{9,11},{10,... | collective-permute-start | bytes 122888 | tf_op jit(solution)/shard_map/ppermute | solution.py:219
  19.6 5.9 %collective-permute-start.6 = (bf16[16,1280]{1,0:T(8,128)(2,1)S(1)}, bf16[16,1280]{1,0:T(8,128)(2,1)S(1)}, u32[]{:S(2)}, u32[]{:S(2)}) collective-permute-start(bf16[16,1280]{1,0:T(8,128)(2,1)S(1)} %get-tuple-element.25.refs_0_), channel_id=1, source_target_pairs={{0,3},{1,2},{2,1},{3,0},{4,7},{5,6},{6,5},{7,4},{8,11},{9,10},{10,... | collective-permute-start | bytes 122888 | tf_op jit(solution)/shard_map/ppermute | solution.py:219
  25.5 1.7 %copy-start.3 = (bf16[1280,1024]{1,0:T(8,128)(2,1)S(1)}, bf16[1280,1024]{1,0:T(8,128)(2,1)}, u32[]{:S(2)}) copy-start(bf16[1280,1024]{1,0:T(8,128)(2,1)} %refs_4_.1) | copy-start | bytes 7864324
  28.3 5.1 %collective-permute-start.7 = (bf16[64,1024]{1,0:T(8,128)(2,1)S(1)}, bf16[64,1024]{1,0:T(8,128)(2,1)S(1)}, u32[]{:S(2)}, u32[]{:S(2)}) collective-permute-start(bf16[64,1024]{1,0:T(8,128)(2,1)S(1)} %shard_map.93.refs_0_.refs_4_), channel_id=1, source_target_pairs={{0,1},{1,0},{2,3},{3,2},{4,5},{5,4},{6,7},{7,6},{8,9},{9,8},{10,11... | collective-permute-start | bytes 393224 | tf_op jit(solution)/shard_map/ppermute | solution.py:219
  28.4 12.5 %collective-permute-start.8 = (bf16[64,1024]{1,0:T(8,128)(2,1)S(1)}, bf16[64,1024]{1,0:T(8,128)(2,1)S(1)}, u32[]{:S(2)}, u32[]{:S(2)}) collective-permute-start(bf16[64,1024]{1,0:T(8,128)(2,1)S(1)} %shard_map.93.refs_0_.refs_4_), channel_id=1, source_target_pairs={{0,2},{1,3},{2,0},{3,1},{4,6},{5,7},{6,4},{7,5},{8,10},{9,11},{10,... | collective-permute-start | bytes 393224 | tf_op jit(solution)/shard_map/ppermute | solution.py:219
  33.4 7.5 %collective-permute-start.9 = (bf16[64,1024]{1,0:T(8,128)(2,1)S(1)}, bf16[64,1024]{1,0:T(8,128)(2,1)S(1)}, u32[]{:S(2)}, u32[]{:S(2)}) collective-permute-start(bf16[64,1024]{1,0:T(8,128)(2,1)S(1)} %shard_map.93.refs_0_.refs_4_), channel_id=1, source_target_pairs={{0,3},{1,2},{2,1},{3,0},{4,7},{5,6},{6,5},{7,4},{8,11},{9,10},{10,... | collective-permute-start | bytes 393224 | tf_op jit(solution)/shard_map/ppermute | solution.py:219
  41.7 6.4 %collective-permute-start.12 = (bf16[2,64,512]{2,1,0:T(8,128)(2,1)S(1)}, bf16[2,64,512]{2,1,0:T(8,128)(2,1)S(1)}, u32[]{:S(2)}, u32[]{:S(2)}) collective-permute-start(bf16[2,64,512]{2,1,0:T(8,128)(2,1)S(1)} %get-tuple-element.27), channel_id=1, source_target_pairs={{0,8},{4,12},{8,0},{12,4},{16,24},{20,28},{24,16},{28,20},{1,9},{5... | collective-permute-start | bytes 393224 | tf_op jit(solution)/shard_map/ppermute | solution.py:216
  42.3 7.1 %collective-permute-start.13 = (bf16[2,64,512]{2,1,0:T(8,128)(2,1)S(1)}, bf16[2,64,512]{2,1,0:T(8,128)(2,1)S(1)}, u32[]{:S(2)}, u32[]{:S(2)}) collective-permute-start(bf16[2,64,512]{2,1,0:T(8,128)(2,1)S(1)} %get-tuple-element.28), channel_id=1, source_target_pairs={{0,16},{4,20},{8,24},{12,28},{16,0},{20,4},{24,8},{28,12},{1,17},{... | collective-permute-start | bytes 393224 | tf_op jit(solution)/shard_map/ppermute | solution.py:216
  48.1 5.9 %collective-permute-start.14 = (bf16[2,64,512]{2,1,0:T(8,128)(2,1)S(1)}, bf16[2,64,512]{2,1,0:T(8,128)(2,1)S(1)}, u32[]{:S(2)}, u32[]{:S(2)}) collective-permute-start(bf16[2,64,512]{2,1,0:T(8,128)(2,1)S(1)} %get-tuple-element.29), channel_id=1, source_target_pairs={{0,24},{4,28},{8,16},{12,20},{16,8},{20,12},{24,0},{28,4},{1,25},{... | collective-permute-start | bytes 393224 | tf_op jit(solution)/shard_map/ppermute | solution.py:216
  57.1 11.7 %collective-permute-start.15 = (bf16[64,3584]{1,0:T(8,128)(2,1)S(1)}, bf16[64,3584]{1,0:T(8,128)(2,1)S(1)}, u32[]{:S(2)}, u32[]{:S(2)}) collective-permute-start(bf16[64,3584]{1,0:T(8,128)(2,1)S(1)} %get-tuple-element.30), channel_id=1, source_target_pairs={{0,8},{4,12},{8,0},{12,4},{16,24},{20,28},{24,16},{28,20},{1,9},{5... | collective-permute-start | bytes 1376264 | tf_op jit(solution)/shard_map/ppermute | solution.py:216
  57.2 14.3 %collective-permute-start.16 = (bf16[64,3584]{1,0:T(8,128)(2,1)S(1)}, bf16[64,3584]{1,0:T(8,128)(2,1)S(1)}, u32[]{:S(2)}, u32[]{:S(2)}) collective-permute-start(bf16[64,3584]{1,0:T(8,128)(2,1)S(1)} %get-tuple-element.31), channel_id=1, source_target_pairs={{0,16},{4,20},{8,24},{12,28},{16,0},{20,4},{24,8},{28,12},{1,17},{... | collective-permute-start | bytes 1376264 | tf_op jit(solution)/shard_map/ppermute | solution.py:216
  59.1 18.6 %collective-permute-start.17 = (bf16[64,3584]{1,0:T(8,128)(2,1)S(1)}, bf16[64,3584]{1,0:T(8,128)(2,1)S(1)}, u32[]{:S(2)}, u32[]{:S(2)}) collective-permute-start(bf16[64,3584]{1,0:T(8,128)(2,1)S(1)} %get-tuple-element.32), channel_id=1, source_target_pairs={{0,24},{4,28},{8,16},{12,20},{16,8},{20,12},{24,0},{28,4},{1,25},{... | collective-permute-start | bytes 1376264 | tf_op jit(solution)/shard_map/ppermute | solution.py:216
  63.5 25.8 %copy-start = (bf16[1792,512]{1,0:T(8,128)(2,1)S(1)}, bf16[1792,512]{1,0:T(8,128)(2,1)}, u32[]{:S(2)}) copy-start(bf16[1792,512]{1,0:T(8,128)(2,1)} %refs_3_.5) | copy-start | bytes 5505028
  78.5 7.0 %collective-permute-start.19 = (bf16[64,1792]{1,0:T(8,128)(2,1)S(1)}, bf16[64,1792]{1,0:T(8,128)(2,1)S(1)}, u32[]{:S(2)}, u32[]{:S(2)}) collective-permute-start(bf16[64,1792]{1,0:T(8,128)(2,1)S(1)} %shard_map.97.refs_0_), channel_id=1, source_target_pairs={{0,8},{4,12},{8,0},{12,4},{16,24},{20,28},{24,16},{28,20},{1,9},{5... | collective-permute-start | bytes 688136 | tf_op jit(solution)/shard_map/ppermute | solution.py:216
  78.6 10.7 %collective-permute-start.20 = (bf16[64,1792]{1,0:T(8,128)(2,1)S(1)}, bf16[64,1792]{1,0:T(8,128)(2,1)S(1)}, u32[]{:S(2)}, u32[]{:S(2)}) collective-permute-start(bf16[64,1792]{1,0:T(8,128)(2,1)S(1)} %shard_map.97.refs_0_), channel_id=1, source_target_pairs={{0,16},{4,20},{8,24},{12,28},{16,0},{20,4},{24,8},{28,12},{1,17},{... | collective-permute-start | bytes 688136 | tf_op jit(solution)/shard_map/ppermute | solution.py:216
  79.3 10.0 %collective-permute-start.21 = (bf16[64,1792]{1,0:T(8,128)(2,1)S(1)}, bf16[64,1792]{1,0:T(8,128)(2,1)S(1)}, u32[]{:S(2)}, u32[]{:S(2)}) collective-permute-start(bf16[64,1792]{1,0:T(8,128)(2,1)S(1)} %shard_map.97.refs_0_), channel_id=1, source_target_pairs={{0,24},{4,28},{8,16},{12,20},{16,8},{20,12},{24,0},{28,4},{1,25},{... | collective-permute-start | bytes 688136 | tf_op jit(solution)/shard_map/ppermute | solution.py:216
  90.7 5.6 %collective-permute-start.22 = (bf16[2,64,512]{2,1,0:T(8,128)(2,1)S(1)}, bf16[2,64,512]{2,1,0:T(8,128)(2,1)S(1)}, u32[]{:S(2)}, u32[]{:S(2)}) collective-permute-start(bf16[2,64,512]{2,1,0:T(8,128)(2,1)S(1)} %get-tuple-element.33), channel_id=1, source_target_pairs={{0,8},{4,12},{8,0},{12,4},{16,24},{20,28},{24,16},{28,20},{1,9},{5... | collective-permute-start | bytes 393224 | tf_op jit(solution)/shard_map/ppermute | solution.py:216
  93.4 6.4 %collective-permute-start.23 = (bf16[2,64,512]{2,1,0:T(8,128)(2,1)S(1)}, bf16[2,64,512]{2,1,0:T(8,128)(2,1)S(1)}, u32[]{:S(2)}, u32[]{:S(2)}) collective-permute-start(bf16[2,64,512]{2,1,0:T(8,128)(2,1)S(1)} %get-tuple-element.34), channel_id=1, source_target_pairs={{0,16},{4,20},{8,24},{12,28},{16,0},{20,4},{24,8},{28,12},{1,17},{... | collective-permute-start | bytes 393224 | tf_op jit(solution)/shard_map/ppermute | solution.py:216
  93.4 19.5 %copy-start.4 = (bf16[1024,1280]{1,0:T(8,128)(2,1)S(1)}, bf16[1024,1280]{1,0:T(8,128)(2,1)}, u32[]{:S(2)}) copy-start(bf16[1024,1280]{1,0:T(8,128)(2,1)} %refs_5_.3) | copy-start | bytes 7864324
  93.4 6.4 %collective-permute-start.24 = (bf16[2,64,512]{2,1,0:T(8,128)(2,1)S(1)}, bf16[2,64,512]{2,1,0:T(8,128)(2,1)S(1)}, u32[]{:S(2)}, u32[]{:S(2)}) collective-permute-start(bf16[2,64,512]{2,1,0:T(8,128)(2,1)S(1)} %get-tuple-element.35), channel_id=1, source_target_pairs={{0,24},{4,28},{8,16},{12,20},{16,8},{20,12},{24,0},{28,4},{1,25},{... | collective-permute-start | bytes 393224 | tf_op jit(solution)/shard_map/ppermute | solution.py:216
  100.4 6.0 %collective-permute-start.25 = (bf16[64,1024]{1,0:T(8,128)(2,1)S(1)}, bf16[64,1024]{1,0:T(8,128)(2,1)S(1)}, u32[]{:S(2)}, u32[]{:S(2)}) collective-permute-start(bf16[64,1024]{1,0:T(8,128)(2,1)S(1)} %get-tuple-element.37), channel_id=1, source_target_pairs={{0,1},{1,0},{2,3},{3,2},{4,5},{5,4},{6,7},{7,6},{8,9},{9,8},{10,11... | collective-permute-start | bytes 393224 | tf_op jit(solution)/shard_map/ppermute | solution.py:219
  103.0 9.9 %collective-permute-start.26 = (bf16[64,1024]{1,0:T(8,128)(2,1)S(1)}, bf16[64,1024]{1,0:T(8,128)(2,1)S(1)}, u32[]{:S(2)}, u32[]{:S(2)}) collective-permute-start(bf16[64,1024]{1,0:T(8,128)(2,1)S(1)} %get-tuple-element.38), channel_id=1, source_target_pairs={{0,2},{1,3},{2,0},{3,1},{4,6},{5,7},{6,4},{7,5},{8,10},{9,11},{10,... | collective-permute-start | bytes 393224 | tf_op jit(solution)/shard_map/ppermute | solution.py:219
  104.5 8.4 %collective-permute-start.27 = (bf16[64,1024]{1,0:T(8,128)(2,1)S(1)}, bf16[64,1024]{1,0:T(8,128)(2,1)S(1)}, u32[]{:S(2)}, u32[]{:S(2)}) collective-permute-start(bf16[64,1024]{1,0:T(8,128)(2,1)S(1)} %get-tuple-element.39), channel_id=1, source_target_pairs={{0,3},{1,2},{2,1},{3,0},{4,7},{5,6},{6,5},{7,4},{8,11},{9,10},{10,... | collective-permute-start | bytes 393224 | tf_op jit(solution)/shard_map/ppermute | solution.py:219
  112.8 17.3 %copy-start.8 = (s32[192]{0:T(256)S(1)}, s32[192]{0:T(256)}, u32[]{:S(2)}) copy-start(s32[192]{0:T(256)} %param.11) | copy-start | bytes 2308
  112.8 17.4 %copy-start.9 = (bf16[31,1280]{1,0:T(8,128)(2,1)S(1)}, bf16[31,1280]{1,0:T(8,128)(2,1)}, u32[]{:S(2)}) copy-start(bf16[31,1280]{1,0:T(8,128)(2,1)} %param.12) | copy-start | bytes 238084
  112.8 17.4 %copy-start.5 = (bf16[192,1280]{1,0:T(8,128)(2,1)S(1)}, bf16[192,1280]{1,0:T(8,128)(2,1)}, u32[]{:S(2)}) copy-start(bf16[192,1280]{1,0:T(8,128)(2,1)} %refs_7_.1) | copy-start | bytes 1474564
  114.0 4.5 %collective-permute-start.28 = (bf16[16,1280]{1,0:T(8,128)(2,1)S(1)}, bf16[16,1280]{1,0:T(8,128)(2,1)S(1)}, u32[]{:S(2)}, u32[]{:S(2)}) collective-permute-start(bf16[16,1280]{1,0:T(8,128)(2,1)S(1)} %get-tuple-element.41), channel_id=1, source_target_pairs={{0,1},{1,0},{2,3},{3,2},{4,5},{5,4},{6,7},{7,6},{8,9},{9,8},{10,11... | collective-permute-start | bytes 122888 | tf_op jit(solution)/shard_map/ppermute | solution.py:219
  116.0 4.9 %collective-permute-start.29 = (bf16[16,1280]{1,0:T(8,128)(2,1)S(1)}, bf16[16,1280]{1,0:T(8,128)(2,1)S(1)}, u32[]{:S(2)}, u32[]{:S(2)}) collective-permute-start(bf16[16,1280]{1,0:T(8,128)(2,1)S(1)} %get-tuple-element.42), channel_id=1, source_target_pairs={{0,2},{1,3},{2,0},{3,1},{4,6},{5,7},{6,4},{7,5},{8,10},{9,11},{10,... | collective-permute-start | bytes 122888 | tf_op jit(solution)/shard_map/ppermute | solution.py:219
  116.6 5.8 %collective-permute-start.30 = (bf16[16,1280]{1,0:T(8,128)(2,1)S(1)}, bf16[16,1280]{1,0:T(8,128)(2,1)S(1)}, u32[]{:S(2)}, u32[]{:S(2)}) collective-permute-start(bf16[16,1280]{1,0:T(8,128)(2,1)S(1)} %get-tuple-element.43), channel_id=1, source_target_pairs={{0,3},{1,2},{2,1},{3,0},{4,7},{5,6},{6,5},{7,4},{8,11},{9,10},{10,... | collective-permute-start | bytes 122888 | tf_op jit(solution)/shard_map/ppermute | solution.py:219
  123.0 4.1 %collective-permute-start.31 = (bf16[16,1280]{1,0:T(8,128)(2,1)S(1)}, bf16[16,1280]{1,0:T(8,128)(2,1)S(1)}, u32[]{:S(2)}, u32[]{:S(2)}) collective-permute-start(bf16[16,1280]{1,0:T(8,128)(2,1)S(1)} %shard_map.102.refs_0_), channel_id=1, source_target_pairs={{0,8},{4,12},{8,0},{12,4},{16,24},{20,28},{24,16},{28,20},{1,9},{5... | collective-permute-start | bytes 122888 | tf_op jit(solution)/shard_map/ppermute | solution.py:216
  123.9 4.0 %collective-permute-start.32 = (bf16[16,1280]{1,0:T(8,128)(2,1)S(1)}, bf16[16,1280]{1,0:T(8,128)(2,1)S(1)}, u32[]{:S(2)}, u32[]{:S(2)}) collective-permute-start(bf16[16,1280]{1,0:T(8,128)(2,1)S(1)} %shard_map.102.refs_0_), channel_id=1, source_target_pairs={{0,16},{4,20},{8,24},{12,28},{16,0},{20,4},{24,8},{28,12},{1,17},{... | collective-permute-start | bytes 122888 | tf_op jit(solution)/shard_map/ppermute | solution.py:216
  125.1 4.9 %collective-permute-start.33 = (bf16[16,1280]{1,0:T(8,128)(2,1)S(1)}, bf16[16,1280]{1,0:T(8,128)(2,1)S(1)}, u32[]{:S(2)}, u32[]{:S(2)}) collective-permute-start(bf16[16,1280]{1,0:T(8,128)(2,1)S(1)} %shard_map.102.refs_0_), channel_id=1, source_target_pairs={{0,24},{4,28},{8,16},{12,20},{16,8},{20,12},{24,0},{28,4},{1,25},{... | collective-permute-start | bytes 122888 | tf_op jit(solution)/shard_map/ppermute | solution.py:216
  130.0 1.8 %collective-permute-start.34 = (bf16[4,16,1280]{2,1,0:T(8,128)(2,1)S(1)}, bf16[4,16,1280]{2,1,0:T(8,128)(2,1)S(1)}, u32[]{:S(2)}, u32[]{:S(2)}) collective-permute-start(bf16[4,16,1280]{2,1,0:T(8,128)(2,1)S(1)} %pad_maximum_fusion.1), channel_id=1, source_target_pairs={{0,4},{4,0},{8,12},{12,8},{16,20},{20,16},{24,28},{28,24},{1,5},{5... | collective-permute-start | bytes 491528 | tf_op jit(solution)/shard_map/ppermute | solution.py:213

commit v2 on v1

v2 whole, which is shorter than its diff:
```python
import functools
import math

import jax
import jax.numpy as jnp
from jax import lax
from jax.experimental import pallas as pl
from jax.experimental.pallas import tpu as pltpu
from jax.sharding import PartitionSpec as P

HD = 128
ROWS = 16
norm_epsilon = 1e-05

VMEM = pl.BlockSpec(memory_space=pltpu.VMEM)
SMEM = pl.BlockSpec(memory_space=pltpu.SMEM)
HBM = pl.BlockSpec(memory_space=pl.ANY)
BF16 = jnp.bfloat16
F32 = jnp.float32


def shape(dims, dtype=BF16):
    return jax.ShapeDtypeStruct(tuple(dims), dtype)


def call(kernel, outs, ids, *arrays, hbm=(), through=(), scratch=(), flops=0, limit=40):
    n, t, o = len(arrays), len(through), len(outs)

    def run(ids, *refs):
        kernel(ids, *refs[:n], *refs[n + t : n + t + o], *refs[n + 2 * t + o :])

    moved = sum(a.size * a.dtype.itemsize for a in arrays)
    moved += sum(math.prod(a.shape) * a.dtype.itemsize for a in outs)
    return pl.pallas_call(
        run,
        out_shape=list(outs) + [shape(a.shape, a.dtype) for a in through],
        in_specs=[SMEM] + [HBM if i in hbm else VMEM for i in range(n)] + [HBM] * t,
        out_specs=[VMEM] * o + [HBM] * t,
        scratch_shapes=list(scratch),
        input_output_aliases={1 + n + i: o + i for i in range(t)},
        compiler_params=pltpu.CompilerParams(vmem_limit_bytes=limit * 1024 * 1024),
        cost_estimate=pl.CostEstimate(flops=int(flops), bytes_accessed=int(moved), transcendentals=0),
    )(ids, *arrays, *through)


def dot(a, b):
    return jnp.dot(a, b, preferred_element_type=F32)


def pool_kernel(slots, ids, seg_in, enc_in, out, seg, enc, sems):
    copies = [
        pltpu.make_async_copy(seg_in, seg, sems.at[0]),
        pltpu.make_async_copy(enc_in, enc, sems.at[1]),
    ]
    for copy in copies:
        copy.start()
    for copy in copies:
        copy.wait()
    patch = lax.broadcasted_iota(jnp.int32, (slots, seg.shape[1]), 0)
    member = seg[...] == patch
    lengths = jnp.sum(member.astype(F32), axis=1, keepdims=True)
    sums = dot(member.astype(BF16), enc[...])
    pooled = sums / jnp.maximum(lengths, 1.0)
    total = jnp.max(seg[...].astype(F32)) + 1.0
    row = lax.broadcasted_iota(jnp.int32, pooled.shape, 0)
    out[...] = jnp.where(row == slots - 1, total, pooled).astype(BF16)


def pack_kernel(chips, slots, ids, *refs):
    mine, theirs = refs[:chips], refs[chips]
    out, start_out, select_out, packed = refs[chips + 1 :]
    q, c = ids[0], ids[1]
    blocks = 2 * chips
    lanes = blocks * slots
    for k in range(chips):
        packed[k * slots : (k + 1) * slots, :] = mine[k][...]
    packed[chips * slots :, :] = theirs[...]
    lane = lax.broadcasted_iota(jnp.int32, (1, lanes), 1)
    block = lane // slots
    patch = lane - block * slots
    part = block // chips
    place = 2 * ((block - part * chips) ^ q) + (part ^ c)
    line, column = (lax.broadcasted_iota(jnp.int32, select_out.shape, d) for d in range(2))
    target = 2 * ((line // (2 * ROWS)) ^ q) + (((line // ROWS) % 2) ^ c)
    start = jnp.zeros((1, lanes), F32)
    total = jnp.zeros((1, lanes), F32)
    own = jnp.zeros((1, lanes), F32)
    target_start = jnp.zeros(select_out.shape, F32)
    target_total = jnp.zeros(select_out.shape, F32)
    for b in range(blocks):
        count = packed[(b + 1) * slots - 1 : (b + 1) * slots, 0:lanes].astype(F32)
        where = 2 * ((b % chips) ^ q) + ((b // chips) ^ c)
        start += jnp.where(place > where, count, 0.0)
        total += jnp.where(block == b, count, 0.0)
        own += jnp.where(2 * q + c > where, count, 0.0)
        count = count[:, : select_out.shape[1]]
        target_start += jnp.where(target > where, count, 0.0)
        target_total += jnp.where(target == where, count, 0.0)
    wanted = 2 * (q * ROWS + lax.broadcasted_iota(jnp.int32, (ROWS, lanes), 0)) + c
    found = (start.astype(jnp.int32) + patch == wanted) & (patch < total.astype(jnp.int32))
    out[...] = dot(found.astype(BF16), packed[...]).astype(BF16)
    start_out[...] = jnp.broadcast_to(own[:, 0:HD].astype(jnp.int32), start_out.shape)
    first = target_start.astype(jnp.int32)
    patch = ((c - first) & 1) + 2 * (line % ROWS)
    position = 2 * (((column // ROWS) ^ q) * ROWS + column % ROWS) + c
    found = (first + patch == position) & (patch < target_total.astype(jnp.int32))
    select_out[...] = found.astype(BF16)


def x_kernel(groups, ids, *refs):
    pieces, w_in = refs[:groups], refs[groups]
    out, packed, w, sems = refs[groups + 1 :]
    wide = w.shape[1]
    step = 256 if wide % 256 == 0 else wide
    copies = []
    for i in range(wide // step):
        part = pl.ds(i * step, step)
        copies.append(pltpu.make_async_copy(w_in.at[:, part], w.at[:, part], sems.at[i]))
        copies[-1].start()
    for k in range(groups):
        packed[ids[2] ^ k] = pieces[k][...]
    rows = packed[...].reshape(groups * ROWS, packed.shape[2])
    for i, copy in enumerate(copies):
        copy.wait()
        part = slice(i * step, (i + 1) * step)
        out[:, part] = dot(rows, w[:, part]).astype(BF16)


def spread_kernel(groups, chips, ids, *refs):
    pieces, outs, scale, units = refs[:groups], refs[groups : groups + chips], refs[-2], refs[-1]
    q, c, z = ids[0], ids[1], ids[2]
    unit = units.shape[2]
    per = 2 * chips // groups
    for k in range(groups):
        for u in range(per):
            units[(z ^ k) * per + u] = pieces[k][:, u * unit : (u + 1) * unit]
    for k in range(chips):
        for h in range(2):
            outs[k][h] = units[2 * (q ^ k) + (c ^ h)]
    squares = jnp.zeros((units.shape[1], 1), F32)
    for k in range(groups):
        wide = pieces[k][...].astype(F32)
        squares += jnp.sum(wide * wide, axis=1, keepdims=True)
    scale[...] = jnp.broadcast_to(lax.rsqrt(squares / (2 * chips * unit) + norm_epsilon), scale.shape)


def gate_kernel(ids, piece, gate_a, gate_b, up_a, up_b, out):
    wide = gate_a.shape[1]
    a, b = piece[0], piece[1]
    out[:, :wide] = (dot(a, gate_a[...]) + dot(b, gate_b[...])).astype(BF16)
    out[:, wide:] = (dot(a, up_a[...]) + dot(b, up_b[...])).astype(BF16)


def hidden_kernel(ids, scale, *refs):
    pieces, out = refs[:-1], refs[-1]
    wide = out.shape[1]
    gate = sum(p[:, :wide].astype(F32) for p in pieces) * scale[:, 0:1]
    up = sum(p[:, wide:].astype(F32) for p in pieces) * scale[:, 0:1]
    out[...] = (gate / (1.0 + jnp.exp(-gate)) * up).astype(BF16)


def down_kernel(chips, groups, ids, *refs):
    pieces, ws, outs, held = refs[:chips], refs[chips : chips + 2], refs[chips + 2 : -1], refs[-1]
    rows = jnp.concatenate([p[...] for p in pieces], axis=0)
    unit = ws[0].shape[1]
    for h, w in enumerate(ws):
        y = dot(rows, w[...]).astype(BF16)
        held[:, :, :, h * unit : (h + 1) * unit] = y.reshape(chips, groups, ROWS, unit)
    for m in range(groups):
        for k in range(chips):
            outs[m][k * ROWS : (k + 1) * ROWS, :] = held[k, ids[2] ^ m]


def out_kernel(chips, groups, ids, *refs):
    sums, refs = refs[:groups], refs[groups:]
    xs, refs = refs[:chips], refs[chips:]
    ws, select, outs = refs[:4], refs[4], refs[5:]
    unit = xs[0].shape[2]
    mine = pl.ds(pl.multiple_of(ids[2] * ROWS, ROWS), ROWS)
    y = None
    for h in range(2):
        part = slice(h * unit, (h + 1) * unit)
        x = jnp.concatenate([p[h, mine, :] for p in xs], axis=0)
        down = sum(p[:, part].astype(F32) for p in sums)
        residual = (x.astype(F32) + down).astype(BF16)
        for i in range(2):
            w = ws[2 * h + i]
            term = dot(residual[:, i * w.shape[0] : (i + 1) * w.shape[0]], w[...])
            y = term if y is None else y + term
    rows = dot(select[...], y.astype(BF16)).astype(BF16)
    for k in range(chips):
        outs[k][...] = rows[k * 2 * ROWS : (k + 1) * 2 * ROWS]


def add_kernel(ids, *refs):
    pieces, mine, theirs = refs[:-2], refs[-2], refs[-1]
    total = sum(p[...].astype(F32) for p in pieces).astype(BF16)
    mine[...] = total[:ROWS]
    theirs[...] = total[ROWS:]


def pick_kernel(groups, ids, *refs):
    sources, out, sem = refs[:groups], refs[groups], refs[groups + 1]
    for h in range(groups):

        @pl.when((ids[0] ^ ids[2]) == h)
        def _():
            copy = pltpu.make_async_copy(sources[h], out, sem)
            copy.start()
            copy.wait()


def weights_kernel(ids, seg, dec, keys, out):
    slots = keys.shape[0]
    patch = lax.broadcasted_iota(jnp.int32, (dec.shape[0], slots), 1)
    allowed = patch <= seg[...]
    for h in range(out.shape[0]):
        part = slice(h * HD, (h + 1) * HD)
        scores = lax.dot_general(dec[:, part], keys[:, part], (((1,), (1,)), ((), ())), preferred_element_type=F32)
        scores = jnp.where(allowed, scores / math.sqrt(HD), -1e30)
        expon = jnp.exp(scores - jnp.max(scores, axis=1, keepdims=True))
        out[h] = (expon / jnp.sum(expon, axis=1, keepdims=True)).astype(BF16)


def mix_kernel(ids, mine, theirs, start, weights, dec, out):
    c = ids[1]
    slots = weights.shape[2]
    every = jnp.concatenate([mine[...], theirs[...]], axis=0)
    patch = lax.broadcasted_iota(jnp.int32, (slots, 2 * ROWS), 0)
    line = lax.broadcasted_iota(jnp.int32, (slots, 2 * ROWS), 1)
    parity = (c + line // ROWS - start[0:1, 0:1]) & 1
    values = dot((patch == parity + 2 * (line % ROWS)).astype(BF16), every).astype(BF16)
    for h in range(weights.shape[0]):
        part = slice(h * HD, (h + 1) * HD)
        out[:, part] = (dec[:, part].astype(F32) + dot(weights[h], values[:, part])).astype(BF16)


def body(enc_states, dec_states, segments, patch_keys, w_in, w_gate, w_up, w_down, w_out):
    seq, groups = lax.axis_size("seq"), lax.axis_size("mp")
    chips = seq // 2
    bytes_, width = enc_states.shape
    slots = patch_keys.shape[0] + 1
    heads = width // HD
    rows = groups * ROWS
    wide = w_in.shape[1]
    unit = w_gate.shape[0]
    ffw = w_gate.shape[1]
    index = lax.axis_index("seq")
    ids = jnp.stack([index // 2, index % 2, lax.axis_index("mp")]).astype(jnp.int32)

    def sibling(a):
        return lax.ppermute(a, "seq", [(i, i ^ 1) for i in range(seq)])

    def chip(a, k):
        return lax.ppermute(a, "seq", [(i, i ^ (2 * k)) for i in range(seq)])

    def plane(a, k):
        return lax.ppermute(a, "mp", [(i, i ^ k) for i in range(groups)])

    def spread_along(a, h, o):
        pairs = [(s * groups + ((s // 2) ^ h), s * groups + ((s // 2) ^ h ^ o)) for s in range(seq)]
        return lax.ppermute(a, ("seq", "mp"), pairs)

    def tree(a, have, offsets):
        have = dict(have)
        for o in offsets:
            for h in list(have):
                have[h ^ o] = spread_along(have[h], h, o)
        return have

    offsets = [1 << i for i in reversed(range(groups.bit_length() - 1))]
    half = unit // 2
    out_a = lax.dynamic_slice_in_dim(w_out, ids[1] * unit, half, 0)
    out_b = lax.dynamic_slice_in_dim(w_out, ids[1] * unit + half, half, 0)
    far_a = spread_along(out_a, 0, offsets[0])

    [pooled] = call(
        functools.partial(pool_kernel, slots),
        [shape((slots, width))],
        ids,
        segments.reshape(1, bytes_),
        enc_states,
        hbm=(0, 1),
        scratch=[
            pltpu.VMEM((1, bytes_), jnp.int32),
            pltpu.VMEM((bytes_, width), BF16),
            pltpu.SemaphoreType.DMA((2,)),
        ],
    )
    gathered = [pooled] + [chip(pooled, k) for k in range(1, chips)]
    theirs = sibling(jnp.concatenate(gathered, axis=0))
    packed, start, select = call(
        functools.partial(pack_kernel, chips, slots),
        [shape((ROWS, width)), shape((8, HD), jnp.int32), shape((seq * ROWS, chips * ROWS))],
        ids,
        *gathered,
        theirs,
        scratch=[pltpu.VMEM((seq * slots, width), BF16)],
    )
    gate_b, up_b, down_b = sibling(w_gate), sibling(w_up), sibling(w_down)
    pieces = [packed] + [plane(packed, k) for k in range(1, groups)]
    [x] = call(
        functools.partial(x_kernel, groups),
        [shape((rows, wide))],
        ids,
        *pieces,
        w_in,
        hbm=(groups,),
        scratch=[
            pltpu.VMEM((groups, ROWS, width), BF16),
            pltpu.VMEM((width, wide), BF16),
            pltpu.SemaphoreType.DMA((max(1, wide // 256),)),
        ],
        flops=2 * rows * width * wide,
    )
    pieces = [x] + [plane(x, k) for k in range(1, groups)]
    *xs, scale, out_a, out_b, far_a = call(
        functools.partial(spread_kernel, groups, chips),
        [shape((2, rows, unit)) for _ in range(chips)] + [shape((rows, HD), F32)],
        ids,
        *pieces,
        through=[out_a, out_b, far_a],
        scratch=[pltpu.VMEM((seq, rows, unit), BF16)],
    )

    def gate(piece, through=()):
        return call(
            gate_kernel,
            [shape((rows, 2 * ffw))],
            ids,
            piece,
            w_gate,
            gate_b,
            w_up,
            up_b,
            through=through,
            flops=8 * rows * unit * ffw,
        )

    far_b = spread_along(out_b, 0, offsets[0])
    partial, out_a, out_b, far_a = gate(xs[0], [out_a, out_b, far_a])
    xs = [xs[0]] + [chip(xs[k], k) for k in range(1, chips)]
    partial = [partial] + [chip(gate(xs[k])[0], k) for k in range(1, chips)]
    all_a = tree(out_a, {0: out_a, offsets[0]: far_a}, offsets[1:])
    all_b = tree(out_b, {0: out_b, offsets[0]: far_b}, offsets[1:])

    keys = jnp.pad(patch_keys, ((0, 1), (0, 0)))
    [weights] = call(
        weights_kernel, [shape((heads, bytes_, slots))], ids, segments.reshape(bytes_, 1), dec_states, keys
    )
    hidden, weights = call(hidden_kernel, [shape((rows, ffw))], ids, scale, *partial, through=[weights])
    hidden = [hidden] + [chip(hidden, k) for k in range(1, chips)]
    sums = call(
        functools.partial(down_kernel, chips, groups),
        [shape((chips * ROWS, 2 * unit)) for _ in range(groups)],
        ids,
        *hidden,
        w_down,
        down_b,
        scratch=[pltpu.VMEM((chips, groups, ROWS, 2 * unit), BF16)],
        flops=4 * chips * rows * unit * ffw,
    )
    sums = [sums[0]] + [plane(sums[k], k) for k in range(1, groups)]

    def pick(have):
        [mine] = call(
            functools.partial(pick_kernel, groups),
            [shape((half, width))],
            ids,
            *[have[h] for h in range(groups)],
            hbm=range(groups),
            scratch=[pltpu.SemaphoreType.DMA],
        )
        return mine

    mine_a, mine_b = pick(all_a), pick(all_b)
    outs = call(
        functools.partial(out_kernel, chips, groups),
        [shape((2 * ROWS, width)) for _ in range(chips)],
        ids,
        *sums,
        *xs,
        mine_a,
        mine_b,
        sibling(mine_a),
        sibling(mine_b),
        select,
        flops=2 * rows * width * wide,
    )
    outs = [outs[0]] + [chip(outs[k], k) for k in range(1, chips)]
    mine, theirs = call(add_kernel, [shape((ROWS, width))] * 2, ids, *outs)
    [decoded] = call(
        mix_kernel, [shape((bytes_, width))], ids, mine, sibling(theirs), start, weights, dec_states
    )
    return decoded


def solution(mesh):
    placed = (
        P(("seq", "mp"), None),
        P(("seq", "mp"), None),
        P(("seq", "mp")),
        P(("seq", "mp"), None),
        P(None, "mp"),
        P("seq", "mp"),
        P("seq", "mp"),
        P("mp", "seq"),
        P("mp", None),
    )
    return jax.shard_map(
        body, mesh=mesh, in_specs=placed, out_specs=P(("seq", "mp"), None), check_vma=False
    )
```

time: 134 us -> 165 us (1.23)
  waiting for transfers between devices: 61.3 us -> 83.5 us
  Pallas kernels: 18.6 us -> 30 us
  starting transfers between devices: 49.7 us -> 41.2 us
  local copies, waits for them, and re-layouts: 3.61 us -> 9.25 us
    ppermute x12 -> x9, waiting for transfers between devices: 17.3 us -> 37.7 us  [plane(): return lax.ppermute(a, 'mp', [(i, i ^ k) for i in range(groups)])]
    ppermute x12 -> x9, starting transfers between devices: 26.2 us -> 6.88 us  [plane(): return lax.ppermute(a, 'mp', [(i, i ^ k) for i in range(groups)])]
    ppermute x0 -> x6, waiting for transfers between devices: none -> 19 us  [spread_along(): return lax.ppermute(a, ('seq', 'mp'), pairs)]
    ppermute x18 -> x15, waiting for transfers between devices: 42.4 us -> 25.5 us  [chip(): return lax.ppermute(a, 'seq', [(i, i ^ 2 * k) for i in range(seq)])]
    ppermute x0 -> x6, starting transfers between devices: none -> 16.8 us  [spread_along(): return lax.ppermute(a, ('seq', 'mp'), pairs)]
    pallas_call x14 -> x16, Pallas kernels: 18.6 us -> 30 us  [call(): pl.pallas_call(run, out_shape=list(outs) + [shape(a.shape, a.dtype) for a...]
    ppermute x18 -> x15, starting transfers between devices: 22.9 us -> 16.3 us  [chip(): return lax.ppermute(a, 'seq', [(i, i ^ 2 * k) for i in range(seq)])]
    unnamed x20 -> x32, local copies, waits for them, and re-layouts: 3.48 us -> 6.21 us
  transfers between devices with their start and end apart: 35 -> 37, of which waited for: 23 -> 22; matrix products, arithmetic and copies ran while one was open for 0% -> 2% of each run, Pallas kernels for 10% -> 15%
where the time goes in v2:
time: 165 us; the launch traced here: 164 us
  waiting for transfers between devices  83.5 us (51%)
  starting transfers between devices  41.2 us (25%)
  Pallas kernels  30 us (18%)
  local copies, waits for them, and re-layouts  9.25 us (6%)
    ppermute x9, waiting for transfers between devices, plane(): return lax.ppermute(a, 'mp', [(i, i ^ k) for i in range(groups)])  37.7 us
    pallas_call x16, Pallas kernels, call(): pl.pallas_call(run, out_shape=list(outs) + [shape(a.shape, a.dtype) for a...  30 us
    ppermute x15, waiting for transfers between devices, chip(): return lax.ppermute(a, 'seq', [(i, i ^ 2 * k) for i in range(seq)])  25.5 us
    ppermute x6, waiting for transfers between devices, spread_along(): return lax.ppermute(a, ('seq', 'mp'), pairs)  19 us
    ppermute x6, starting transfers between devices, spread_along(): return lax.ppermute(a, ('seq', 'mp'), pairs)  16.8 us
    ppermute x15, starting transfers between devices, chip(): return lax.ppermute(a, 'seq', [(i, i ^ 2 * k) for i in range(seq)])  16.3 us
    ppermute x9, starting transfers between devices, plane(): return lax.ppermute(a, 'mp', [(i, i ^ k) for i in range(groups)])  6.88 us
    unnamed x32, local copies, waits for them, and re-layouts  6.21 us
  transfers between devices with their start and end apart: 37, of which 22 were waited for; matrix products, arithmetic and copies ran while one was open for 2% of the time, Pallas kernels for 15%

profile of v2, /device:TPU:0, one launch (start us, length us, event | category | flops | bytes accessed | tf_op | source)
XLA Modules:
  0.0 164.4 jit_solution(4917900197326598927)
XLA Ops:
  0.1 1.0 copy-done.6
  1.1 0.7 copy-done.14
  1.8 1.1 shard_map.91.refs_0_
  2.9 3.0 %collective-permute-start = (bf16[32,1280]{1,0:T(8,128)(2,1)S(1)}, bf16[32,1280]{1,0:T(8,128)(2,1)S(1)}, u32[]{:S(2)}, u32[]{:S(2)}) collective-permute-start(bf16[32,1280]{1,0:T(8,128)(2,1)S(1)} %shard_map.91.refs_0_), channel_id=1, source_target_pairs={{0,8},{4,12},{8,0},{12,4},{16,24},{20,28},{24,16},{28,20},{1,9},{5... | collective-permute-start | bytes 245768 | tf_op jit(solution)/shard_map/ppermute | solution.py:255
  5.9 1.5 collective-permute-start.1
  7.9 0.7 collective-permute-done.refs_1_
  8.6 2.6 %collective-permute-done.1.refs_2_ = bf16[32,1280]{1,0:T(8,128)(2,1)S(1)} collective-permute-done((bf16[32,1280]{1,0:T(8,128)(2,1)S(1)}, bf16[32,1280]{1,0:T(8,128)(2,1)S(1)}, u32[]{:S(2)}, u32[]{:S(2)}) %collective-permute-start.1) | collective-permute-done | bytes 81952 | tf_op jit(solution)/shard_map/ppermute | solution.py:255
  11.2 1.5 collective-permute-done.2.refs_3_
  12.9 1.4 constant_dynamic-slice_fusion
  14.2 4.5 %collective-permute-start.10 = (bf16[256,1280]{1,0:T(8,128)(2,1)S(1)}, bf16[256,1280]{1,0:T(8,128)(2,1)S(1)}, u32[]{:S(2)}, u32[]{:S(2)}) collective-permute-start(bf16[256,1280]{1,0:T(8,128)(2,1)S(1)} %get-tuple-element.60.refs_4_), channel_id=1, source_target_pairs={{0,2},{4,6},{9,11},{13,15},{18,16},{22,20},{27,25},{31,29}} | collective-permute-start | bytes 1966088 | tf_op jit(solution)/shard_map/ppermute | solution.py:262
  18.8 0.9 shard_map.92
  20.1 14.6 %collective-permute-done.4.refs_1_ = bf16[16,1280]{1,0:T(8,128)(2,1)S(1)} collective-permute-done((bf16[16,1280]{1,0:T(8,128)(2,1)S(1)}, bf16[16,1280]{1,0:T(8,128)(2,1)S(1)}, u32[]{:S(2)}, u32[]{:S(2)}) %collective-permute-start.4) | collective-permute-done | bytes 40992 | tf_op jit(solution)/shard_map/ppermute | solution.py:258
  34.7 0.9 collective-permute-done.5.refs_2_
  35.6 5.0 %collective-permute-done.6.refs_3_ = bf16[16,1280]{1,0:T(8,128)(2,1)S(1)} collective-permute-done((bf16[16,1280]{1,0:T(8,128)(2,1)S(1)}, bf16[16,1280]{1,0:T(8,128)(2,1)S(1)}, u32[]{:S(2)}, u32[]{:S(2)}) %collective-permute-start.6) | collective-permute-done | bytes 40992 | tf_op jit(solution)/shard_map/ppermute | solution.py:258
  40.5 2.2 %shard_map.93.refs_0_ = bf16[64,1024]{1,0:T(8,128)(2,1)S(1)} custom-call(s32[3]{0:T(128)S(1)} %pad_add_fusion.ids, bf16[16,1280]{1,0:T(8,128)(2,1)S(1)} %get-tuple-element.32.refs_0_, bf16[16,1280]{1,0:T(8,128)(2,1)S(1)} %collective-permute-done.4.refs_1_, bf16[16,1280]{1,0:T(8,128)(2,1)S(1)} %collective-permute-done.5.refs_2_, ...), custom_call_target="tpu_custom_call" | custom-call | flops 167772160 | bytes 2916352 | tf_op jit(solution)/shard_map/pallas_call | solution.py:34
  42.8 1.0 collective-permute-start.7
  43.8 4.9 %collective-permute-done.7.refs_1_ = bf16[64,1024]{1,0:T(8,128)(2,1)S(1)} collective-permute-done((bf16[64,1024]{1,0:T(8,128)(2,1)S(1)}, bf16[64,1024]{1,0:T(8,128)(2,1)S(1)}, u32[]{:S(2)}, u32[]{:S(2)}) %collective-permute-start.7) | collective-permute-done | bytes 131104 | tf_op jit(solution)/shard_map/ppermute | solution.py:258
  49.0 4.7 %collective-permute-done.8.refs_2_ = bf16[64,1024]{1,0:T(8,128)(2,1)S(1)} collective-permute-done((bf16[64,1024]{1,0:T(8,128)(2,1)S(1)}, bf16[64,1024]{1,0:T(8,128)(2,1)S(1)}, u32[]{:S(2)}, u32[]{:S(2)}) %collective-permute-start.8) | collective-permute-done | bytes 131104 | tf_op jit(solution)/shard_map/ppermute | solution.py:258
  53.6 1.9 %collective-permute-done.9.refs_3_ = bf16[64,1024]{1,0:T(8,128)(2,1)S(1)} collective-permute-done((bf16[64,1024]{1,0:T(8,128)(2,1)S(1)}, bf16[64,1024]{1,0:T(8,128)(2,1)S(1)}, u32[]{:S(2)}, u32[]{:S(2)}) %collective-permute-start.9) | collective-permute-done | bytes 131104 | tf_op jit(solution)/shard_map/ppermute | solution.py:258
  55.6 0.7 shard_map.94
  56.3 3.4 %collective-permute-start.29 = (bf16[256,1280]{1,0:T(8,128)(2,1)S(1)}, bf16[256,1280]{1,0:T(8,128)(2,1)S(1)}, u32[]{:S(2)}, u32[]{:S(2)}) collective-permute-start(bf16[256,1280]{1,0:T(8,128)(2,1)S(1)} %get-tuple-element.36.refs_6_), channel_id=1, source_target_pairs={{0,2},{4,6},{9,11},{13,15},{18,16},{22,20},{27,25},{31,29}} | collective-permute-start | bytes 1966088 | tf_op jit(solution)/shard_map/ppermute | solution.py:262
  59.8 12.9 %collective-permute-done.29.refs_2_ = bf16[256,1280]{1,0:T(8,128)(2,1)S(1)} collective-permute-done((bf16[256,1280]{1,0:T(8,128)(2,1)S(1)}, bf16[256,1280]{1,0:T(8,128)(2,1)S(1)}, u32[]{:S(2)}, u32[]{:S(2)}) %collective-permute-start.29) | collective-permute-done | bytes 655392 | tf_op jit(solution)/shard_map/ppermute | solution.py:262
  72.7 0.7 collective-permute-start.30
  73.6 2.9 %shard_map.95 = (bf16[64,3584]{1,0:T(8,128)(2,1)S(1)}, bf16[256,1280]{1,0:T(8,128)(2,1)S(1)}, bf16[256,1280]{1,0:T(8,128)(2,1)S(1)}, bf16[256,1280]{1,0:T(8,128)(2,1)S(1)}) custom-call(s32[3]{0:T(128)S(1)} %pad_add_fusion.ids, bf16[2,64,512]{2,1,0:T(8,128)(2,1)S(1)} %get-tuple-element.34.refs_0_.refs_4_, ...), custom_call_target="tpu_custom_call", output_to_operand_aliasing={{1}: (6, {}), {2}: (7, {}), {3}: (8, {})} | custom-call | flops 469762048 | bytes 7929856 | tf_op jit(solution)/shard_map/pallas_call | solution.py:34
  76.6 6.1 %collective-permute-start.28 = (bf16[256,1280]{1,0:T(8,128)(2,1)S(1)}, bf16[256,1280]{1,0:T(8,128)(2,1)S(1)}, u32[]{:S(2)}, u32[]{:S(2)}) collective-permute-start(bf16[256,1280]{1,0:T(8,128)(2,1)S(1)} %get-tuple-element.49.refs_0_), channel_id=1, source_target_pairs={{0,1},{4,5},{9,8},{13,12},{18,19},{22,23},{27,26},{31,30}} | collective-permute-start | bytes 1966088 | tf_op jit(solution)/shard_map/ppermute | solution.py:262
  82.7 1.3 collective-permute-start.26
  84.1 5.9 %collective-permute-done.17.refs_0_.refs_7_ = bf16[2,64,512]{2,1,0:T(8,128)(2,1)S(1)} collective-permute-done((bf16[2,64,512]{2,1,0:T(8,128)(2,1)S(1)}, bf16[2,64,512]{2,1,0:T(8,128)(2,1)S(1)}, u32[]{:S(2)}, u32[]{:S(2)}) %collective-permute-start.17) | collective-permute-done | bytes 131104 | tf_op jit(solution)/shard_map/ppermute | solution.py:255
  89.9 0.7 collective-permute-start.27
  90.6 2.9 %shard_map.96 = bf16[64,3584]{1,0:T(8,128)(2,1)S(1)} custom-call(s32[3]{0:T(128)S(1)} %pad_add_fusion.ids, bf16[2,64,512]{2,1,0:T(8,128)(2,1)S(1)} %collective-permute-done.13.refs_0_.refs_5_, bf16[512,1792]{1,0:T(8,128)(2,1)S(1)} %copy-done, bf16[512,1792]{1,0:T(8,128)(2,1)S(1)} %collective-permute-done.11.refs_2_, bf16[512,1792]{1,0:T(8,128)(2,1)S(1)} %copy-done.1, ...), custom_call_target="tpu_custom_call" | custom-call | flops 469762048 | bytes 7929856 | tf_op jit(solution)/shard_map/pallas_call | solution.py:34
  93.7 3.7 %shard_map.97 = bf16[64,3584]{1,0:T(8,128)(2,1)} custom-call(s32[3]{0:T(128)S(1)} %pad_add_fusion.ids, bf16[2,64,512]{2,1,0:T(8,128)(2,1)S(1)} %collective-permute-done.15.refs_0_.refs_6_, bf16[512,1792]{1,0:T(8,128)(2,1)S(1)} %copy-done, bf16[512,1792]{1,0:T(8,128)(2,1)S(1)} %collective-permute-done.11.refs_2_, bf16[512,1792]{1,0:T(8,128)(2,1)S(1)} %copy-done.1, ...), custom_call_target="tpu_custom_call" | custom-call | flops 469762048 | bytes 7929856 | tf_op jit(solution)/shard_map/pallas_call | solution.py:34
  97.3 3.7 %shard_map.98 = bf16[64,3584]{1,0:T(8,128)(2,1)} custom-call(s32[3]{0:T(128)S(1)} %pad_add_fusion.ids, bf16[2,64,512]{2,1,0:T(8,128)(2,1)S(1)} %collective-permute-done.17.refs_0_.refs_7_, bf16[512,1792]{1,0:T(8,128)(2,1)S(1)} %copy-done, bf16[512,1792]{1,0:T(8,128)(2,1)S(1)} %collective-permute-done.11.refs_2_, bf16[512,1792]{1,0:T(8,128)(2,1)S(1)} %copy-done.1, ...), custom_call_target="tpu_custom_call" | custom-call | flops 469762048 | bytes 7929856 | tf_op jit(solution)/shard_map/pallas_call | solution.py:34
  101.0 1.1 collective-permute-start.16
  102.2 6.1 %collective-permute-done.26.refs_1_ = bf16[256,1280]{1,0:T(8,128)(2,1)S(1)} collective-permute-done((bf16[256,1280]{1,0:T(8,128)(2,1)S(1)}, bf16[256,1280]{1,0:T(8,128)(2,1)S(1)}, u32[]{:S(2)}, u32[]{:S(2)}) %collective-permute-start.26) | collective-permute-done | bytes 655392 | tf_op jit(solution)/shard_map/ppermute | solution.py:262
  108.2 0.8 shard_map.103.refs_9_
  109.1 1.0 shard_map.102.refs_8_
  110.1 0.8 copy-done.9
  111.4 0.8 copy.17.refs_0_
  112.2 0.9 pad.4.refs_2_
  113.1 0.9 copy-done.11
  114.0 1.5 shard_map.99.refs_5_
  115.5 4.1 %collective-permute-done.16.refs_3_ = bf16[64,3584]{1,0:T(8,128)(2,1)} collective-permute-done((bf16[64,3584]{1,0:T(8,128)(2,1)}, bf16[64,3584]{1,0:T(8,128)(2,1)}, u32[]{:S(2)}, u32[]{:S(2)}) %collective-permute-start.16) | collective-permute-done | bytes 458784 | tf_op jit(solution)/shard_map/ppermute | solution.py:255
  119.6 1.0 copy-done.8
  120.7 1.0 copy-done.10
  121.7 0.8 copy-done.13
  122.4 1.7 %shard_map.100 = (bf16[64,1792]{1,0:T(8,128)(2,1)S(1)}, bf16[10,192,32]{2,1,0:T(8,128)(2,1)S(1)}) custom-call(s32[3]{0:T(128)S(1)} %pad_add_fusion.ids, f32[64,128]{1,0:T(8,128)S(1)} %copy-done.13, bf16[64,3584]{1,0:T(8,128)(2,1)S(1)} %copy-done.8, bf16[64,3584]{1,0:T(8,128)(2,1)S(1)} %copy-done.10, ...), custom_call_target="tpu_custom_call", output_to_operand_aliasing={{1}: (6, {})} | custom-call | bytes 2097152 | tf_op jit(solution)/shard_map/pallas_call | solution.py:34
  124.1 2.1 %collective-permute-start.19 = (bf16[64,1792]{1,0:T(8,128)(2,1)S(1)}, bf16[64,1792]{1,0:T(8,128)(2,1)S(1)}, u32[]{:S(2)}, u32[]{:S(2)}) collective-permute-start(bf16[64,1792]{1,0:T(8,128)(2,1)S(1)} %get-tuple-element.42.refs_0_), channel_id=1, source_target_pairs={{0,8},{4,12},{8,0},{12,4},{16,24},{20,28},{24,16},{28,20},{1,9},{5... | collective-permute-start | bytes 688136 | tf_op jit(solution)/shard_map/ppermute | solution.py:255
  126.2 1.5 collective-permute-start.21
  127.7 2.5 %collective-permute-done.19.refs_1_ = bf16[64,1792]{1,0:T(8,128)(2,1)S(1)} collective-permute-done((bf16[64,1792]{1,0:T(8,128)(2,1)S(1)}, bf16[64,1792]{1,0:T(8,128)(2,1)S(1)}, u32[]{:S(2)}, u32[]{:S(2)}) %collective-permute-start.19) | collective-permute-done | bytes 229408 | tf_op jit(solution)/shard_map/ppermute | solution.py:255
  130.3 4.4 %collective-permute-done.20.refs_2_ = bf16[64,1792]{1,0:T(8,128)(2,1)S(1)} collective-permute-done((bf16[64,1792]{1,0:T(8,128)(2,1)S(1)}, bf16[64,1792]{1,0:T(8,128)(2,1)S(1)}, u32[]{:S(2)}, u32[]{:S(2)}) %collective-permute-start.20) | collective-permute-done | bytes 229408 | tf_op jit(solution)/shard_map/ppermute | solution.py:255
  134.7 3.2 %shard_map.101 = (bf16[64,1024]{1,0:T(8,128)(2,1)S(1)}, bf16[64,1024]{1,0:T(8,128)(2,1)S(1)}, bf16[64,1024]{1,0:T(8,128)(2,1)S(1)}, bf16[64,1024]{1,0:T(8,128)(2,1)S(1)}) custom-call(s32[3]{0:T(128)S(1)} %pad_add_fusion.ids, bf16[64,1792]{1,0:T(8,128)(2,1)S(1)} %get-tuple-element.42.refs_0_, bf16[64,1792]{1,0:T(8,128)(2,1)S(1)} %collective-permute-done.19.refs_1_, ...), custom_call_target="tpu_custom_call" | custom-call | flops 939524096 | bytes 5111808 | tf_op jit(solution)/shard_map/pallas_call | solution.py:34
  137.9 1.8 %collective-permute-start.23 = (bf16[64,1024]{1,0:T(8,128)(2,1)S(1)}, bf16[64,1024]{1,0:T(8,128)(2,1)S(1)}, u32[]{:S(2)}, u32[]{:S(2)}) collective-permute-start(bf16[64,1024]{1,0:T(8,128)(2,1)S(1)} %get-tuple-element.44), channel_id=1, source_target_pairs={{0,1},{1,0},{2,3},{3,2},{4,5},{5,4},{6,7},{7,6},{8,9},{9,8},{10,11... | collective-permute-start | bytes 393224 | tf_op jit(solution)/shard_map/ppermute | solution.py:258
  139.7 1.9 %collective-permute-start.24 = (bf16[64,1024]{1,0:T(8,128)(2,1)S(1)}, bf16[64,1024]{1,0:T(8,128)(2,1)S(1)}, u32[]{:S(2)}, u32[]{:S(2)}) collective-permute-start(bf16[64,1024]{1,0:T(8,128)(2,1)S(1)} %get-tuple-element.45), channel_id=1, source_target_pairs={{0,2},{1,3},{2,0},{3,1},{4,6},{5,7},{6,4},{7,5},{8,10},{9,11},{10,... | collective-permute-start | bytes 393224 | tf_op jit(solution)/shard_map/ppermute | solution.py:258
  141.7 1.4 collective-permute-start.25
  143.1 1.3 collective-permute-done.23.refs_1_
  144.4 1.7 %collective-permute-done.24.refs_2_ = bf16[64,1024]{1,0:T(8,128)(2,1)S(1)} collective-permute-done((bf16[64,1024]{1,0:T(8,128)(2,1)S(1)}, bf16[64,1024]{1,0:T(8,128)(2,1)S(1)}, u32[]{:S(2)}, u32[]{:S(2)}) %collective-permute-start.24) | collective-permute-done | bytes 131104 | tf_op jit(solution)/shard_map/ppermute | solution.py:258
  146.1 2.8 %collective-permute-done.25.refs_3_ = bf16[64,1024]{1,0:T(8,128)(2,1)S(1)} collective-permute-done((bf16[64,1024]{1,0:T(8,128)(2,1)S(1)}, bf16[64,1024]{1,0:T(8,128)(2,1)S(1)}, u32[]{:S(2)}, u32[]{:S(2)}) %collective-permute-start.25) | collective-permute-done | bytes 131104 | tf_op jit(solution)/shard_map/ppermute | solution.py:258
  148.9 1.4 shard_map.104
  150.3 5.1 %collective-permute-start.33 = (bf16[32,1280]{1,0:T(8,128)(2,1)S(1)}, bf16[32,1280]{1,0:T(8,128)(2,1)S(1)}, u32[]{:S(2)}, u32[]{:S(2)}) collective-permute-start(bf16[32,1280]{1,0:T(8,128)(2,1)S(1)} %get-tuple-element.52), channel_id=1, source_target_pairs={{0,8},{4,12},{8,0},{12,4},{16,24},{20,28},{24,16},{28,20},{1,9},{5... | collective-permute-start | bytes 245768 | tf_op jit(solution)/shard_map/ppermute | solution.py:255
  155.4 1.5 collective-permute-start.35
  157.0 0.9 collective-permute-done.33.refs_1_
  157.9 2.0 %collective-permute-done.34.refs_2_ = bf16[32,1280]{1,0:T(8,128)(2,1)S(1)} collective-permute-done((bf16[32,1280]{1,0:T(8,128)(2,1)S(1)}, bf16[32,1280]{1,0:T(8,128)(2,1)S(1)}, u32[]{:S(2)}, u32[]{:S(2)}) %collective-permute-start.34) | collective-permute-done | bytes 81952 | tf_op jit(solution)/shard_map/ppermute | solution.py:255
  159.9 0.9 collective-permute-done.35.refs_3_
  161.5 1.2 collective-permute-done.36.refs_1_
  162.7 1.7 %shard_map.106 = bf16[192,1280]{1,0:T(8,128)(2,1)} custom-call(s32[3]{0:T(128)S(1)} %pad_add_fusion.ids, bf16[16,1280]{1,0:T(8,128)(2,1)S(1)} %get-tuple-element.55.refs_0_, bf16[16,1280]{1,0:T(8,128)(2,1)S(1)} %collective-permute-done.36.refs_1_, s32[8,128]{1,0:T(8,128)S(1)} %get-tuple-element.57.refs_2_, ...), custom_call_target="tpu_custom_call" | custom-call | bytes 1191936 | tf_op jit(solution)/shard_map/pallas_call | solution.py:34
  (63 shorter events, 3.1 us)
Async XLA Ops:
  0.1 1.0 copy-start.6
  1.1 0.7 copy-start.14
  2.9 5.7 %collective-permute-start = (bf16[32,1280]{1,0:T(8,128)(2,1)S(1)}, bf16[32,1280]{1,0:T(8,128)(2,1)S(1)}, u32[]{:S(2)}, u32[]{:S(2)}) collective-permute-start(bf16[32,1280]{1,0:T(8,128)(2,1)S(1)} %shard_map.91.refs_0_), channel_id=1, source_target_pairs={{0,8},{4,12},{8,0},{12,4},{16,24},{20,28},{24,16},{28,20},{1,9},{5... | collective-permute-start | bytes 245768 | tf_op jit(solution)/shard_map/ppermute | solution.py:255
  5.9 5.3 %collective-permute-start.1 = (bf16[32,1280]{1,0:T(8,128)(2,1)S(1)}, bf16[32,1280]{1,0:T(8,128)(2,1)S(1)}, u32[]{:S(2)}, u32[]{:S(2)}) collective-permute-start(bf16[32,1280]{1,0:T(8,128)(2,1)S(1)} %shard_map.91.refs_0_), channel_id=1, source_target_pairs={{0,16},{4,20},{8,24},{12,28},{16,0},{20,4},{24,8},{28,12},{1,17},{... | collective-permute-start | bytes 245768 | tf_op jit(solution)/shard_map/ppermute | solution.py:255
  7.4 5.3 %collective-permute-start.2 = (bf16[32,1280]{1,0:T(8,128)(2,1)S(1)}, bf16[32,1280]{1,0:T(8,128)(2,1)S(1)}, u32[]{:S(2)}, u32[]{:S(2)}) collective-permute-start(bf16[32,1280]{1,0:T(8,128)(2,1)S(1)} %shard_map.91.refs_0_), channel_id=1, source_target_pairs={{0,24},{4,28},{8,16},{12,20},{16,8},{20,12},{24,0},{28,4},{1,25},{... | collective-permute-start | bytes 245768 | tf_op jit(solution)/shard_map/ppermute | solution.py:255
  7.4 66.1 %collective-permute-start.11 = (bf16[512,1792]{1,0:T(8,128)(2,1)}, bf16[512,1792]{1,0:T(8,128)(2,1)S(1)}, u32[]{:S(2)}, u32[]{:S(2)}) collective-permute-start(bf16[512,1792]{1,0:T(8,128)(2,1)} %refs_1_.10), channel_id=1, source_target_pairs={{0,4},{4,0},{8,12},{12,8},{16,20},{20,16},{24,28},{28,24},{1,5},{5... | collective-permute-start | bytes 5505032 | tf_op jit(solution)/shard_map/ppermute | solution.py:252
  7.4 66.2 %collective-permute-start.12 = (bf16[512,1792]{1,0:T(8,128)(2,1)}, bf16[512,1792]{1,0:T(8,128)(2,1)}, u32[]{:S(2)}, u32[]{:S(2)}) collective-permute-start(bf16[512,1792]{1,0:T(8,128)(2,1)} %refs_3_.7), channel_id=1, source_target_pairs={{0,4},{4,0},{8,12},{12,8},{16,20},{20,16},{24,28},{28,24},{1,5},{5... | collective-permute-start | bytes 5505032 | tf_op jit(solution)/shard_map/ppermute | solution.py:252
  7.9 32.6 %copy-start.2 = (bf16[1280,1024]{1,0:T(8,128)(2,1)S(1)}, bf16[1280,1024]{1,0:T(8,128)(2,1)}, u32[]{:S(2)}) copy-start(bf16[1280,1024]{1,0:T(8,128)(2,1)} %refs_4_.3) | copy-start | bytes 7864324
  12.8 6.0 %collective-permute-start.3 = (bf16[128,1280]{1,0:T(8,128)(2,1)S(1)}, bf16[128,1280]{1,0:T(8,128)(2,1)S(1)}, u32[]{:S(2)}, u32[]{:S(2)}) collective-permute-start(bf16[128,1280]{1,0:T(8,128)(2,1)S(1)} %pad_maximum_fusion), channel_id=1, source_target_pairs={{0,4},{4,0},{8,12},{12,8},{16,20},{20,16},{24,28},{28,24},{1,5},{5... | collective-permute-start | bytes 983048 | tf_op jit(solution)/shard_map/ppermute | solution.py:252
  14.2 41.3 %collective-permute-start.10 = (bf16[256,1280]{1,0:T(8,128)(2,1)S(1)}, bf16[256,1280]{1,0:T(8,128)(2,1)S(1)}, u32[]{:S(2)}, u32[]{:S(2)}) collective-permute-start(bf16[256,1280]{1,0:T(8,128)(2,1)S(1)} %get-tuple-element.60.refs_4_), channel_id=1, source_target_pairs={{0,2},{4,6},{9,11},{13,15},{18,16},{22,20},{27,25},{31,29}} | collective-permute-start | bytes 1966088 | tf_op jit(solution)/shard_map/ppermute | solution.py:262
  19.7 15.0 %collective-permute-start.4 = (bf16[16,1280]{1,0:T(8,128)(2,1)S(1)}, bf16[16,1280]{1,0:T(8,128)(2,1)S(1)}, u32[]{:S(2)}, u32[]{:S(2)}) collective-permute-start(bf16[16,1280]{1,0:T(8,128)(2,1)S(1)} %get-tuple-element.32.refs_0_), channel_id=1, source_target_pairs={{0,1},{1,0},{2,3},{3,2},{4,5},{5,4},{6,7},{7,6},{8,9},{9,8},{10,11... | collective-permute-start | bytes 122888 | tf_op jit(solution)/shard_map/ppermute | solution.py:258
  19.8 15.8 %collective-permute-start.5 = (bf16[16,1280]{1,0:T(8,128)(2,1)S(1)}, bf16[16,1280]{1,0:T(8,128)(2,1)S(1)}, u32[]{:S(2)}, u32[]{:S(2)}) collective-permute-start(bf16[16,1280]{1,0:T(8,128)(2,1)S(1)} %get-tuple-element.32.refs_0_), channel_id=1, source_target_pairs={{0,2},{1,3},{2,0},{3,1},{4,6},{5,7},{6,4},{7,5},{8,10},{9,11},{10,... | collective-permute-start | bytes 122888 | tf_op jit(solution)/shard_map/ppermute | solution.py:258
  34.7 5.8 %collective-permute-start.6 = (bf16[16,1280]{1,0:T(8,128)(2,1)S(1)}, bf16[16,1280]{1,0:T(8,128)(2,1)S(1)}, u32[]{:S(2)}, u32[]{:S(2)}) collective-permute-start(bf16[16,1280]{1,0:T(8,128)(2,1)S(1)} %get-tuple-element.32.refs_0_), channel_id=1, source_target_pairs={{0,3},{1,2},{2,1},{3,0},{4,7},{5,6},{6,5},{7,4},{8,11},{9,10},{10,... | collective-permute-start | bytes 122888 | tf_op jit(solution)/shard_map/ppermute | solution.py:258
  40.5 33.1 %copy-start.1 = (bf16[512,1792]{1,0:T(8,128)(2,1)S(1)}, bf16[512,1792]{1,0:T(8,128)(2,1)}, u32[]{:S(2)}) copy-start(bf16[512,1792]{1,0:T(8,128)(2,1)} %refs_3_.7) | copy-start | bytes 5505028
  42.7 30.9 %copy-start = (bf16[512,1792]{1,0:T(8,128)(2,1)S(1)}, bf16[512,1792]{1,0:T(8,128)(2,1)}, u32[]{:S(2)}) copy-start(bf16[512,1792]{1,0:T(8,128)(2,1)} %refs_1_.10) | copy-start | bytes 5505028
  42.8 5.9 %collective-permute-start.7 = (bf16[64,1024]{1,0:T(8,128)(2,1)S(1)}, bf16[64,1024]{1,0:T(8,128)(2,1)S(1)}, u32[]{:S(2)}, u32[]{:S(2)}) collective-permute-start(bf16[64,1024]{1,0:T(8,128)(2,1)S(1)} %shard_map.93.refs_0_), channel_id=1, source_target_pairs={{0,1},{1,0},{2,3},{3,2},{4,5},{5,4},{6,7},{7,6},{8,9},{9,8},{10,11... | collective-permute-start | bytes 393224 | tf_op jit(solution)/shard_map/ppermute | solution.py:258
  43.8 9.8 %collective-permute-start.8 = (bf16[64,1024]{1,0:T(8,128)(2,1)S(1)}, bf16[64,1024]{1,0:T(8,128)(2,1)S(1)}, u32[]{:S(2)}, u32[]{:S(2)}) collective-permute-start(bf16[64,1024]{1,0:T(8,128)(2,1)S(1)} %shard_map.93.refs_0_), channel_id=1, source_target_pairs={{0,2},{1,3},{2,0},{3,1},{4,6},{5,7},{6,4},{7,5},{8,10},{9,11},{10,... | collective-permute-start | bytes 393224 | tf_op jit(solution)/shard_map/ppermute | solution.py:258
  48.7 6.9 %collective-permute-start.9 = (bf16[64,1024]{1,0:T(8,128)(2,1)S(1)}, bf16[64,1024]{1,0:T(8,128)(2,1)S(1)}, u32[]{:S(2)}, u32[]{:S(2)}) collective-permute-start(bf16[64,1024]{1,0:T(8,128)(2,1)S(1)} %shard_map.93.refs_0_), channel_id=1, source_target_pairs={{0,3},{1,2},{2,1},{3,0},{4,7},{5,6},{6,5},{7,4},{8,11},{9,10},{10,... | collective-permute-start | bytes 393224 | tf_op jit(solution)/shard_map/ppermute | solution.py:258
  56.3 20.3 %copy-start.12 = (f32[64,128]{1,0:T(8,128)}, f32[64,128]{1,0:T(8,128)S(1)}, u32[]{:S(2)}) copy-start(f32[64,128]{1,0:T(8,128)S(1)} %get-tuple-element.33.refs_0_) | copy-start | bytes 98308
  56.3 16.4 %collective-permute-start.29 = (bf16[256,1280]{1,0:T(8,128)(2,1)S(1)}, bf16[256,1280]{1,0:T(8,128)(2,1)S(1)}, u32[]{:S(2)}, u32[]{:S(2)}) collective-permute-start(bf16[256,1280]{1,0:T(8,128)(2,1)S(1)} %get-tuple-element.36.refs_6_), channel_id=1, source_target_pairs={{0,2},{4,6},{9,11},{13,15},{18,16},{22,20},{27,25},{31,29}} | collective-permute-start | bytes 1966088 | tf_op jit(solution)/shard_map/ppermute | solution.py:262
  59.7 66.5 %collective-permute-start.22 = (bf16[1792,512]{1,0:T(8,128)(2,1)}, bf16[1792,512]{1,0:T(8,128)(2,1)}, u32[]{:S(2)}, u32[]{:S(2)}) collective-permute-start(bf16[1792,512]{1,0:T(8,128)(2,1)} %refs_4_.4), channel_id=1, source_target_pairs={{0,4},{4,0},{8,12},{12,8},{16,20},{20,16},{24,28},{28,24},{1,5},{5... | collective-permute-start | bytes 5505032 | tf_op jit(solution)/shard_map/ppermute | solution.py:252
  72.7 20.8 %collective-permute-start.30 = (bf16[256,1280]{1,0:T(8,128)(2,1)S(1)}, bf16[256,1280]{1,0:T(8,128)(2,1)S(1)}, u32[]{:S(2)}, u32[]{:S(2)}) collective-permute-start(bf16[256,1280]{1,0:T(8,128)(2,1)S(1)} %collective-permute-done.29.refs_2_), channel_id=1, source_target_pairs={{2,3},{6,7},{11,10},{15,14},{16,17},{20,21},{25,24},{29,28}} | collective-permute-start | bytes 1966088 | tf_op jit(solution)/shard_map/ppermute | solution.py:262
  73.4 9.2 %collective-permute-start.13 = (bf16[2,64,512]{2,1,0:T(8,128)(2,1)S(1)}, bf16[2,64,512]{2,1,0:T(8,128)(2,1)S(1)}, u32[]{:S(2)}, u32[]{:S(2)}) collective-permute-start(bf16[2,64,512]{2,1,0:T(8,128)(2,1)S(1)} %get-tuple-element.39), channel_id=1, source_target_pairs={{0,8},{4,12},{8,0},{12,4},{16,24},{20,28},{24,16},{28,20},{1,9},{5... | collective-permute-start | bytes 393224 | tf_op jit(solution)/shard_map/ppermute | solution.py:255
  73.5 10.5 %collective-permute-start.15 = (bf16[2,64,512]{2,1,0:T(8,128)(2,1)S(1)}, bf16[2,64,512]{2,1,0:T(8,128)(2,1)S(1)}, u32[]{:S(2)}, u32[]{:S(2)}) collective-permute-start(bf16[2,64,512]{2,1,0:T(8,128)(2,1)S(1)} %get-tuple-element.40), channel_id=1, source_target_pairs={{0,16},{4,20},{8,24},{12,28},{16,0},{20,4},{24,8},{28,12},{1,17},{... | collective-permute-start | bytes 393224 | tf_op jit(solution)/shard_map/ppermute | solution.py:255
  76.6 17.0 %copy-start.7 = (bf16[64,3584]{1,0:T(8,128)(2,1)}, bf16[64,3584]{1,0:T(8,128)(2,1)S(1)}, u32[]{:S(2)}) copy-start(bf16[64,3584]{1,0:T(8,128)(2,1)S(1)} %get-tuple-element.38.refs_1_) | copy-start | bytes 1376260
  76.6 24.4 %collective-permute-start.28 = (bf16[256,1280]{1,0:T(8,128)(2,1)S(1)}, bf16[256,1280]{1,0:T(8,128)(2,1)S(1)}, u32[]{:S(2)}, u32[]{:S(2)}) collective-permute-start(bf16[256,1280]{1,0:T(8,128)(2,1)S(1)} %get-tuple-element.49.refs_0_), channel_id=1, source_target_pairs={{0,1},{4,5},{9,8},{13,12},{18,19},{22,23},{27,26},{31,30}} | collective-permute-start | bytes 1966088 | tf_op jit(solution)/shard_map/ppermute | solution.py:262
  82.7 25.6 %collective-permute-start.26 = (bf16[256,1280]{1,0:T(8,128)(2,1)S(1)}, bf16[256,1280]{1,0:T(8,128)(2,1)S(1)}, u32[]{:S(2)}, u32[]{:S(2)}) collective-permute-start(bf16[256,1280]{1,0:T(8,128)(2,1)S(1)} %get-tuple-element.47.refs_0_), channel_id=1, source_target_pairs={{0,1},{4,5},{9,8},{13,12},{18,19},{22,23},{27,26},{31,30}} | collective-permute-start | bytes 1966088 | tf_op jit(solution)/shard_map/ppermute | solution.py:262
  84.0 5.9 %collective-permute-start.17 = (bf16[2,64,512]{2,1,0:T(8,128)(2,1)S(1)}, bf16[2,64,512]{2,1,0:T(8,128)(2,1)S(1)}, u32[]{:S(2)}, u32[]{:S(2)}) collective-permute-start(bf16[2,64,512]{2,1,0:T(8,128)(2,1)S(1)} %get-tuple-element.41), channel_id=1, source_target_pairs={{0,24},{4,28},{8,16},{12,20},{16,8},{20,12},{24,0},{28,4},{1,25},{... | collective-permute-start | bytes 393224 | tf_op jit(solution)/shard_map/ppermute | solution.py:255
  89.9 7.4 %copy-start.4 = (bf16[2,64,512]{2,1,0:T(8,128)(2,1)}, bf16[2,64,512]{2,1,0:T(8,128)(2,1)S(1)}, u32[]{:S(2)}) copy-start(bf16[2,64,512]{2,1,0:T(8,128)(2,1)S(1)} %collective-permute-done.17.refs_0_.refs_7_) | copy-start | bytes 393220
  89.9 19.1 %collective-permute-start.27 = (bf16[256,1280]{1,0:T(8,128)(2,1)S(1)}, bf16[256,1280]{1,0:T(8,128)(2,1)S(1)}, u32[]{:S(2)}, u32[]{:S(2)}) collective-permute-start(bf16[256,1280]{1,0:T(8,128)(2,1)S(1)} %get-tuple-element.48.refs_2_), channel_id=1, source_target_pairs={{2,3},{6,7},{11,10},{15,14},{16,17},{20,21},{25,24},{29,28}} | collective-permute-start | bytes 1966088 | tf_op jit(solution)/shard_map/ppermute | solution.py:262
  93.6 16.5 %collective-permute-start.14 = (bf16[64,3584]{1,0:T(8,128)(2,1)S(1)}, bf16[64,3584]{1,0:T(8,128)(2,1)S(1)}, u32[]{:S(2)}, u32[]{:S(2)}) collective-permute-start(bf16[64,3584]{1,0:T(8,128)(2,1)S(1)} %shard_map.96), channel_id=1, source_target_pairs={{0,8},{4,12},{8,0},{12,4},{16,24},{20,28},{24,16},{28,20},{1,9},{5... | collective-permute-start | bytes 1376264 | tf_op jit(solution)/shard_map/ppermute | solution.py:255
  101.0 18.6 %collective-permute-start.16 = (bf16[64,3584]{1,0:T(8,128)(2,1)}, bf16[64,3584]{1,0:T(8,128)(2,1)}, u32[]{:S(2)}, u32[]{:S(2)}) collective-permute-start(bf16[64,3584]{1,0:T(8,128)(2,1)} %shard_map.97), channel_id=1, source_target_pairs={{0,16},{4,20},{8,24},{12,28},{16,0},{20,4},{24,8},{28,12},{1,17},{... | collective-permute-start | bytes 1376264 | tf_op jit(solution)/shard_map/ppermute | solution.py:255
  108.2 11.4 %collective-permute-start.18 = (bf16[64,3584]{1,0:T(8,128)(2,1)}, bf16[64,3584]{1,0:T(8,128)(2,1)}, u32[]{:S(2)}, u32[]{:S(2)}) collective-permute-start(bf16[64,3584]{1,0:T(8,128)(2,1)} %shard_map.98), channel_id=1, source_target_pairs={{0,24},{4,28},{8,16},{12,20},{16,8},{20,12},{24,0},{28,4},{1,25},{... | collective-permute-start | bytes 1376264 | tf_op jit(solution)/shard_map/ppermute | solution.py:255
  109.0 2.4 %copy-start.15 = (s32[192]{0:T(256)S(1)}, s32[192]{0:T(256)}, u32[]{:S(2)}) copy-start(s32[192]{0:T(256)} %param.11) | copy-start | bytes 2308
  109.0 4.0 %copy-start.3 = (bf16[192,1280]{1,0:T(8,128)(2,1)S(1)}, bf16[192,1280]{1,0:T(8,128)(2,1)}, u32[]{:S(2)}) copy-start(bf16[192,1280]{1,0:T(8,128)(2,1)} %refs_4_.5) | copy-start | bytes 1474564
  109.0 39.9 %collective-permute-start.32 = (bf16[256,1280]{1,0:T(8,128)(2,1)S(1)}, bf16[256,1280]{1,0:T(8,128)(2,1)S(1)}, u32[]{:S(2)}, u32[]{:S(2)}) collective-permute-start(bf16[256,1280]{1,0:T(8,128)(2,1)S(1)} %shard_map.103.refs_9_), channel_id=1, source_target_pairs={{0,4},{4,0},{8,12},{12,8},{16,20},{20,16},{24,28},{28,24},{1,5},{5... | collective-permute-start | bytes 1966088 | tf_op jit(solution)/shard_map/ppermute | solution.py:252
  110.1 0.8 copy-start.9
  110.9 38.0 %collective-permute-start.31 = (bf16[256,1280]{1,0:T(8,128)(2,1)S(1)}, bf16[256,1280]{1,0:T(8,128)(2,1)S(1)}, u32[]{:S(2)}, u32[]{:S(2)}) collective-permute-start(bf16[256,1280]{1,0:T(8,128)(2,1)S(1)} %shard_map.102.refs_8_), channel_id=1, source_target_pairs={{0,4},{4,0},{8,12},{12,8},{16,20},{20,16},{24,28},{28,24},{1,5},{5... | collective-permute-start | bytes 1966088 | tf_op jit(solution)/shard_map/ppermute | solution.py:252
  113.1 0.9 copy-start.11
  119.6 1.0 copy-start.8
  120.7 1.0 copy-start.10
  121.7 0.8 copy-start.13
  124.1 24.8 %copy-start.5 = (bf16[2,64,512]{2,1,0:T(8,128)(2,1)S(1)}, bf16[2,64,512]{2,1,0:T(8,128)(2,1)}, u32[]{:S(2)}) copy-start(bf16[2,64,512]{2,1,0:T(8,128)(2,1)} %copy-done.4) | copy-start | bytes 393220
  124.1 6.2 %collective-permute-start.19 = (bf16[64,1792]{1,0:T(8,128)(2,1)S(1)}, bf16[64,1792]{1,0:T(8,128)(2,1)S(1)}, u32[]{:S(2)}, u32[]{:S(2)}) collective-permute-start(bf16[64,1792]{1,0:T(8,128)(2,1)S(1)} %get-tuple-element.42.refs_0_), channel_id=1, source_target_pairs={{0,8},{4,12},{8,0},{12,4},{16,24},{20,28},{24,16},{28,20},{1,9},{5... | collective-permute-start | bytes 688136 | tf_op jit(solution)/shard_map/ppermute | solution.py:255
  126.2 8.5 %collective-permute-start.20 = (bf16[64,1792]{1,0:T(8,128)(2,1)S(1)}, bf16[64,1792]{1,0:T(8,128)(2,1)S(1)}, u32[]{:S(2)}, u32[]{:S(2)}) collective-permute-start(bf16[64,1792]{1,0:T(8,128)(2,1)S(1)} %get-tuple-element.42.refs_0_), channel_id=1, source_target_pairs={{0,16},{4,20},{8,24},{12,28},{16,0},{20,4},{24,8},{28,12},{1,17},{... | collective-permute-start | bytes 688136 | tf_op jit(solution)/shard_map/ppermute | solution.py:255
  126.2 8.5 %collective-permute-start.21 = (bf16[64,1792]{1,0:T(8,128)(2,1)S(1)}, bf16[64,1792]{1,0:T(8,128)(2,1)S(1)}, u32[]{:S(2)}, u32[]{:S(2)}) collective-permute-start(bf16[64,1792]{1,0:T(8,128)(2,1)S(1)} %get-tuple-element.42.refs_0_), channel_id=1, source_target_pairs={{0,24},{4,28},{8,16},{12,20},{16,8},{20,12},{24,0},{28,4},{1,25},{... | collective-permute-start | bytes 688136 | tf_op jit(solution)/shard_map/ppermute | solution.py:255
  137.9 6.5 %collective-permute-start.23 = (bf16[64,1024]{1,0:T(8,128)(2,1)S(1)}, bf16[64,1024]{1,0:T(8,128)(2,1)S(1)}, u32[]{:S(2)}, u32[]{:S(2)}) collective-permute-start(bf16[64,1024]{1,0:T(8,128)(2,1)S(1)} %get-tuple-element.44), channel_id=1, source_target_pairs={{0,1},{1,0},{2,3},{3,2},{4,5},{5,4},{6,7},{7,6},{8,9},{9,8},{10,11... | collective-permute-start | bytes 393224 | tf_op jit(solution)/shard_map/ppermute | solution.py:258
  139.7 6.4 %collective-permute-start.24 = (bf16[64,1024]{1,0:T(8,128)(2,1)S(1)}, bf16[64,1024]{1,0:T(8,128)(2,1)S(1)}, u32[]{:S(2)}, u32[]{:S(2)}) collective-permute-start(bf16[64,1024]{1,0:T(8,128)(2,1)S(1)} %get-tuple-element.45), channel_id=1, source_target_pairs={{0,2},{1,3},{2,0},{3,1},{4,6},{5,7},{6,4},{7,5},{8,10},{9,11},{10,... | collective-permute-start | bytes 393224 | tf_op jit(solution)/shard_map/ppermute | solution.py:258
  141.7 7.2 %collective-permute-start.25 = (bf16[64,1024]{1,0:T(8,128)(2,1)S(1)}, bf16[64,1024]{1,0:T(8,128)(2,1)S(1)}, u32[]{:S(2)}, u32[]{:S(2)}) collective-permute-start(bf16[64,1024]{1,0:T(8,128)(2,1)S(1)} %get-tuple-element.46), channel_id=1, source_target_pairs={{0,3},{1,2},{2,1},{3,0},{4,7},{5,6},{6,5},{7,4},{8,11},{9,10},{10,... | collective-permute-start | bytes 393224 | tf_op jit(solution)/shard_map/ppermute | solution.py:258
  150.3 7.5 %collective-permute-start.33 = (bf16[32,1280]{1,0:T(8,128)(2,1)S(1)}, bf16[32,1280]{1,0:T(8,128)(2,1)S(1)}, u32[]{:S(2)}, u32[]{:S(2)}) collective-permute-start(bf16[32,1280]{1,0:T(8,128)(2,1)S(1)} %get-tuple-element.52), channel_id=1, source_target_pairs={{0,8},{4,12},{8,0},{12,4},{16,24},{20,28},{24,16},{28,20},{1,9},{5... | collective-permute-start | bytes 245768 | tf_op jit(solution)/shard_map/ppermute | solution.py:255
  155.4 4.4 %collective-permute-start.34 = (bf16[32,1280]{1,0:T(8,128)(2,1)S(1)}, bf16[32,1280]{1,0:T(8,128)(2,1)S(1)}, u32[]{:S(2)}, u32[]{:S(2)}) collective-permute-start(bf16[32,1280]{1,0:T(8,128)(2,1)S(1)} %get-tuple-element.53), channel_id=1, source_target_pairs={{0,16},{4,20},{8,24},{12,28},{16,0},{20,4},{24,8},{28,12},{1,17},{... | collective-permute-start | bytes 245768 | tf_op jit(solution)/shard_map/ppermute | solution.py:255
  155.4 5.3 %collective-permute-start.35 = (bf16[32,1280]{1,0:T(8,128)(2,1)S(1)}, bf16[32,1280]{1,0:T(8,128)(2,1)S(1)}, u32[]{:S(2)}, u32[]{:S(2)}) collective-permute-start(bf16[32,1280]{1,0:T(8,128)(2,1)S(1)} %get-tuple-element.54), channel_id=1, source_target_pairs={{0,24},{4,28},{8,16},{12,20},{16,8},{20,12},{24,0},{28,4},{1,25},{... | collective-permute-start | bytes 245768 | tf_op jit(solution)/shard_map/ppermute | solution.py:255
  161.4 1.3 collective-permute-start.36

commit v3 on v1

--- a/solution.py
+++ b/solution.py
@@ -14,6 +14,7 @@
 
 VMEM = pl.BlockSpec(memory_space=pltpu.VMEM)
 SMEM = pl.BlockSpec(memory_space=pltpu.SMEM)
+HBM = pl.BlockSpec(memory_space=pl.ANY)
 BF16 = jnp.bfloat16
 F32 = jnp.float32
 
@@ -22,18 +23,25 @@
     return jax.ShapeDtypeStruct(tuple(dims), dtype)
 
 
-def call(kernel, out, ids, *arrays, scratch=(), flops=0, limit=40):
+def call(kernel, outs, ids, *arrays, hbm=(), through=(), scratch=(), flops=0, limit=20):
+    n, t, o = len(arrays), len(through), len(outs)
+
+    def run(ids, *refs):
+        kernel(ids, *refs[:n], *refs[n + t : n + t + o], *refs[n + 2 * t + o :])
+
     moved = sum(a.size * a.dtype.itemsize for a in arrays)
-    moved += sum(math.prod(o.shape) * o.dtype.itemsize for o in jax.tree.leaves(out))
-    return pl.pallas_call(
-        kernel,
-        out_shape=out,
-        in_specs=[SMEM] + [VMEM] * len(arrays),
-        out_specs=jax.tree.map(lambda _: VMEM, out),
+    moved += sum(math.prod(a.shape) * a.dtype.itemsize for a in outs)
+    results = pl.pallas_call(
+        run,
+        out_shape=list(outs) + [shape(a.shape, a.dtype) for a in through],
+        in_specs=[SMEM] + [HBM if i in hbm else VMEM for i in range(n)] + [HBM] * t,
+        out_specs=[VMEM] * o + [HBM] * t,
         scratch_shapes=list(scratch),
+        input_output_aliases={1 + n + i: o + i for i in range(t)},
         compiler_params=pltpu.CompilerParams(vmem_limit_bytes=limit * 1024 * 1024),
         cost_estimate=pl.CostEstimate(flops=int(flops), bytes_accessed=int(moved), transcendentals=0),
-    )(ids, *arrays)
+    )(ids, *arrays, *through)
+    return list(results)
 
 
 def dot(a, b):
@@ -88,22 +96,22 @@
     out[...] = dot(rows, w[...]).astype(BF16)
 
 
-def norm_kernel(groups, chips, ids, *refs):
-    pieces, outs, units = refs[:groups], refs[groups : groups + chips], refs[groups + chips]
+def spread_kernel(groups, chips, ids, *refs):
+    pieces, outs, scale, units = refs[:groups], refs[groups : groups + chips], refs[-2], refs[-1]
     q, c, z = ids[0], ids[1], ids[2]
     unit = units.shape[2]
     per = 2 * chips // groups
+    for k in range(groups):
+        for u in range(per):
+            units[(z ^ k) * per + u] = pieces[k][:, u * unit : (u + 1) * unit]
+    for k in range(chips):
+        for h in range(2):
+            outs[k][h] = units[2 * (q ^ k) + (c ^ h)]
     squares = jnp.zeros((units.shape[1], 1), F32)
     for k in range(groups):
         wide = pieces[k][...].astype(F32)
         squares += jnp.sum(wide * wide, axis=1, keepdims=True)
-        for u in range(per):
-            units[(z ^ k) * per + u] = pieces[k][:, u * unit : (u + 1) * unit]
-    scale = lax.rsqrt(squares / (2 * chips * unit) + norm_epsilon)
-    for k in range(chips):
-        for h in range(2):
-            piece = units[2 * (q ^ k) + (c ^ h)].astype(F32)
-            outs[k][h] = (piece * scale).astype(BF16)
+    scale[...] = jnp.broadcast_to(lax.rsqrt(squares / (2 * chips * unit) + norm_epsilon), scale.shape)
 
 
 def gate_kernel(count, ids, *refs):
@@ -121,11 +129,11 @@
         outs[k][:, wide:] = up[k * rows : (k + 1) * rows]
 
 
-def hidden_kernel(ids, *refs):
+def hidden_kernel(ids, scale, *refs):
     pieces, out = refs[:-1], refs[-1]
     wide = out.shape[1]
-    gate = sum(p[:, :wide].astype(F32) for p in pieces)
-    up = sum(p[:, wide:].astype(F32) for p in pieces)
+    gate = sum(p[:, :wide].astype(F32) for p in pieces) * scale[:, 0:1]
+    up = sum(p[:, wide:].astype(F32) for p in pieces) * scale[:, 0:1]
     out[...] = (gate / (1.0 + jnp.exp(-gate)) * up).astype(BF16)
 
 
@@ -218,38 +226,46 @@
     def plane(a, k):
         return lax.ppermute(a, "mp", [(i, i ^ k) for i in range(groups)])
 
-    pooled = call(functools.partial(pool_kernel, slots), shape((slots, width)), ids, segments.reshape(1, bytes_), enc_states)
+    [pooled] = call(
+        functools.partial(pool_kernel, slots),
+        [shape((slots, width))],
+        ids,
+        segments.reshape(1, bytes_),
+        enc_states,
+    )
+    siblings = [sibling(w) for w in (w_gate, w_up)]
     gathered = [pooled] + [chip(pooled, k) for k in range(1, chips)]
     theirs = sibling(jnp.concatenate(gathered, axis=0))
-    packed, start = call(
+    packed, start, gate_b, up_b = call(
         functools.partial(pack_kernel, chips, slots),
-        (shape((ROWS, width)), shape((8, HD), jnp.int32)),
+        [shape((ROWS, width)), shape((8, HD), jnp.int32)],
         ids,
         *gathered,
         theirs,
+        through=siblings,
         scratch=[pltpu.VMEM((seq * slots, width), BF16)],
     )
-    gate_b, up_b, down_b = sibling(w_gate), sibling(w_up), sibling(w_down)
     pieces = [packed] + [plane(packed, k) for k in range(1, groups)]
-    x = call(
+    x, down_b = call(
         functools.partial(x_kernel, groups),
-        shape((rows, wide)),
+        [shape((rows, wide))],
         ids,
         *pieces,
         w_in,
+        through=[sibling(w_down)],
         scratch=[pltpu.VMEM((groups, ROWS, width), BF16)],
         flops=2 * rows * width * wide,
     )
     pieces = [x] + [plane(x, k) for k in range(1, groups)]
-    normed = call(
-        functools.partial(norm_kernel, groups, chips),
-        [shape((2, rows, unit)) for _ in range(chips)],
+    *sent, scale = call(
+        functools.partial(spread_kernel, groups, chips),
+        [shape((2, rows, unit)) for _ in range(chips)] + [shape((rows, HD), F32)],
         ids,
         *pieces,
         scratch=[pltpu.VMEM((seq, rows, unit), BF16)],
     )
 
-    def gate(pieces):
+    def gate(pieces, through=()):
         return call(
             functools.partial(gate_kernel, len(pieces)),
             [shape((rows, 2 * ffw)) for _ in pieces],
@@ -259,13 +275,21 @@
             gate_b,
             w_up,
             up_b,
+            through=through,
             flops=8 * len(pieces) * rows * unit * ffw,
         )
 
-    arrived = [chip(normed[k], k) for k in range(1, chips)]
-    partial = gate([normed[0]]) + gate(arrived)
-    partial = [partial[0]] + [chip(partial[k], k) for k in range(1, chips)]
-    hidden = call(hidden_kernel, shape((rows, ffw)), ids, *partial)
+    arrived = [chip(sent[k], k) for k in range(1, chips)]
+    partial = gate(arrived[:-1])
+    last, own = gate(arrived[-1:], [sent[0]])
+    partial = [chip(p, k + 1) for k, p in enumerate(partial + [last])]
+    partial = gate([own]) + partial
+
+    keys = jnp.pad(patch_keys, ((0, 1), (0, 0)))
+    [weights] = call(
+        weights_kernel, [shape((heads, bytes_, slots))], ids, segments.reshape(bytes_, 1), dec_states, keys
+    )
+    hidden, weights = call(hidden_kernel, [shape((rows, ffw))], ids, scale, *partial, through=[weights])
 
     def down(pieces):
         return call(
@@ -300,14 +324,12 @@
         flops=2 * rows * width * wide,
     )
     outs = [outs[0]] + [plane(outs[k], k) for k in range(1, groups)]
-    outputs = call(add_kernel, shape((ROWS, width)), ids, *outs)
+    [outputs] = call(add_kernel, [shape((ROWS, width))], ids, *outs)
     outputs = [outputs] + [chip(outputs, k) for k in range(1, chips)]
     theirs = sibling(jnp.stack(outputs))
-    keys = jnp.pad(patch_keys, ((0, 1), (0, 0)))
-    weights = call(weights_kernel, shape((heads, bytes_, slots)), ids, segments.reshape(bytes_, 1), dec_states, keys)
-    return call(
+    [decoded] = call(
         functools.partial(mix_kernel, chips),
-        shape((bytes_, width)),
+        [shape((bytes_, width))],
         ids,
         *outputs,
         theirs,
@@ -316,6 +338,7 @@
         dec_states,
         scratch=[pltpu.VMEM((seq, ROWS, width), BF16)],
     )
+    return decoded
 
 
 def solution(mesh):

time: 134 us -> 128 us (0.955)
  waiting for transfers between devices: 61.3 us -> 48.8 us
  Pallas kernels: 18.6 us -> 25.3 us
  starting transfers between devices: 49.7 us -> 45.8 us
  local copies, waits for them, and re-layouts: 3.61 us -> 7.28 us
    ppermute x18, waiting for transfers between devices: 42.4 us -> 21.6 us  [chip(): return lax.ppermute(a, 'seq', [(i, i ^ 2 * k) for i in range(seq)])]
    ppermute x12, waiting for transfers between devices: 17.3 us -> 24.2 us  [plane(): return lax.ppermute(a, 'mp', [(i, i ^ k) for i in range(groups)])]
    pallas_call x14 -> x15, Pallas kernels: 18.6 us -> 25.3 us  [call(): pl.pallas_call(run, out_shape=list(outs) + [shape(a.shape, a.dtype) for a...]
    ppermute x12, starting transfers between devices: 26.2 us -> 20.2 us  [plane(): return lax.ppermute(a, 'mp', [(i, i ^ k) for i in range(groups)])]
    unnamed x20 -> x24, local copies, waits for them, and re-layouts: 3.48 us -> 5.62 us
    ppermute x18, starting transfers between devices: 22.9 us -> 24.4 us  [chip(): return lax.ppermute(a, 'seq', [(i, i ^ 2 * k) for i in range(seq)])]
    ppermute x5, waiting for transfers between devices: 1.63 us -> 3.01 us  [sibling(): return lax.ppermute(a, 'seq', [(i, i ^ 1) for i in range(seq)])]
  transfers between devices with their start and end apart: 35 -> 35, of which waited for: 23 -> 24; matrix products, arithmetic and copies ran while one was open for 0% -> 1% of each run, Pallas kernels for 10% -> 12%
where the time goes in v3:
time: 128 us; the launch traced here: 127 us
  waiting for transfers between devices  48.8 us (38%)
  starting transfers between devices  45.8 us (36%)
  Pallas kernels  25.3 us (20%)
  local copies, waits for them, and re-layouts  7.28 us (6%)
    pallas_call x15, Pallas kernels, call(): pl.pallas_call(run, out_shape=list(outs) + [shape(a.shape, a.dtype) for a...  25.3 us
    ppermute x18, starting transfers between devices, chip(): return lax.ppermute(a, 'seq', [(i, i ^ 2 * k) for i in range(seq)])  24.4 us
    ppermute x12, waiting for transfers between devices, plane(): return lax.ppermute(a, 'mp', [(i, i ^ k) for i in range(groups)])  24.2 us
    ppermute x18, waiting for transfers between devices, chip(): return lax.ppermute(a, 'seq', [(i, i ^ 2 * k) for i in range(seq)])  21.6 us
    ppermute x12, starting transfers between devices, plane(): return lax.ppermute(a, 'mp', [(i, i ^ k) for i in range(groups)])  20.2 us
    unnamed x24, local copies, waits for them, and re-layouts  5.62 us
    ppermute x5, waiting for transfers between devices, sibling(): return lax.ppermute(a, 'seq', [(i, i ^ 1) for i in range(seq)])  3.01 us
  transfers between devices with their start and end apart: 35, of which 24 were waited for; matrix products, arithmetic and copies ran while one was open for 1% of the time, Pallas kernels for 12%

profile of v3, /device:TPU:0, one launch (start us, length us, event | category | flops | bytes accessed | tf_op | source)
XLA Modules:
  0.0 127.4 jit_solution(13371490311860313210)
XLA Ops:
  1.0 1.0 copy-done.8
  2.1 0.7 copy-done.10
  2.8 0.8 shard_map.91.refs_0_
  3.5 2.5 %collective-permute-start = (bf16[32,1280]{1,0:T(8,128)(2,1)S(1)}, bf16[32,1280]{1,0:T(8,128)(2,1)S(1)}, u32[]{:S(2)}, u32[]{:S(2)}) collective-permute-start(bf16[32,1280]{1,0:T(8,128)(2,1)S(1)} %shard_map.91.refs_0_), channel_id=1, source_target_pairs={{0,8},{4,12},{8,0},{12,4},{16,24},{20,28},{24,16},{28,20},{1,9},{5... | collective-permute-start | bytes 245768 | tf_op jit(solution)/shard_map/ppermute | solution.py:224
  6.0 1.5 %collective-permute-start.1 = (bf16[32,1280]{1,0:T(8,128)(2,1)S(1)}, bf16[32,1280]{1,0:T(8,128)(2,1)S(1)}, u32[]{:S(2)}, u32[]{:S(2)}) collective-permute-start(bf16[32,1280]{1,0:T(8,128)(2,1)S(1)} %shard_map.91.refs_0_), channel_id=1, source_target_pairs={{0,16},{4,20},{8,24},{12,28},{16,0},{20,4},{24,8},{28,12},{1,17},{... | collective-permute-start | bytes 245768 | tf_op jit(solution)/shard_map/ppermute | solution.py:224
  7.6 1.6 %collective-permute-done.refs_1_ = bf16[32,1280]{1,0:T(8,128)(2,1)S(1)} collective-permute-done((bf16[32,1280]{1,0:T(8,128)(2,1)S(1)}, bf16[32,1280]{1,0:T(8,128)(2,1)S(1)}, u32[]{:S(2)}, u32[]{:S(2)}) %collective-permute-start) | collective-permute-done | bytes 81952 | tf_op jit(solution)/shard_map/ppermute | solution.py:224
  9.2 2.7 %collective-permute-start.2 = (bf16[32,1280]{1,0:T(8,128)(2,1)S(1)}, bf16[32,1280]{1,0:T(8,128)(2,1)S(1)}, u32[]{:S(2)}, u32[]{:S(2)}) collective-permute-start(bf16[32,1280]{1,0:T(8,128)(2,1)S(1)} %shard_map.91.refs_0_), channel_id=1, source_target_pairs={{0,24},{4,28},{8,16},{12,20},{16,8},{20,12},{24,0},{28,4},{1,25},{... | collective-permute-start | bytes 245768 | tf_op jit(solution)/shard_map/ppermute | solution.py:224
  11.9 2.6 %collective-permute-done.2.refs_3_ = bf16[32,1280]{1,0:T(8,128)(2,1)S(1)} collective-permute-done((bf16[32,1280]{1,0:T(8,128)(2,1)S(1)}, bf16[32,1280]{1,0:T(8,128)(2,1)S(1)}, u32[]{:S(2)}, u32[]{:S(2)}) %collective-permute-start.2) | collective-permute-done | bytes 81952 | tf_op jit(solution)/shard_map/ppermute | solution.py:224
  14.6 1.6 %collective-permute-done.3.refs_4_ = bf16[128,1280]{1,0:T(8,128)(2,1)S(1)} collective-permute-done((bf16[128,1280]{1,0:T(8,128)(2,1)S(1)}, bf16[128,1280]{1,0:T(8,128)(2,1)S(1)}, u32[]{:S(2)}, u32[]{:S(2)}) %collective-permute-start.3) | collective-permute-done | bytes 327712 | tf_op jit(solution)/shard_map/ppermute | solution.py:221
  16.2 0.8 shard_map.92
  17.0 1.9 %collective-permute-start.6 = (bf16[16,1280]{1,0:T(8,128)(2,1)S(1)}, bf16[16,1280]{1,0:T(8,128)(2,1)S(1)}, u32[]{:S(2)}, u32[]{:S(2)}) collective-permute-start(bf16[16,1280]{1,0:T(8,128)(2,1)S(1)} %get-tuple-element.33.refs_0_), channel_id=1, source_target_pairs={{0,1},{1,0},{2,3},{3,2},{4,5},{5,4},{6,7},{7,6},{8,9},{9,8},{10,11... | collective-permute-start | bytes 122888 | tf_op jit(solution)/shard_map/ppermute | solution.py:227
  18.9 2.6 %collective-permute-start.7 = (bf16[16,1280]{1,0:T(8,128)(2,1)S(1)}, bf16[16,1280]{1,0:T(8,128)(2,1)S(1)}, u32[]{:S(2)}, u32[]{:S(2)}) collective-permute-start(bf16[16,1280]{1,0:T(8,128)(2,1)S(1)} %get-tuple-element.33.refs_0_), channel_id=1, source_target_pairs={{0,2},{1,3},{2,0},{3,1},{4,6},{5,7},{6,4},{7,5},{8,10},{9,11},{10,... | collective-permute-start | bytes 122888 | tf_op jit(solution)/shard_map/ppermute | solution.py:227
  21.5 3.1 %collective-permute-done.7.refs_2_ = bf16[16,1280]{1,0:T(8,128)(2,1)S(1)} collective-permute-done((bf16[16,1280]{1,0:T(8,128)(2,1)S(1)}, bf16[16,1280]{1,0:T(8,128)(2,1)S(1)}, u32[]{:S(2)}, u32[]{:S(2)}) %collective-permute-start.7) | collective-permute-done | bytes 40992 | tf_op jit(solution)/shard_map/ppermute | solution.py:227
  24.6 2.6 %collective-permute-done.8.refs_3_ = bf16[16,1280]{1,0:T(8,128)(2,1)S(1)} collective-permute-done((bf16[16,1280]{1,0:T(8,128)(2,1)S(1)}, bf16[16,1280]{1,0:T(8,128)(2,1)S(1)}, u32[]{:S(2)}, u32[]{:S(2)}) %collective-permute-start.8) | collective-permute-done | bytes 40992 | tf_op jit(solution)/shard_map/ppermute | solution.py:227
  27.3 1.1 shard_map.93
  28.5 1.2 collective-permute-start.11
  29.7 3.2 %collective-permute-start.12 = (bf16[64,1024]{1,0:T(8,128)(2,1)S(1)}, bf16[64,1024]{1,0:T(8,128)(2,1)S(1)}, u32[]{:S(2)}, u32[]{:S(2)}) collective-permute-start(bf16[64,1024]{1,0:T(8,128)(2,1)S(1)} %get-tuple-element.34.refs_0_.refs_4_), channel_id=1, source_target_pairs={{0,3},{1,2},{2,1},{3,0},{4,7},{5,6},{6,5},{7,4},{8,11},{9,10},{10,... | collective-permute-start | bytes 393224 | tf_op jit(solution)/shard_map/ppermute | solution.py:227
  32.9 1.0 collective-permute-done.10.refs_1_
  33.9 6.5 %collective-permute-done.11.refs_2_ = bf16[64,1024]{1,0:T(8,128)(2,1)S(1)} collective-permute-done((bf16[64,1024]{1,0:T(8,128)(2,1)S(1)}, bf16[64,1024]{1,0:T(8,128)(2,1)S(1)}, u32[]{:S(2)}, u32[]{:S(2)}) %collective-permute-start.11) | collective-permute-done | bytes 131104 | tf_op jit(solution)/shard_map/ppermute | solution.py:227
  40.4 0.7 shard_map.94
  41.1 1.6 %collective-permute-start.14 = (bf16[2,64,512]{2,1,0:T(8,128)(2,1)S(1)}, bf16[2,64,512]{2,1,0:T(8,128)(2,1)S(1)}, u32[]{:S(2)}, u32[]{:S(2)}) collective-permute-start(bf16[2,64,512]{2,1,0:T(8,128)(2,1)S(1)} %get-tuple-element.41), channel_id=1, source_target_pairs={{0,8},{4,12},{8,0},{12,4},{16,24},{20,28},{24,16},{28,20},{1,9},{5... | collective-permute-start | bytes 393224 | tf_op jit(solution)/shard_map/ppermute | solution.py:224
  42.6 1.5 %collective-permute-start.15 = (bf16[2,64,512]{2,1,0:T(8,128)(2,1)S(1)}, bf16[2,64,512]{2,1,0:T(8,128)(2,1)S(1)}, u32[]{:S(2)}, u32[]{:S(2)}) collective-permute-start(bf16[2,64,512]{2,1,0:T(8,128)(2,1)S(1)} %get-tuple-element.42), channel_id=1, source_target_pairs={{0,16},{4,20},{8,24},{12,28},{16,0},{20,4},{24,8},{28,12},{1,17},{... | collective-permute-start | bytes 393224 | tf_op jit(solution)/shard_map/ppermute | solution.py:224
  44.6 1.5 %collective-permute-done.14.refs_0_ = bf16[2,64,512]{2,1,0:T(8,128)(2,1)S(1)} collective-permute-done((bf16[2,64,512]{2,1,0:T(8,128)(2,1)S(1)}, bf16[2,64,512]{2,1,0:T(8,128)(2,1)S(1)}, u32[]{:S(2)}, u32[]{:S(2)}) %collective-permute-start.14) | collective-permute-done | bytes 131104 | tf_op jit(solution)/shard_map/ppermute | solution.py:224
  46.1 1.5 %collective-permute-done.15.refs_1_ = bf16[2,64,512]{2,1,0:T(8,128)(2,1)S(1)} collective-permute-done((bf16[2,64,512]{2,1,0:T(8,128)(2,1)S(1)}, bf16[2,64,512]{2,1,0:T(8,128)(2,1)S(1)}, u32[]{:S(2)}, u32[]{:S(2)}) %collective-permute-start.15) | collective-permute-done | bytes 131104 | tf_op jit(solution)/shard_map/ppermute | solution.py:224
  47.6 3.6 %shard_map.97 = (bf16[64,3584]{1,0:T(8,128)(2,1)}, bf16[64,3584]{1,0:T(8,128)(2,1)}) custom-call(s32[3]{0:T(128)S(1)} %pad_add_fusion.ids, bf16[2,64,512]{2,1,0:T(8,128)(2,1)S(1)} %collective-permute-done.14.refs_0_, bf16[2,64,512]{2,1,0:T(8,128)(2,1)S(1)} %collective-permute-done.15.refs_1_, bf16[512,1792]{1,0:T(8,128)(2,1)S(1)} %copy-done, ...), custom_call_target="tpu_custom_call" | custom-call | flops 939524096 | bytes 8519680 | tf_op jit(solution)/shard_map/pallas_call | solution.py:34
  51.7 1.5 %collective-permute-start.17 = (bf16[64,3584]{1,0:T(8,128)(2,1)}, bf16[64,3584]{1,0:T(8,128)(2,1)S(1)}, u32[]{:S(2)}, u32[]{:S(2)}) collective-permute-start(bf16[64,3584]{1,0:T(8,128)(2,1)} %get-tuple-element.44), channel_id=1, source_target_pairs={{0,16},{4,20},{8,24},{12,28},{16,0},{20,4},{24,8},{28,12},{1,17},{... | collective-permute-start | bytes 1376264 | tf_op jit(solution)/shard_map/ppermute | solution.py:224
  53.2 3.7 %shard_map.95 = (bf16[64,3584]{1,0:T(8,128)(2,1)}, bf16[2,64,512]{2,1,0:T(8,128)(2,1)S(1)}) custom-call(s32[3]{0:T(128)S(1)} %pad_add_fusion.ids, bf16[2,64,512]{2,1,0:T(8,128)(2,1)S(1)} %collective-permute-done.13.refs_0_, bf16[512,1792]{1,0:T(8,128)(2,1)S(1)} %copy-done, ...), custom_call_target="tpu_custom_call", output_to_operand_aliasing={{1}: (6, {})} | custom-call | flops 469762048 | bytes 7929856 | tf_op jit(solution)/shard_map/pallas_call | solution.py:34
  56.9 1.4 %collective-permute-start.18 = (bf16[64,3584]{1,0:T(8,128)(2,1)}, bf16[64,3584]{1,0:T(8,128)(2,1)}, u32[]{:S(2)}, u32[]{:S(2)}) collective-permute-start(bf16[64,3584]{1,0:T(8,128)(2,1)} %get-tuple-element.45), channel_id=1, source_target_pairs={{0,24},{4,28},{8,16},{12,20},{16,8},{20,12},{24,0},{28,4},{1,25},{... | collective-permute-start | bytes 1376264 | tf_op jit(solution)/shard_map/ppermute | solution.py:224
  58.4 0.8 copy.15.refs_0_
  59.1 0.9 pad.4.refs_2_
  60.1 0.9 copy-done.9
  60.9 1.5 %shard_map.98.refs_5_ = bf16[10,192,32]{2,1,0:T(8,128)(2,1)S(1)} custom-call(s32[3]{0:T(128)S(1)} %pad_add_fusion.ids, s32[192,1]{1,0:T(8,128)S(1)} %copy-done.9, bf16[192,1280]{1,0:T(8,128)(2,1)S(1)} %copy-done.7, bf16[32,1280]{1,0:T(8,128)(2,1)S(1)} %pad.4.refs_2_), custom_call_target="tpu_custom_call" | custom-call | bytes 697088 | tf_op jit(solution)/shard_map/pallas_call | solution.py:34
  62.5 1.5 %copy-done.1 = bf16[512,1792]{1,0:T(8,128)(2,1)S(1)} copy-done((bf16[512,1792]{1,0:T(8,128)(2,1)S(1)}, bf16[512,1792]{1,0:T(8,128)(2,1)}, u32[]{:S(2)}) %copy-start.1) | copy-done | bytes 1835032
  64.0 1.5 %copy-done.3 = bf16[512,1792]{1,0:T(8,128)(2,1)S(1)} copy-done((bf16[512,1792]{1,0:T(8,128)(2,1)S(1)}, bf16[512,1792]{1,0:T(8,128)(2,1)}, u32[]{:S(2)}) %copy-start.3) | copy-done | bytes 1835032
  65.5 2.9 %shard_map.96.refs_1_ = bf16[64,3584]{1,0:T(8,128)(2,1)S(1)} custom-call(s32[3]{0:T(128)S(1)} %pad_add_fusion.ids, bf16[2,64,512]{2,1,0:T(8,128)(2,1)S(1)} %get-tuple-element.40.refs_0_, bf16[512,1792]{1,0:T(8,128)(2,1)S(1)} %copy-done.1, bf16[512,1792]{1,0:T(8,128)(2,1)S(1)} %get-tuple-element.37.refs_2_.refs_3_, bf16[512,1792]{1,0:T(8,128)(2,1)S(1)} %copy-done.3, ...), custom_call_target="tpu_custom_call" | custom-call | flops 469762048 | bytes 7929856 | tf_op jit(solution)/shard_map/pallas_call | solution.py:34
  68.4 1.2 collective-permute-done.17.refs_3_
  69.6 2.2 %collective-permute-done.18.refs_4_ = bf16[64,3584]{1,0:T(8,128)(2,1)} collective-permute-done((bf16[64,3584]{1,0:T(8,128)(2,1)}, bf16[64,3584]{1,0:T(8,128)(2,1)}, u32[]{:S(2)}, u32[]{:S(2)}) %collective-permute-start.18) | collective-permute-done | bytes 458784 | tf_op jit(solution)/shard_map/ppermute | solution.py:224
  71.7 1.5 %shard_map.99 = (bf16[64,1792]{1,0:T(8,128)(2,1)S(1)}, bf16[10,192,32]{2,1,0:T(8,128)(2,1)S(1)}) custom-call(s32[3]{0:T(128)S(1)} %pad_add_fusion.ids, f32[64,128]{1,0:T(8,128)S(1)} %get-tuple-element.35.refs_0_, bf16[64,3584]{1,0:T(8,128)(2,1)S(1)} %shard_map.96.refs_1_, ...), custom_call_target="tpu_custom_call", output_to_operand_aliasing={{1}: (6, {})} | custom-call | bytes 2097152 | tf_op jit(solution)/shard_map/pallas_call | solution.py:34
  73.4 1.9 %collective-permute-start.20 = (bf16[64,1792]{1,0:T(8,128)(2,1)S(1)}, bf16[64,1792]{1,0:T(8,128)(2,1)S(1)}, u32[]{:S(2)}, u32[]{:S(2)}) collective-permute-start(bf16[64,1792]{1,0:T(8,128)(2,1)S(1)} %get-tuple-element.46.refs_0_), channel_id=1, source_target_pairs={{0,16},{4,20},{8,24},{12,28},{16,0},{20,4},{24,8},{28,12},{1,17},{... | collective-permute-start | bytes 688136 | tf_op jit(solution)/shard_map/ppermute | solution.py:224
  75.3 1.5 %collective-permute-start.21 = (bf16[64,1792]{1,0:T(8,128)(2,1)S(1)}, bf16[64,1792]{1,0:T(8,128)(2,1)S(1)}, u32[]{:S(2)}, u32[]{:S(2)}) collective-permute-start(bf16[64,1792]{1,0:T(8,128)(2,1)S(1)} %get-tuple-element.46.refs_0_), channel_id=1, source_target_pairs={{0,24},{4,28},{8,16},{12,20},{16,8},{20,12},{24,0},{28,4},{1,25},{... | collective-permute-start | bytes 688136 | tf_op jit(solution)/shard_map/ppermute | solution.py:224
  76.8 2.5 %collective-permute-done.19.refs_0_ = bf16[64,1792]{1,0:T(8,128)(2,1)S(1)} collective-permute-done((bf16[64,1792]{1,0:T(8,128)(2,1)S(1)}, bf16[64,1792]{1,0:T(8,128)(2,1)S(1)}, u32[]{:S(2)}, u32[]{:S(2)}) %collective-permute-start.19) | collective-permute-done | bytes 229408 | tf_op jit(solution)/shard_map/ppermute | solution.py:224
  79.4 2.0 %collective-permute-done.20.refs_1_ = bf16[64,1792]{1,0:T(8,128)(2,1)S(1)} collective-permute-done((bf16[64,1792]{1,0:T(8,128)(2,1)S(1)}, bf16[64,1792]{1,0:T(8,128)(2,1)S(1)}, u32[]{:S(2)}, u32[]{:S(2)}) %collective-permute-start.20) | collective-permute-done | bytes 229408 | tf_op jit(solution)/shard_map/ppermute | solution.py:224
  81.4 1.3 %collective-permute-done.21.refs_2_ = bf16[64,1792]{1,0:T(8,128)(2,1)S(1)} collective-permute-done((bf16[64,1792]{1,0:T(8,128)(2,1)S(1)}, bf16[64,1792]{1,0:T(8,128)(2,1)S(1)}, u32[]{:S(2)}, u32[]{:S(2)}) %collective-permute-start.21) | collective-permute-done | bytes 229408 | tf_op jit(solution)/shard_map/ppermute | solution.py:224
  82.7 2.4 %shard_map.101 = (bf16[2,64,512]{2,1,0:T(8,128)(2,1)S(1)}, bf16[2,64,512]{2,1,0:T(8,128)(2,1)S(1)}, bf16[2,64,512]{2,1,0:T(8,128)(2,1)S(1)}) custom-call(s32[3]{0:T(128)S(1)} %pad_add_fusion.ids, bf16[64,1792]{1,0:T(8,128)(2,1)S(1)} %collective-permute-done.19.refs_0_, bf16[64,1792]{1,0:T(8,128)(2,1)S(1)} %collective-permute-done.20.refs_1_, ...), custom_call_target="tpu_custom_call" | custom-call | flops 704643072 | bytes 4751360 | tf_op jit(solution)/shard_map/pallas_call | solution.py:34
  85.1 1.2 collective-permute-start.22
  86.8 1.8 %collective-permute-start.24 = (bf16[2,64,512]{2,1,0:T(8,128)(2,1)S(1)}, bf16[2,64,512]{2,1,0:T(8,128)(2,1)S(1)}, u32[]{:S(2)}, u32[]{:S(2)}) collective-permute-start(bf16[2,64,512]{2,1,0:T(8,128)(2,1)S(1)} %get-tuple-element.50), channel_id=1, source_target_pairs={{0,24},{4,28},{8,16},{12,20},{16,8},{20,12},{24,0},{28,4},{1,25},{... | collective-permute-start | bytes 393224 | tf_op jit(solution)/shard_map/ppermute | solution.py:224
  88.6 2.2 %shard_map.100.refs_0_ = bf16[2,64,512]{2,1,0:T(8,128)(2,1)S(1)} custom-call(s32[3]{0:T(128)S(1)} %pad_add_fusion.ids, bf16[64,1792]{1,0:T(8,128)(2,1)S(1)} %get-tuple-element.46.refs_0_, bf16[1792,512]{1,0:T(8,128)(2,1)S(1)} %copy-done.4, bf16[1792,512]{1,0:T(8,128)(2,1)} %get-tuple-element.47.refs_2_.refs_4_), custom_call_target="tpu_custom_call" | custom-call | flops 234881024 | bytes 4030464 | tf_op jit(solution)/shard_map/pallas_call | solution.py:34
  91.3 1.4 %collective-permute-done.24.refs_3_ = bf16[2,64,512]{2,1,0:T(8,128)(2,1)S(1)} collective-permute-done((bf16[2,64,512]{2,1,0:T(8,128)(2,1)S(1)}, bf16[2,64,512]{2,1,0:T(8,128)(2,1)S(1)}, u32[]{:S(2)}, u32[]{:S(2)}) %collective-permute-start.24) | collective-permute-done | bytes 131104 | tf_op jit(solution)/shard_map/ppermute | solution.py:224
  92.7 0.6 shard_map.102
  93.3 4.4 %collective-permute-start.25 = (bf16[64,1024]{1,0:T(8,128)(2,1)S(1)}, bf16[64,1024]{1,0:T(8,128)(2,1)S(1)}, u32[]{:S(2)}, u32[]{:S(2)}) collective-permute-start(bf16[64,1024]{1,0:T(8,128)(2,1)S(1)} %get-tuple-element.52), channel_id=1, source_target_pairs={{0,1},{1,0},{2,3},{3,2},{4,5},{5,4},{6,7},{7,6},{8,9},{9,8},{10,11... | collective-permute-start | bytes 393224 | tf_op jit(solution)/shard_map/ppermute | solution.py:227
  97.7 2.4 %collective-permute-start.27 = (bf16[64,1024]{1,0:T(8,128)(2,1)S(1)}, bf16[64,1024]{1,0:T(8,128)(2,1)S(1)}, u32[]{:S(2)}, u32[]{:S(2)}) collective-permute-start(bf16[64,1024]{1,0:T(8,128)(2,1)S(1)} %get-tuple-element.54), channel_id=1, source_target_pairs={{0,3},{1,2},{2,1},{3,0},{4,7},{5,6},{6,5},{7,4},{8,11},{9,10},{10,... | collective-permute-start | bytes 393224 | tf_op jit(solution)/shard_map/ppermute | solution.py:227
  100.6 7.0 %collective-permute-done.26.refs_2_ = bf16[64,1024]{1,0:T(8,128)(2,1)S(1)} collective-permute-done((bf16[64,1024]{1,0:T(8,128)(2,1)S(1)}, bf16[64,1024]{1,0:T(8,128)(2,1)S(1)}, u32[]{:S(2)}, u32[]{:S(2)}) %collective-permute-start.26) | collective-permute-done | bytes 131104 | tf_op jit(solution)/shard_map/ppermute | solution.py:227
  107.7 1.1 shard_map.103
  108.8 2.0 %collective-permute-start.28 = (bf16[16,1280]{1,0:T(8,128)(2,1)S(1)}, bf16[16,1280]{1,0:T(8,128)(2,1)S(1)}, u32[]{:S(2)}, u32[]{:S(2)}) collective-permute-start(bf16[16,1280]{1,0:T(8,128)(2,1)S(1)} %get-tuple-element.56), channel_id=1, source_target_pairs={{0,1},{1,0},{2,3},{3,2},{4,5},{5,4},{6,7},{7,6},{8,9},{9,8},{10,11... | collective-permute-start | bytes 122888 | tf_op jit(solution)/shard_map/ppermute | solution.py:227
  110.8 2.4 %collective-permute-start.30 = (bf16[16,1280]{1,0:T(8,128)(2,1)S(1)}, bf16[16,1280]{1,0:T(8,128)(2,1)S(1)}, u32[]{:S(2)}, u32[]{:S(2)}) collective-permute-start(bf16[16,1280]{1,0:T(8,128)(2,1)S(1)} %get-tuple-element.58), channel_id=1, source_target_pairs={{0,3},{1,2},{2,1},{3,0},{4,7},{5,6},{6,5},{7,4},{8,11},{9,10},{10,... | collective-permute-start | bytes 122888 | tf_op jit(solution)/shard_map/ppermute | solution.py:227
  113.3 2.5 %collective-permute-done.29.refs_2_ = bf16[16,1280]{1,0:T(8,128)(2,1)S(1)} collective-permute-done((bf16[16,1280]{1,0:T(8,128)(2,1)S(1)}, bf16[16,1280]{1,0:T(8,128)(2,1)S(1)}, u32[]{:S(2)}, u32[]{:S(2)}) %collective-permute-start.29) | collective-permute-done | bytes 40992 | tf_op jit(solution)/shard_map/ppermute | solution.py:227
  115.7 0.9 collective-permute-done.30.refs_3_
  116.7 0.6 shard_map.104.refs_0_
  117.2 0.6 collective-permute-start.31
  117.8 1.5 %collective-permute-start.32 = (bf16[16,1280]{1,0:T(8,128)(2,1)S(1)}, bf16[16,1280]{1,0:T(8,128)(2,1)S(1)}, u32[]{:S(2)}, u32[]{:S(2)}) collective-permute-start(bf16[16,1280]{1,0:T(8,128)(2,1)S(1)} %shard_map.104.refs_0_), channel_id=1, source_target_pairs={{0,16},{4,20},{8,24},{12,28},{16,0},{20,4},{24,8},{28,12},{1,17},{... | collective-permute-start | bytes 122888 | tf_op jit(solution)/shard_map/ppermute | solution.py:224
  119.3 1.5 %collective-permute-start.33 = (bf16[16,1280]{1,0:T(8,128)(2,1)S(1)}, bf16[16,1280]{1,0:T(8,128)(2,1)S(1)}, u32[]{:S(2)}, u32[]{:S(2)}) collective-permute-start(bf16[16,1280]{1,0:T(8,128)(2,1)S(1)} %shard_map.104.refs_0_), channel_id=1, source_target_pairs={{0,24},{4,28},{8,16},{12,20},{16,8},{20,12},{24,0},{28,4},{1,25},{... | collective-permute-start | bytes 122888 | tf_op jit(solution)/shard_map/ppermute | solution.py:224
  121.8 2.4 %collective-permute-done.33.refs_3_ = bf16[16,1280]{1,0:T(8,128)(2,1)S(1)} collective-permute-done((bf16[16,1280]{1,0:T(8,128)(2,1)S(1)}, bf16[16,1280]{1,0:T(8,128)(2,1)S(1)}, u32[]{:S(2)}, u32[]{:S(2)}) %collective-permute-start.33) | collective-permute-done | bytes 40992 | tf_op jit(solution)/shard_map/ppermute | solution.py:224
  124.3 1.4 %collective-permute-done.34.refs_4_ = bf16[4,16,1280]{2,1,0:T(8,128)(2,1)S(1)} collective-permute-done((bf16[4,16,1280]{2,1,0:T(8,128)(2,1)S(1)}, bf16[4,16,1280]{2,1,0:T(8,128)(2,1)S(1)}, u32[]{:S(2)}, u32[]{:S(2)}) %collective-permute-start.34) | collective-permute-done | bytes 163872 | tf_op jit(solution)/shard_map/ppermute | solution.py:221
  125.6 1.8 %shard_map.105 = bf16[192,1280]{1,0:T(8,128)(2,1)} custom-call(s32[3]{0:T(128)S(1)} %pad_add_fusion.ids, bf16[16,1280]{1,0:T(8,128)(2,1)S(1)} %shard_map.104.refs_0_, bf16[16,1280]{1,0:T(8,128)(2,1)S(1)} %collective-permute-done.31.refs_1_, bf16[16,1280]{1,0:T(8,128)(2,1)S(1)} %collective-permute-done.32.refs_2_, ...), custom_call_target="tpu_custom_call" | custom-call | bytes 1437696 | tf_op jit(solution)/shard_map/pallas_call | solution.py:34
  (50 shorter events, 4.9 us)
Async XLA Ops:
  0.0 16.2 %collective-permute-start.4 = (bf16[512,1792]{1,0:T(8,128)(2,1)}, bf16[512,1792]{1,0:T(8,128)(2,1)S(1)}, u32[]{:S(2)}, u32[]{:S(2)}) collective-permute-start(bf16[512,1792]{1,0:T(8,128)(2,1)} %refs_2_.1), channel_id=1, source_target_pairs={{0,4},{4,0},{8,12},{12,8},{16,20},{20,16},{24,28},{28,24},{1,5},{5... | collective-permute-start | bytes 5505032 | tf_op jit(solution)/shard_map/ppermute | solution.py:221
  0.5 15.8 %collective-permute-start.5 = (bf16[512,1792]{1,0:T(8,128)(2,1)}, bf16[512,1792]{1,0:T(8,128)(2,1)}, u32[]{:S(2)}, u32[]{:S(2)}) collective-permute-start(bf16[512,1792]{1,0:T(8,128)(2,1)} %refs_4_.3), channel_id=1, source_target_pairs={{0,4},{4,0},{8,12},{12,8},{16,20},{20,16},{24,28},{28,24},{1,5},{5... | collective-permute-start | bytes 5505032 | tf_op jit(solution)/shard_map/ppermute | solution.py:221
  0.5 21.0 %collective-permute-start.9 = (bf16[1792,512]{1,0:T(8,128)(2,1)}, bf16[1792,512]{1,0:T(8,128)(2,1)}, u32[]{:S(2)}, u32[]{:S(2)}) collective-permute-start(bf16[1792,512]{1,0:T(8,128)(2,1)} %refs_3_.5), channel_id=1, source_target_pairs={{0,4},{4,0},{8,12},{12,8},{16,20},{20,16},{24,28},{28,24},{1,5},{5... | collective-permute-start | bytes 5505032 | tf_op jit(solution)/shard_map/ppermute | solution.py:221
  1.0 1.0 copy-start.8
  2.1 0.7 copy-start.10
  3.5 5.6 %collective-permute-start = (bf16[32,1280]{1,0:T(8,128)(2,1)S(1)}, bf16[32,1280]{1,0:T(8,128)(2,1)S(1)}, u32[]{:S(2)}, u32[]{:S(2)}) collective-permute-start(bf16[32,1280]{1,0:T(8,128)(2,1)S(1)} %shard_map.91.refs_0_), channel_id=1, source_target_pairs={{0,8},{4,12},{8,0},{12,4},{16,24},{20,28},{24,16},{28,20},{1,9},{5... | collective-permute-start | bytes 245768 | tf_op jit(solution)/shard_map/ppermute | solution.py:224
  6.0 5.8 %collective-permute-start.1 = (bf16[32,1280]{1,0:T(8,128)(2,1)S(1)}, bf16[32,1280]{1,0:T(8,128)(2,1)S(1)}, u32[]{:S(2)}, u32[]{:S(2)}) collective-permute-start(bf16[32,1280]{1,0:T(8,128)(2,1)S(1)} %shard_map.91.refs_0_), channel_id=1, source_target_pairs={{0,16},{4,20},{8,24},{12,28},{16,0},{20,4},{24,8},{28,12},{1,17},{... | collective-permute-start | bytes 245768 | tf_op jit(solution)/shard_map/ppermute | solution.py:224
  9.2 5.3 %collective-permute-start.2 = (bf16[32,1280]{1,0:T(8,128)(2,1)S(1)}, bf16[32,1280]{1,0:T(8,128)(2,1)S(1)}, u32[]{:S(2)}, u32[]{:S(2)}) collective-permute-start(bf16[32,1280]{1,0:T(8,128)(2,1)S(1)} %shard_map.91.refs_0_), channel_id=1, source_target_pairs={{0,24},{4,28},{8,16},{12,20},{16,8},{20,12},{24,0},{28,4},{1,25},{... | collective-permute-start | bytes 245768 | tf_op jit(solution)/shard_map/ppermute | solution.py:224
  14.5 12.8 %copy-start.5 = (bf16[1280,1024]{1,0:T(8,128)(2,1)S(1)}, bf16[1280,1024]{1,0:T(8,128)(2,1)}, u32[]{:S(2)}) copy-start(bf16[1280,1024]{1,0:T(8,128)(2,1)} %refs_4_.2) | copy-start | bytes 7864324
  14.5 1.7 %collective-permute-start.3 = (bf16[128,1280]{1,0:T(8,128)(2,1)S(1)}, bf16[128,1280]{1,0:T(8,128)(2,1)S(1)}, u32[]{:S(2)}, u32[]{:S(2)}) collective-permute-start(bf16[128,1280]{1,0:T(8,128)(2,1)S(1)} %pad_maximum_fusion), channel_id=1, source_target_pairs={{0,4},{4,0},{8,12},{12,8},{16,20},{20,16},{24,28},{28,24},{1,5},{5... | collective-permute-start | bytes 983048 | tf_op jit(solution)/shard_map/ppermute | solution.py:221
  17.0 30.6 %copy-start = (bf16[512,1792]{1,0:T(8,128)(2,1)S(1)}, bf16[512,1792]{1,0:T(8,128)(2,1)}, u32[]{:S(2)}) copy-start(bf16[512,1792]{1,0:T(8,128)(2,1)} %refs_2_.1) | copy-start | bytes 5505028
  17.0 30.6 %copy-start.2 = (bf16[512,1792]{1,0:T(8,128)(2,1)S(1)}, bf16[512,1792]{1,0:T(8,128)(2,1)}, u32[]{:S(2)}) copy-start(bf16[512,1792]{1,0:T(8,128)(2,1)} %refs_4_.3) | copy-start | bytes 5505028
  17.0 4.5 %collective-permute-start.6 = (bf16[16,1280]{1,0:T(8,128)(2,1)S(1)}, bf16[16,1280]{1,0:T(8,128)(2,1)S(1)}, u32[]{:S(2)}, u32[]{:S(2)}) collective-permute-start(bf16[16,1280]{1,0:T(8,128)(2,1)S(1)} %get-tuple-element.33.refs_0_), channel_id=1, source_target_pairs={{0,1},{1,0},{2,3},{3,2},{4,5},{5,4},{6,7},{7,6},{8,9},{9,8},{10,11... | collective-permute-start | bytes 122888 | tf_op jit(solution)/shard_map/ppermute | solution.py:227
  18.9 5.7 %collective-permute-start.7 = (bf16[16,1280]{1,0:T(8,128)(2,1)S(1)}, bf16[16,1280]{1,0:T(8,128)(2,1)S(1)}, u32[]{:S(2)}, u32[]{:S(2)}) collective-permute-start(bf16[16,1280]{1,0:T(8,128)(2,1)S(1)} %get-tuple-element.33.refs_0_), channel_id=1, source_target_pairs={{0,2},{1,3},{2,0},{3,1},{4,6},{5,7},{6,4},{7,5},{8,10},{9,11},{10,... | collective-permute-start | bytes 122888 | tf_op jit(solution)/shard_map/ppermute | solution.py:227
  21.5 5.8 %collective-permute-start.8 = (bf16[16,1280]{1,0:T(8,128)(2,1)S(1)}, bf16[16,1280]{1,0:T(8,128)(2,1)S(1)}, u32[]{:S(2)}, u32[]{:S(2)}) collective-permute-start(bf16[16,1280]{1,0:T(8,128)(2,1)S(1)} %get-tuple-element.33.refs_0_), channel_id=1, source_target_pairs={{0,3},{1,2},{2,1},{3,0},{4,7},{5,6},{6,5},{7,4},{8,11},{9,10},{10,... | collective-permute-start | bytes 122888 | tf_op jit(solution)/shard_map/ppermute | solution.py:227
  28.4 5.5 %collective-permute-start.10 = (bf16[64,1024]{1,0:T(8,128)(2,1)S(1)}, bf16[64,1024]{1,0:T(8,128)(2,1)S(1)}, u32[]{:S(2)}, u32[]{:S(2)}) collective-permute-start(bf16[64,1024]{1,0:T(8,128)(2,1)S(1)} %get-tuple-element.34.refs_0_.refs_4_), channel_id=1, source_target_pairs={{0,1},{1,0},{2,3},{3,2},{4,5},{5,4},{6,7},{7,6},{8,9},{9,8},{10,11... | collective-permute-start | bytes 393224 | tf_op jit(solution)/shard_map/ppermute | solution.py:227
  28.5 11.9 %collective-permute-start.11 = (bf16[64,1024]{1,0:T(8,128)(2,1)S(1)}, bf16[64,1024]{1,0:T(8,128)(2,1)S(1)}, u32[]{:S(2)}, u32[]{:S(2)}) collective-permute-start(bf16[64,1024]{1,0:T(8,128)(2,1)S(1)} %get-tuple-element.34.refs_0_.refs_4_), channel_id=1, source_target_pairs={{0,2},{1,3},{2,0},{3,1},{4,6},{5,7},{6,4},{7,5},{8,10},{9,11},{10,... | collective-permute-start | bytes 393224 | tf_op jit(solution)/shard_map/ppermute | solution.py:227
  29.7 10.7 %collective-permute-start.12 = (bf16[64,1024]{1,0:T(8,128)(2,1)S(1)}, bf16[64,1024]{1,0:T(8,128)(2,1)S(1)}, u32[]{:S(2)}, u32[]{:S(2)}) collective-permute-start(bf16[64,1024]{1,0:T(8,128)(2,1)S(1)} %get-tuple-element.34.refs_0_.refs_4_), channel_id=1, source_target_pairs={{0,3},{1,2},{2,1},{3,0},{4,7},{5,6},{6,5},{7,4},{8,11},{9,10},{10,... | collective-permute-start | bytes 393224 | tf_op jit(solution)/shard_map/ppermute | solution.py:227
  41.1 5.0 %collective-permute-start.14 = (bf16[2,64,512]{2,1,0:T(8,128)(2,1)S(1)}, bf16[2,64,512]{2,1,0:T(8,128)(2,1)S(1)}, u32[]{:S(2)}, u32[]{:S(2)}) collective-permute-start(bf16[2,64,512]{2,1,0:T(8,128)(2,1)S(1)} %get-tuple-element.41), channel_id=1, source_target_pairs={{0,8},{4,12},{8,0},{12,4},{16,24},{20,28},{24,16},{28,20},{1,9},{5... | collective-permute-start | bytes 393224 | tf_op jit(solution)/shard_map/ppermute | solution.py:224
  42.6 5.0 %collective-permute-start.15 = (bf16[2,64,512]{2,1,0:T(8,128)(2,1)S(1)}, bf16[2,64,512]{2,1,0:T(8,128)(2,1)S(1)}, u32[]{:S(2)}, u32[]{:S(2)}) collective-permute-start(bf16[2,64,512]{2,1,0:T(8,128)(2,1)S(1)} %get-tuple-element.42), channel_id=1, source_target_pairs={{0,16},{4,20},{8,24},{12,28},{16,0},{20,4},{24,8},{28,12},{1,17},{... | collective-permute-start | bytes 393224 | tf_op jit(solution)/shard_map/ppermute | solution.py:224
  44.2 9.1 %collective-permute-start.13 = (bf16[2,64,512]{2,1,0:T(8,128)(2,1)S(1)}, bf16[2,64,512]{2,1,0:T(8,128)(2,1)S(1)}, u32[]{:S(2)}, u32[]{:S(2)}) collective-permute-start(bf16[2,64,512]{2,1,0:T(8,128)(2,1)S(1)} %get-tuple-element.36), channel_id=1, source_target_pairs={{0,24},{4,28},{8,16},{12,20},{16,8},{20,12},{24,0},{28,4},{1,25},{... | collective-permute-start | bytes 393224 | tf_op jit(solution)/shard_map/ppermute | solution.py:224
  51.2 17.2 %collective-permute-start.16 = (bf16[64,3584]{1,0:T(8,128)(2,1)}, bf16[64,3584]{1,0:T(8,128)(2,1)S(1)}, u32[]{:S(2)}, u32[]{:S(2)}) collective-permute-start(bf16[64,3584]{1,0:T(8,128)(2,1)} %get-tuple-element.43), channel_id=1, source_target_pairs={{0,8},{4,12},{8,0},{12,4},{16,24},{20,28},{24,16},{28,20},{1,9},{5... | collective-permute-start | bytes 1376264 | tf_op jit(solution)/shard_map/ppermute | solution.py:224
  51.7 17.9 %collective-permute-start.17 = (bf16[64,3584]{1,0:T(8,128)(2,1)}, bf16[64,3584]{1,0:T(8,128)(2,1)S(1)}, u32[]{:S(2)}, u32[]{:S(2)}) collective-permute-start(bf16[64,3584]{1,0:T(8,128)(2,1)} %get-tuple-element.44), channel_id=1, source_target_pairs={{0,16},{4,20},{8,24},{12,28},{16,0},{20,4},{24,8},{28,12},{1,17},{... | collective-permute-start | bytes 1376264 | tf_op jit(solution)/shard_map/ppermute | solution.py:224
  53.2 5.2 %copy-start.11 = (s32[192]{0:T(256)S(1)}, s32[192]{0:T(256)}, u32[]{:S(2)}) copy-start(s32[192]{0:T(256)} %param.11) | copy-start | bytes 2308
  53.2 6.8 %copy-start.7 = (bf16[192,1280]{1,0:T(8,128)(2,1)S(1)}, bf16[192,1280]{1,0:T(8,128)(2,1)}, u32[]{:S(2)}) copy-start(bf16[192,1280]{1,0:T(8,128)(2,1)} %refs_7_.1) | copy-start | bytes 1474564
  56.9 14.8 %collective-permute-start.18 = (bf16[64,3584]{1,0:T(8,128)(2,1)}, bf16[64,3584]{1,0:T(8,128)(2,1)}, u32[]{:S(2)}, u32[]{:S(2)}) collective-permute-start(bf16[64,3584]{1,0:T(8,128)(2,1)} %get-tuple-element.45), channel_id=1, source_target_pairs={{0,24},{4,28},{8,16},{12,20},{16,8},{20,12},{24,0},{28,4},{1,25},{... | collective-permute-start | bytes 1376264 | tf_op jit(solution)/shard_map/ppermute | solution.py:224
  60.0 0.9 copy-start.9
  62.5 1.5 %copy-start.1 = (bf16[512,1792]{1,0:T(8,128)(2,1)S(1)}, bf16[512,1792]{1,0:T(8,128)(2,1)}, u32[]{:S(2)}) copy-start(bf16[512,1792]{1,0:T(8,128)(2,1)} %refs_2_.1) | copy-start | bytes 5505028
  64.0 1.5 %copy-start.3 = (bf16[512,1792]{1,0:T(8,128)(2,1)S(1)}, bf16[512,1792]{1,0:T(8,128)(2,1)}, u32[]{:S(2)}) copy-start(bf16[512,1792]{1,0:T(8,128)(2,1)} %refs_4_.3) | copy-start | bytes 5505028
  68.4 14.3 %copy-start.4 = (bf16[1792,512]{1,0:T(8,128)(2,1)S(1)}, bf16[1792,512]{1,0:T(8,128)(2,1)}, u32[]{:S(2)}) copy-start(bf16[1792,512]{1,0:T(8,128)(2,1)} %refs_3_.5) | copy-start | bytes 5505028
  73.3 6.1 %collective-permute-start.19 = (bf16[64,1792]{1,0:T(8,128)(2,1)S(1)}, bf16[64,1792]{1,0:T(8,128)(2,1)S(1)}, u32[]{:S(2)}, u32[]{:S(2)}) collective-permute-start(bf16[64,1792]{1,0:T(8,128)(2,1)S(1)} %get-tuple-element.46.refs_0_), channel_id=1, source_target_pairs={{0,8},{4,12},{8,0},{12,4},{16,24},{20,28},{24,16},{28,20},{1,9},{5... | collective-permute-start | bytes 688136 | tf_op jit(solution)/shard_map/ppermute | solution.py:224
  73.4 7.9 %collective-permute-start.20 = (bf16[64,1792]{1,0:T(8,128)(2,1)S(1)}, bf16[64,1792]{1,0:T(8,128)(2,1)S(1)}, u32[]{:S(2)}, u32[]{:S(2)}) collective-permute-start(bf16[64,1792]{1,0:T(8,128)(2,1)S(1)} %get-tuple-element.46.refs_0_), channel_id=1, source_target_pairs={{0,16},{4,20},{8,24},{12,28},{16,0},{20,4},{24,8},{28,12},{1,17},{... | collective-permute-start | bytes 688136 | tf_op jit(solution)/shard_map/ppermute | solution.py:224
  75.3 7.3 %collective-permute-start.21 = (bf16[64,1792]{1,0:T(8,128)(2,1)S(1)}, bf16[64,1792]{1,0:T(8,128)(2,1)S(1)}, u32[]{:S(2)}, u32[]{:S(2)}) collective-permute-start(bf16[64,1792]{1,0:T(8,128)(2,1)S(1)} %get-tuple-element.46.refs_0_), channel_id=1, source_target_pairs={{0,24},{4,28},{8,16},{12,20},{16,8},{20,12},{24,0},{28,4},{1,25},{... | collective-permute-start | bytes 688136 | tf_op jit(solution)/shard_map/ppermute | solution.py:224
  85.1 5.8 %collective-permute-start.22 = (bf16[2,64,512]{2,1,0:T(8,128)(2,1)S(1)}, bf16[2,64,512]{2,1,0:T(8,128)(2,1)S(1)}, u32[]{:S(2)}, u32[]{:S(2)}) collective-permute-start(bf16[2,64,512]{2,1,0:T(8,128)(2,1)S(1)} %get-tuple-element.48), channel_id=1, source_target_pairs={{0,8},{4,12},{8,0},{12,4},{16,24},{20,28},{24,16},{28,20},{1,9},{5... | collective-permute-start | bytes 393224 | tf_op jit(solution)/shard_map/ppermute | solution.py:224
  86.3 5.0 %collective-permute-start.23 = (bf16[2,64,512]{2,1,0:T(8,128)(2,1)S(1)}, bf16[2,64,512]{2,1,0:T(8,128)(2,1)S(1)}, u32[]{:S(2)}, u32[]{:S(2)}) collective-permute-start(bf16[2,64,512]{2,1,0:T(8,128)(2,1)S(1)} %get-tuple-element.49), channel_id=1, source_target_pairs={{0,16},{4,20},{8,24},{12,28},{16,0},{20,4},{24,8},{28,12},{1,17},{... | collective-permute-start | bytes 393224 | tf_op jit(solution)/shard_map/ppermute | solution.py:224
  86.8 20.9 %copy-start.6 = (bf16[1024,1280]{1,0:T(8,128)(2,1)S(1)}, bf16[1024,1280]{1,0:T(8,128)(2,1)}, u32[]{:S(2)}) copy-start(bf16[1024,1280]{1,0:T(8,128)(2,1)} %refs_5_.1) | copy-start | bytes 7864324
  86.8 5.9 %collective-permute-start.24 = (bf16[2,64,512]{2,1,0:T(8,128)(2,1)S(1)}, bf16[2,64,512]{2,1,0:T(8,128)(2,1)S(1)}, u32[]{:S(2)}, u32[]{:S(2)}) collective-permute-start(bf16[2,64,512]{2,1,0:T(8,128)(2,1)S(1)} %get-tuple-element.50), channel_id=1, source_target_pairs={{0,24},{4,28},{8,16},{12,20},{16,8},{20,12},{24,0},{28,4},{1,25},{... | collective-permute-start | bytes 393224 | tf_op jit(solution)/shard_map/ppermute | solution.py:224
  93.3 7.3 %collective-permute-start.25 = (bf16[64,1024]{1,0:T(8,128)(2,1)S(1)}, bf16[64,1024]{1,0:T(8,128)(2,1)S(1)}, u32[]{:S(2)}, u32[]{:S(2)}) collective-permute-start(bf16[64,1024]{1,0:T(8,128)(2,1)S(1)} %get-tuple-element.52), channel_id=1, source_target_pairs={{0,1},{1,0},{2,3},{3,2},{4,5},{5,4},{6,7},{7,6},{8,9},{9,8},{10,11... | collective-permute-start | bytes 393224 | tf_op jit(solution)/shard_map/ppermute | solution.py:227
  97.7 10.0 %collective-permute-start.26 = (bf16[64,1024]{1,0:T(8,128)(2,1)S(1)}, bf16[64,1024]{1,0:T(8,128)(2,1)S(1)}, u32[]{:S(2)}, u32[]{:S(2)}) collective-permute-start(bf16[64,1024]{1,0:T(8,128)(2,1)S(1)} %get-tuple-element.53), channel_id=1, source_target_pairs={{0,2},{1,3},{2,0},{3,1},{4,6},{5,7},{6,4},{7,5},{8,10},{9,11},{10,... | collective-permute-start | bytes 393224 | tf_op jit(solution)/shard_map/ppermute | solution.py:227
  97.7 10.0 %collective-permute-start.27 = (bf16[64,1024]{1,0:T(8,128)(2,1)S(1)}, bf16[64,1024]{1,0:T(8,128)(2,1)S(1)}, u32[]{:S(2)}, u32[]{:S(2)}) collective-permute-start(bf16[64,1024]{1,0:T(8,128)(2,1)S(1)} %get-tuple-element.54), channel_id=1, source_target_pairs={{0,3},{1,2},{2,1},{3,0},{4,7},{5,6},{6,5},{7,4},{8,11},{9,10},{10,... | collective-permute-start | bytes 393224 | tf_op jit(solution)/shard_map/ppermute | solution.py:227
  108.8 4.5 %collective-permute-start.28 = (bf16[16,1280]{1,0:T(8,128)(2,1)S(1)}, bf16[16,1280]{1,0:T(8,128)(2,1)S(1)}, u32[]{:S(2)}, u32[]{:S(2)}) collective-permute-start(bf16[16,1280]{1,0:T(8,128)(2,1)S(1)} %get-tuple-element.56), channel_id=1, source_target_pairs={{0,1},{1,0},{2,3},{3,2},{4,5},{5,4},{6,7},{7,6},{8,9},{9,8},{10,11... | collective-permute-start | bytes 122888 | tf_op jit(solution)/shard_map/ppermute | solution.py:227
  110.8 4.9 %collective-permute-start.29 = (bf16[16,1280]{1,0:T(8,128)(2,1)S(1)}, bf16[16,1280]{1,0:T(8,128)(2,1)S(1)}, u32[]{:S(2)}, u32[]{:S(2)}) collective-permute-start(bf16[16,1280]{1,0:T(8,128)(2,1)S(1)} %get-tuple-element.57), channel_id=1, source_target_pairs={{0,2},{1,3},{2,0},{3,1},{4,6},{5,7},{6,4},{7,5},{8,10},{9,11},{10,... | collective-permute-start | bytes 122888 | tf_op jit(solution)/shard_map/ppermute | solution.py:227
  110.8 5.8 %collective-permute-start.30 = (bf16[16,1280]{1,0:T(8,128)(2,1)S(1)}, bf16[16,1280]{1,0:T(8,128)(2,1)S(1)}, u32[]{:S(2)}, u32[]{:S(2)}) collective-permute-start(bf16[16,1280]{1,0:T(8,128)(2,1)S(1)} %get-tuple-element.58), channel_id=1, source_target_pairs={{0,3},{1,2},{2,1},{3,0},{4,7},{5,6},{6,5},{7,4},{8,11},{9,10},{10,... | collective-permute-start | bytes 122888 | tf_op jit(solution)/shard_map/ppermute | solution.py:227
  117.2 4.1 %collective-permute-start.31 = (bf16[16,1280]{1,0:T(8,128)(2,1)S(1)}, bf16[16,1280]{1,0:T(8,128)(2,1)S(1)}, u32[]{:S(2)}, u32[]{:S(2)}) collective-permute-start(bf16[16,1280]{1,0:T(8,128)(2,1)S(1)} %shard_map.104.refs_0_), channel_id=1, source_target_pairs={{0,8},{4,12},{8,0},{12,4},{16,24},{20,28},{24,16},{28,20},{1,9},{5... | collective-permute-start | bytes 122888 | tf_op jit(solution)/shard_map/ppermute | solution.py:224
  117.8 4.0 %collective-permute-start.32 = (bf16[16,1280]{1,0:T(8,128)(2,1)S(1)}, bf16[16,1280]{1,0:T(8,128)(2,1)S(1)}, u32[]{:S(2)}, u32[]{:S(2)}) collective-permute-start(bf16[16,1280]{1,0:T(8,128)(2,1)S(1)} %shard_map.104.refs_0_), channel_id=1, source_target_pairs={{0,16},{4,20},{8,24},{12,28},{16,0},{20,4},{24,8},{28,12},{1,17},{... | collective-permute-start | bytes 122888 | tf_op jit(solution)/shard_map/ppermute | solution.py:224
  119.3 4.9 %collective-permute-start.33 = (bf16[16,1280]{1,0:T(8,128)(2,1)S(1)}, bf16[16,1280]{1,0:T(8,128)(2,1)S(1)}, u32[]{:S(2)}, u32[]{:S(2)}) collective-permute-start(bf16[16,1280]{1,0:T(8,128)(2,1)S(1)} %shard_map.104.refs_0_), channel_id=1, source_target_pairs={{0,24},{4,28},{8,16},{12,20},{16,8},{20,12},{24,0},{28,4},{1,25},{... | collective-permute-start | bytes 122888 | tf_op jit(solution)/shard_map/ppermute | solution.py:224
  124.2 1.5 %collective-permute-start.34 = (bf16[4,16,1280]{2,1,0:T(8,128)(2,1)S(1)}, bf16[4,16,1280]{2,1,0:T(8,128)(2,1)S(1)}, u32[]{:S(2)}, u32[]{:S(2)}) collective-permute-start(bf16[4,16,1280]{2,1,0:T(8,128)(2,1)S(1)} %pad_maximum_fusion.1), channel_id=1, source_target_pairs={{0,4},{4,0},{8,12},{12,8},{16,20},{20,16},{24,28},{28,24},{1,5},{5... | collective-permute-start | bytes 491528 | tf_op jit(solution)/shard_map/ppermute | solution.py:221

commit v4 on v3

--- a/solution.py
+++ b/solution.py
@@ -23,24 +23,23 @@
     return jax.ShapeDtypeStruct(tuple(dims), dtype)
 
 
-def call(kernel, outs, ids, *arrays, hbm=(), through=(), scratch=(), flops=0, limit=20):
-    n, t, o = len(arrays), len(through), len(outs)
+def call(kernel, outs, ids, *arrays, after=(), scratch=(), flops=0, limit=20):
+    n, t = len(arrays), len(after)
 
     def run(ids, *refs):
-        kernel(ids, *refs[:n], *refs[n + t : n + t + o], *refs[n + 2 * t + o :])
+        kernel(ids, *refs[:n], *refs[n + t :])
 
     moved = sum(a.size * a.dtype.itemsize for a in arrays)
     moved += sum(math.prod(a.shape) * a.dtype.itemsize for a in outs)
     results = pl.pallas_call(
         run,
-        out_shape=list(outs) + [shape(a.shape, a.dtype) for a in through],
-        in_specs=[SMEM] + [HBM if i in hbm else VMEM for i in range(n)] + [HBM] * t,
-        out_specs=[VMEM] * o + [HBM] * t,
+        out_shape=list(outs),
+        in_specs=[SMEM] + [VMEM] * n + [HBM] * t,
+        out_specs=[VMEM] * len(outs),
         scratch_shapes=list(scratch),
-        input_output_aliases={1 + n + i: o + i for i in range(t)},
         compiler_params=pltpu.CompilerParams(vmem_limit_bytes=limit * 1024 * 1024),
         cost_estimate=pl.CostEstimate(flops=int(flops), bytes_accessed=int(moved), transcendentals=0),
-    )(ids, *arrays, *through)
+    )(ids, *arrays, *after)
     return list(results)
 
 
@@ -178,12 +177,12 @@
     slots = keys.shape[0]
     patch = lax.broadcasted_iota(jnp.int32, (dec.shape[0], slots), 1)
     allowed = patch <= seg[...]
-    for h in range(out.shape[0]):
+    for h in range(dec.shape[1] // HD):
         part = slice(h * HD, (h + 1) * HD)
         scores = lax.dot_general(dec[:, part], keys[:, part], (((1,), (1,)), ((), ())), preferred_element_type=F32)
         scores = jnp.where(allowed, scores / math.sqrt(HD), -1e30)
         expon = jnp.exp(scores - jnp.max(scores, axis=1, keepdims=True))
-        out[h] = (expon / jnp.sum(expon, axis=1, keepdims=True)).astype(BF16)
+        out[:, h * slots : (h + 1) * slots] = (expon / jnp.sum(expon, axis=1, keepdims=True)).astype(BF16)
 
 
 def mix_kernel(chips, ids, *refs):
@@ -194,14 +193,22 @@
         rows[2 * (q ^ k) + c] = mine[k][...]
         rows[2 * (q ^ k) + 1 - c] = theirs[k]
     every = rows[...].reshape(2 * chips * ROWS, rows.shape[2])
-    slots = weights.shape[2]
+    heads = dec.shape[1] // HD
+    slots = weights.shape[1] // heads
     patch = lax.broadcasted_iota(jnp.int32, (slots, every.shape[0]), 0)
     position = lax.broadcasted_iota(jnp.int32, (slots, every.shape[0]), 1)
     found = (position - start[0:1, 0:1] == patch).astype(BF16)
     values = dot(found, every).astype(BF16)
-    for h in range(weights.shape[0]):
-        part = slice(h * HD, (h + 1) * HD)
-        out[:, part] = (dec[:, part].astype(F32) + dot(weights[h], values[:, part])).astype(BF16)
+    some = max(1, 128 // slots)
+    for h in range(0, heads, some):
+        n = min(some, heads - h)
+        part = slice(h * HD, (h + n) * HD)
+        line = lax.broadcasted_iota(jnp.int32, (n * slots, n * HD), 0) // slots
+        column = lax.broadcasted_iota(jnp.int32, (n * slots, n * HD), 1) // HD
+        spread = jnp.concatenate([values[:, part]] * n, axis=0)
+        spread = jnp.where(line == column, spread, jnp.zeros_like(spread))
+        mixed = dot(weights[:, h * slots : (h + n) * slots], spread)
+        out[:, part] = (dec[:, part].astype(F32) + mixed).astype(BF16)
 
 
 def body(enc_states, dec_states, segments, patch_keys, w_in, w_gate, w_up, w_down, w_out):
@@ -226,6 +233,13 @@
     def plane(a, k):
         return lax.ppermute(a, "mp", [(i, i ^ k) for i in range(groups)])
 
+    def chips_of(arrays):
+        return [chip(a, k + 1) for k, a in enumerate(arrays)]
+
+    def planes_of(arrays):
+        done = [plane(a, k + 1) for k, a in reversed(list(enumerate(arrays)))]
+        return done[::-1]
+
     [pooled] = call(
         functools.partial(pool_kernel, slots),
         [shape((slots, width))],
@@ -233,30 +247,31 @@
         segments.reshape(1, bytes_),
         enc_states,
     )
-    siblings = [sibling(w) for w in (w_gate, w_up)]
-    gathered = [pooled] + [chip(pooled, k) for k in range(1, chips)]
+    gate_b, up_b = sibling(w_gate), sibling(w_up)
+    gathered = [pooled] + chips_of([pooled] * (chips - 1))
     theirs = sibling(jnp.concatenate(gathered, axis=0))
-    packed, start, gate_b, up_b = call(
+    packed, start = call(
         functools.partial(pack_kernel, chips, slots),
         [shape((ROWS, width)), shape((8, HD), jnp.int32)],
         ids,
         *gathered,
         theirs,
-        through=siblings,
+        after=[gate_b, up_b],
         scratch=[pltpu.VMEM((seq * slots, width), BF16)],
     )
-    pieces = [packed] + [plane(packed, k) for k in range(1, groups)]
-    x, down_b = call(
+    late, packed = lax.optimization_barrier((w_down, packed))
+    down_b = sibling(late)
+    pieces = [packed] + planes_of([packed] * (groups - 1))
+    [x] = call(
         functools.partial(x_kernel, groups),
         [shape((rows, wide))],
         ids,
         *pieces,
         w_in,
-        through=[sibling(w_down)],
         scratch=[pltpu.VMEM((groups, ROWS, width), BF16)],
         flops=2 * rows * width * wide,
     )
-    pieces = [x] + [plane(x, k) for k in range(1, groups)]
+    pieces = [x] + planes_of([x] * (groups - 1))
     *sent, scale = call(
         functools.partial(spread_kernel, groups, chips),
         [shape((2, rows, unit)) for _ in range(chips)] + [shape((rows, HD), F32)],
@@ -265,7 +280,7 @@
         scratch=[pltpu.VMEM((seq, rows, unit), BF16)],
     )
 
-    def gate(pieces, through=()):
+    def gate(pieces, after=()):
         return call(
             functools.partial(gate_kernel, len(pieces)),
             [shape((rows, 2 * ffw)) for _ in pieces],
@@ -275,21 +290,20 @@
             gate_b,
             w_up,
             up_b,
-            through=through,
+            after=after,
             flops=8 * len(pieces) * rows * unit * ffw,
         )
 
-    arrived = [chip(sent[k], k) for k in range(1, chips)]
+    arrived = chips_of(sent[1:])
     partial = gate(arrived[:-1])
-    last, own = gate(arrived[-1:], [sent[0]])
-    partial = [chip(p, k + 1) for k, p in enumerate(partial + [last])]
-    partial = gate([own]) + partial
+    last, own = gate([arrived[-1], sent[0]], partial[:1])
+    partial = [own] + chips_of(partial + [last])
 
     keys = jnp.pad(patch_keys, ((0, 1), (0, 0)))
     [weights] = call(
-        weights_kernel, [shape((heads, bytes_, slots))], ids, segments.reshape(bytes_, 1), dec_states, keys
-    )
-    hidden, weights = call(hidden_kernel, [shape((rows, ffw))], ids, scale, *partial, through=[weights])
+        weights_kernel, [shape((bytes_, heads * slots))], ids, segments.reshape(bytes_, 1), dec_states, keys
+    )
+    [hidden] = call(hidden_kernel, [shape((rows, ffw))], ids, scale, *partial, after=[weights])
 
     def down(pieces):
         return call(
@@ -302,9 +316,9 @@
             flops=4 * len(pieces) * rows * unit * ffw,
         )
 
-    arrived = [chip(hidden, k) for k in range(1, chips)]
+    arrived = chips_of([hidden] * (chips - 1))
     columns = down([hidden]) + down(arrived)
-    columns = [columns[0]] + [chip(columns[k], k) for k in range(1, chips)]
+    columns = [columns[0]] + chips_of(columns[1:])
     slices = call(
         functools.partial(regroup_kernel, chips, groups),
         [shape((rows, wide)) for _ in range(groups)],
@@ -312,7 +326,7 @@
         *columns,
         scratch=[pltpu.VMEM((seq, rows, unit), BF16)],
     )
-    slices = [slices[0]] + [plane(slices[k], k) for k in range(1, groups)]
+    slices = [slices[0]] + planes_of(slices[1:])
     outs = call(
         functools.partial(out_kernel, groups),
         [shape((ROWS, width)) for _ in range(groups)],
@@ -323,9 +337,9 @@
         scratch=[pltpu.VMEM((groups, ROWS, width), BF16)],
         flops=2 * rows * width * wide,
     )
-    outs = [outs[0]] + [plane(outs[k], k) for k in range(1, groups)]
+    outs = [outs[0]] + planes_of(outs[1:])
     [outputs] = call(add_kernel, [shape((ROWS, width))], ids, *outs)
-    outputs = [outputs] + [chip(outputs, k) for k in range(1, chips)]
+    outputs = [outputs] + chips_of([outputs] * (chips - 1))
     theirs = sibling(jnp.stack(outputs))
     [decoded] = call(
         functools.partial(mix_kernel, chips),

time: 128 us -> 125 us (0.977)
  waiting for transfers between devices: 48.8 us -> 55.5 us
  local copies, waits for them, and re-layouts: 7.28 us -> 3.66 us
  starting transfers between devices: 45.8 us -> 42.3 us
  Pallas kernels: 25.3 us -> 23.3 us
    ppermute x18, waiting for transfers between devices: 21.6 us -> 27.8 us  [chip(): return lax.ppermute(a, 'seq', [(i, i ^ 2 * k) for i in range(seq)])]
    ppermute x18, starting transfers between devices: 24.4 us -> 22.2 us  [chip(): return lax.ppermute(a, 'seq', [(i, i ^ 2 * k) for i in range(seq)])]
    unnamed x24 -> x22, local copies, waits for them, and re-layouts: 5.62 us -> 3.54 us
    pallas_call x15 -> x14, Pallas kernels: 25.3 us -> 23.3 us  [call(): pl.pallas_call(run, out_shape=list(outs), in_specs=[SMEM] + [VMEM] * n +...]
  transfers between devices with their start and end apart: 35 -> 35, of which waited for: 24 -> 24; matrix products, arithmetic and copies ran while one was open for 1% -> 0% of each run, Pallas kernels for 12% -> 12%
where the time goes in v4:
time: 125 us
  waiting for transfers between devices  55.5 us (44%)
  starting transfers between devices  42.3 us (34%)
  Pallas kernels  23.3 us (19%)
  local copies, waits for them, and re-layouts  3.66 us (3%)
    ppermute x18, waiting for transfers between devices, chip(): return lax.ppermute(a, 'seq', [(i, i ^ 2 * k) for i in range(seq)])  27.8 us
    ppermute x12, waiting for transfers between devices, plane(): return lax.ppermute(a, 'mp', [(i, i ^ k) for i in range(groups)])  24.8 us
    pallas_call x14, Pallas kernels, call(): pl.pallas_call(run, out_shape=list(outs), in_specs=[SMEM] + [VMEM] * n +...  23.3 us
    ppermute x18, starting transfers between devices, chip(): return lax.ppermute(a, 'seq', [(i, i ^ 2 * k) for i in range(seq)])  22.2 us
    ppermute x12, starting transfers between devices, plane(): return lax.ppermute(a, 'mp', [(i, i ^ k) for i in range(groups)])  19.2 us
    unnamed x22, local copies, waits for them, and re-layouts  3.54 us
    ppermute x5, waiting for transfers between devices, sibling(): return lax.ppermute(a, 'seq', [(i, i ^ 1) for i in range(seq)])  3.01 us
  transfers between devices with their start and end apart: 35, of which 24 were waited for; matrix products, arithmetic and copies ran while one was open for 0% of the time, Pallas kernels for 12%

profile of v4, /device:TPU:0, one launch (start us, length us, event | category | flops | bytes accessed | tf_op | source)
XLA Modules:
  0.0 125.1 jit_solution(9272404216702920227)
XLA Ops:
  0.6 1.0 copy-done.5
  1.6 0.7 copy-done.8
  2.3 0.8 shard_map.91.refs_0_
  3.1 3.0 %collective-permute-start = (bf16[32,1280]{1,0:T(8,128)(2,1)S(1)}, bf16[32,1280]{1,0:T(8,128)(2,1)S(1)}, u32[]{:S(2)}, u32[]{:S(2)}) collective-permute-start(bf16[32,1280]{1,0:T(8,128)(2,1)S(1)} %shard_map.91.refs_0_), channel_id=1, source_target_pairs={{0,8},{4,12},{8,0},{12,4},{16,24},{20,28},{24,16},{28,20},{1,9},{5... | collective-permute-start | bytes 245768 | tf_op jit(solution)/shard_map/ppermute | solution.py:231
  6.0 1.5 %collective-permute-start.1 = (bf16[32,1280]{1,0:T(8,128)(2,1)S(1)}, bf16[32,1280]{1,0:T(8,128)(2,1)S(1)}, u32[]{:S(2)}, u32[]{:S(2)}) collective-permute-start(bf16[32,1280]{1,0:T(8,128)(2,1)S(1)} %shard_map.91.refs_0_), channel_id=1, source_target_pairs={{0,16},{4,20},{8,24},{12,28},{16,0},{20,4},{24,8},{28,12},{1,17},{... | collective-permute-start | bytes 245768 | tf_op jit(solution)/shard_map/ppermute | solution.py:231
  7.6 1.1 collective-permute-done.refs_1_
  8.6 1.8 %collective-permute-done.1.refs_2_ = bf16[32,1280]{1,0:T(8,128)(2,1)S(1)} collective-permute-done((bf16[32,1280]{1,0:T(8,128)(2,1)S(1)}, bf16[32,1280]{1,0:T(8,128)(2,1)S(1)}, u32[]{:S(2)}, u32[]{:S(2)}) %collective-permute-start.1) | collective-permute-done | bytes 81952 | tf_op jit(solution)/shard_map/ppermute | solution.py:231
  10.5 2.4 %collective-permute-done.2.refs_3_ = bf16[32,1280]{1,0:T(8,128)(2,1)S(1)} collective-permute-done((bf16[32,1280]{1,0:T(8,128)(2,1)S(1)}, bf16[32,1280]{1,0:T(8,128)(2,1)S(1)}, u32[]{:S(2)}, u32[]{:S(2)}) %collective-permute-start.2) | collective-permute-done | bytes 81952 | tf_op jit(solution)/shard_map/ppermute | solution.py:231
  13.0 1.6 %collective-permute-done.3.refs_4_ = bf16[128,1280]{1,0:T(8,128)(2,1)S(1)} collective-permute-done((bf16[128,1280]{1,0:T(8,128)(2,1)S(1)}, bf16[128,1280]{1,0:T(8,128)(2,1)S(1)}, u32[]{:S(2)}, u32[]{:S(2)}) %collective-permute-start.3) | collective-permute-done | bytes 327712 | tf_op jit(solution)/shard_map/ppermute | solution.py:228
  14.6 0.8 shard_map.92
  15.6 1.6 %collective-permute-start.6 = (bf16[16,1280]{1,0:T(8,128)(2,1)S(1)}, bf16[16,1280]{1,0:T(8,128)(2,1)S(1)}, u32[]{:S(2)}, u32[]{:S(2)}) collective-permute-start(bf16[16,1280]{1,0:T(8,128)(2,1)S(1)} %get-tuple-element.30.refs_0_), channel_id=1, source_target_pairs={{0,1},{1,0},{2,3},{3,2},{4,5},{5,4},{6,7},{7,6},{8,9},{9,8},{10,11... | collective-permute-start | bytes 122888 | tf_op jit(solution)/shard_map/ppermute | solution.py:234
  17.2 2.6 %collective-permute-start.7 = (bf16[16,1280]{1,0:T(8,128)(2,1)S(1)}, bf16[16,1280]{1,0:T(8,128)(2,1)S(1)}, u32[]{:S(2)}, u32[]{:S(2)}) collective-permute-start(bf16[16,1280]{1,0:T(8,128)(2,1)S(1)} %get-tuple-element.30.refs_0_), channel_id=1, source_target_pairs={{0,2},{1,3},{2,0},{3,1},{4,6},{5,7},{6,4},{7,5},{8,10},{9,11},{10,... | collective-permute-start | bytes 122888 | tf_op jit(solution)/shard_map/ppermute | solution.py:234
  20.0 2.8 %collective-permute-done.7.refs_2_ = bf16[16,1280]{1,0:T(8,128)(2,1)S(1)} collective-permute-done((bf16[16,1280]{1,0:T(8,128)(2,1)S(1)}, bf16[16,1280]{1,0:T(8,128)(2,1)S(1)}, u32[]{:S(2)}, u32[]{:S(2)}) %collective-permute-start.7) | collective-permute-done | bytes 40992 | tf_op jit(solution)/shard_map/ppermute | solution.py:234
  22.9 2.7 %collective-permute-done.8.refs_3_ = bf16[16,1280]{1,0:T(8,128)(2,1)S(1)} collective-permute-done((bf16[16,1280]{1,0:T(8,128)(2,1)S(1)}, bf16[16,1280]{1,0:T(8,128)(2,1)S(1)}, u32[]{:S(2)}, u32[]{:S(2)}) %collective-permute-start.8) | collective-permute-done | bytes 40992 | tf_op jit(solution)/shard_map/ppermute | solution.py:234
  25.6 1.1 shard_map.93.refs_0_.refs_4_
  26.8 1.3 %collective-permute-start.10 = (bf16[64,1024]{1,0:T(8,128)(2,1)S(1)}, bf16[64,1024]{1,0:T(8,128)(2,1)S(1)}, u32[]{:S(2)}, u32[]{:S(2)}) collective-permute-start(bf16[64,1024]{1,0:T(8,128)(2,1)S(1)} %shard_map.93.refs_0_.refs_4_), channel_id=1, source_target_pairs={{0,2},{1,3},{2,0},{3,1},{4,6},{5,7},{6,4},{7,5},{8,10},{9,11},{10,... | collective-permute-start | bytes 393224 | tf_op jit(solution)/shard_map/ppermute | solution.py:234
  28.1 3.1 %collective-permute-start.11 = (bf16[64,1024]{1,0:T(8,128)(2,1)S(1)}, bf16[64,1024]{1,0:T(8,128)(2,1)S(1)}, u32[]{:S(2)}, u32[]{:S(2)}) collective-permute-start(bf16[64,1024]{1,0:T(8,128)(2,1)S(1)} %shard_map.93.refs_0_.refs_4_), channel_id=1, source_target_pairs={{0,3},{1,2},{2,1},{3,0},{4,7},{5,6},{6,5},{7,4},{8,11},{9,10},{10,... | collective-permute-start | bytes 393224 | tf_op jit(solution)/shard_map/ppermute | solution.py:234
  31.2 1.3 %collective-permute-done.9.refs_1_ = bf16[64,1024]{1,0:T(8,128)(2,1)S(1)} collective-permute-done((bf16[64,1024]{1,0:T(8,128)(2,1)S(1)}, bf16[64,1024]{1,0:T(8,128)(2,1)S(1)}, u32[]{:S(2)}, u32[]{:S(2)}) %collective-permute-start.9) | collective-permute-done | bytes 131104 | tf_op jit(solution)/shard_map/ppermute | solution.py:234
  32.5 6.4 %collective-permute-done.10.refs_2_ = bf16[64,1024]{1,0:T(8,128)(2,1)S(1)} collective-permute-done((bf16[64,1024]{1,0:T(8,128)(2,1)S(1)}, bf16[64,1024]{1,0:T(8,128)(2,1)S(1)}, u32[]{:S(2)}, u32[]{:S(2)}) %collective-permute-start.10) | collective-permute-done | bytes 131104 | tf_op jit(solution)/shard_map/ppermute | solution.py:234
  38.9 0.7 shard_map.94
  39.6 0.6 collective-permute-start.13
  40.2 0.8 collective-permute-start.14
  41.0 2.2 %collective-permute-start.12 = (bf16[2,64,512]{2,1,0:T(8,128)(2,1)S(1)}, bf16[2,64,512]{2,1,0:T(8,128)(2,1)S(1)}, u32[]{:S(2)}, u32[]{:S(2)}) collective-permute-start(bf16[2,64,512]{2,1,0:T(8,128)(2,1)S(1)} %get-tuple-element.32), channel_id=1, source_target_pairs={{0,24},{4,28},{8,16},{12,20},{16,8},{20,12},{24,0},{28,4},{1,25},{... | collective-permute-start | bytes 393224 | tf_op jit(solution)/shard_map/ppermute | solution.py:231
  43.2 1.5 %collective-permute-done.13.refs_0_ = bf16[2,64,512]{2,1,0:T(8,128)(2,1)S(1)} collective-permute-done((bf16[2,64,512]{2,1,0:T(8,128)(2,1)S(1)}, bf16[2,64,512]{2,1,0:T(8,128)(2,1)S(1)}, u32[]{:S(2)}, u32[]{:S(2)}) %collective-permute-start.13) | collective-permute-done | bytes 131104 | tf_op jit(solution)/shard_map/ppermute | solution.py:231
  45.2 3.6 %shard_map.95 = (bf16[64,3584]{1,0:T(8,128)(2,1)}, bf16[64,3584]{1,0:T(8,128)(2,1)}) custom-call(s32[3]{0:T(128)S(1)} %pad_add_fusion.ids, bf16[2,64,512]{2,1,0:T(8,128)(2,1)S(1)} %collective-permute-done.13.refs_0_, bf16[2,64,512]{2,1,0:T(8,128)(2,1)S(1)} %collective-permute-done.14.refs_1_, bf16[512,1792]{1,0:T(8,128)(2,1)S(1)} %copy-done, ...), custom_call_target="tpu_custom_call" | custom-call | flops 939524096 | bytes 8519680 | tf_op jit(solution)/shard_map/pallas_call | solution.py:34
  48.7 1.5 %collective-permute-start.15 = (bf16[64,3584]{1,0:T(8,128)(2,1)}, bf16[64,3584]{1,0:T(8,128)(2,1)S(1)}, u32[]{:S(2)}, u32[]{:S(2)}) collective-permute-start(bf16[64,3584]{1,0:T(8,128)(2,1)} %get-tuple-element.36.refs_6_), channel_id=1, source_target_pairs={{0,8},{4,12},{8,0},{12,4},{16,24},{20,28},{24,16},{28,20},{1,9},{5... | collective-permute-start | bytes 1376264 | tf_op jit(solution)/shard_map/ppermute | solution.py:231
  50.2 0.7 collective-permute-start.16
  51.0 3.5 %shard_map.96 = (bf16[64,3584]{1,0:T(8,128)(2,1)}, bf16[64,3584]{1,0:T(8,128)(2,1)S(1)}) custom-call(s32[3]{0:T(128)S(1)} %pad_add_fusion.ids, bf16[2,64,512]{2,1,0:T(8,128)(2,1)S(1)} %collective-permute-done.12.refs_0_, bf16[2,64,512]{2,1,0:T(8,128)(2,1)S(1)} %get-tuple-element.33.refs_1_, bf16[512,1792]{1,0:T(8,128)(2,1)S(1)} %copy-done, ...), custom_call_target="tpu_custom_call" | custom-call | flops 939524096 | bytes 8519680 | tf_op jit(solution)/shard_map/pallas_call | solution.py:34
  54.4 0.8 copy-done.6
  55.2 1.3 %collective-permute-start.17 = (bf16[64,3584]{1,0:T(8,128)(2,1)}, bf16[64,3584]{1,0:T(8,128)(2,1)S(1)}, u32[]{:S(2)}, u32[]{:S(2)}) collective-permute-start(bf16[64,3584]{1,0:T(8,128)(2,1)} %get-tuple-element.39), channel_id=1, source_target_pairs={{0,24},{4,28},{8,16},{12,20},{16,8},{20,12},{24,0},{28,4},{1,25},{... | collective-permute-start | bytes 1376264 | tf_op jit(solution)/shard_map/ppermute | solution.py:231
  56.6 2.1 %shard_map.97.refs_5_.refs_6_ = bf16[192,320]{1,0:T(8,128)(2,1)S(1)} custom-call(s32[3]{0:T(128)S(1)} %pad_add_fusion.ids, s32[192,1]{1,0:T(8,128)S(1)} %copy.10.refs_0_, bf16[192,1280]{1,0:T(8,128)(2,1)S(1)} %copy-done.4, bf16[32,1280]{1,0:T(8,128)(2,1)S(1)} %pad.4.refs_2_), custom_call_target="tpu_custom_call" | custom-call | bytes 697088 | tf_op jit(solution)/shard_map/pallas_call | solution.py:34
  58.7 2.5 %collective-permute-done.15.refs_2_ = bf16[64,3584]{1,0:T(8,128)(2,1)S(1)} collective-permute-done((bf16[64,3584]{1,0:T(8,128)(2,1)}, bf16[64,3584]{1,0:T(8,128)(2,1)S(1)}, u32[]{:S(2)}, u32[]{:S(2)}) %collective-permute-start.15) | collective-permute-done | bytes 458784 | tf_op jit(solution)/shard_map/ppermute | solution.py:231
  61.2 7.6 %collective-permute-done.16.refs_3_ = bf16[64,3584]{1,0:T(8,128)(2,1)S(1)} collective-permute-done((bf16[64,3584]{1,0:T(8,128)(2,1)}, bf16[64,3584]{1,0:T(8,128)(2,1)S(1)}, u32[]{:S(2)}, u32[]{:S(2)}) %collective-permute-start.16) | collective-permute-done | bytes 458784 | tf_op jit(solution)/shard_map/ppermute | solution.py:231
  68.7 1.0 copy-done.7
  69.8 1.0 shard_map.98.refs_0_
  70.8 0.6 collective-permute-start.19
  71.4 1.0 collective-permute-start.20
  72.3 2.0 %collective-permute-start.21 = (bf16[64,1792]{1,0:T(8,128)(2,1)S(1)}, bf16[64,1792]{1,0:T(8,128)(2,1)S(1)}, u32[]{:S(2)}, u32[]{:S(2)}) collective-permute-start(bf16[64,1792]{1,0:T(8,128)(2,1)S(1)} %shard_map.98.refs_0_), channel_id=1, source_target_pairs={{0,24},{4,28},{8,16},{12,20},{16,8},{20,12},{24,0},{28,4},{1,25},{... | collective-permute-start | bytes 688136 | tf_op jit(solution)/shard_map/ppermute | solution.py:231
  74.4 2.5 %collective-permute-done.19.refs_0_ = bf16[64,1792]{1,0:T(8,128)(2,1)S(1)} collective-permute-done((bf16[64,1792]{1,0:T(8,128)(2,1)S(1)}, bf16[64,1792]{1,0:T(8,128)(2,1)S(1)}, u32[]{:S(2)}, u32[]{:S(2)}) %collective-permute-start.19) | collective-permute-done | bytes 229408 | tf_op jit(solution)/shard_map/ppermute | solution.py:231
  76.9 3.0 %collective-permute-done.20.refs_1_ = bf16[64,1792]{1,0:T(8,128)(2,1)S(1)} collective-permute-done((bf16[64,1792]{1,0:T(8,128)(2,1)S(1)}, bf16[64,1792]{1,0:T(8,128)(2,1)S(1)}, u32[]{:S(2)}, u32[]{:S(2)}) %collective-permute-start.20) | collective-permute-done | bytes 229408 | tf_op jit(solution)/shard_map/ppermute | solution.py:231
  79.9 2.9 %shard_map.100 = (bf16[2,64,512]{2,1,0:T(8,128)(2,1)S(1)}, bf16[2,64,512]{2,1,0:T(8,128)(2,1)S(1)}, bf16[2,64,512]{2,1,0:T(8,128)(2,1)S(1)}) custom-call(s32[3]{0:T(128)S(1)} %pad_add_fusion.ids, bf16[64,1792]{1,0:T(8,128)(2,1)S(1)} %collective-permute-done.19.refs_0_, bf16[64,1792]{1,0:T(8,128)(2,1)S(1)} %collective-permute-done.20.refs_1_, ...), custom_call_target="tpu_custom_call" | custom-call | flops 704643072 | bytes 4751360 | tf_op jit(solution)/shard_map/pallas_call | solution.py:34
  82.8 1.6 %collective-permute-start.22 = (bf16[2,64,512]{2,1,0:T(8,128)(2,1)S(1)}, bf16[2,64,512]{2,1,0:T(8,128)(2,1)S(1)}, u32[]{:S(2)}, u32[]{:S(2)}) collective-permute-start(bf16[2,64,512]{2,1,0:T(8,128)(2,1)S(1)} %get-tuple-element.41), channel_id=1, source_target_pairs={{0,8},{4,12},{8,0},{12,4},{16,24},{20,28},{24,16},{28,20},{1,9},{5... | collective-permute-start | bytes 393224 | tf_op jit(solution)/shard_map/ppermute | solution.py:231
  84.4 0.8 collective-permute-start.23
  85.2 1.2 collective-permute-start.24
  86.4 2.8 %shard_map.99.refs_0_ = bf16[2,64,512]{2,1,0:T(8,128)(2,1)S(1)} custom-call(s32[3]{0:T(128)S(1)} %pad_add_fusion.ids, bf16[64,1792]{1,0:T(8,128)(2,1)S(1)} %shard_map.98.refs_0_, bf16[1792,512]{1,0:T(8,128)(2,1)} %refs_3_.1, bf16[1792,512]{1,0:T(8,128)(2,1)} %collective-permute-done.18.refs_2_.refs_4_), custom_call_target="tpu_custom_call" | custom-call | flops 234881024 | bytes 4030464 | tf_op jit(solution)/shard_map/pallas_call | solution.py:34
  89.4 1.7 %collective-permute-done.24.refs_3_ = bf16[2,64,512]{2,1,0:T(8,128)(2,1)S(1)} collective-permute-done((bf16[2,64,512]{2,1,0:T(8,128)(2,1)S(1)}, bf16[2,64,512]{2,1,0:T(8,128)(2,1)S(1)}, u32[]{:S(2)}, u32[]{:S(2)}) %collective-permute-start.24) | collective-permute-done | bytes 131104 | tf_op jit(solution)/shard_map/ppermute | solution.py:231
  91.0 0.6 shard_map.101
  91.6 2.6 %collective-permute-start.25 = (bf16[64,1024]{1,0:T(8,128)(2,1)S(1)}, bf16[64,1024]{1,0:T(8,128)(2,1)S(1)}, u32[]{:S(2)}, u32[]{:S(2)}) collective-permute-start(bf16[64,1024]{1,0:T(8,128)(2,1)S(1)} %get-tuple-element.45), channel_id=1, source_target_pairs={{0,1},{1,0},{2,3},{3,2},{4,5},{5,4},{6,7},{7,6},{8,9},{9,8},{10,11... | collective-permute-start | bytes 393224 | tf_op jit(solution)/shard_map/ppermute | solution.py:234
  94.2 1.0 collective-permute-start.26
  95.2 1.5 %collective-permute-start.27 = (bf16[64,1024]{1,0:T(8,128)(2,1)S(1)}, bf16[64,1024]{1,0:T(8,128)(2,1)S(1)}, u32[]{:S(2)}, u32[]{:S(2)}) collective-permute-start(bf16[64,1024]{1,0:T(8,128)(2,1)S(1)} %get-tuple-element.47), channel_id=1, source_target_pairs={{0,3},{1,2},{2,1},{3,0},{4,7},{5,6},{6,5},{7,4},{8,11},{9,10},{10,... | collective-permute-start | bytes 393224 | tf_op jit(solution)/shard_map/ppermute | solution.py:234
  97.2 6.7 %collective-permute-done.26.refs_2_ = bf16[64,1024]{1,0:T(8,128)(2,1)S(1)} collective-permute-done((bf16[64,1024]{1,0:T(8,128)(2,1)S(1)}, bf16[64,1024]{1,0:T(8,128)(2,1)S(1)}, u32[]{:S(2)}, u32[]{:S(2)}) %collective-permute-start.26) | collective-permute-done | bytes 131104 | tf_op jit(solution)/shard_map/ppermute | solution.py:234
  103.9 1.1 shard_map.102
  105.0 2.9 %collective-permute-start.28 = (bf16[16,1280]{1,0:T(8,128)(2,1)S(1)}, bf16[16,1280]{1,0:T(8,128)(2,1)S(1)}, u32[]{:S(2)}, u32[]{:S(2)}) collective-permute-start(bf16[16,1280]{1,0:T(8,128)(2,1)S(1)} %get-tuple-element.49), channel_id=1, source_target_pairs={{0,1},{1,0},{2,3},{3,2},{4,5},{5,4},{6,7},{7,6},{8,9},{9,8},{10,11... | collective-permute-start | bytes 122888 | tf_op jit(solution)/shard_map/ppermute | solution.py:234
  107.8 0.9 collective-permute-start.29
  108.8 1.5 %collective-permute-start.30 = (bf16[16,1280]{1,0:T(8,128)(2,1)S(1)}, bf16[16,1280]{1,0:T(8,128)(2,1)S(1)}, u32[]{:S(2)}, u32[]{:S(2)}) collective-permute-start(bf16[16,1280]{1,0:T(8,128)(2,1)S(1)} %get-tuple-element.51), channel_id=1, source_target_pairs={{0,3},{1,2},{2,1},{3,0},{4,7},{5,6},{6,5},{7,4},{8,11},{9,10},{10,... | collective-permute-start | bytes 122888 | tf_op jit(solution)/shard_map/ppermute | solution.py:234
  110.3 2.7 %collective-permute-done.29.refs_2_ = bf16[16,1280]{1,0:T(8,128)(2,1)S(1)} collective-permute-done((bf16[16,1280]{1,0:T(8,128)(2,1)S(1)}, bf16[16,1280]{1,0:T(8,128)(2,1)S(1)}, u32[]{:S(2)}, u32[]{:S(2)}) %collective-permute-start.29) | collective-permute-done | bytes 40992 | tf_op jit(solution)/shard_map/ppermute | solution.py:234
  113.0 1.6 %collective-permute-done.30.refs_3_ = bf16[16,1280]{1,0:T(8,128)(2,1)S(1)} collective-permute-done((bf16[16,1280]{1,0:T(8,128)(2,1)S(1)}, bf16[16,1280]{1,0:T(8,128)(2,1)S(1)}, u32[]{:S(2)}, u32[]{:S(2)}) %collective-permute-start.30) | collective-permute-done | bytes 40992 | tf_op jit(solution)/shard_map/ppermute | solution.py:234
  115.2 0.8 collective-permute-start.31
  116.0 0.9 collective-permute-start.32
  116.9 1.8 %collective-permute-start.33 = (bf16[16,1280]{1,0:T(8,128)(2,1)S(1)}, bf16[16,1280]{1,0:T(8,128)(2,1)S(1)}, u32[]{:S(2)}, u32[]{:S(2)}) collective-permute-start(bf16[16,1280]{1,0:T(8,128)(2,1)S(1)} %shard_map.103.refs_0_), channel_id=1, source_target_pairs={{0,24},{4,28},{8,16},{12,20},{16,8},{20,12},{24,0},{28,4},{1,25},{... | collective-permute-start | bytes 122888 | tf_op jit(solution)/shard_map/ppermute | solution.py:231
  119.2 0.8 collective-permute-done.32.refs_2_
  120.0 1.8 %collective-permute-done.33.refs_3_ = bf16[16,1280]{1,0:T(8,128)(2,1)S(1)} collective-permute-done((bf16[16,1280]{1,0:T(8,128)(2,1)S(1)}, bf16[16,1280]{1,0:T(8,128)(2,1)S(1)}, u32[]{:S(2)}, u32[]{:S(2)}) %collective-permute-start.33) | collective-permute-done | bytes 40992 | tf_op jit(solution)/shard_map/ppermute | solution.py:231
  121.9 1.4 %collective-permute-done.34.refs_4_ = bf16[4,16,1280]{2,1,0:T(8,128)(2,1)S(1)} collective-permute-done((bf16[4,16,1280]{2,1,0:T(8,128)(2,1)S(1)}, bf16[4,16,1280]{2,1,0:T(8,128)(2,1)S(1)}, u32[]{:S(2)}, u32[]{:S(2)}) %collective-permute-start.34) | collective-permute-done | bytes 163872 | tf_op jit(solution)/shard_map/ppermute | solution.py:228
  123.3 1.8 %shard_map.104 = bf16[192,1280]{1,0:T(8,128)(2,1)} custom-call(s32[3]{0:T(128)S(1)} %pad_add_fusion.ids, bf16[16,1280]{1,0:T(8,128)(2,1)S(1)} %shard_map.103.refs_0_, bf16[16,1280]{1,0:T(8,128)(2,1)S(1)} %collective-permute-done.31.refs_1_, bf16[16,1280]{1,0:T(8,128)(2,1)S(1)} %collective-permute-done.32.refs_2_, ...), custom_call_target="tpu_custom_call" | custom-call | bytes 1437696 | tf_op jit(solution)/shard_map/pallas_call | solution.py:34
  (47 shorter events, 3.7 us)
Async XLA Ops:
  0.0 14.6 %collective-permute-start.4 = (bf16[512,1792]{1,0:T(8,128)(2,1)}, bf16[512,1792]{1,0:T(8,128)(2,1)S(1)}, u32[]{:S(2)}, u32[]{:S(2)}) collective-permute-start(bf16[512,1792]{1,0:T(8,128)(2,1)} %refs_2_.3), channel_id=1, source_target_pairs={{0,4},{4,0},{8,12},{12,8},{16,20},{20,16},{24,28},{28,24},{1,5},{5... | collective-permute-start | bytes 5505032 | tf_op jit(solution)/shard_map/ppermute | solution.py:228
  0.5 14.2 %collective-permute-start.5 = (bf16[512,1792]{1,0:T(8,128)(2,1)}, bf16[512,1792]{1,0:T(8,128)(2,1)}, u32[]{:S(2)}, u32[]{:S(2)}) collective-permute-start(bf16[512,1792]{1,0:T(8,128)(2,1)} %refs_4_.5), channel_id=1, source_target_pairs={{0,4},{4,0},{8,12},{12,8},{16,20},{20,16},{24,28},{28,24},{1,5},{5... | collective-permute-start | bytes 5505032 | tf_op jit(solution)/shard_map/ppermute | solution.py:228
  0.6 1.0 copy-start.5
  1.6 0.7 copy-start.8
  3.1 5.6 %collective-permute-start = (bf16[32,1280]{1,0:T(8,128)(2,1)S(1)}, bf16[32,1280]{1,0:T(8,128)(2,1)S(1)}, u32[]{:S(2)}, u32[]{:S(2)}) collective-permute-start(bf16[32,1280]{1,0:T(8,128)(2,1)S(1)} %shard_map.91.refs_0_), channel_id=1, source_target_pairs={{0,8},{4,12},{8,0},{12,4},{16,24},{20,28},{24,16},{28,20},{1,9},{5... | collective-permute-start | bytes 245768 | tf_op jit(solution)/shard_map/ppermute | solution.py:231
  6.0 4.4 %collective-permute-start.1 = (bf16[32,1280]{1,0:T(8,128)(2,1)S(1)}, bf16[32,1280]{1,0:T(8,128)(2,1)S(1)}, u32[]{:S(2)}, u32[]{:S(2)}) collective-permute-start(bf16[32,1280]{1,0:T(8,128)(2,1)S(1)} %shard_map.91.refs_0_), channel_id=1, source_target_pairs={{0,16},{4,20},{8,24},{12,28},{16,0},{20,4},{24,8},{28,12},{1,17},{... | collective-permute-start | bytes 245768 | tf_op jit(solution)/shard_map/ppermute | solution.py:231
  7.6 5.3 %collective-permute-start.2 = (bf16[32,1280]{1,0:T(8,128)(2,1)S(1)}, bf16[32,1280]{1,0:T(8,128)(2,1)S(1)}, u32[]{:S(2)}, u32[]{:S(2)}) collective-permute-start(bf16[32,1280]{1,0:T(8,128)(2,1)S(1)} %shard_map.91.refs_0_), channel_id=1, source_target_pairs={{0,24},{4,28},{8,16},{12,20},{16,8},{20,12},{24,0},{28,4},{1,25},{... | collective-permute-start | bytes 245768 | tf_op jit(solution)/shard_map/ppermute | solution.py:231
  12.9 12.7 %copy-start.2 = (bf16[1280,1024]{1,0:T(8,128)(2,1)S(1)}, bf16[1280,1024]{1,0:T(8,128)(2,1)}, u32[]{:S(2)}) copy-start(bf16[1280,1024]{1,0:T(8,128)(2,1)} %refs_4_.3) | copy-start | bytes 7864324
  12.9 1.7 %collective-permute-start.3 = (bf16[128,1280]{1,0:T(8,128)(2,1)S(1)}, bf16[128,1280]{1,0:T(8,128)(2,1)S(1)}, u32[]{:S(2)}, u32[]{:S(2)}) collective-permute-start(bf16[128,1280]{1,0:T(8,128)(2,1)S(1)} %pad_maximum_fusion), channel_id=1, source_target_pairs={{0,4},{4,0},{8,12},{12,8},{16,20},{20,16},{24,28},{28,24},{1,5},{5... | collective-permute-start | bytes 983048 | tf_op jit(solution)/shard_map/ppermute | solution.py:228
  14.6 30.5 %copy-start.1 = (bf16[512,1792]{1,0:T(8,128)(2,1)S(1)}, bf16[512,1792]{1,0:T(8,128)(2,1)}, u32[]{:S(2)}) copy-start(bf16[512,1792]{1,0:T(8,128)(2,1)} %refs_4_.5) | copy-start | bytes 5505028
  15.4 29.8 %copy-start = (bf16[512,1792]{1,0:T(8,128)(2,1)S(1)}, bf16[512,1792]{1,0:T(8,128)(2,1)}, u32[]{:S(2)}) copy-start(bf16[512,1792]{1,0:T(8,128)(2,1)} %refs_2_.3) | copy-start | bytes 5505028
  15.4 64.5 %collective-permute-start.18 = (bf16[1792,512]{1,0:T(8,128)(2,1)}, bf16[1792,512]{1,0:T(8,128)(2,1)}, u32[]{:S(2)}, u32[]{:S(2)}) collective-permute-start(bf16[1792,512]{1,0:T(8,128)(2,1)} %refs_3_.1), channel_id=1, source_target_pairs={{0,4},{4,0},{8,12},{12,8},{16,20},{20,16},{24,28},{28,24},{1,5},{5... | collective-permute-start | bytes 5505032 | tf_op jit(solution)/shard_map/ppermute | solution.py:228
  15.6 4.4 %collective-permute-start.6 = (bf16[16,1280]{1,0:T(8,128)(2,1)S(1)}, bf16[16,1280]{1,0:T(8,128)(2,1)S(1)}, u32[]{:S(2)}, u32[]{:S(2)}) collective-permute-start(bf16[16,1280]{1,0:T(8,128)(2,1)S(1)} %get-tuple-element.30.refs_0_), channel_id=1, source_target_pairs={{0,1},{1,0},{2,3},{3,2},{4,5},{5,4},{6,7},{7,6},{8,9},{9,8},{10,11... | collective-permute-start | bytes 122888 | tf_op jit(solution)/shard_map/ppermute | solution.py:234
  17.2 5.7 %collective-permute-start.7 = (bf16[16,1280]{1,0:T(8,128)(2,1)S(1)}, bf16[16,1280]{1,0:T(8,128)(2,1)S(1)}, u32[]{:S(2)}, u32[]{:S(2)}) collective-permute-start(bf16[16,1280]{1,0:T(8,128)(2,1)S(1)} %get-tuple-element.30.refs_0_), channel_id=1, source_target_pairs={{0,2},{1,3},{2,0},{3,1},{4,6},{5,7},{6,4},{7,5},{8,10},{9,11},{10,... | collective-permute-start | bytes 122888 | tf_op jit(solution)/shard_map/ppermute | solution.py:234
  19.8 5.8 %collective-permute-start.8 = (bf16[16,1280]{1,0:T(8,128)(2,1)S(1)}, bf16[16,1280]{1,0:T(8,128)(2,1)S(1)}, u32[]{:S(2)}, u32[]{:S(2)}) collective-permute-start(bf16[16,1280]{1,0:T(8,128)(2,1)S(1)} %get-tuple-element.30.refs_0_), channel_id=1, source_target_pairs={{0,3},{1,2},{2,1},{3,0},{4,7},{5,6},{6,5},{7,4},{8,11},{9,10},{10,... | collective-permute-start | bytes 122888 | tf_op jit(solution)/shard_map/ppermute | solution.py:234
  26.7 5.8 %collective-permute-start.9 = (bf16[64,1024]{1,0:T(8,128)(2,1)S(1)}, bf16[64,1024]{1,0:T(8,128)(2,1)S(1)}, u32[]{:S(2)}, u32[]{:S(2)}) collective-permute-start(bf16[64,1024]{1,0:T(8,128)(2,1)S(1)} %shard_map.93.refs_0_.refs_4_), channel_id=1, source_target_pairs={{0,1},{1,0},{2,3},{3,2},{4,5},{5,4},{6,7},{7,6},{8,9},{9,8},{10,11... | collective-permute-start | bytes 393224 | tf_op jit(solution)/shard_map/ppermute | solution.py:234
  26.8 12.1 %collective-permute-start.10 = (bf16[64,1024]{1,0:T(8,128)(2,1)S(1)}, bf16[64,1024]{1,0:T(8,128)(2,1)S(1)}, u32[]{:S(2)}, u32[]{:S(2)}) collective-permute-start(bf16[64,1024]{1,0:T(8,128)(2,1)S(1)} %shard_map.93.refs_0_.refs_4_), channel_id=1, source_target_pairs={{0,2},{1,3},{2,0},{3,1},{4,6},{5,7},{6,4},{7,5},{8,10},{9,11},{10,... | collective-permute-start | bytes 393224 | tf_op jit(solution)/shard_map/ppermute | solution.py:234
  28.1 10.8 %collective-permute-start.11 = (bf16[64,1024]{1,0:T(8,128)(2,1)S(1)}, bf16[64,1024]{1,0:T(8,128)(2,1)S(1)}, u32[]{:S(2)}, u32[]{:S(2)}) collective-permute-start(bf16[64,1024]{1,0:T(8,128)(2,1)S(1)} %shard_map.93.refs_0_.refs_4_), channel_id=1, source_target_pairs={{0,3},{1,2},{2,1},{3,0},{4,7},{5,6},{6,5},{7,4},{8,11},{9,10},{10,... | collective-permute-start | bytes 393224 | tf_op jit(solution)/shard_map/ppermute | solution.py:234
  39.6 5.0 %collective-permute-start.13 = (bf16[2,64,512]{2,1,0:T(8,128)(2,1)S(1)}, bf16[2,64,512]{2,1,0:T(8,128)(2,1)S(1)}, u32[]{:S(2)}, u32[]{:S(2)}) collective-permute-start(bf16[2,64,512]{2,1,0:T(8,128)(2,1)S(1)} %get-tuple-element.34), channel_id=1, source_target_pairs={{0,8},{4,12},{8,0},{12,4},{16,24},{20,28},{24,16},{28,20},{1,9},{5... | collective-permute-start | bytes 393224 | tf_op jit(solution)/shard_map/ppermute | solution.py:231
  40.2 5.0 %collective-permute-start.14 = (bf16[2,64,512]{2,1,0:T(8,128)(2,1)S(1)}, bf16[2,64,512]{2,1,0:T(8,128)(2,1)S(1)}, u32[]{:S(2)}, u32[]{:S(2)}) collective-permute-start(bf16[2,64,512]{2,1,0:T(8,128)(2,1)S(1)} %get-tuple-element.35), channel_id=1, source_target_pairs={{0,16},{4,20},{8,24},{12,28},{16,0},{20,4},{24,8},{28,12},{1,17},{... | collective-permute-start | bytes 393224 | tf_op jit(solution)/shard_map/ppermute | solution.py:231
  41.0 10.0 %collective-permute-start.12 = (bf16[2,64,512]{2,1,0:T(8,128)(2,1)S(1)}, bf16[2,64,512]{2,1,0:T(8,128)(2,1)S(1)}, u32[]{:S(2)}, u32[]{:S(2)}) collective-permute-start(bf16[2,64,512]{2,1,0:T(8,128)(2,1)S(1)} %get-tuple-element.32), channel_id=1, source_target_pairs={{0,24},{4,28},{8,16},{12,20},{16,8},{20,12},{24,0},{28,4},{1,25},{... | collective-permute-start | bytes 393224 | tf_op jit(solution)/shard_map/ppermute | solution.py:231
  48.7 12.4 %collective-permute-start.15 = (bf16[64,3584]{1,0:T(8,128)(2,1)}, bf16[64,3584]{1,0:T(8,128)(2,1)S(1)}, u32[]{:S(2)}, u32[]{:S(2)}) collective-permute-start(bf16[64,3584]{1,0:T(8,128)(2,1)} %get-tuple-element.36.refs_6_), channel_id=1, source_target_pairs={{0,8},{4,12},{8,0},{12,4},{16,24},{20,28},{24,16},{28,20},{1,9},{5... | collective-permute-start | bytes 1376264 | tf_op jit(solution)/shard_map/ppermute | solution.py:231
  50.2 18.5 %collective-permute-start.16 = (bf16[64,3584]{1,0:T(8,128)(2,1)}, bf16[64,3584]{1,0:T(8,128)(2,1)S(1)}, u32[]{:S(2)}, u32[]{:S(2)}) collective-permute-start(bf16[64,3584]{1,0:T(8,128)(2,1)} %get-tuple-element.38), channel_id=1, source_target_pairs={{0,16},{4,20},{8,24},{12,28},{16,0},{20,4},{24,8},{28,12},{1,17},{... | collective-permute-start | bytes 1376264 | tf_op jit(solution)/shard_map/ppermute | solution.py:231
  51.0 5.5 %copy-start.9 = (s32[192]{0:T(256)S(1)}, s32[192]{0:T(256)}, u32[]{:S(2)}) copy-start(s32[192]{0:T(256)} %param.11) | copy-start | bytes 2308
  51.0 5.6 %copy-start.10 = (bf16[31,1280]{1,0:T(8,128)(2,1)S(1)}, bf16[31,1280]{1,0:T(8,128)(2,1)}, u32[]{:S(2)}) copy-start(bf16[31,1280]{1,0:T(8,128)(2,1)} %param.12) | copy-start | bytes 238084
  51.0 5.7 %copy-start.4 = (bf16[192,1280]{1,0:T(8,128)(2,1)S(1)}, bf16[192,1280]{1,0:T(8,128)(2,1)}, u32[]{:S(2)}) copy-start(bf16[192,1280]{1,0:T(8,128)(2,1)} %refs_7_.1) | copy-start | bytes 1474564
  54.4 0.8 copy-start.6
  55.2 13.5 %collective-permute-start.17 = (bf16[64,3584]{1,0:T(8,128)(2,1)}, bf16[64,3584]{1,0:T(8,128)(2,1)S(1)}, u32[]{:S(2)}, u32[]{:S(2)}) collective-permute-start(bf16[64,3584]{1,0:T(8,128)(2,1)} %get-tuple-element.39), channel_id=1, source_target_pairs={{0,24},{4,28},{8,16},{12,20},{16,8},{20,12},{24,0},{28,4},{1,25},{... | collective-permute-start | bytes 1376264 | tf_op jit(solution)/shard_map/ppermute | solution.py:231
  68.7 1.0 copy-start.7
  70.8 6.1 %collective-permute-start.19 = (bf16[64,1792]{1,0:T(8,128)(2,1)S(1)}, bf16[64,1792]{1,0:T(8,128)(2,1)S(1)}, u32[]{:S(2)}, u32[]{:S(2)}) collective-permute-start(bf16[64,1792]{1,0:T(8,128)(2,1)S(1)} %shard_map.98.refs_0_), channel_id=1, source_target_pairs={{0,8},{4,12},{8,0},{12,4},{16,24},{20,28},{24,16},{28,20},{1,9},{5... | collective-permute-start | bytes 688136 | tf_op jit(solution)/shard_map/ppermute | solution.py:231
  71.4 8.5 %collective-permute-start.20 = (bf16[64,1792]{1,0:T(8,128)(2,1)S(1)}, bf16[64,1792]{1,0:T(8,128)(2,1)S(1)}, u32[]{:S(2)}, u32[]{:S(2)}) collective-permute-start(bf16[64,1792]{1,0:T(8,128)(2,1)S(1)} %shard_map.98.refs_0_), channel_id=1, source_target_pairs={{0,16},{4,20},{8,24},{12,28},{16,0},{20,4},{24,8},{28,12},{1,17},{... | collective-permute-start | bytes 688136 | tf_op jit(solution)/shard_map/ppermute | solution.py:231
  72.3 7.5 %collective-permute-start.21 = (bf16[64,1792]{1,0:T(8,128)(2,1)S(1)}, bf16[64,1792]{1,0:T(8,128)(2,1)S(1)}, u32[]{:S(2)}, u32[]{:S(2)}) collective-permute-start(bf16[64,1792]{1,0:T(8,128)(2,1)S(1)} %shard_map.98.refs_0_), channel_id=1, source_target_pairs={{0,24},{4,28},{8,16},{12,20},{16,8},{20,12},{24,0},{28,4},{1,25},{... | collective-permute-start | bytes 688136 | tf_op jit(solution)/shard_map/ppermute | solution.py:231
  82.8 6.4 %collective-permute-start.22 = (bf16[2,64,512]{2,1,0:T(8,128)(2,1)S(1)}, bf16[2,64,512]{2,1,0:T(8,128)(2,1)S(1)}, u32[]{:S(2)}, u32[]{:S(2)}) collective-permute-start(bf16[2,64,512]{2,1,0:T(8,128)(2,1)S(1)} %get-tuple-element.41), channel_id=1, source_target_pairs={{0,8},{4,12},{8,0},{12,4},{16,24},{20,28},{24,16},{28,20},{1,9},{5... | collective-permute-start | bytes 393224 | tf_op jit(solution)/shard_map/ppermute | solution.py:231
  84.4 5.0 %collective-permute-start.23 = (bf16[2,64,512]{2,1,0:T(8,128)(2,1)S(1)}, bf16[2,64,512]{2,1,0:T(8,128)(2,1)S(1)}, u32[]{:S(2)}, u32[]{:S(2)}) collective-permute-start(bf16[2,64,512]{2,1,0:T(8,128)(2,1)S(1)} %get-tuple-element.42), channel_id=1, source_target_pairs={{0,16},{4,20},{8,24},{12,28},{16,0},{20,4},{24,8},{28,12},{1,17},{... | collective-permute-start | bytes 393224 | tf_op jit(solution)/shard_map/ppermute | solution.py:231
  85.2 18.7 %copy-start.3 = (bf16[1024,1280]{1,0:T(8,128)(2,1)S(1)}, bf16[1024,1280]{1,0:T(8,128)(2,1)}, u32[]{:S(2)}) copy-start(bf16[1024,1280]{1,0:T(8,128)(2,1)} %refs_5_.1) | copy-start | bytes 7864324
  85.2 5.9 %collective-permute-start.24 = (bf16[2,64,512]{2,1,0:T(8,128)(2,1)S(1)}, bf16[2,64,512]{2,1,0:T(8,128)(2,1)S(1)}, u32[]{:S(2)}, u32[]{:S(2)}) collective-permute-start(bf16[2,64,512]{2,1,0:T(8,128)(2,1)S(1)} %get-tuple-element.43), channel_id=1, source_target_pairs={{0,24},{4,28},{8,16},{12,20},{16,8},{20,12},{24,0},{28,4},{1,25},{... | collective-permute-start | bytes 393224 | tf_op jit(solution)/shard_map/ppermute | solution.py:231
  91.6 5.6 %collective-permute-start.25 = (bf16[64,1024]{1,0:T(8,128)(2,1)S(1)}, bf16[64,1024]{1,0:T(8,128)(2,1)S(1)}, u32[]{:S(2)}, u32[]{:S(2)}) collective-permute-start(bf16[64,1024]{1,0:T(8,128)(2,1)S(1)} %get-tuple-element.45), channel_id=1, source_target_pairs={{0,1},{1,0},{2,3},{3,2},{4,5},{5,4},{6,7},{7,6},{8,9},{9,8},{10,11... | collective-permute-start | bytes 393224 | tf_op jit(solution)/shard_map/ppermute | solution.py:234
  94.2 9.6 %collective-permute-start.26 = (bf16[64,1024]{1,0:T(8,128)(2,1)S(1)}, bf16[64,1024]{1,0:T(8,128)(2,1)S(1)}, u32[]{:S(2)}, u32[]{:S(2)}) collective-permute-start(bf16[64,1024]{1,0:T(8,128)(2,1)S(1)} %get-tuple-element.46), channel_id=1, source_target_pairs={{0,2},{1,3},{2,0},{3,1},{4,6},{5,7},{6,4},{7,5},{8,10},{9,11},{10,... | collective-permute-start | bytes 393224 | tf_op jit(solution)/shard_map/ppermute | solution.py:234
  95.2 8.6 %collective-permute-start.27 = (bf16[64,1024]{1,0:T(8,128)(2,1)S(1)}, bf16[64,1024]{1,0:T(8,128)(2,1)S(1)}, u32[]{:S(2)}, u32[]{:S(2)}) collective-permute-start(bf16[64,1024]{1,0:T(8,128)(2,1)S(1)} %get-tuple-element.47), channel_id=1, source_target_pairs={{0,3},{1,2},{2,1},{3,0},{4,7},{5,6},{6,5},{7,4},{8,11},{9,10},{10,... | collective-permute-start | bytes 393224 | tf_op jit(solution)/shard_map/ppermute | solution.py:234
  105.0 5.3 %collective-permute-start.28 = (bf16[16,1280]{1,0:T(8,128)(2,1)S(1)}, bf16[16,1280]{1,0:T(8,128)(2,1)S(1)}, u32[]{:S(2)}, u32[]{:S(2)}) collective-permute-start(bf16[16,1280]{1,0:T(8,128)(2,1)S(1)} %get-tuple-element.49), channel_id=1, source_target_pairs={{0,1},{1,0},{2,3},{3,2},{4,5},{5,4},{6,7},{7,6},{8,9},{9,8},{10,11... | collective-permute-start | bytes 122888 | tf_op jit(solution)/shard_map/ppermute | solution.py:234
  107.8 5.2 %collective-permute-start.29 = (bf16[16,1280]{1,0:T(8,128)(2,1)S(1)}, bf16[16,1280]{1,0:T(8,128)(2,1)S(1)}, u32[]{:S(2)}, u32[]{:S(2)}) collective-permute-start(bf16[16,1280]{1,0:T(8,128)(2,1)S(1)} %get-tuple-element.50), channel_id=1, source_target_pairs={{0,2},{1,3},{2,0},{3,1},{4,6},{5,7},{6,4},{7,5},{8,10},{9,11},{10,... | collective-permute-start | bytes 122888 | tf_op jit(solution)/shard_map/ppermute | solution.py:234
  108.8 5.8 %collective-permute-start.30 = (bf16[16,1280]{1,0:T(8,128)(2,1)S(1)}, bf16[16,1280]{1,0:T(8,128)(2,1)S(1)}, u32[]{:S(2)}, u32[]{:S(2)}) collective-permute-start(bf16[16,1280]{1,0:T(8,128)(2,1)S(1)} %get-tuple-element.51), channel_id=1, source_target_pairs={{0,3},{1,2},{2,1},{3,0},{4,7},{5,6},{6,5},{7,4},{8,11},{9,10},{10,... | collective-permute-start | bytes 122888 | tf_op jit(solution)/shard_map/ppermute | solution.py:234
  115.2 4.1 %collective-permute-start.31 = (bf16[16,1280]{1,0:T(8,128)(2,1)S(1)}, bf16[16,1280]{1,0:T(8,128)(2,1)S(1)}, u32[]{:S(2)}, u32[]{:S(2)}) collective-permute-start(bf16[16,1280]{1,0:T(8,128)(2,1)S(1)} %shard_map.103.refs_0_), channel_id=1, source_target_pairs={{0,8},{4,12},{8,0},{12,4},{16,24},{20,28},{24,16},{28,20},{1,9},{5... | collective-permute-start | bytes 122888 | tf_op jit(solution)/shard_map/ppermute | solution.py:231
  116.0 4.0 %collective-permute-start.32 = (bf16[16,1280]{1,0:T(8,128)(2,1)S(1)}, bf16[16,1280]{1,0:T(8,128)(2,1)S(1)}, u32[]{:S(2)}, u32[]{:S(2)}) collective-permute-start(bf16[16,1280]{1,0:T(8,128)(2,1)S(1)} %shard_map.103.refs_0_), channel_id=1, source_target_pairs={{0,16},{4,20},{8,24},{12,28},{16,0},{20,4},{24,8},{28,12},{1,17},{... | collective-permute-start | bytes 122888 | tf_op jit(solution)/shard_map/ppermute | solution.py:231
  116.9 4.9 %collective-permute-start.33 = (bf16[16,1280]{1,0:T(8,128)(2,1)S(1)}, bf16[16,1280]{1,0:T(8,128)(2,1)S(1)}, u32[]{:S(2)}, u32[]{:S(2)}) collective-permute-start(bf16[16,1280]{1,0:T(8,128)(2,1)S(1)} %shard_map.103.refs_0_), channel_id=1, source_target_pairs={{0,24},{4,28},{8,16},{12,20},{16,8},{20,12},{24,0},{28,4},{1,25},{... | collective-permute-start | bytes 122888 | tf_op jit(solution)/shard_map/ppermute | solution.py:231
  121.8 1.5 %collective-permute-start.34 = (bf16[4,16,1280]{2,1,0:T(8,128)(2,1)S(1)}, bf16[4,16,1280]{2,1,0:T(8,128)(2,1)S(1)}, u32[]{:S(2)}, u32[]{:S(2)}) collective-permute-start(bf16[4,16,1280]{2,1,0:T(8,128)(2,1)S(1)} %pad_maximum_fusion.1), channel_id=1, source_target_pairs={{0,4},{4,0},{8,12},{12,8},{16,20},{20,16},{24,28},{28,24},{1,5},{5... | collective-permute-start | bytes 491528 | tf_op jit(solution)/shard_map/ppermute | solution.py:228

commit v5 on v4

--- a/solution.py
+++ b/solution.py
@@ -87,6 +87,10 @@
     start_out[...] = jnp.broadcast_to(own[:, 0:HD].astype(jnp.int32), start_out.shape)
 
 
+def away(k, core, groups):
+    return jnp.where(core == 1, 3 - k, k) if k in (1, 2) and groups > 2 else k
+
+
 def x_kernel(groups, ids, *refs):
     pieces, w, out, packed = refs[:groups], refs[groups], refs[groups + 1], refs[groups + 2]
     for k in range(groups):
@@ -102,7 +106,7 @@
     per = 2 * chips // groups
     for k in range(groups):
         for u in range(per):
-            units[(z ^ k) * per + u] = pieces[k][:, u * unit : (u + 1) * unit]
+            units[(z ^ away(k, c, groups)) * per + u] = pieces[k][:, u * unit : (u + 1) * unit]
     for k in range(chips):
         for h in range(2):
             outs[k][h] = units[2 * (q ^ k) + (c ^ h)]
@@ -236,8 +240,13 @@
     def chips_of(arrays):
         return [chip(a, k + 1) for k, a in enumerate(arrays)]
 
-    def planes_of(arrays):
-        done = [plane(a, k + 1) for k, a in reversed(list(enumerate(arrays)))]
+    def plane_by_core(a, k):
+        other = 3 - k if k in (1, 2) and groups > 2 else k
+        pairs = [(i * groups + z, i * groups + (z ^ (other if i % 2 else k))) for i in range(seq) for z in range(groups)]
+        return lax.ppermute(a, ("seq", "mp"), pairs)
+
+    def planes_of(arrays, move=plane):
+        done = [move(a, k + 1) for k, a in reversed(list(enumerate(arrays)))]
         return done[::-1]
 
     [pooled] = call(
@@ -271,7 +280,7 @@
         scratch=[pltpu.VMEM((groups, ROWS, width), BF16)],
         flops=2 * rows * width * wide,
     )
-    pieces = [x] + planes_of([x] * (groups - 1))
+    pieces = [x] + planes_of([x] * (groups - 1), plane_by_core)
     *sent, scale = call(
         functools.partial(spread_kernel, groups, chips),
         [shape((2, rows, unit)) for _ in range(chips)] + [shape((rows, HD), F32)],

time: 125 us -> 123 us (0.984)
  waiting for transfers between devices: 55.5 us -> 53.2 us
    ppermute x12 -> x9, waiting for transfers between devices: 24.8 us -> 15.2 us  [plane(): return lax.ppermute(a, 'mp', [(i, i ^ k) for i in range(groups)])]
    ppermute x0 -> x3, waiting for transfers between devices: none -> 6.26 us  [plane_by_core(): return lax.ppermute(a, ('seq', 'mp'), pairs)]
    ppermute x12 -> x9, starting transfers between devices: 19.2 us -> 13.8 us  [plane(): return lax.ppermute(a, 'mp', [(i, i ^ k) for i in range(groups)])]
    ppermute x0 -> x3, starting transfers between devices: none -> 4.44 us  [plane_by_core(): return lax.ppermute(a, ('seq', 'mp'), pairs)]
    ppermute x18, starting transfers between devices: 22.2 us -> 23.5 us  [chip(): return lax.ppermute(a, 'seq', [(i, i ^ 2 * k) for i in range(seq)])]
  transfers between devices with their start and end apart: 35 -> 35, of which waited for: 24 -> 25; matrix products, arithmetic and copies ran while one was open for 0% -> 0% of each run, Pallas kernels for 12% -> 13%
where the time goes in v5:
time: 123 us
  waiting for transfers between devices  53.2 us (43%)
  starting transfers between devices  42.7 us (35%)
  Pallas kernels  23.3 us (19%)
  local copies, waits for them, and re-layouts  3.66 us (3%)
    ppermute x18, waiting for transfers between devices, chip(): return lax.ppermute(a, 'seq', [(i, i ^ 2 * k) for i in range(seq)])  28.8 us
    ppermute x18, starting transfers between devices, chip(): return lax.ppermute(a, 'seq', [(i, i ^ 2 * k) for i in range(seq)])  23.5 us
    pallas_call x14, Pallas kernels, call(): pl.pallas_call(run, out_shape=list(outs), in_specs=[SMEM] + [VMEM] * n +...  23.3 us
    ppermute x9, waiting for transfers between devices, plane(): return lax.ppermute(a, 'mp', [(i, i ^ k) for i in range(groups)])  15.2 us
    ppermute x9, starting transfers between devices, plane(): return lax.ppermute(a, 'mp', [(i, i ^ k) for i in range(groups)])  13.8 us
    ppermute x3, waiting for transfers between devices, plane_by_core(): return lax.ppermute(a, ('seq', 'mp'), pairs)  6.26 us
    ppermute x3, starting transfers between devices, plane_by_core(): return lax.ppermute(a, ('seq', 'mp'), pairs)  4.44 us
    unnamed x22, local copies, waits for them, and re-layouts  3.54 us
  transfers between devices with their start and end apart: 35, of which 25 were waited for; matrix products, arithmetic and copies ran while one was open for 0% of the time, Pallas kernels for 13%

profile of v5, /device:TPU:0, one launch (start us, length us, event | category | flops | bytes accessed | tf_op | source)
XLA Modules:
  0.0 123.2 jit_solution(17783202408955824554)
XLA Ops:
  0.6 1.0 copy-done.5
  1.6 0.7 copy-done.8
  2.3 0.8 shard_map.91.refs_0_
  3.1 3.0 %collective-permute-start = (bf16[32,1280]{1,0:T(8,128)(2,1)S(1)}, bf16[32,1280]{1,0:T(8,128)(2,1)S(1)}, u32[]{:S(2)}, u32[]{:S(2)}) collective-permute-start(bf16[32,1280]{1,0:T(8,128)(2,1)S(1)} %shard_map.91.refs_0_), channel_id=1, source_target_pairs={{0,8},{4,12},{8,0},{12,4},{16,24},{20,28},{24,16},{28,20},{1,9},{5... | collective-permute-start | bytes 245768 | tf_op jit(solution)/shard_map/ppermute | solution.py:235
  6.0 1.5 %collective-permute-start.1 = (bf16[32,1280]{1,0:T(8,128)(2,1)S(1)}, bf16[32,1280]{1,0:T(8,128)(2,1)S(1)}, u32[]{:S(2)}, u32[]{:S(2)}) collective-permute-start(bf16[32,1280]{1,0:T(8,128)(2,1)S(1)} %shard_map.91.refs_0_), channel_id=1, source_target_pairs={{0,16},{4,20},{8,24},{12,28},{16,0},{20,4},{24,8},{28,12},{1,17},{... | collective-permute-start | bytes 245768 | tf_op jit(solution)/shard_map/ppermute | solution.py:235
  7.6 1.1 collective-permute-done.refs_1_
  8.6 1.8 %collective-permute-done.1.refs_2_ = bf16[32,1280]{1,0:T(8,128)(2,1)S(1)} collective-permute-done((bf16[32,1280]{1,0:T(8,128)(2,1)S(1)}, bf16[32,1280]{1,0:T(8,128)(2,1)S(1)}, u32[]{:S(2)}, u32[]{:S(2)}) %collective-permute-start.1) | collective-permute-done | bytes 81952 | tf_op jit(solution)/shard_map/ppermute | solution.py:235
  10.5 2.4 %collective-permute-done.2.refs_3_ = bf16[32,1280]{1,0:T(8,128)(2,1)S(1)} collective-permute-done((bf16[32,1280]{1,0:T(8,128)(2,1)S(1)}, bf16[32,1280]{1,0:T(8,128)(2,1)S(1)}, u32[]{:S(2)}, u32[]{:S(2)}) %collective-permute-start.2) | collective-permute-done | bytes 81952 | tf_op jit(solution)/shard_map/ppermute | solution.py:235
  13.0 1.6 %collective-permute-done.3.refs_4_ = bf16[128,1280]{1,0:T(8,128)(2,1)S(1)} collective-permute-done((bf16[128,1280]{1,0:T(8,128)(2,1)S(1)}, bf16[128,1280]{1,0:T(8,128)(2,1)S(1)}, u32[]{:S(2)}, u32[]{:S(2)}) %collective-permute-start.3) | collective-permute-done | bytes 327712 | tf_op jit(solution)/shard_map/ppermute | solution.py:232
  14.6 0.8 shard_map.92
  15.6 1.6 %collective-permute-start.6 = (bf16[16,1280]{1,0:T(8,128)(2,1)S(1)}, bf16[16,1280]{1,0:T(8,128)(2,1)S(1)}, u32[]{:S(2)}, u32[]{:S(2)}) collective-permute-start(bf16[16,1280]{1,0:T(8,128)(2,1)S(1)} %get-tuple-element.30.refs_0_), channel_id=1, source_target_pairs={{0,1},{1,0},{2,3},{3,2},{4,5},{5,4},{6,7},{7,6},{8,9},{9,8},{10,11... | collective-permute-start | bytes 122888 | tf_op jit(solution)/shard_map/ppermute | solution.py:238
  17.2 2.6 %collective-permute-start.7 = (bf16[16,1280]{1,0:T(8,128)(2,1)S(1)}, bf16[16,1280]{1,0:T(8,128)(2,1)S(1)}, u32[]{:S(2)}, u32[]{:S(2)}) collective-permute-start(bf16[16,1280]{1,0:T(8,128)(2,1)S(1)} %get-tuple-element.30.refs_0_), channel_id=1, source_target_pairs={{0,2},{1,3},{2,0},{3,1},{4,6},{5,7},{6,4},{7,5},{8,10},{9,11},{10,... | collective-permute-start | bytes 122888 | tf_op jit(solution)/shard_map/ppermute | solution.py:238
  20.0 2.8 %collective-permute-done.7.refs_2_ = bf16[16,1280]{1,0:T(8,128)(2,1)S(1)} collective-permute-done((bf16[16,1280]{1,0:T(8,128)(2,1)S(1)}, bf16[16,1280]{1,0:T(8,128)(2,1)S(1)}, u32[]{:S(2)}, u32[]{:S(2)}) %collective-permute-start.7) | collective-permute-done | bytes 40992 | tf_op jit(solution)/shard_map/ppermute | solution.py:238
  22.9 2.7 %collective-permute-done.8.refs_3_ = bf16[16,1280]{1,0:T(8,128)(2,1)S(1)} collective-permute-done((bf16[16,1280]{1,0:T(8,128)(2,1)S(1)}, bf16[16,1280]{1,0:T(8,128)(2,1)S(1)}, u32[]{:S(2)}, u32[]{:S(2)}) %collective-permute-start.8) | collective-permute-done | bytes 40992 | tf_op jit(solution)/shard_map/ppermute | solution.py:238
  25.6 1.1 shard_map.93.refs_0_.refs_4_
  26.8 1.3 %collective-permute-start.10 = (bf16[64,1024]{1,0:T(8,128)(2,1)S(1)}, bf16[64,1024]{1,0:T(8,128)(2,1)S(1)}, u32[]{:S(2)}, u32[]{:S(2)}) collective-permute-start(bf16[64,1024]{1,0:T(8,128)(2,1)S(1)} %shard_map.93.refs_0_.refs_4_), channel_id=1, source_target_pairs={{0,2},{1,3},{2,0},{3,1},{4,5},{5,4},{6,7},{7,6},{8,10},{9,11},{10,... | collective-permute-start | bytes 393224 | tf_op jit(solution)/shard_map/ppermute | solution.py:246
  28.1 3.1 %collective-permute-start.11 = (bf16[64,1024]{1,0:T(8,128)(2,1)S(1)}, bf16[64,1024]{1,0:T(8,128)(2,1)S(1)}, u32[]{:S(2)}, u32[]{:S(2)}) collective-permute-start(bf16[64,1024]{1,0:T(8,128)(2,1)S(1)} %shard_map.93.refs_0_.refs_4_), channel_id=1, source_target_pairs={{0,3},{1,2},{2,1},{3,0},{4,7},{5,6},{6,5},{7,4},{8,11},{9,10},{10,... | collective-permute-start | bytes 393224 | tf_op jit(solution)/shard_map/ppermute | solution.py:246
  31.2 2.8 %collective-permute-done.9.refs_1_ = bf16[64,1024]{1,0:T(8,128)(2,1)S(1)} collective-permute-done((bf16[64,1024]{1,0:T(8,128)(2,1)S(1)}, bf16[64,1024]{1,0:T(8,128)(2,1)S(1)}, u32[]{:S(2)}, u32[]{:S(2)}) %collective-permute-start.9) | collective-permute-done | bytes 131104 | tf_op jit(solution)/shard_map/ppermute | solution.py:246
  33.9 3.5 %collective-permute-done.10.refs_2_ = bf16[64,1024]{1,0:T(8,128)(2,1)S(1)} collective-permute-done((bf16[64,1024]{1,0:T(8,128)(2,1)S(1)}, bf16[64,1024]{1,0:T(8,128)(2,1)S(1)}, u32[]{:S(2)}, u32[]{:S(2)}) %collective-permute-start.10) | collective-permute-done | bytes 131104 | tf_op jit(solution)/shard_map/ppermute | solution.py:246
  37.4 0.7 shard_map.94
  38.2 0.6 collective-permute-start.13
  38.8 0.8 collective-permute-start.14
  39.5 2.2 %collective-permute-start.12 = (bf16[2,64,512]{2,1,0:T(8,128)(2,1)S(1)}, bf16[2,64,512]{2,1,0:T(8,128)(2,1)S(1)}, u32[]{:S(2)}, u32[]{:S(2)}) collective-permute-start(bf16[2,64,512]{2,1,0:T(8,128)(2,1)S(1)} %get-tuple-element.32), channel_id=1, source_target_pairs={{0,24},{4,28},{8,16},{12,20},{16,8},{20,12},{24,0},{28,4},{1,25},{... | collective-permute-start | bytes 393224 | tf_op jit(solution)/shard_map/ppermute | solution.py:235
  41.7 1.8 %collective-permute-done.13.refs_0_ = bf16[2,64,512]{2,1,0:T(8,128)(2,1)S(1)} collective-permute-done((bf16[2,64,512]{2,1,0:T(8,128)(2,1)S(1)}, bf16[2,64,512]{2,1,0:T(8,128)(2,1)S(1)}, u32[]{:S(2)}, u32[]{:S(2)}) %collective-permute-start.13) | collective-permute-done | bytes 131104 | tf_op jit(solution)/shard_map/ppermute | solution.py:235
  43.9 3.6 %shard_map.95 = (bf16[64,3584]{1,0:T(8,128)(2,1)}, bf16[64,3584]{1,0:T(8,128)(2,1)}) custom-call(s32[3]{0:T(128)S(1)} %pad_add_fusion.ids, bf16[2,64,512]{2,1,0:T(8,128)(2,1)S(1)} %collective-permute-done.13.refs_0_, bf16[2,64,512]{2,1,0:T(8,128)(2,1)S(1)} %collective-permute-done.14.refs_1_, bf16[512,1792]{1,0:T(8,128)(2,1)S(1)} %copy-done, ...), custom_call_target="tpu_custom_call" | custom-call | flops 939524096 | bytes 8519680 | tf_op jit(solution)/shard_map/pallas_call | solution.py:34
  47.4 3.3 %collective-permute-start.15 = (bf16[64,3584]{1,0:T(8,128)(2,1)}, bf16[64,3584]{1,0:T(8,128)(2,1)S(1)}, u32[]{:S(2)}, u32[]{:S(2)}) collective-permute-start(bf16[64,3584]{1,0:T(8,128)(2,1)} %get-tuple-element.36.refs_6_), channel_id=1, source_target_pairs={{0,8},{4,12},{8,0},{12,4},{16,24},{20,28},{24,16},{28,20},{1,9},{5... | collective-permute-start | bytes 1376264 | tf_op jit(solution)/shard_map/ppermute | solution.py:235
  50.8 1.0 collective-permute-start.16
  51.8 3.5 %shard_map.96 = (bf16[64,3584]{1,0:T(8,128)(2,1)}, bf16[64,3584]{1,0:T(8,128)(2,1)S(1)}) custom-call(s32[3]{0:T(128)S(1)} %pad_add_fusion.ids, bf16[2,64,512]{2,1,0:T(8,128)(2,1)S(1)} %collective-permute-done.12.refs_0_, bf16[2,64,512]{2,1,0:T(8,128)(2,1)S(1)} %get-tuple-element.33.refs_1_, bf16[512,1792]{1,0:T(8,128)(2,1)S(1)} %copy-done, ...), custom_call_target="tpu_custom_call" | custom-call | flops 939524096 | bytes 8519680 | tf_op jit(solution)/shard_map/pallas_call | solution.py:34
  55.3 0.8 copy-done.6
  56.7 2.1 %shard_map.97.refs_5_.refs_6_ = bf16[192,320]{1,0:T(8,128)(2,1)S(1)} custom-call(s32[3]{0:T(128)S(1)} %pad_add_fusion.ids, s32[192,1]{1,0:T(8,128)S(1)} %copy.10.refs_0_, bf16[192,1280]{1,0:T(8,128)(2,1)S(1)} %copy-done.4, bf16[32,1280]{1,0:T(8,128)(2,1)S(1)} %pad.4.refs_2_), custom_call_target="tpu_custom_call" | custom-call | bytes 697088 | tf_op jit(solution)/shard_map/pallas_call | solution.py:34
  58.7 3.1 %collective-permute-done.15.refs_2_ = bf16[64,3584]{1,0:T(8,128)(2,1)S(1)} collective-permute-done((bf16[64,3584]{1,0:T(8,128)(2,1)}, bf16[64,3584]{1,0:T(8,128)(2,1)S(1)}, u32[]{:S(2)}, u32[]{:S(2)}) %collective-permute-start.15) | collective-permute-done | bytes 458784 | tf_op jit(solution)/shard_map/ppermute | solution.py:235
  61.8 7.4 %collective-permute-done.16.refs_3_ = bf16[64,3584]{1,0:T(8,128)(2,1)S(1)} collective-permute-done((bf16[64,3584]{1,0:T(8,128)(2,1)}, bf16[64,3584]{1,0:T(8,128)(2,1)S(1)}, u32[]{:S(2)}, u32[]{:S(2)}) %collective-permute-start.16) | collective-permute-done | bytes 458784 | tf_op jit(solution)/shard_map/ppermute | solution.py:235
  69.2 1.0 copy-done.7
  70.2 1.0 shard_map.98.refs_0_
  71.4 1.3 %collective-permute-start.20 = (bf16[64,1792]{1,0:T(8,128)(2,1)S(1)}, bf16[64,1792]{1,0:T(8,128)(2,1)S(1)}, u32[]{:S(2)}, u32[]{:S(2)}) collective-permute-start(bf16[64,1792]{1,0:T(8,128)(2,1)S(1)} %shard_map.98.refs_0_), channel_id=1, source_target_pairs={{0,16},{4,20},{8,24},{12,28},{16,0},{20,4},{24,8},{28,12},{1,17},{... | collective-permute-start | bytes 688136 | tf_op jit(solution)/shard_map/ppermute | solution.py:235
  72.7 2.1 %collective-permute-start.21 = (bf16[64,1792]{1,0:T(8,128)(2,1)S(1)}, bf16[64,1792]{1,0:T(8,128)(2,1)S(1)}, u32[]{:S(2)}, u32[]{:S(2)}) collective-permute-start(bf16[64,1792]{1,0:T(8,128)(2,1)S(1)} %shard_map.98.refs_0_), channel_id=1, source_target_pairs={{0,24},{4,28},{8,16},{12,20},{16,8},{20,12},{24,0},{28,4},{1,25},{... | collective-permute-start | bytes 688136 | tf_op jit(solution)/shard_map/ppermute | solution.py:235
  74.8 2.5 %collective-permute-done.19.refs_0_ = bf16[64,1792]{1,0:T(8,128)(2,1)S(1)} collective-permute-done((bf16[64,1792]{1,0:T(8,128)(2,1)S(1)}, bf16[64,1792]{1,0:T(8,128)(2,1)S(1)}, u32[]{:S(2)}, u32[]{:S(2)}) %collective-permute-start.19) | collective-permute-done | bytes 229408 | tf_op jit(solution)/shard_map/ppermute | solution.py:235
  77.4 3.0 %collective-permute-done.21.refs_2_ = bf16[64,1792]{1,0:T(8,128)(2,1)S(1)} collective-permute-done((bf16[64,1792]{1,0:T(8,128)(2,1)S(1)}, bf16[64,1792]{1,0:T(8,128)(2,1)S(1)}, u32[]{:S(2)}, u32[]{:S(2)}) %collective-permute-start.21) | collective-permute-done | bytes 229408 | tf_op jit(solution)/shard_map/ppermute | solution.py:235
  80.4 2.9 %shard_map.100 = (bf16[2,64,512]{2,1,0:T(8,128)(2,1)S(1)}, bf16[2,64,512]{2,1,0:T(8,128)(2,1)S(1)}, bf16[2,64,512]{2,1,0:T(8,128)(2,1)S(1)}) custom-call(s32[3]{0:T(128)S(1)} %pad_add_fusion.ids, bf16[64,1792]{1,0:T(8,128)(2,1)S(1)} %collective-permute-done.19.refs_0_, bf16[64,1792]{1,0:T(8,128)(2,1)S(1)} %collective-permute-done.20.refs_1_, ...), custom_call_target="tpu_custom_call" | custom-call | flops 704643072 | bytes 4751360 | tf_op jit(solution)/shard_map/pallas_call | solution.py:34
  83.3 1.5 %collective-permute-start.22 = (bf16[2,64,512]{2,1,0:T(8,128)(2,1)S(1)}, bf16[2,64,512]{2,1,0:T(8,128)(2,1)S(1)}, u32[]{:S(2)}, u32[]{:S(2)}) collective-permute-start(bf16[2,64,512]{2,1,0:T(8,128)(2,1)S(1)} %get-tuple-element.41), channel_id=1, source_target_pairs={{0,8},{4,12},{8,0},{12,4},{16,24},{20,28},{24,16},{28,20},{1,9},{5... | collective-permute-start | bytes 393224 | tf_op jit(solution)/shard_map/ppermute | solution.py:235
  84.9 1.3 %collective-permute-start.23 = (bf16[2,64,512]{2,1,0:T(8,128)(2,1)S(1)}, bf16[2,64,512]{2,1,0:T(8,128)(2,1)S(1)}, u32[]{:S(2)}, u32[]{:S(2)}) collective-permute-start(bf16[2,64,512]{2,1,0:T(8,128)(2,1)S(1)} %get-tuple-element.42), channel_id=1, source_target_pairs={{0,16},{4,20},{8,24},{12,28},{16,0},{20,4},{24,8},{28,12},{1,17},{... | collective-permute-start | bytes 393224 | tf_op jit(solution)/shard_map/ppermute | solution.py:235
  86.1 0.8 collective-permute-start.24
  86.9 2.8 %shard_map.99.refs_0_ = bf16[2,64,512]{2,1,0:T(8,128)(2,1)S(1)} custom-call(s32[3]{0:T(128)S(1)} %pad_add_fusion.ids, bf16[64,1792]{1,0:T(8,128)(2,1)S(1)} %shard_map.98.refs_0_, bf16[1792,512]{1,0:T(8,128)(2,1)} %refs_3_.1, bf16[1792,512]{1,0:T(8,128)(2,1)} %collective-permute-done.18.refs_2_.refs_4_), custom_call_target="tpu_custom_call" | custom-call | flops 234881024 | bytes 4030464 | tf_op jit(solution)/shard_map/pallas_call | solution.py:34
  89.8 2.2 %collective-permute-done.24.refs_3_ = bf16[2,64,512]{2,1,0:T(8,128)(2,1)S(1)} collective-permute-done((bf16[2,64,512]{2,1,0:T(8,128)(2,1)S(1)}, bf16[2,64,512]{2,1,0:T(8,128)(2,1)S(1)}, u32[]{:S(2)}, u32[]{:S(2)}) %collective-permute-start.24) | collective-permute-done | bytes 131104 | tf_op jit(solution)/shard_map/ppermute | solution.py:235
  92.0 0.6 shard_map.101
  92.7 0.7 collective-permute-start.26
  93.4 3.7 %collective-permute-start.27 = (bf16[64,1024]{1,0:T(8,128)(2,1)S(1)}, bf16[64,1024]{1,0:T(8,128)(2,1)S(1)}, u32[]{:S(2)}, u32[]{:S(2)}) collective-permute-start(bf16[64,1024]{1,0:T(8,128)(2,1)S(1)} %get-tuple-element.47), channel_id=1, source_target_pairs={{0,3},{1,2},{2,1},{3,0},{4,7},{5,6},{6,5},{7,4},{8,11},{9,10},{10,... | collective-permute-start | bytes 393224 | tf_op jit(solution)/shard_map/ppermute | solution.py:238
  97.1 2.5 %collective-permute-done.25.refs_1_ = bf16[64,1024]{1,0:T(8,128)(2,1)S(1)} collective-permute-done((bf16[64,1024]{1,0:T(8,128)(2,1)S(1)}, bf16[64,1024]{1,0:T(8,128)(2,1)S(1)}, u32[]{:S(2)}, u32[]{:S(2)}) %collective-permute-start.25) | collective-permute-done | bytes 131104 | tf_op jit(solution)/shard_map/ppermute | solution.py:238
  99.6 3.2 %collective-permute-done.27.refs_3_ = bf16[64,1024]{1,0:T(8,128)(2,1)S(1)} collective-permute-done((bf16[64,1024]{1,0:T(8,128)(2,1)S(1)}, bf16[64,1024]{1,0:T(8,128)(2,1)S(1)}, u32[]{:S(2)}, u32[]{:S(2)}) %collective-permute-start.27) | collective-permute-done | bytes 131104 | tf_op jit(solution)/shard_map/ppermute | solution.py:238
  102.7 1.1 shard_map.102
  103.9 2.5 %collective-permute-start.28 = (bf16[16,1280]{1,0:T(8,128)(2,1)S(1)}, bf16[16,1280]{1,0:T(8,128)(2,1)S(1)}, u32[]{:S(2)}, u32[]{:S(2)}) collective-permute-start(bf16[16,1280]{1,0:T(8,128)(2,1)S(1)} %get-tuple-element.49), channel_id=1, source_target_pairs={{0,1},{1,0},{2,3},{3,2},{4,5},{5,4},{6,7},{7,6},{8,9},{9,8},{10,11... | collective-permute-start | bytes 122888 | tf_op jit(solution)/shard_map/ppermute | solution.py:238
  106.4 0.5 collective-permute-start.29
  107.0 1.9 %collective-permute-start.30 = (bf16[16,1280]{1,0:T(8,128)(2,1)S(1)}, bf16[16,1280]{1,0:T(8,128)(2,1)S(1)}, u32[]{:S(2)}, u32[]{:S(2)}) collective-permute-start(bf16[16,1280]{1,0:T(8,128)(2,1)S(1)} %get-tuple-element.51), channel_id=1, source_target_pairs={{0,3},{1,2},{2,1},{3,0},{4,7},{5,6},{6,5},{7,4},{8,11},{9,10},{10,... | collective-permute-start | bytes 122888 | tf_op jit(solution)/shard_map/ppermute | solution.py:238
  108.9 2.5 %collective-permute-done.29.refs_2_ = bf16[16,1280]{1,0:T(8,128)(2,1)S(1)} collective-permute-done((bf16[16,1280]{1,0:T(8,128)(2,1)S(1)}, bf16[16,1280]{1,0:T(8,128)(2,1)S(1)}, u32[]{:S(2)}, u32[]{:S(2)}) %collective-permute-start.29) | collective-permute-done | bytes 40992 | tf_op jit(solution)/shard_map/ppermute | solution.py:238
  111.3 1.5 %collective-permute-done.30.refs_3_ = bf16[16,1280]{1,0:T(8,128)(2,1)S(1)} collective-permute-done((bf16[16,1280]{1,0:T(8,128)(2,1)S(1)}, bf16[16,1280]{1,0:T(8,128)(2,1)S(1)}, u32[]{:S(2)}, u32[]{:S(2)}) %collective-permute-start.30) | collective-permute-done | bytes 40992 | tf_op jit(solution)/shard_map/ppermute | solution.py:238
  112.8 0.6 shard_map.103.refs_0_
  113.3 0.6 collective-permute-start.31
  113.9 1.1 collective-permute-start.32
  115.0 1.9 %collective-permute-start.33 = (bf16[16,1280]{1,0:T(8,128)(2,1)S(1)}, bf16[16,1280]{1,0:T(8,128)(2,1)S(1)}, u32[]{:S(2)}, u32[]{:S(2)}) collective-permute-start(bf16[16,1280]{1,0:T(8,128)(2,1)S(1)} %shard_map.103.refs_0_), channel_id=1, source_target_pairs={{0,24},{4,28},{8,16},{12,20},{16,8},{20,12},{24,0},{28,4},{1,25},{... | collective-permute-start | bytes 122888 | tf_op jit(solution)/shard_map/ppermute | solution.py:235
  116.9 0.5 collective-permute-done.31.refs_1_
  117.4 0.5 collective-permute-done.32.refs_2_
  117.9 2.0 %collective-permute-done.33.refs_3_ = bf16[16,1280]{1,0:T(8,128)(2,1)S(1)} collective-permute-done((bf16[16,1280]{1,0:T(8,128)(2,1)S(1)}, bf16[16,1280]{1,0:T(8,128)(2,1)S(1)}, u32[]{:S(2)}, u32[]{:S(2)}) %collective-permute-start.33) | collective-permute-done | bytes 40992 | tf_op jit(solution)/shard_map/ppermute | solution.py:235
  120.0 1.4 %collective-permute-done.34.refs_4_ = bf16[4,16,1280]{2,1,0:T(8,128)(2,1)S(1)} collective-permute-done((bf16[4,16,1280]{2,1,0:T(8,128)(2,1)S(1)}, bf16[4,16,1280]{2,1,0:T(8,128)(2,1)S(1)}, u32[]{:S(2)}, u32[]{:S(2)}) %collective-permute-start.34) | collective-permute-done | bytes 163872 | tf_op jit(solution)/shard_map/ppermute | solution.py:232
  121.4 1.8 %shard_map.104 = bf16[192,1280]{1,0:T(8,128)(2,1)} custom-call(s32[3]{0:T(128)S(1)} %pad_add_fusion.ids, bf16[16,1280]{1,0:T(8,128)(2,1)S(1)} %shard_map.103.refs_0_, bf16[16,1280]{1,0:T(8,128)(2,1)S(1)} %collective-permute-done.31.refs_1_, bf16[16,1280]{1,0:T(8,128)(2,1)S(1)} %collective-permute-done.32.refs_2_, ...), custom_call_target="tpu_custom_call" | custom-call | bytes 1437696 | tf_op jit(solution)/shard_map/pallas_call | solution.py:34
  (47 shorter events, 2.6 us)
Async XLA Ops:
  0.0 14.6 %collective-permute-start.4 = (bf16[512,1792]{1,0:T(8,128)(2,1)}, bf16[512,1792]{1,0:T(8,128)(2,1)S(1)}, u32[]{:S(2)}, u32[]{:S(2)}) collective-permute-start(bf16[512,1792]{1,0:T(8,128)(2,1)} %refs_2_.3), channel_id=1, source_target_pairs={{0,4},{4,0},{8,12},{12,8},{16,20},{20,16},{24,28},{28,24},{1,5},{5... | collective-permute-start | bytes 5505032 | tf_op jit(solution)/shard_map/ppermute | solution.py:232
  0.5 14.2 %collective-permute-start.5 = (bf16[512,1792]{1,0:T(8,128)(2,1)}, bf16[512,1792]{1,0:T(8,128)(2,1)}, u32[]{:S(2)}, u32[]{:S(2)}) collective-permute-start(bf16[512,1792]{1,0:T(8,128)(2,1)} %refs_4_.5), channel_id=1, source_target_pairs={{0,4},{4,0},{8,12},{12,8},{16,20},{20,16},{24,28},{28,24},{1,5},{5... | collective-permute-start | bytes 5505032 | tf_op jit(solution)/shard_map/ppermute | solution.py:232
  0.6 1.0 copy-start.5
  1.6 0.7 copy-start.8
  3.1 5.6 %collective-permute-start = (bf16[32,1280]{1,0:T(8,128)(2,1)S(1)}, bf16[32,1280]{1,0:T(8,128)(2,1)S(1)}, u32[]{:S(2)}, u32[]{:S(2)}) collective-permute-start(bf16[32,1280]{1,0:T(8,128)(2,1)S(1)} %shard_map.91.refs_0_), channel_id=1, source_target_pairs={{0,8},{4,12},{8,0},{12,4},{16,24},{20,28},{24,16},{28,20},{1,9},{5... | collective-permute-start | bytes 245768 | tf_op jit(solution)/shard_map/ppermute | solution.py:235
  6.0 4.4 %collective-permute-start.1 = (bf16[32,1280]{1,0:T(8,128)(2,1)S(1)}, bf16[32,1280]{1,0:T(8,128)(2,1)S(1)}, u32[]{:S(2)}, u32[]{:S(2)}) collective-permute-start(bf16[32,1280]{1,0:T(8,128)(2,1)S(1)} %shard_map.91.refs_0_), channel_id=1, source_target_pairs={{0,16},{4,20},{8,24},{12,28},{16,0},{20,4},{24,8},{28,12},{1,17},{... | collective-permute-start | bytes 245768 | tf_op jit(solution)/shard_map/ppermute | solution.py:235
  7.6 5.3 %collective-permute-start.2 = (bf16[32,1280]{1,0:T(8,128)(2,1)S(1)}, bf16[32,1280]{1,0:T(8,128)(2,1)S(1)}, u32[]{:S(2)}, u32[]{:S(2)}) collective-permute-start(bf16[32,1280]{1,0:T(8,128)(2,1)S(1)} %shard_map.91.refs_0_), channel_id=1, source_target_pairs={{0,24},{4,28},{8,16},{12,20},{16,8},{20,12},{24,0},{28,4},{1,25},{... | collective-permute-start | bytes 245768 | tf_op jit(solution)/shard_map/ppermute | solution.py:235
  12.9 12.7 %copy-start.2 = (bf16[1280,1024]{1,0:T(8,128)(2,1)S(1)}, bf16[1280,1024]{1,0:T(8,128)(2,1)}, u32[]{:S(2)}) copy-start(bf16[1280,1024]{1,0:T(8,128)(2,1)} %refs_4_.3) | copy-start | bytes 7864324
  12.9 1.7 %collective-permute-start.3 = (bf16[128,1280]{1,0:T(8,128)(2,1)S(1)}, bf16[128,1280]{1,0:T(8,128)(2,1)S(1)}, u32[]{:S(2)}, u32[]{:S(2)}) collective-permute-start(bf16[128,1280]{1,0:T(8,128)(2,1)S(1)} %pad_maximum_fusion), channel_id=1, source_target_pairs={{0,4},{4,0},{8,12},{12,8},{16,20},{20,16},{24,28},{28,24},{1,5},{5... | collective-permute-start | bytes 983048 | tf_op jit(solution)/shard_map/ppermute | solution.py:232
  14.6 29.2 %copy-start.1 = (bf16[512,1792]{1,0:T(8,128)(2,1)S(1)}, bf16[512,1792]{1,0:T(8,128)(2,1)}, u32[]{:S(2)}) copy-start(bf16[512,1792]{1,0:T(8,128)(2,1)} %refs_4_.5) | copy-start | bytes 5505028
  15.4 28.5 %copy-start = (bf16[512,1792]{1,0:T(8,128)(2,1)S(1)}, bf16[512,1792]{1,0:T(8,128)(2,1)}, u32[]{:S(2)}) copy-start(bf16[512,1792]{1,0:T(8,128)(2,1)} %refs_2_.3) | copy-start | bytes 5505028
  15.4 65.0 %collective-permute-start.18 = (bf16[1792,512]{1,0:T(8,128)(2,1)}, bf16[1792,512]{1,0:T(8,128)(2,1)}, u32[]{:S(2)}, u32[]{:S(2)}) collective-permute-start(bf16[1792,512]{1,0:T(8,128)(2,1)} %refs_3_.1), channel_id=1, source_target_pairs={{0,4},{4,0},{8,12},{12,8},{16,20},{20,16},{24,28},{28,24},{1,5},{5... | collective-permute-start | bytes 5505032 | tf_op jit(solution)/shard_map/ppermute | solution.py:232
  15.6 4.4 %collective-permute-start.6 = (bf16[16,1280]{1,0:T(8,128)(2,1)S(1)}, bf16[16,1280]{1,0:T(8,128)(2,1)S(1)}, u32[]{:S(2)}, u32[]{:S(2)}) collective-permute-start(bf16[16,1280]{1,0:T(8,128)(2,1)S(1)} %get-tuple-element.30.refs_0_), channel_id=1, source_target_pairs={{0,1},{1,0},{2,3},{3,2},{4,5},{5,4},{6,7},{7,6},{8,9},{9,8},{10,11... | collective-permute-start | bytes 122888 | tf_op jit(solution)/shard_map/ppermute | solution.py:238
  17.2 5.7 %collective-permute-start.7 = (bf16[16,1280]{1,0:T(8,128)(2,1)S(1)}, bf16[16,1280]{1,0:T(8,128)(2,1)S(1)}, u32[]{:S(2)}, u32[]{:S(2)}) collective-permute-start(bf16[16,1280]{1,0:T(8,128)(2,1)S(1)} %get-tuple-element.30.refs_0_), channel_id=1, source_target_pairs={{0,2},{1,3},{2,0},{3,1},{4,6},{5,7},{6,4},{7,5},{8,10},{9,11},{10,... | collective-permute-start | bytes 122888 | tf_op jit(solution)/shard_map/ppermute | solution.py:238
  19.8 5.8 %collective-permute-start.8 = (bf16[16,1280]{1,0:T(8,128)(2,1)S(1)}, bf16[16,1280]{1,0:T(8,128)(2,1)S(1)}, u32[]{:S(2)}, u32[]{:S(2)}) collective-permute-start(bf16[16,1280]{1,0:T(8,128)(2,1)S(1)} %get-tuple-element.30.refs_0_), channel_id=1, source_target_pairs={{0,3},{1,2},{2,1},{3,0},{4,7},{5,6},{6,5},{7,4},{8,11},{9,10},{10,... | collective-permute-start | bytes 122888 | tf_op jit(solution)/shard_map/ppermute | solution.py:238
  26.7 7.2 %collective-permute-start.9 = (bf16[64,1024]{1,0:T(8,128)(2,1)S(1)}, bf16[64,1024]{1,0:T(8,128)(2,1)S(1)}, u32[]{:S(2)}, u32[]{:S(2)}) collective-permute-start(bf16[64,1024]{1,0:T(8,128)(2,1)S(1)} %shard_map.93.refs_0_.refs_4_), channel_id=1, source_target_pairs={{0,1},{1,0},{2,3},{3,2},{4,6},{5,7},{6,4},{7,5},{8,9},{9,8},{10,11... | collective-permute-start | bytes 393224 | tf_op jit(solution)/shard_map/ppermute | solution.py:246
  26.8 10.6 %collective-permute-start.10 = (bf16[64,1024]{1,0:T(8,128)(2,1)S(1)}, bf16[64,1024]{1,0:T(8,128)(2,1)S(1)}, u32[]{:S(2)}, u32[]{:S(2)}) collective-permute-start(bf16[64,1024]{1,0:T(8,128)(2,1)S(1)} %shard_map.93.refs_0_.refs_4_), channel_id=1, source_target_pairs={{0,2},{1,3},{2,0},{3,1},{4,5},{5,4},{6,7},{7,6},{8,10},{9,11},{10,... | collective-permute-start | bytes 393224 | tf_op jit(solution)/shard_map/ppermute | solution.py:246
  28.1 9.3 %collective-permute-start.11 = (bf16[64,1024]{1,0:T(8,128)(2,1)S(1)}, bf16[64,1024]{1,0:T(8,128)(2,1)S(1)}, u32[]{:S(2)}, u32[]{:S(2)}) collective-permute-start(bf16[64,1024]{1,0:T(8,128)(2,1)S(1)} %shard_map.93.refs_0_.refs_4_), channel_id=1, source_target_pairs={{0,3},{1,2},{2,1},{3,0},{4,7},{5,6},{6,5},{7,4},{8,11},{9,10},{10,... | collective-permute-start | bytes 393224 | tf_op jit(solution)/shard_map/ppermute | solution.py:246
  38.2 5.4 %collective-permute-start.13 = (bf16[2,64,512]{2,1,0:T(8,128)(2,1)S(1)}, bf16[2,64,512]{2,1,0:T(8,128)(2,1)S(1)}, u32[]{:S(2)}, u32[]{:S(2)}) collective-permute-start(bf16[2,64,512]{2,1,0:T(8,128)(2,1)S(1)} %get-tuple-element.34), channel_id=1, source_target_pairs={{0,8},{4,12},{8,0},{12,4},{16,24},{20,28},{24,16},{28,20},{1,9},{5... | collective-permute-start | bytes 393224 | tf_op jit(solution)/shard_map/ppermute | solution.py:235
  38.8 5.1 %collective-permute-start.14 = (bf16[2,64,512]{2,1,0:T(8,128)(2,1)S(1)}, bf16[2,64,512]{2,1,0:T(8,128)(2,1)S(1)}, u32[]{:S(2)}, u32[]{:S(2)}) collective-permute-start(bf16[2,64,512]{2,1,0:T(8,128)(2,1)S(1)} %get-tuple-element.35), channel_id=1, source_target_pairs={{0,16},{4,20},{8,24},{12,28},{16,0},{20,4},{24,8},{28,12},{1,17},{... | collective-permute-start | bytes 393224 | tf_op jit(solution)/shard_map/ppermute | solution.py:235
  39.5 12.3 %collective-permute-start.12 = (bf16[2,64,512]{2,1,0:T(8,128)(2,1)S(1)}, bf16[2,64,512]{2,1,0:T(8,128)(2,1)S(1)}, u32[]{:S(2)}, u32[]{:S(2)}) collective-permute-start(bf16[2,64,512]{2,1,0:T(8,128)(2,1)S(1)} %get-tuple-element.32), channel_id=1, source_target_pairs={{0,24},{4,28},{8,16},{12,20},{16,8},{20,12},{24,0},{28,4},{1,25},{... | collective-permute-start | bytes 393224 | tf_op jit(solution)/shard_map/ppermute | solution.py:235
  47.4 14.3 %collective-permute-start.15 = (bf16[64,3584]{1,0:T(8,128)(2,1)}, bf16[64,3584]{1,0:T(8,128)(2,1)S(1)}, u32[]{:S(2)}, u32[]{:S(2)}) collective-permute-start(bf16[64,3584]{1,0:T(8,128)(2,1)} %get-tuple-element.36.refs_6_), channel_id=1, source_target_pairs={{0,8},{4,12},{8,0},{12,4},{16,24},{20,28},{24,16},{28,20},{1,9},{5... | collective-permute-start | bytes 1376264 | tf_op jit(solution)/shard_map/ppermute | solution.py:235
  50.8 18.4 %collective-permute-start.16 = (bf16[64,3584]{1,0:T(8,128)(2,1)}, bf16[64,3584]{1,0:T(8,128)(2,1)S(1)}, u32[]{:S(2)}, u32[]{:S(2)}) collective-permute-start(bf16[64,3584]{1,0:T(8,128)(2,1)} %get-tuple-element.38), channel_id=1, source_target_pairs={{0,16},{4,20},{8,24},{12,28},{16,0},{20,4},{24,8},{28,12},{1,17},{... | collective-permute-start | bytes 1376264 | tf_op jit(solution)/shard_map/ppermute | solution.py:235
  51.8 4.7 %copy-start.9 = (s32[192]{0:T(256)S(1)}, s32[192]{0:T(256)}, u32[]{:S(2)}) copy-start(s32[192]{0:T(256)} %param.11) | copy-start | bytes 2308
  51.8 4.8 %copy-start.10 = (bf16[31,1280]{1,0:T(8,128)(2,1)S(1)}, bf16[31,1280]{1,0:T(8,128)(2,1)}, u32[]{:S(2)}) copy-start(bf16[31,1280]{1,0:T(8,128)(2,1)} %param.12) | copy-start | bytes 238084
  51.8 4.8 %copy-start.4 = (bf16[192,1280]{1,0:T(8,128)(2,1)S(1)}, bf16[192,1280]{1,0:T(8,128)(2,1)}, u32[]{:S(2)}) copy-start(bf16[192,1280]{1,0:T(8,128)(2,1)} %refs_7_.1) | copy-start | bytes 1474564
  55.3 0.8 copy-start.6
  56.1 13.1 %collective-permute-start.17 = (bf16[64,3584]{1,0:T(8,128)(2,1)}, bf16[64,3584]{1,0:T(8,128)(2,1)S(1)}, u32[]{:S(2)}, u32[]{:S(2)}) collective-permute-start(bf16[64,3584]{1,0:T(8,128)(2,1)} %get-tuple-element.39), channel_id=1, source_target_pairs={{0,24},{4,28},{8,16},{12,20},{16,8},{20,12},{24,0},{28,4},{1,25},{... | collective-permute-start | bytes 1376264 | tf_op jit(solution)/shard_map/ppermute | solution.py:235
  69.2 1.0 copy-start.7
  71.3 6.1 %collective-permute-start.19 = (bf16[64,1792]{1,0:T(8,128)(2,1)S(1)}, bf16[64,1792]{1,0:T(8,128)(2,1)S(1)}, u32[]{:S(2)}, u32[]{:S(2)}) collective-permute-start(bf16[64,1792]{1,0:T(8,128)(2,1)S(1)} %shard_map.98.refs_0_), channel_id=1, source_target_pairs={{0,8},{4,12},{8,0},{12,4},{16,24},{20,28},{24,16},{28,20},{1,9},{5... | collective-permute-start | bytes 688136 | tf_op jit(solution)/shard_map/ppermute | solution.py:235
  71.4 6.0 %collective-permute-start.20 = (bf16[64,1792]{1,0:T(8,128)(2,1)S(1)}, bf16[64,1792]{1,0:T(8,128)(2,1)S(1)}, u32[]{:S(2)}, u32[]{:S(2)}) collective-permute-start(bf16[64,1792]{1,0:T(8,128)(2,1)S(1)} %shard_map.98.refs_0_), channel_id=1, source_target_pairs={{0,16},{4,20},{8,24},{12,28},{16,0},{20,4},{24,8},{28,12},{1,17},{... | collective-permute-start | bytes 688136 | tf_op jit(solution)/shard_map/ppermute | solution.py:235
  72.7 7.7 %collective-permute-start.21 = (bf16[64,1792]{1,0:T(8,128)(2,1)S(1)}, bf16[64,1792]{1,0:T(8,128)(2,1)S(1)}, u32[]{:S(2)}, u32[]{:S(2)}) collective-permute-start(bf16[64,1792]{1,0:T(8,128)(2,1)S(1)} %shard_map.98.refs_0_), channel_id=1, source_target_pairs={{0,24},{4,28},{8,16},{12,20},{16,8},{20,12},{24,0},{28,4},{1,25},{... | collective-permute-start | bytes 688136 | tf_op jit(solution)/shard_map/ppermute | solution.py:235
  83.3 6.4 %collective-permute-start.22 = (bf16[2,64,512]{2,1,0:T(8,128)(2,1)S(1)}, bf16[2,64,512]{2,1,0:T(8,128)(2,1)S(1)}, u32[]{:S(2)}, u32[]{:S(2)}) collective-permute-start(bf16[2,64,512]{2,1,0:T(8,128)(2,1)S(1)} %get-tuple-element.41), channel_id=1, source_target_pairs={{0,8},{4,12},{8,0},{12,4},{16,24},{20,28},{24,16},{28,20},{1,9},{5... | collective-permute-start | bytes 393224 | tf_op jit(solution)/shard_map/ppermute | solution.py:235
  84.9 5.0 %collective-permute-start.23 = (bf16[2,64,512]{2,1,0:T(8,128)(2,1)S(1)}, bf16[2,64,512]{2,1,0:T(8,128)(2,1)S(1)}, u32[]{:S(2)}, u32[]{:S(2)}) collective-permute-start(bf16[2,64,512]{2,1,0:T(8,128)(2,1)S(1)} %get-tuple-element.42), channel_id=1, source_target_pairs={{0,16},{4,20},{8,24},{12,28},{16,0},{20,4},{24,8},{28,12},{1,17},{... | collective-permute-start | bytes 393224 | tf_op jit(solution)/shard_map/ppermute | solution.py:235
  86.1 16.6 %copy-start.3 = (bf16[1024,1280]{1,0:T(8,128)(2,1)S(1)}, bf16[1024,1280]{1,0:T(8,128)(2,1)}, u32[]{:S(2)}) copy-start(bf16[1024,1280]{1,0:T(8,128)(2,1)} %refs_5_.1) | copy-start | bytes 7864324
  86.1 5.9 %collective-permute-start.24 = (bf16[2,64,512]{2,1,0:T(8,128)(2,1)S(1)}, bf16[2,64,512]{2,1,0:T(8,128)(2,1)S(1)}, u32[]{:S(2)}, u32[]{:S(2)}) collective-permute-start(bf16[2,64,512]{2,1,0:T(8,128)(2,1)S(1)} %get-tuple-element.43), channel_id=1, source_target_pairs={{0,24},{4,28},{8,16},{12,20},{16,8},{20,12},{24,0},{28,4},{1,25},{... | collective-permute-start | bytes 393224 | tf_op jit(solution)/shard_map/ppermute | solution.py:235
  92.6 6.9 %collective-permute-start.25 = (bf16[64,1024]{1,0:T(8,128)(2,1)S(1)}, bf16[64,1024]{1,0:T(8,128)(2,1)S(1)}, u32[]{:S(2)}, u32[]{:S(2)}) collective-permute-start(bf16[64,1024]{1,0:T(8,128)(2,1)S(1)} %get-tuple-element.45), channel_id=1, source_target_pairs={{0,1},{1,0},{2,3},{3,2},{4,5},{5,4},{6,7},{7,6},{8,9},{9,8},{10,11... | collective-permute-start | bytes 393224 | tf_op jit(solution)/shard_map/ppermute | solution.py:238
  92.7 6.9 %collective-permute-start.26 = (bf16[64,1024]{1,0:T(8,128)(2,1)S(1)}, bf16[64,1024]{1,0:T(8,128)(2,1)S(1)}, u32[]{:S(2)}, u32[]{:S(2)}) collective-permute-start(bf16[64,1024]{1,0:T(8,128)(2,1)S(1)} %get-tuple-element.46), channel_id=1, source_target_pairs={{0,2},{1,3},{2,0},{3,1},{4,6},{5,7},{6,4},{7,5},{8,10},{9,11},{10,... | collective-permute-start | bytes 393224 | tf_op jit(solution)/shard_map/ppermute | solution.py:238
  93.4 9.4 %collective-permute-start.27 = (bf16[64,1024]{1,0:T(8,128)(2,1)S(1)}, bf16[64,1024]{1,0:T(8,128)(2,1)S(1)}, u32[]{:S(2)}, u32[]{:S(2)}) collective-permute-start(bf16[64,1024]{1,0:T(8,128)(2,1)S(1)} %get-tuple-element.47), channel_id=1, source_target_pairs={{0,3},{1,2},{2,1},{3,0},{4,7},{5,6},{6,5},{7,4},{8,11},{9,10},{10,... | collective-permute-start | bytes 393224 | tf_op jit(solution)/shard_map/ppermute | solution.py:238
  103.9 5.0 %collective-permute-start.28 = (bf16[16,1280]{1,0:T(8,128)(2,1)S(1)}, bf16[16,1280]{1,0:T(8,128)(2,1)S(1)}, u32[]{:S(2)}, u32[]{:S(2)}) collective-permute-start(bf16[16,1280]{1,0:T(8,128)(2,1)S(1)} %get-tuple-element.49), channel_id=1, source_target_pairs={{0,1},{1,0},{2,3},{3,2},{4,5},{5,4},{6,7},{7,6},{8,9},{9,8},{10,11... | collective-permute-start | bytes 122888 | tf_op jit(solution)/shard_map/ppermute | solution.py:238
  106.4 4.9 %collective-permute-start.29 = (bf16[16,1280]{1,0:T(8,128)(2,1)S(1)}, bf16[16,1280]{1,0:T(8,128)(2,1)S(1)}, u32[]{:S(2)}, u32[]{:S(2)}) collective-permute-start(bf16[16,1280]{1,0:T(8,128)(2,1)S(1)} %get-tuple-element.50), channel_id=1, source_target_pairs={{0,2},{1,3},{2,0},{3,1},{4,6},{5,7},{6,4},{7,5},{8,10},{9,11},{10,... | collective-permute-start | bytes 122888 | tf_op jit(solution)/shard_map/ppermute | solution.py:238
  107.0 5.8 %collective-permute-start.30 = (bf16[16,1280]{1,0:T(8,128)(2,1)S(1)}, bf16[16,1280]{1,0:T(8,128)(2,1)S(1)}, u32[]{:S(2)}, u32[]{:S(2)}) collective-permute-start(bf16[16,1280]{1,0:T(8,128)(2,1)S(1)} %get-tuple-element.51), channel_id=1, source_target_pairs={{0,3},{1,2},{2,1},{3,0},{4,7},{5,6},{6,5},{7,4},{8,11},{9,10},{10,... | collective-permute-start | bytes 122888 | tf_op jit(solution)/shard_map/ppermute | solution.py:238
  113.3 4.1 %collective-permute-start.31 = (bf16[16,1280]{1,0:T(8,128)(2,1)S(1)}, bf16[16,1280]{1,0:T(8,128)(2,1)S(1)}, u32[]{:S(2)}, u32[]{:S(2)}) collective-permute-start(bf16[16,1280]{1,0:T(8,128)(2,1)S(1)} %shard_map.103.refs_0_), channel_id=1, source_target_pairs={{0,8},{4,12},{8,0},{12,4},{16,24},{20,28},{24,16},{28,20},{1,9},{5... | collective-permute-start | bytes 122888 | tf_op jit(solution)/shard_map/ppermute | solution.py:235
  113.9 4.0 %collective-permute-start.32 = (bf16[16,1280]{1,0:T(8,128)(2,1)S(1)}, bf16[16,1280]{1,0:T(8,128)(2,1)S(1)}, u32[]{:S(2)}, u32[]{:S(2)}) collective-permute-start(bf16[16,1280]{1,0:T(8,128)(2,1)S(1)} %shard_map.103.refs_0_), channel_id=1, source_target_pairs={{0,16},{4,20},{8,24},{12,28},{16,0},{20,4},{24,8},{28,12},{1,17},{... | collective-permute-start | bytes 122888 | tf_op jit(solution)/shard_map/ppermute | solution.py:235
  115.0 4.9 %collective-permute-start.33 = (bf16[16,1280]{1,0:T(8,128)(2,1)S(1)}, bf16[16,1280]{1,0:T(8,128)(2,1)S(1)}, u32[]{:S(2)}, u32[]{:S(2)}) collective-permute-start(bf16[16,1280]{1,0:T(8,128)(2,1)S(1)} %shard_map.103.refs_0_), channel_id=1, source_target_pairs={{0,24},{4,28},{8,16},{12,20},{16,8},{20,12},{24,0},{28,4},{1,25},{... | collective-permute-start | bytes 122888 | tf_op jit(solution)/shard_map/ppermute | solution.py:235
  119.9 1.5 %collective-permute-start.34 = (bf16[4,16,1280]{2,1,0:T(8,128)(2,1)S(1)}, bf16[4,16,1280]{2,1,0:T(8,128)(2,1)S(1)}, u32[]{:S(2)}, u32[]{:S(2)}) collective-permute-start(bf16[4,16,1280]{2,1,0:T(8,128)(2,1)S(1)} %pad_maximum_fusion.1), channel_id=1, source_target_pairs={{0,4},{4,0},{8,12},{12,8},{16,20},{20,16},{24,28},{28,24},{1,5},{5... | collective-permute-start | bytes 491528 | tf_op jit(solution)/shard_map/ppermute | solution.py:232

commit v6 on v5

--- a/solution.py
+++ b/solution.py
@@ -56,6 +56,10 @@
     total = jnp.max(seg[...].astype(F32)) + 1.0
     row = lax.broadcasted_iota(jnp.int32, pooled.shape, 0)
     out[...] = jnp.where(row == slots - 1, total, pooled).astype(BF16)
+
+
+def across(k, core):
+    return jnp.where((core == 1) & ((k == 1) | (k == 2)), 3 - k, k)
 
 
 def pack_kernel(chips, slots, ids, *refs):
@@ -71,13 +75,13 @@
     block = lane // slots
     patch = lane - block * slots
     part = block // chips
-    place = 2 * ((block - part * chips) ^ q) + (part ^ c)
+    place = 2 * (across(block - part * chips, part ^ c) ^ q) + (part ^ c)
     start = jnp.zeros((1, lanes), F32)
     total = jnp.zeros((1, lanes), F32)
     own = jnp.zeros((1, lanes), F32)
     for b in range(blocks):
         count = packed[(b + 1) * slots - 1 : (b + 1) * slots, 0:lanes].astype(F32)
-        where = 2 * ((b % chips) ^ q) + ((b // chips) ^ c)
+        where = 2 * (across(b % chips, (b // chips) ^ c) ^ q) + ((b // chips) ^ c)
         start += jnp.where(place > where, count, 0.0)
         total += jnp.where(block == b, count, 0.0)
         own += jnp.where(2 * q + c > where, count, 0.0)
@@ -194,8 +198,8 @@
     start, weights, dec, out, rows = refs[chips + 1 :]
     q, c = ids[0], ids[1]
     for k in range(chips):
-        rows[2 * (q ^ k) + c] = mine[k][...]
-        rows[2 * (q ^ k) + 1 - c] = theirs[k]
+        rows[2 * (q ^ across(k, c)) + c] = mine[k][...]
+        rows[2 * (q ^ across(k, 1 - c)) + 1 - c] = theirs[k]
     every = rows[...].reshape(2 * chips * ROWS, rows.shape[2])
     heads = dec.shape[1] // HD
     slots = weights.shape[1] // heads
@@ -237,8 +241,12 @@
     def plane(a, k):
         return lax.ppermute(a, "mp", [(i, i ^ k) for i in range(groups)])
 
-    def chips_of(arrays):
-        return [chip(a, k + 1) for k, a in enumerate(arrays)]
+    def chip_by_core(a, k):
+        other = 3 - k if k in (1, 2) and chips > 2 else k
+        return lax.ppermute(a, "seq", [(i, i ^ (2 * (other if i % 2 else k))) for i in range(seq)])
+
+    def chips_of(arrays, move=chip):
+        return [move(a, k + 1) for k, a in enumerate(arrays)]
 
     def plane_by_core(a, k):
         other = 3 - k if k in (1, 2) and groups > 2 else k
@@ -257,7 +265,7 @@
         enc_states,
     )
     gate_b, up_b = sibling(w_gate), sibling(w_up)
-    gathered = [pooled] + chips_of([pooled] * (chips - 1))
+    gathered = [pooled] + chips_of([pooled] * (chips - 1), chip_by_core)
     theirs = sibling(jnp.concatenate(gathered, axis=0))
     packed, start = call(
         functools.partial(pack_kernel, chips, slots),
@@ -348,7 +356,7 @@
     )
     outs = [outs[0]] + planes_of(outs[1:])
     [outputs] = call(add_kernel, [shape((ROWS, width))], ids, *outs)
-    outputs = [outputs] + chips_of([outputs] * (chips - 1))
+    outputs = [outputs] + chips_of([outputs] * (chips - 1), chip_by_core)
     theirs = sibling(jnp.stack(outputs))
     [decoded] = call(
         functools.partial(mix_kernel, chips),

time: 123 us -> 123 us (level)
    ppermute x18 -> x12, starting transfers between devices: 23.5 us -> 15.1 us  [chip(): return lax.ppermute(a, 'seq', [(i, i ^ 2 * k) for i in range(seq)])]
    ppermute x0 -> x6, waiting for transfers between devices: none -> 8.26 us  [chip_by_core(): lax.ppermute(a, 'seq', [(i, i ^ 2 * (other if i % 2 else k)) for i in ran...]
    ppermute x0 -> x6, starting transfers between devices: none -> 8.07 us  [chip_by_core(): lax.ppermute(a, 'seq', [(i, i ^ 2 * (other if i % 2 else k)) for i in ran...]
    ppermute x18 -> x12, waiting for transfers between devices: 28.8 us -> 20.9 us  [chip(): return lax.ppermute(a, 'seq', [(i, i ^ 2 * k) for i in range(seq)])]
  transfers between devices with their start and end apart: 35 -> 35, of which waited for: 25 -> 24; matrix products, arithmetic and copies ran while one was open for 0% -> 0% of each run, Pallas kernels for 13% -> 13%
where the time goes in v6:
time: 123 us
  waiting for transfers between devices  53.6 us (44%)
  starting transfers between devices  42.3 us (34%)
  Pallas kernels  23.4 us (19%)
  local copies, waits for them, and re-layouts  3.66 us (3%)
    pallas_call x14, Pallas kernels, call(): pl.pallas_call(run, out_shape=list(outs), in_specs=[SMEM] + [VMEM] * n +...  23.4 us
    ppermute x12, waiting for transfers between devices, chip(): return lax.ppermute(a, 'seq', [(i, i ^ 2 * k) for i in range(seq)])  20.9 us
    ppermute x9, waiting for transfers between devices, plane(): return lax.ppermute(a, 'mp', [(i, i ^ k) for i in range(groups)])  15.2 us
    ppermute x12, starting transfers between devices, chip(): return lax.ppermute(a, 'seq', [(i, i ^ 2 * k) for i in range(seq)])  15.1 us
    ppermute x9, starting transfers between devices, plane(): return lax.ppermute(a, 'mp', [(i, i ^ k) for i in range(groups)])  13.8 us
    ppermute x6, waiting for transfers between devices, chip_by_core(): lax.ppermute(a, 'seq', [(i, i ^ 2 * (other if i % 2 else k)) for i in ran...  8.26 us
    ppermute x6, starting transfers between devices, chip_by_core(): lax.ppermute(a, 'seq', [(i, i ^ 2 * (other if i % 2 else k)) for i in ran...  8.07 us
    ppermute x3, waiting for transfers between devices, plane_by_core(): return lax.ppermute(a, ('seq', 'mp'), pairs)  6.26 us
  transfers between devices with their start and end apart: 35, of which 24 were waited for; matrix products, arithmetic and copies ran while one was open for 0% of the time, Pallas kernels for 13%

profile of v6, /device:TPU:0, one launch (start us, length us, event | category | flops | bytes accessed | tf_op | source)
XLA Modules:
  0.0 123.2 jit_solution(11733481368418711091)
XLA Ops:
  0.6 1.0 copy-done.5
  1.6 0.7 copy-done.8
  2.3 0.8 shard_map.91.refs_0_
  3.1 3.0 %collective-permute-start = (bf16[32,1280]{1,0:T(8,128)(2,1)S(1)}, bf16[32,1280]{1,0:T(8,128)(2,1)S(1)}, u32[]{:S(2)}, u32[]{:S(2)}) collective-permute-start(bf16[32,1280]{1,0:T(8,128)(2,1)S(1)} %shard_map.91.refs_0_), channel_id=1, source_target_pairs={{0,8},{4,20},{8,0},{12,28},{16,24},{20,4},{24,16},{28,12},{1,9},{5... | collective-permute-start | bytes 245768 | tf_op jit(solution)/shard_map/ppermute | solution.py:246
  6.0 1.5 %collective-permute-start.1 = (bf16[32,1280]{1,0:T(8,128)(2,1)S(1)}, bf16[32,1280]{1,0:T(8,128)(2,1)S(1)}, u32[]{:S(2)}, u32[]{:S(2)}) collective-permute-start(bf16[32,1280]{1,0:T(8,128)(2,1)S(1)} %shard_map.91.refs_0_), channel_id=1, source_target_pairs={{0,16},{4,12},{8,24},{12,4},{16,0},{20,28},{24,8},{28,20},{1,17},{... | collective-permute-start | bytes 245768 | tf_op jit(solution)/shard_map/ppermute | solution.py:246
  7.6 1.0 collective-permute-done.refs_1_
  8.6 1.9 %collective-permute-done.1.refs_2_ = bf16[32,1280]{1,0:T(8,128)(2,1)S(1)} collective-permute-done((bf16[32,1280]{1,0:T(8,128)(2,1)S(1)}, bf16[32,1280]{1,0:T(8,128)(2,1)S(1)}, u32[]{:S(2)}, u32[]{:S(2)}) %collective-permute-start.1) | collective-permute-done | bytes 81952 | tf_op jit(solution)/shard_map/ppermute | solution.py:246
  10.5 2.4 %collective-permute-done.2.refs_3_ = bf16[32,1280]{1,0:T(8,128)(2,1)S(1)} collective-permute-done((bf16[32,1280]{1,0:T(8,128)(2,1)S(1)}, bf16[32,1280]{1,0:T(8,128)(2,1)S(1)}, u32[]{:S(2)}, u32[]{:S(2)}) %collective-permute-start.2) | collective-permute-done | bytes 81952 | tf_op jit(solution)/shard_map/ppermute | solution.py:246
  13.0 1.6 %collective-permute-done.3.refs_4_ = bf16[128,1280]{1,0:T(8,128)(2,1)S(1)} collective-permute-done((bf16[128,1280]{1,0:T(8,128)(2,1)S(1)}, bf16[128,1280]{1,0:T(8,128)(2,1)S(1)}, u32[]{:S(2)}, u32[]{:S(2)}) %collective-permute-start.3) | collective-permute-done | bytes 327712 | tf_op jit(solution)/shard_map/ppermute | solution.py:236
  14.6 0.8 shard_map.92
  15.6 1.6 %collective-permute-start.6 = (bf16[16,1280]{1,0:T(8,128)(2,1)S(1)}, bf16[16,1280]{1,0:T(8,128)(2,1)S(1)}, u32[]{:S(2)}, u32[]{:S(2)}) collective-permute-start(bf16[16,1280]{1,0:T(8,128)(2,1)S(1)} %get-tuple-element.30.refs_0_), channel_id=1, source_target_pairs={{0,1},{1,0},{2,3},{3,2},{4,5},{5,4},{6,7},{7,6},{8,9},{9,8},{10,11... | collective-permute-start | bytes 122888 | tf_op jit(solution)/shard_map/ppermute | solution.py:242
  17.2 2.6 %collective-permute-start.7 = (bf16[16,1280]{1,0:T(8,128)(2,1)S(1)}, bf16[16,1280]{1,0:T(8,128)(2,1)S(1)}, u32[]{:S(2)}, u32[]{:S(2)}) collective-permute-start(bf16[16,1280]{1,0:T(8,128)(2,1)S(1)} %get-tuple-element.30.refs_0_), channel_id=1, source_target_pairs={{0,2},{1,3},{2,0},{3,1},{4,6},{5,7},{6,4},{7,5},{8,10},{9,11},{10,... | collective-permute-start | bytes 122888 | tf_op jit(solution)/shard_map/ppermute | solution.py:242
  20.0 2.8 %collective-permute-done.7.refs_2_ = bf16[16,1280]{1,0:T(8,128)(2,1)S(1)} collective-permute-done((bf16[16,1280]{1,0:T(8,128)(2,1)S(1)}, bf16[16,1280]{1,0:T(8,128)(2,1)S(1)}, u32[]{:S(2)}, u32[]{:S(2)}) %collective-permute-start.7) | collective-permute-done | bytes 40992 | tf_op jit(solution)/shard_map/ppermute | solution.py:242
  22.9 2.7 %collective-permute-done.8.refs_3_ = bf16[16,1280]{1,0:T(8,128)(2,1)S(1)} collective-permute-done((bf16[16,1280]{1,0:T(8,128)(2,1)S(1)}, bf16[16,1280]{1,0:T(8,128)(2,1)S(1)}, u32[]{:S(2)}, u32[]{:S(2)}) %collective-permute-start.8) | collective-permute-done | bytes 40992 | tf_op jit(solution)/shard_map/ppermute | solution.py:242
  25.6 1.1 shard_map.93.refs_0_.refs_4_
  26.8 1.3 %collective-permute-start.10 = (bf16[64,1024]{1,0:T(8,128)(2,1)S(1)}, bf16[64,1024]{1,0:T(8,128)(2,1)S(1)}, u32[]{:S(2)}, u32[]{:S(2)}) collective-permute-start(bf16[64,1024]{1,0:T(8,128)(2,1)S(1)} %shard_map.93.refs_0_.refs_4_), channel_id=1, source_target_pairs={{0,2},{1,3},{2,0},{3,1},{4,5},{5,4},{6,7},{7,6},{8,10},{9,11},{10,... | collective-permute-start | bytes 393224 | tf_op jit(solution)/shard_map/ppermute | solution.py:254
  28.1 3.1 %collective-permute-start.11 = (bf16[64,1024]{1,0:T(8,128)(2,1)S(1)}, bf16[64,1024]{1,0:T(8,128)(2,1)S(1)}, u32[]{:S(2)}, u32[]{:S(2)}) collective-permute-start(bf16[64,1024]{1,0:T(8,128)(2,1)S(1)} %shard_map.93.refs_0_.refs_4_), channel_id=1, source_target_pairs={{0,3},{1,2},{2,1},{3,0},{4,7},{5,6},{6,5},{7,4},{8,11},{9,10},{10,... | collective-permute-start | bytes 393224 | tf_op jit(solution)/shard_map/ppermute | solution.py:254
  31.2 2.8 %collective-permute-done.9.refs_1_ = bf16[64,1024]{1,0:T(8,128)(2,1)S(1)} collective-permute-done((bf16[64,1024]{1,0:T(8,128)(2,1)S(1)}, bf16[64,1024]{1,0:T(8,128)(2,1)S(1)}, u32[]{:S(2)}, u32[]{:S(2)}) %collective-permute-start.9) | collective-permute-done | bytes 131104 | tf_op jit(solution)/shard_map/ppermute | solution.py:254
  33.9 3.5 %collective-permute-done.10.refs_2_ = bf16[64,1024]{1,0:T(8,128)(2,1)S(1)} collective-permute-done((bf16[64,1024]{1,0:T(8,128)(2,1)S(1)}, bf16[64,1024]{1,0:T(8,128)(2,1)S(1)}, u32[]{:S(2)}, u32[]{:S(2)}) %collective-permute-start.10) | collective-permute-done | bytes 131104 | tf_op jit(solution)/shard_map/ppermute | solution.py:254
  37.4 0.7 shard_map.94
  38.2 0.6 collective-permute-start.13
  38.8 1.1 collective-permute-start.14
  39.9 1.8 %collective-permute-start.12 = (bf16[2,64,512]{2,1,0:T(8,128)(2,1)S(1)}, bf16[2,64,512]{2,1,0:T(8,128)(2,1)S(1)}, u32[]{:S(2)}, u32[]{:S(2)}) collective-permute-start(bf16[2,64,512]{2,1,0:T(8,128)(2,1)S(1)} %get-tuple-element.32), channel_id=1, source_target_pairs={{0,24},{4,28},{8,16},{12,20},{16,8},{20,12},{24,0},{28,4},{1,25},{... | collective-permute-start | bytes 393224 | tf_op jit(solution)/shard_map/ppermute | solution.py:239
  41.7 1.8 %collective-permute-done.13.refs_0_ = bf16[2,64,512]{2,1,0:T(8,128)(2,1)S(1)} collective-permute-done((bf16[2,64,512]{2,1,0:T(8,128)(2,1)S(1)}, bf16[2,64,512]{2,1,0:T(8,128)(2,1)S(1)}, u32[]{:S(2)}, u32[]{:S(2)}) %collective-permute-start.13) | collective-permute-done | bytes 131104 | tf_op jit(solution)/shard_map/ppermute | solution.py:239
  43.5 0.7 collective-permute-done.14.refs_1_
  44.2 3.6 %shard_map.95 = (bf16[64,3584]{1,0:T(8,128)(2,1)}, bf16[64,3584]{1,0:T(8,128)(2,1)}) custom-call(s32[3]{0:T(128)S(1)} %pad_add_fusion.ids, bf16[2,64,512]{2,1,0:T(8,128)(2,1)S(1)} %collective-permute-done.13.refs_0_, bf16[2,64,512]{2,1,0:T(8,128)(2,1)S(1)} %collective-permute-done.14.refs_1_, bf16[512,1792]{1,0:T(8,128)(2,1)S(1)} %copy-done, ...), custom_call_target="tpu_custom_call" | custom-call | flops 939524096 | bytes 8519680 | tf_op jit(solution)/shard_map/pallas_call | solution.py:34
  47.8 3.0 %collective-permute-start.15 = (bf16[64,3584]{1,0:T(8,128)(2,1)}, bf16[64,3584]{1,0:T(8,128)(2,1)S(1)}, u32[]{:S(2)}, u32[]{:S(2)}) collective-permute-start(bf16[64,3584]{1,0:T(8,128)(2,1)} %get-tuple-element.36.refs_6_), channel_id=1, source_target_pairs={{0,8},{4,12},{8,0},{12,4},{16,24},{20,28},{24,16},{28,20},{1,9},{5... | collective-permute-start | bytes 1376264 | tf_op jit(solution)/shard_map/ppermute | solution.py:239
  50.8 1.1 collective-permute-start.16
  51.9 3.5 %shard_map.96 = (bf16[64,3584]{1,0:T(8,128)(2,1)}, bf16[64,3584]{1,0:T(8,128)(2,1)S(1)}) custom-call(s32[3]{0:T(128)S(1)} %pad_add_fusion.ids, bf16[2,64,512]{2,1,0:T(8,128)(2,1)S(1)} %collective-permute-done.12.refs_0_, bf16[2,64,512]{2,1,0:T(8,128)(2,1)S(1)} %get-tuple-element.33.refs_1_, bf16[512,1792]{1,0:T(8,128)(2,1)S(1)} %copy-done, ...), custom_call_target="tpu_custom_call" | custom-call | flops 939524096 | bytes 8519680 | tf_op jit(solution)/shard_map/pallas_call | solution.py:34
  55.3 0.8 copy-done.6
  56.7 2.1 %shard_map.97.refs_5_.refs_6_ = bf16[192,320]{1,0:T(8,128)(2,1)S(1)} custom-call(s32[3]{0:T(128)S(1)} %pad_add_fusion.ids, s32[192,1]{1,0:T(8,128)S(1)} %copy.10.refs_0_, bf16[192,1280]{1,0:T(8,128)(2,1)S(1)} %copy-done.4, bf16[32,1280]{1,0:T(8,128)(2,1)S(1)} %pad.4.refs_2_), custom_call_target="tpu_custom_call" | custom-call | bytes 697088 | tf_op jit(solution)/shard_map/pallas_call | solution.py:34
  58.7 3.1 %collective-permute-done.15.refs_2_ = bf16[64,3584]{1,0:T(8,128)(2,1)S(1)} collective-permute-done((bf16[64,3584]{1,0:T(8,128)(2,1)}, bf16[64,3584]{1,0:T(8,128)(2,1)S(1)}, u32[]{:S(2)}, u32[]{:S(2)}) %collective-permute-start.15) | collective-permute-done | bytes 458784 | tf_op jit(solution)/shard_map/ppermute | solution.py:239
  61.8 7.4 %collective-permute-done.16.refs_3_ = bf16[64,3584]{1,0:T(8,128)(2,1)S(1)} collective-permute-done((bf16[64,3584]{1,0:T(8,128)(2,1)}, bf16[64,3584]{1,0:T(8,128)(2,1)S(1)}, u32[]{:S(2)}, u32[]{:S(2)}) %collective-permute-start.16) | collective-permute-done | bytes 458784 | tf_op jit(solution)/shard_map/ppermute | solution.py:239
  69.2 1.0 copy-done.7
  70.2 1.0 shard_map.98.refs_0_
  71.7 0.9 collective-permute-start.20
  72.7 2.1 %collective-permute-start.21 = (bf16[64,1792]{1,0:T(8,128)(2,1)S(1)}, bf16[64,1792]{1,0:T(8,128)(2,1)S(1)}, u32[]{:S(2)}, u32[]{:S(2)}) collective-permute-start(bf16[64,1792]{1,0:T(8,128)(2,1)S(1)} %shard_map.98.refs_0_), channel_id=1, source_target_pairs={{0,24},{4,28},{8,16},{12,20},{16,8},{20,12},{24,0},{28,4},{1,25},{... | collective-permute-start | bytes 688136 | tf_op jit(solution)/shard_map/ppermute | solution.py:239
  74.8 2.5 %collective-permute-done.19.refs_0_ = bf16[64,1792]{1,0:T(8,128)(2,1)S(1)} collective-permute-done((bf16[64,1792]{1,0:T(8,128)(2,1)S(1)}, bf16[64,1792]{1,0:T(8,128)(2,1)S(1)}, u32[]{:S(2)}, u32[]{:S(2)}) %collective-permute-start.19) | collective-permute-done | bytes 229408 | tf_op jit(solution)/shard_map/ppermute | solution.py:239
  77.8 2.6 %collective-permute-done.21.refs_2_ = bf16[64,1792]{1,0:T(8,128)(2,1)S(1)} collective-permute-done((bf16[64,1792]{1,0:T(8,128)(2,1)S(1)}, bf16[64,1792]{1,0:T(8,128)(2,1)S(1)}, u32[]{:S(2)}, u32[]{:S(2)}) %collective-permute-start.21) | collective-permute-done | bytes 229408 | tf_op jit(solution)/shard_map/ppermute | solution.py:239
  80.4 2.9 %shard_map.100 = (bf16[2,64,512]{2,1,0:T(8,128)(2,1)S(1)}, bf16[2,64,512]{2,1,0:T(8,128)(2,1)S(1)}, bf16[2,64,512]{2,1,0:T(8,128)(2,1)S(1)}) custom-call(s32[3]{0:T(128)S(1)} %pad_add_fusion.ids, bf16[64,1792]{1,0:T(8,128)(2,1)S(1)} %collective-permute-done.19.refs_0_, bf16[64,1792]{1,0:T(8,128)(2,1)S(1)} %collective-permute-done.20.refs_1_, ...), custom_call_target="tpu_custom_call" | custom-call | flops 704643072 | bytes 4751360 | tf_op jit(solution)/shard_map/pallas_call | solution.py:34
  83.4 1.5 %collective-permute-start.22 = (bf16[2,64,512]{2,1,0:T(8,128)(2,1)S(1)}, bf16[2,64,512]{2,1,0:T(8,128)(2,1)S(1)}, u32[]{:S(2)}, u32[]{:S(2)}) collective-permute-start(bf16[2,64,512]{2,1,0:T(8,128)(2,1)S(1)} %get-tuple-element.41), channel_id=1, source_target_pairs={{0,8},{4,12},{8,0},{12,4},{16,24},{20,28},{24,16},{28,20},{1,9},{5... | collective-permute-start | bytes 393224 | tf_op jit(solution)/shard_map/ppermute | solution.py:239
  84.8 1.3 %collective-permute-start.23 = (bf16[2,64,512]{2,1,0:T(8,128)(2,1)S(1)}, bf16[2,64,512]{2,1,0:T(8,128)(2,1)S(1)}, u32[]{:S(2)}, u32[]{:S(2)}) collective-permute-start(bf16[2,64,512]{2,1,0:T(8,128)(2,1)S(1)} %get-tuple-element.42), channel_id=1, source_target_pairs={{0,16},{4,20},{8,24},{12,28},{16,0},{20,4},{24,8},{28,12},{1,17},{... | collective-permute-start | bytes 393224 | tf_op jit(solution)/shard_map/ppermute | solution.py:239
  86.2 0.7 collective-permute-start.24
  86.9 2.9 %shard_map.99.refs_0_ = bf16[2,64,512]{2,1,0:T(8,128)(2,1)S(1)} custom-call(s32[3]{0:T(128)S(1)} %pad_add_fusion.ids, bf16[64,1792]{1,0:T(8,128)(2,1)S(1)} %shard_map.98.refs_0_, bf16[1792,512]{1,0:T(8,128)(2,1)} %refs_3_.1, bf16[1792,512]{1,0:T(8,128)(2,1)} %collective-permute-done.18.refs_2_.refs_4_), custom_call_target="tpu_custom_call" | custom-call | flops 234881024 | bytes 4030464 | tf_op jit(solution)/shard_map/pallas_call | solution.py:34
  89.8 2.3 %collective-permute-done.24.refs_3_ = bf16[2,64,512]{2,1,0:T(8,128)(2,1)S(1)} collective-permute-done((bf16[2,64,512]{2,1,0:T(8,128)(2,1)S(1)}, bf16[2,64,512]{2,1,0:T(8,128)(2,1)S(1)}, u32[]{:S(2)}, u32[]{:S(2)}) %collective-permute-start.24) | collective-permute-done | bytes 131104 | tf_op jit(solution)/shard_map/ppermute | solution.py:239
  92.1 0.6 shard_map.101
  92.8 0.7 collective-permute-start.26
  93.4 3.7 %collective-permute-start.27 = (bf16[64,1024]{1,0:T(8,128)(2,1)S(1)}, bf16[64,1024]{1,0:T(8,128)(2,1)S(1)}, u32[]{:S(2)}, u32[]{:S(2)}) collective-permute-start(bf16[64,1024]{1,0:T(8,128)(2,1)S(1)} %get-tuple-element.47), channel_id=1, source_target_pairs={{0,3},{1,2},{2,1},{3,0},{4,7},{5,6},{6,5},{7,4},{8,11},{9,10},{10,... | collective-permute-start | bytes 393224 | tf_op jit(solution)/shard_map/ppermute | solution.py:242
  97.1 2.5 %collective-permute-done.25.refs_1_ = bf16[64,1024]{1,0:T(8,128)(2,1)S(1)} collective-permute-done((bf16[64,1024]{1,0:T(8,128)(2,1)S(1)}, bf16[64,1024]{1,0:T(8,128)(2,1)S(1)}, u32[]{:S(2)}, u32[]{:S(2)}) %collective-permute-start.25) | collective-permute-done | bytes 131104 | tf_op jit(solution)/shard_map/ppermute | solution.py:242
  99.6 3.2 %collective-permute-done.27.refs_3_ = bf16[64,1024]{1,0:T(8,128)(2,1)S(1)} collective-permute-done((bf16[64,1024]{1,0:T(8,128)(2,1)S(1)}, bf16[64,1024]{1,0:T(8,128)(2,1)S(1)}, u32[]{:S(2)}, u32[]{:S(2)}) %collective-permute-start.27) | collective-permute-done | bytes 131104 | tf_op jit(solution)/shard_map/ppermute | solution.py:242
  102.8 1.1 shard_map.102
  103.9 2.5 %collective-permute-start.28 = (bf16[16,1280]{1,0:T(8,128)(2,1)S(1)}, bf16[16,1280]{1,0:T(8,128)(2,1)S(1)}, u32[]{:S(2)}, u32[]{:S(2)}) collective-permute-start(bf16[16,1280]{1,0:T(8,128)(2,1)S(1)} %get-tuple-element.49), channel_id=1, source_target_pairs={{0,1},{1,0},{2,3},{3,2},{4,5},{5,4},{6,7},{7,6},{8,9},{9,8},{10,11... | collective-permute-start | bytes 122888 | tf_op jit(solution)/shard_map/ppermute | solution.py:242
  106.5 0.6 collective-permute-start.29
  107.0 1.9 %collective-permute-start.30 = (bf16[16,1280]{1,0:T(8,128)(2,1)S(1)}, bf16[16,1280]{1,0:T(8,128)(2,1)S(1)}, u32[]{:S(2)}, u32[]{:S(2)}) collective-permute-start(bf16[16,1280]{1,0:T(8,128)(2,1)S(1)} %get-tuple-element.51), channel_id=1, source_target_pairs={{0,3},{1,2},{2,1},{3,0},{4,7},{5,6},{6,5},{7,4},{8,11},{9,10},{10,... | collective-permute-start | bytes 122888 | tf_op jit(solution)/shard_map/ppermute | solution.py:242
  108.9 2.5 %collective-permute-done.29.refs_2_ = bf16[16,1280]{1,0:T(8,128)(2,1)S(1)} collective-permute-done((bf16[16,1280]{1,0:T(8,128)(2,1)S(1)}, bf16[16,1280]{1,0:T(8,128)(2,1)S(1)}, u32[]{:S(2)}, u32[]{:S(2)}) %collective-permute-start.29) | collective-permute-done | bytes 40992 | tf_op jit(solution)/shard_map/ppermute | solution.py:242
  111.4 1.5 %collective-permute-done.30.refs_3_ = bf16[16,1280]{1,0:T(8,128)(2,1)S(1)} collective-permute-done((bf16[16,1280]{1,0:T(8,128)(2,1)S(1)}, bf16[16,1280]{1,0:T(8,128)(2,1)S(1)}, u32[]{:S(2)}, u32[]{:S(2)}) %collective-permute-start.30) | collective-permute-done | bytes 40992 | tf_op jit(solution)/shard_map/ppermute | solution.py:242
  112.8 0.6 shard_map.103.refs_0_
  113.4 0.7 collective-permute-start.31
  114.1 0.9 collective-permute-start.32
  115.0 2.0 %collective-permute-start.33 = (bf16[16,1280]{1,0:T(8,128)(2,1)S(1)}, bf16[16,1280]{1,0:T(8,128)(2,1)S(1)}, u32[]{:S(2)}, u32[]{:S(2)}) collective-permute-start(bf16[16,1280]{1,0:T(8,128)(2,1)S(1)} %shard_map.103.refs_0_), channel_id=1, source_target_pairs={{0,24},{4,28},{8,16},{12,20},{16,8},{20,12},{24,0},{28,4},{1,25},{... | collective-permute-start | bytes 122888 | tf_op jit(solution)/shard_map/ppermute | solution.py:246
  117.5 0.6 collective-permute-done.32.refs_2_
  118.1 1.8 %collective-permute-done.33.refs_3_ = bf16[16,1280]{1,0:T(8,128)(2,1)S(1)} collective-permute-done((bf16[16,1280]{1,0:T(8,128)(2,1)S(1)}, bf16[16,1280]{1,0:T(8,128)(2,1)S(1)}, u32[]{:S(2)}, u32[]{:S(2)}) %collective-permute-start.33) | collective-permute-done | bytes 40992 | tf_op jit(solution)/shard_map/ppermute | solution.py:246
  120.0 1.4 %collective-permute-done.34.refs_4_ = bf16[4,16,1280]{2,1,0:T(8,128)(2,1)S(1)} collective-permute-done((bf16[4,16,1280]{2,1,0:T(8,128)(2,1)S(1)}, bf16[4,16,1280]{2,1,0:T(8,128)(2,1)S(1)}, u32[]{:S(2)}, u32[]{:S(2)}) %collective-permute-start.34) | collective-permute-done | bytes 163872 | tf_op jit(solution)/shard_map/ppermute | solution.py:236
  121.4 1.8 %shard_map.104 = bf16[192,1280]{1,0:T(8,128)(2,1)} custom-call(s32[3]{0:T(128)S(1)} %pad_add_fusion.ids, bf16[16,1280]{1,0:T(8,128)(2,1)S(1)} %shard_map.103.refs_0_, bf16[16,1280]{1,0:T(8,128)(2,1)S(1)} %collective-permute-done.31.refs_1_, bf16[16,1280]{1,0:T(8,128)(2,1)S(1)} %collective-permute-done.32.refs_2_, ...), custom_call_target="tpu_custom_call" | custom-call | bytes 1437696 | tf_op jit(solution)/shard_map/pallas_call | solution.py:34
  (47 shorter events, 3.4 us)
Async XLA Ops:
  0.0 14.6 %collective-permute-start.4 = (bf16[512,1792]{1,0:T(8,128)(2,1)}, bf16[512,1792]{1,0:T(8,128)(2,1)S(1)}, u32[]{:S(2)}, u32[]{:S(2)}) collective-permute-start(bf16[512,1792]{1,0:T(8,128)(2,1)} %refs_2_.3), channel_id=1, source_target_pairs={{0,4},{4,0},{8,12},{12,8},{16,20},{20,16},{24,28},{28,24},{1,5},{5... | collective-permute-start | bytes 5505032 | tf_op jit(solution)/shard_map/ppermute | solution.py:236
  0.5 14.2 %collective-permute-start.5 = (bf16[512,1792]{1,0:T(8,128)(2,1)}, bf16[512,1792]{1,0:T(8,128)(2,1)}, u32[]{:S(2)}, u32[]{:S(2)}) collective-permute-start(bf16[512,1792]{1,0:T(8,128)(2,1)} %refs_4_.5), channel_id=1, source_target_pairs={{0,4},{4,0},{8,12},{12,8},{16,20},{20,16},{24,28},{28,24},{1,5},{5... | collective-permute-start | bytes 5505032 | tf_op jit(solution)/shard_map/ppermute | solution.py:236
  0.6 1.0 copy-start.5
  1.6 0.7 copy-start.8
  3.1 5.5 %collective-permute-start = (bf16[32,1280]{1,0:T(8,128)(2,1)S(1)}, bf16[32,1280]{1,0:T(8,128)(2,1)S(1)}, u32[]{:S(2)}, u32[]{:S(2)}) collective-permute-start(bf16[32,1280]{1,0:T(8,128)(2,1)S(1)} %shard_map.91.refs_0_), channel_id=1, source_target_pairs={{0,8},{4,20},{8,0},{12,28},{16,24},{20,4},{24,16},{28,12},{1,9},{5... | collective-permute-start | bytes 245768 | tf_op jit(solution)/shard_map/ppermute | solution.py:246
  6.0 4.4 %collective-permute-start.1 = (bf16[32,1280]{1,0:T(8,128)(2,1)S(1)}, bf16[32,1280]{1,0:T(8,128)(2,1)S(1)}, u32[]{:S(2)}, u32[]{:S(2)}) collective-permute-start(bf16[32,1280]{1,0:T(8,128)(2,1)S(1)} %shard_map.91.refs_0_), channel_id=1, source_target_pairs={{0,16},{4,12},{8,24},{12,4},{16,0},{20,28},{24,8},{28,20},{1,17},{... | collective-permute-start | bytes 245768 | tf_op jit(solution)/shard_map/ppermute | solution.py:246
  7.6 5.3 %collective-permute-start.2 = (bf16[32,1280]{1,0:T(8,128)(2,1)S(1)}, bf16[32,1280]{1,0:T(8,128)(2,1)S(1)}, u32[]{:S(2)}, u32[]{:S(2)}) collective-permute-start(bf16[32,1280]{1,0:T(8,128)(2,1)S(1)} %shard_map.91.refs_0_), channel_id=1, source_target_pairs={{0,24},{4,28},{8,16},{12,20},{16,8},{20,12},{24,0},{28,4},{1,25},{... | collective-permute-start | bytes 245768 | tf_op jit(solution)/shard_map/ppermute | solution.py:246
  12.9 12.7 %copy-start.2 = (bf16[1280,1024]{1,0:T(8,128)(2,1)S(1)}, bf16[1280,1024]{1,0:T(8,128)(2,1)}, u32[]{:S(2)}) copy-start(bf16[1280,1024]{1,0:T(8,128)(2,1)} %refs_4_.3) | copy-start | bytes 7864324
  12.9 1.7 %collective-permute-start.3 = (bf16[128,1280]{1,0:T(8,128)(2,1)S(1)}, bf16[128,1280]{1,0:T(8,128)(2,1)S(1)}, u32[]{:S(2)}, u32[]{:S(2)}) collective-permute-start(bf16[128,1280]{1,0:T(8,128)(2,1)S(1)} %pad_maximum_fusion), channel_id=1, source_target_pairs={{0,4},{4,0},{8,12},{12,8},{16,20},{20,16},{24,28},{28,24},{1,5},{5... | collective-permute-start | bytes 983048 | tf_op jit(solution)/shard_map/ppermute | solution.py:236
  14.6 29.6 %copy-start.1 = (bf16[512,1792]{1,0:T(8,128)(2,1)S(1)}, bf16[512,1792]{1,0:T(8,128)(2,1)}, u32[]{:S(2)}) copy-start(bf16[512,1792]{1,0:T(8,128)(2,1)} %refs_4_.5) | copy-start | bytes 5505028
  15.4 28.8 %copy-start = (bf16[512,1792]{1,0:T(8,128)(2,1)S(1)}, bf16[512,1792]{1,0:T(8,128)(2,1)}, u32[]{:S(2)}) copy-start(bf16[512,1792]{1,0:T(8,128)(2,1)} %refs_2_.3) | copy-start | bytes 5505028
  15.4 65.0 %collective-permute-start.18 = (bf16[1792,512]{1,0:T(8,128)(2,1)}, bf16[1792,512]{1,0:T(8,128)(2,1)}, u32[]{:S(2)}, u32[]{:S(2)}) collective-permute-start(bf16[1792,512]{1,0:T(8,128)(2,1)} %refs_3_.1), channel_id=1, source_target_pairs={{0,4},{4,0},{8,12},{12,8},{16,20},{20,16},{24,28},{28,24},{1,5},{5... | collective-permute-start | bytes 5505032 | tf_op jit(solution)/shard_map/ppermute | solution.py:236
  15.6 4.4 %collective-permute-start.6 = (bf16[16,1280]{1,0:T(8,128)(2,1)S(1)}, bf16[16,1280]{1,0:T(8,128)(2,1)S(1)}, u32[]{:S(2)}, u32[]{:S(2)}) collective-permute-start(bf16[16,1280]{1,0:T(8,128)(2,1)S(1)} %get-tuple-element.30.refs_0_), channel_id=1, source_target_pairs={{0,1},{1,0},{2,3},{3,2},{4,5},{5,4},{6,7},{7,6},{8,9},{9,8},{10,11... | collective-permute-start | bytes 122888 | tf_op jit(solution)/shard_map/ppermute | solution.py:242
  17.2 5.7 %collective-permute-start.7 = (bf16[16,1280]{1,0:T(8,128)(2,1)S(1)}, bf16[16,1280]{1,0:T(8,128)(2,1)S(1)}, u32[]{:S(2)}, u32[]{:S(2)}) collective-permute-start(bf16[16,1280]{1,0:T(8,128)(2,1)S(1)} %get-tuple-element.30.refs_0_), channel_id=1, source_target_pairs={{0,2},{1,3},{2,0},{3,1},{4,6},{5,7},{6,4},{7,5},{8,10},{9,11},{10,... | collective-permute-start | bytes 122888 | tf_op jit(solution)/shard_map/ppermute | solution.py:242
  19.8 5.8 %collective-permute-start.8 = (bf16[16,1280]{1,0:T(8,128)(2,1)S(1)}, bf16[16,1280]{1,0:T(8,128)(2,1)S(1)}, u32[]{:S(2)}, u32[]{:S(2)}) collective-permute-start(bf16[16,1280]{1,0:T(8,128)(2,1)S(1)} %get-tuple-element.30.refs_0_), channel_id=1, source_target_pairs={{0,3},{1,2},{2,1},{3,0},{4,7},{5,6},{6,5},{7,4},{8,11},{9,10},{10,... | collective-permute-start | bytes 122888 | tf_op jit(solution)/shard_map/ppermute | solution.py:242
  26.7 7.2 %collective-permute-start.9 = (bf16[64,1024]{1,0:T(8,128)(2,1)S(1)}, bf16[64,1024]{1,0:T(8,128)(2,1)S(1)}, u32[]{:S(2)}, u32[]{:S(2)}) collective-permute-start(bf16[64,1024]{1,0:T(8,128)(2,1)S(1)} %shard_map.93.refs_0_.refs_4_), channel_id=1, source_target_pairs={{0,1},{1,0},{2,3},{3,2},{4,6},{5,7},{6,4},{7,5},{8,9},{9,8},{10,11... | collective-permute-start | bytes 393224 | tf_op jit(solution)/shard_map/ppermute | solution.py:254
  26.8 10.6 %collective-permute-start.10 = (bf16[64,1024]{1,0:T(8,128)(2,1)S(1)}, bf16[64,1024]{1,0:T(8,128)(2,1)S(1)}, u32[]{:S(2)}, u32[]{:S(2)}) collective-permute-start(bf16[64,1024]{1,0:T(8,128)(2,1)S(1)} %shard_map.93.refs_0_.refs_4_), channel_id=1, source_target_pairs={{0,2},{1,3},{2,0},{3,1},{4,5},{5,4},{6,7},{7,6},{8,10},{9,11},{10,... | collective-permute-start | bytes 393224 | tf_op jit(solution)/shard_map/ppermute | solution.py:254
  28.1 9.3 %collective-permute-start.11 = (bf16[64,1024]{1,0:T(8,128)(2,1)S(1)}, bf16[64,1024]{1,0:T(8,128)(2,1)S(1)}, u32[]{:S(2)}, u32[]{:S(2)}) collective-permute-start(bf16[64,1024]{1,0:T(8,128)(2,1)S(1)} %shard_map.93.refs_0_.refs_4_), channel_id=1, source_target_pairs={{0,3},{1,2},{2,1},{3,0},{4,7},{5,6},{6,5},{7,4},{8,11},{9,10},{10,... | collective-permute-start | bytes 393224 | tf_op jit(solution)/shard_map/ppermute | solution.py:254
  38.2 5.4 %collective-permute-start.13 = (bf16[2,64,512]{2,1,0:T(8,128)(2,1)S(1)}, bf16[2,64,512]{2,1,0:T(8,128)(2,1)S(1)}, u32[]{:S(2)}, u32[]{:S(2)}) collective-permute-start(bf16[2,64,512]{2,1,0:T(8,128)(2,1)S(1)} %get-tuple-element.34), channel_id=1, source_target_pairs={{0,8},{4,12},{8,0},{12,4},{16,24},{20,28},{24,16},{28,20},{1,9},{5... | collective-permute-start | bytes 393224 | tf_op jit(solution)/shard_map/ppermute | solution.py:239
  38.8 5.5 %collective-permute-start.14 = (bf16[2,64,512]{2,1,0:T(8,128)(2,1)S(1)}, bf16[2,64,512]{2,1,0:T(8,128)(2,1)S(1)}, u32[]{:S(2)}, u32[]{:S(2)}) collective-permute-start(bf16[2,64,512]{2,1,0:T(8,128)(2,1)S(1)} %get-tuple-element.35), channel_id=1, source_target_pairs={{0,16},{4,20},{8,24},{12,28},{16,0},{20,4},{24,8},{28,12},{1,17},{... | collective-permute-start | bytes 393224 | tf_op jit(solution)/shard_map/ppermute | solution.py:239
  39.9 12.0 %collective-permute-start.12 = (bf16[2,64,512]{2,1,0:T(8,128)(2,1)S(1)}, bf16[2,64,512]{2,1,0:T(8,128)(2,1)S(1)}, u32[]{:S(2)}, u32[]{:S(2)}) collective-permute-start(bf16[2,64,512]{2,1,0:T(8,128)(2,1)S(1)} %get-tuple-element.32), channel_id=1, source_target_pairs={{0,24},{4,28},{8,16},{12,20},{16,8},{20,12},{24,0},{28,4},{1,25},{... | collective-permute-start | bytes 393224 | tf_op jit(solution)/shard_map/ppermute | solution.py:239
  47.8 14.0 %collective-permute-start.15 = (bf16[64,3584]{1,0:T(8,128)(2,1)}, bf16[64,3584]{1,0:T(8,128)(2,1)S(1)}, u32[]{:S(2)}, u32[]{:S(2)}) collective-permute-start(bf16[64,3584]{1,0:T(8,128)(2,1)} %get-tuple-element.36.refs_6_), channel_id=1, source_target_pairs={{0,8},{4,12},{8,0},{12,4},{16,24},{20,28},{24,16},{28,20},{1,9},{5... | collective-permute-start | bytes 1376264 | tf_op jit(solution)/shard_map/ppermute | solution.py:239
  50.8 18.4 %collective-permute-start.16 = (bf16[64,3584]{1,0:T(8,128)(2,1)}, bf16[64,3584]{1,0:T(8,128)(2,1)S(1)}, u32[]{:S(2)}, u32[]{:S(2)}) collective-permute-start(bf16[64,3584]{1,0:T(8,128)(2,1)} %get-tuple-element.38), channel_id=1, source_target_pairs={{0,16},{4,20},{8,24},{12,28},{16,0},{20,4},{24,8},{28,12},{1,17},{... | collective-permute-start | bytes 1376264 | tf_op jit(solution)/shard_map/ppermute | solution.py:239
  51.9 4.6 %copy-start.9 = (s32[192]{0:T(256)S(1)}, s32[192]{0:T(256)}, u32[]{:S(2)}) copy-start(s32[192]{0:T(256)} %param.11) | copy-start | bytes 2308
  51.9 4.7 %copy-start.10 = (bf16[31,1280]{1,0:T(8,128)(2,1)S(1)}, bf16[31,1280]{1,0:T(8,128)(2,1)}, u32[]{:S(2)}) copy-start(bf16[31,1280]{1,0:T(8,128)(2,1)} %param.12) | copy-start | bytes 238084
  51.9 4.8 %copy-start.4 = (bf16[192,1280]{1,0:T(8,128)(2,1)S(1)}, bf16[192,1280]{1,0:T(8,128)(2,1)}, u32[]{:S(2)}) copy-start(bf16[192,1280]{1,0:T(8,128)(2,1)} %refs_7_.1) | copy-start | bytes 1474564
  55.3 0.8 copy-start.6
  56.1 13.1 %collective-permute-start.17 = (bf16[64,3584]{1,0:T(8,128)(2,1)}, bf16[64,3584]{1,0:T(8,128)(2,1)S(1)}, u32[]{:S(2)}, u32[]{:S(2)}) collective-permute-start(bf16[64,3584]{1,0:T(8,128)(2,1)} %get-tuple-element.39), channel_id=1, source_target_pairs={{0,24},{4,28},{8,16},{12,20},{16,8},{20,12},{24,0},{28,4},{1,25},{... | collective-permute-start | bytes 1376264 | tf_op jit(solution)/shard_map/ppermute | solution.py:239
  69.2 1.0 copy-start.7
  71.3 6.1 %collective-permute-start.19 = (bf16[64,1792]{1,0:T(8,128)(2,1)S(1)}, bf16[64,1792]{1,0:T(8,128)(2,1)S(1)}, u32[]{:S(2)}, u32[]{:S(2)}) collective-permute-start(bf16[64,1792]{1,0:T(8,128)(2,1)S(1)} %shard_map.98.refs_0_), channel_id=1, source_target_pairs={{0,8},{4,12},{8,0},{12,4},{16,24},{20,28},{24,16},{28,20},{1,9},{5... | collective-permute-start | bytes 688136 | tf_op jit(solution)/shard_map/ppermute | solution.py:239
  71.7 6.0 %collective-permute-start.20 = (bf16[64,1792]{1,0:T(8,128)(2,1)S(1)}, bf16[64,1792]{1,0:T(8,128)(2,1)S(1)}, u32[]{:S(2)}, u32[]{:S(2)}) collective-permute-start(bf16[64,1792]{1,0:T(8,128)(2,1)S(1)} %shard_map.98.refs_0_), channel_id=1, source_target_pairs={{0,16},{4,20},{8,24},{12,28},{16,0},{20,4},{24,8},{28,12},{1,17},{... | collective-permute-start | bytes 688136 | tf_op jit(solution)/shard_map/ppermute | solution.py:239
  72.7 7.7 %collective-permute-start.21 = (bf16[64,1792]{1,0:T(8,128)(2,1)S(1)}, bf16[64,1792]{1,0:T(8,128)(2,1)S(1)}, u32[]{:S(2)}, u32[]{:S(2)}) collective-permute-start(bf16[64,1792]{1,0:T(8,128)(2,1)S(1)} %shard_map.98.refs_0_), channel_id=1, source_target_pairs={{0,24},{4,28},{8,16},{12,20},{16,8},{20,12},{24,0},{28,4},{1,25},{... | collective-permute-start | bytes 688136 | tf_op jit(solution)/shard_map/ppermute | solution.py:239
  83.4 6.4 %collective-permute-start.22 = (bf16[2,64,512]{2,1,0:T(8,128)(2,1)S(1)}, bf16[2,64,512]{2,1,0:T(8,128)(2,1)S(1)}, u32[]{:S(2)}, u32[]{:S(2)}) collective-permute-start(bf16[2,64,512]{2,1,0:T(8,128)(2,1)S(1)} %get-tuple-element.41), channel_id=1, source_target_pairs={{0,8},{4,12},{8,0},{12,4},{16,24},{20,28},{24,16},{28,20},{1,9},{5... | collective-permute-start | bytes 393224 | tf_op jit(solution)/shard_map/ppermute | solution.py:239
  84.8 5.0 %collective-permute-start.23 = (bf16[2,64,512]{2,1,0:T(8,128)(2,1)S(1)}, bf16[2,64,512]{2,1,0:T(8,128)(2,1)S(1)}, u32[]{:S(2)}, u32[]{:S(2)}) collective-permute-start(bf16[2,64,512]{2,1,0:T(8,128)(2,1)S(1)} %get-tuple-element.42), channel_id=1, source_target_pairs={{0,16},{4,20},{8,24},{12,28},{16,0},{20,4},{24,8},{28,12},{1,17},{... | collective-permute-start | bytes 393224 | tf_op jit(solution)/shard_map/ppermute | solution.py:239
  86.2 16.6 %copy-start.3 = (bf16[1024,1280]{1,0:T(8,128)(2,1)S(1)}, bf16[1024,1280]{1,0:T(8,128)(2,1)}, u32[]{:S(2)}) copy-start(bf16[1024,1280]{1,0:T(8,128)(2,1)} %refs_5_.1) | copy-start | bytes 7864324
  86.2 5.9 %collective-permute-start.24 = (bf16[2,64,512]{2,1,0:T(8,128)(2,1)S(1)}, bf16[2,64,512]{2,1,0:T(8,128)(2,1)S(1)}, u32[]{:S(2)}, u32[]{:S(2)}) collective-permute-start(bf16[2,64,512]{2,1,0:T(8,128)(2,1)S(1)} %get-tuple-element.43), channel_id=1, source_target_pairs={{0,24},{4,28},{8,16},{12,20},{16,8},{20,12},{24,0},{28,4},{1,25},{... | collective-permute-start | bytes 393224 | tf_op jit(solution)/shard_map/ppermute | solution.py:239
  92.7 7.0 %collective-permute-start.25 = (bf16[64,1024]{1,0:T(8,128)(2,1)S(1)}, bf16[64,1024]{1,0:T(8,128)(2,1)S(1)}, u32[]{:S(2)}, u32[]{:S(2)}) collective-permute-start(bf16[64,1024]{1,0:T(8,128)(2,1)S(1)} %get-tuple-element.45), channel_id=1, source_target_pairs={{0,1},{1,0},{2,3},{3,2},{4,5},{5,4},{6,7},{7,6},{8,9},{9,8},{10,11... | collective-permute-start | bytes 393224 | tf_op jit(solution)/shard_map/ppermute | solution.py:242
  92.8 6.9 %collective-permute-start.26 = (bf16[64,1024]{1,0:T(8,128)(2,1)S(1)}, bf16[64,1024]{1,0:T(8,128)(2,1)S(1)}, u32[]{:S(2)}, u32[]{:S(2)}) collective-permute-start(bf16[64,1024]{1,0:T(8,128)(2,1)S(1)} %get-tuple-element.46), channel_id=1, source_target_pairs={{0,2},{1,3},{2,0},{3,1},{4,6},{5,7},{6,4},{7,5},{8,10},{9,11},{10,... | collective-permute-start | bytes 393224 | tf_op jit(solution)/shard_map/ppermute | solution.py:242
  93.4 9.4 %collective-permute-start.27 = (bf16[64,1024]{1,0:T(8,128)(2,1)S(1)}, bf16[64,1024]{1,0:T(8,128)(2,1)S(1)}, u32[]{:S(2)}, u32[]{:S(2)}) collective-permute-start(bf16[64,1024]{1,0:T(8,128)(2,1)S(1)} %get-tuple-element.47), channel_id=1, source_target_pairs={{0,3},{1,2},{2,1},{3,0},{4,7},{5,6},{6,5},{7,4},{8,11},{9,10},{10,... | collective-permute-start | bytes 393224 | tf_op jit(solution)/shard_map/ppermute | solution.py:242
  103.9 5.0 %collective-permute-start.28 = (bf16[16,1280]{1,0:T(8,128)(2,1)S(1)}, bf16[16,1280]{1,0:T(8,128)(2,1)S(1)}, u32[]{:S(2)}, u32[]{:S(2)}) collective-permute-start(bf16[16,1280]{1,0:T(8,128)(2,1)S(1)} %get-tuple-element.49), channel_id=1, source_target_pairs={{0,1},{1,0},{2,3},{3,2},{4,5},{5,4},{6,7},{7,6},{8,9},{9,8},{10,11... | collective-permute-start | bytes 122888 | tf_op jit(solution)/shard_map/ppermute | solution.py:242
  106.5 4.9 %collective-permute-start.29 = (bf16[16,1280]{1,0:T(8,128)(2,1)S(1)}, bf16[16,1280]{1,0:T(8,128)(2,1)S(1)}, u32[]{:S(2)}, u32[]{:S(2)}) collective-permute-start(bf16[16,1280]{1,0:T(8,128)(2,1)S(1)} %get-tuple-element.50), channel_id=1, source_target_pairs={{0,2},{1,3},{2,0},{3,1},{4,6},{5,7},{6,4},{7,5},{8,10},{9,11},{10,... | collective-permute-start | bytes 122888 | tf_op jit(solution)/shard_map/ppermute | solution.py:242
  107.0 5.8 %collective-permute-start.30 = (bf16[16,1280]{1,0:T(8,128)(2,1)S(1)}, bf16[16,1280]{1,0:T(8,128)(2,1)S(1)}, u32[]{:S(2)}, u32[]{:S(2)}) collective-permute-start(bf16[16,1280]{1,0:T(8,128)(2,1)S(1)} %get-tuple-element.51), channel_id=1, source_target_pairs={{0,3},{1,2},{2,1},{3,0},{4,7},{5,6},{6,5},{7,4},{8,11},{9,10},{10,... | collective-permute-start | bytes 122888 | tf_op jit(solution)/shard_map/ppermute | solution.py:242
  113.4 4.1 %collective-permute-start.31 = (bf16[16,1280]{1,0:T(8,128)(2,1)S(1)}, bf16[16,1280]{1,0:T(8,128)(2,1)S(1)}, u32[]{:S(2)}, u32[]{:S(2)}) collective-permute-start(bf16[16,1280]{1,0:T(8,128)(2,1)S(1)} %shard_map.103.refs_0_), channel_id=1, source_target_pairs={{0,8},{4,20},{8,0},{12,28},{16,24},{20,4},{24,16},{28,12},{1,9},{5... | collective-permute-start | bytes 122888 | tf_op jit(solution)/shard_map/ppermute | solution.py:246
  114.1 4.0 %collective-permute-start.32 = (bf16[16,1280]{1,0:T(8,128)(2,1)S(1)}, bf16[16,1280]{1,0:T(8,128)(2,1)S(1)}, u32[]{:S(2)}, u32[]{:S(2)}) collective-permute-start(bf16[16,1280]{1,0:T(8,128)(2,1)S(1)} %shard_map.103.refs_0_), channel_id=1, source_target_pairs={{0,16},{4,12},{8,24},{12,4},{16,0},{20,28},{24,8},{28,20},{1,17},{... | collective-permute-start | bytes 122888 | tf_op jit(solution)/shard_map/ppermute | solution.py:246
  115.0 4.9 %collective-permute-start.33 = (bf16[16,1280]{1,0:T(8,128)(2,1)S(1)}, bf16[16,1280]{1,0:T(8,128)(2,1)S(1)}, u32[]{:S(2)}, u32[]{:S(2)}) collective-permute-start(bf16[16,1280]{1,0:T(8,128)(2,1)S(1)} %shard_map.103.refs_0_), channel_id=1, source_target_pairs={{0,24},{4,28},{8,16},{12,20},{16,8},{20,12},{24,0},{28,4},{1,25},{... | collective-permute-start | bytes 122888 | tf_op jit(solution)/shard_map/ppermute | solution.py:246
  119.9 1.5 %collective-permute-start.34 = (bf16[4,16,1280]{2,1,0:T(8,128)(2,1)S(1)}, bf16[4,16,1280]{2,1,0:T(8,128)(2,1)S(1)}, u32[]{:S(2)}, u32[]{:S(2)}) collective-permute-start(bf16[4,16,1280]{2,1,0:T(8,128)(2,1)S(1)} %pad_maximum_fusion.1), channel_id=1, source_target_pairs={{0,4},{4,0},{8,12},{12,8},{16,20},{20,16},{24,28},{28,24},{1,5},{5... | collective-permute-start | bytes 491528 | tf_op jit(solution)/shard_map/ppermute | solution.py:236

commit v7 on v6

--- a/solution.py
+++ b/solution.py
@@ -164,7 +164,7 @@
             units[2 * (q ^ k) + (c ^ h)] = pieces[k][h]
     for k in range(groups):
         for u in range(per):
-            outs[k][:, u * unit : (u + 1) * unit] = units[(z ^ k) * per + u]
+            outs[k][:, u * unit : (u + 1) * unit] = units[(z ^ away(k, c, groups)) * per + u]
 
 
 def out_kernel(groups, ids, *refs):
@@ -343,7 +343,7 @@
         *columns,
         scratch=[pltpu.VMEM((seq, rows, unit), BF16)],
     )
-    slices = [slices[0]] + planes_of(slices[1:])
+    slices = [slices[0]] + planes_of(slices[1:], plane_by_core)
     outs = call(
         functools.partial(out_kernel, groups),
         [shape((ROWS, width)) for _ in range(groups)],

time: 123 us -> 123 us (level)
    ppermute x3 -> x6, waiting for transfers between devices: 6.26 us -> 12 us  [plane_by_core(): return lax.ppermute(a, ('seq', 'mp'), pairs)]
    ppermute x9 -> x6, waiting for transfers between devices: 15.2 us -> 9.51 us  [plane(): return lax.ppermute(a, 'mp', [(i, i ^ k) for i in range(groups)])]
    ppermute x9 -> x6, starting transfers between devices: 13.8 us -> 9.32 us  [plane(): return lax.ppermute(a, 'mp', [(i, i ^ k) for i in range(groups)])]
    ppermute x3 -> x6, starting transfers between devices: 4.44 us -> 8.89 us  [plane_by_core(): return lax.ppermute(a, ('seq', 'mp'), pairs)]
where the time goes in v7:
time: 123 us
  waiting for transfers between devices  53.6 us (44%)
  starting transfers between devices  42.2 us (34%)
  Pallas kernels  23.4 us (19%)
  local copies, waits for them, and re-layouts  3.66 us (3%)
    pallas_call x14, Pallas kernels, call(): pl.pallas_call(run, out_shape=list(outs), in_specs=[SMEM] + [VMEM] * n +...  23.4 us
    ppermute x12, waiting for transfers between devices, chip(): return lax.ppermute(a, 'seq', [(i, i ^ 2 * k) for i in range(seq)])  20.9 us
    ppermute x12, starting transfers between devices, chip(): return lax.ppermute(a, 'seq', [(i, i ^ 2 * k) for i in range(seq)])  15.1 us
    ppermute x6, waiting for transfers between devices, plane_by_core(): return lax.ppermute(a, ('seq', 'mp'), pairs)  12 us
    ppermute x6, waiting for transfers between devices, plane(): return lax.ppermute(a, 'mp', [(i, i ^ k) for i in range(groups)])  9.51 us
    ppermute x6, starting transfers between devices, plane(): return lax.ppermute(a, 'mp', [(i, i ^ k) for i in range(groups)])  9.32 us
    ppermute x6, starting transfers between devices, plane_by_core(): return lax.ppermute(a, ('seq', 'mp'), pairs)  8.89 us
    ppermute x6, waiting for transfers between devices, chip_by_core(): lax.ppermute(a, 'seq', [(i, i ^ 2 * (other if i % 2 else k)) for i in ran...  8.27 us
  transfers between devices with their start and end apart: 35, of which 24 were waited for; matrix products, arithmetic and copies ran while one was open for 0% of the time, Pallas kernels for 13%

profile of v7, /device:TPU:0, one launch (start us, length us, event | category | flops | bytes accessed | tf_op | source)
XLA Modules:
  0.0 123.2 jit_solution(9922140977555354740)
XLA Ops:
  0.6 1.0 copy-done.5
  1.6 0.7 copy-done.8
  2.3 0.8 shard_map.91.refs_0_
  3.1 3.0 %collective-permute-start = (bf16[32,1280]{1,0:T(8,128)(2,1)S(1)}, bf16[32,1280]{1,0:T(8,128)(2,1)S(1)}, u32[]{:S(2)}, u32[]{:S(2)}) collective-permute-start(bf16[32,1280]{1,0:T(8,128)(2,1)S(1)} %shard_map.91.refs_0_), channel_id=1, source_target_pairs={{0,8},{4,20},{8,0},{12,28},{16,24},{20,4},{24,16},{28,12},{1,9},{5... | collective-permute-start | bytes 245768 | tf_op jit(solution)/shard_map/ppermute | solution.py:246
  6.0 1.5 %collective-permute-start.1 = (bf16[32,1280]{1,0:T(8,128)(2,1)S(1)}, bf16[32,1280]{1,0:T(8,128)(2,1)S(1)}, u32[]{:S(2)}, u32[]{:S(2)}) collective-permute-start(bf16[32,1280]{1,0:T(8,128)(2,1)S(1)} %shard_map.91.refs_0_), channel_id=1, source_target_pairs={{0,16},{4,12},{8,24},{12,4},{16,0},{20,28},{24,8},{28,20},{1,17},{... | collective-permute-start | bytes 245768 | tf_op jit(solution)/shard_map/ppermute | solution.py:246
  7.6 1.0 collective-permute-done.refs_1_
  8.6 1.9 %collective-permute-done.1.refs_2_ = bf16[32,1280]{1,0:T(8,128)(2,1)S(1)} collective-permute-done((bf16[32,1280]{1,0:T(8,128)(2,1)S(1)}, bf16[32,1280]{1,0:T(8,128)(2,1)S(1)}, u32[]{:S(2)}, u32[]{:S(2)}) %collective-permute-start.1) | collective-permute-done | bytes 81952 | tf_op jit(solution)/shard_map/ppermute | solution.py:246
  10.5 2.4 %collective-permute-done.2.refs_3_ = bf16[32,1280]{1,0:T(8,128)(2,1)S(1)} collective-permute-done((bf16[32,1280]{1,0:T(8,128)(2,1)S(1)}, bf16[32,1280]{1,0:T(8,128)(2,1)S(1)}, u32[]{:S(2)}, u32[]{:S(2)}) %collective-permute-start.2) | collective-permute-done | bytes 81952 | tf_op jit(solution)/shard_map/ppermute | solution.py:246
  13.0 1.6 %collective-permute-done.3.refs_4_ = bf16[128,1280]{1,0:T(8,128)(2,1)S(1)} collective-permute-done((bf16[128,1280]{1,0:T(8,128)(2,1)S(1)}, bf16[128,1280]{1,0:T(8,128)(2,1)S(1)}, u32[]{:S(2)}, u32[]{:S(2)}) %collective-permute-start.3) | collective-permute-done | bytes 327712 | tf_op jit(solution)/shard_map/ppermute | solution.py:236
  14.6 0.8 shard_map.92
  15.6 1.6 %collective-permute-start.6 = (bf16[16,1280]{1,0:T(8,128)(2,1)S(1)}, bf16[16,1280]{1,0:T(8,128)(2,1)S(1)}, u32[]{:S(2)}, u32[]{:S(2)}) collective-permute-start(bf16[16,1280]{1,0:T(8,128)(2,1)S(1)} %get-tuple-element.30.refs_0_), channel_id=1, source_target_pairs={{0,1},{1,0},{2,3},{3,2},{4,5},{5,4},{6,7},{7,6},{8,9},{9,8},{10,11... | collective-permute-start | bytes 122888 | tf_op jit(solution)/shard_map/ppermute | solution.py:242
  17.2 2.6 %collective-permute-start.7 = (bf16[16,1280]{1,0:T(8,128)(2,1)S(1)}, bf16[16,1280]{1,0:T(8,128)(2,1)S(1)}, u32[]{:S(2)}, u32[]{:S(2)}) collective-permute-start(bf16[16,1280]{1,0:T(8,128)(2,1)S(1)} %get-tuple-element.30.refs_0_), channel_id=1, source_target_pairs={{0,2},{1,3},{2,0},{3,1},{4,6},{5,7},{6,4},{7,5},{8,10},{9,11},{10,... | collective-permute-start | bytes 122888 | tf_op jit(solution)/shard_map/ppermute | solution.py:242
  20.0 2.8 %collective-permute-done.7.refs_2_ = bf16[16,1280]{1,0:T(8,128)(2,1)S(1)} collective-permute-done((bf16[16,1280]{1,0:T(8,128)(2,1)S(1)}, bf16[16,1280]{1,0:T(8,128)(2,1)S(1)}, u32[]{:S(2)}, u32[]{:S(2)}) %collective-permute-start.7) | collective-permute-done | bytes 40992 | tf_op jit(solution)/shard_map/ppermute | solution.py:242
  22.9 2.7 %collective-permute-done.8.refs_3_ = bf16[16,1280]{1,0:T(8,128)(2,1)S(1)} collective-permute-done((bf16[16,1280]{1,0:T(8,128)(2,1)S(1)}, bf16[16,1280]{1,0:T(8,128)(2,1)S(1)}, u32[]{:S(2)}, u32[]{:S(2)}) %collective-permute-start.8) | collective-permute-done | bytes 40992 | tf_op jit(solution)/shard_map/ppermute | solution.py:242
  25.6 1.1 shard_map.93.refs_0_.refs_4_
  26.8 1.3 %collective-permute-start.10 = (bf16[64,1024]{1,0:T(8,128)(2,1)S(1)}, bf16[64,1024]{1,0:T(8,128)(2,1)S(1)}, u32[]{:S(2)}, u32[]{:S(2)}) collective-permute-start(bf16[64,1024]{1,0:T(8,128)(2,1)S(1)} %shard_map.93.refs_0_.refs_4_), channel_id=1, source_target_pairs={{0,2},{1,3},{2,0},{3,1},{4,5},{5,4},{6,7},{7,6},{8,10},{9,11},{10,... | collective-permute-start | bytes 393224 | tf_op jit(solution)/shard_map/ppermute | solution.py:254
  28.1 3.1 %collective-permute-start.11 = (bf16[64,1024]{1,0:T(8,128)(2,1)S(1)}, bf16[64,1024]{1,0:T(8,128)(2,1)S(1)}, u32[]{:S(2)}, u32[]{:S(2)}) collective-permute-start(bf16[64,1024]{1,0:T(8,128)(2,1)S(1)} %shard_map.93.refs_0_.refs_4_), channel_id=1, source_target_pairs={{0,3},{1,2},{2,1},{3,0},{4,7},{5,6},{6,5},{7,4},{8,11},{9,10},{10,... | collective-permute-start | bytes 393224 | tf_op jit(solution)/shard_map/ppermute | solution.py:254
  31.2 2.8 %collective-permute-done.9.refs_1_ = bf16[64,1024]{1,0:T(8,128)(2,1)S(1)} collective-permute-done((bf16[64,1024]{1,0:T(8,128)(2,1)S(1)}, bf16[64,1024]{1,0:T(8,128)(2,1)S(1)}, u32[]{:S(2)}, u32[]{:S(2)}) %collective-permute-start.9) | collective-permute-done | bytes 131104 | tf_op jit(solution)/shard_map/ppermute | solution.py:254
  33.9 3.5 %collective-permute-done.10.refs_2_ = bf16[64,1024]{1,0:T(8,128)(2,1)S(1)} collective-permute-done((bf16[64,1024]{1,0:T(8,128)(2,1)S(1)}, bf16[64,1024]{1,0:T(8,128)(2,1)S(1)}, u32[]{:S(2)}, u32[]{:S(2)}) %collective-permute-start.10) | collective-permute-done | bytes 131104 | tf_op jit(solution)/shard_map/ppermute | solution.py:254
  37.4 0.7 shard_map.94
  38.2 0.6 collective-permute-start.13
  38.8 1.1 collective-permute-start.14
  39.9 1.8 %collective-permute-start.12 = (bf16[2,64,512]{2,1,0:T(8,128)(2,1)S(1)}, bf16[2,64,512]{2,1,0:T(8,128)(2,1)S(1)}, u32[]{:S(2)}, u32[]{:S(2)}) collective-permute-start(bf16[2,64,512]{2,1,0:T(8,128)(2,1)S(1)} %get-tuple-element.32), channel_id=1, source_target_pairs={{0,24},{4,28},{8,16},{12,20},{16,8},{20,12},{24,0},{28,4},{1,25},{... | collective-permute-start | bytes 393224 | tf_op jit(solution)/shard_map/ppermute | solution.py:239
  41.7 1.8 %collective-permute-done.13.refs_0_ = bf16[2,64,512]{2,1,0:T(8,128)(2,1)S(1)} collective-permute-done((bf16[2,64,512]{2,1,0:T(8,128)(2,1)S(1)}, bf16[2,64,512]{2,1,0:T(8,128)(2,1)S(1)}, u32[]{:S(2)}, u32[]{:S(2)}) %collective-permute-start.13) | collective-permute-done | bytes 131104 | tf_op jit(solution)/shard_map/ppermute | solution.py:239
  43.5 0.7 collective-permute-done.14.refs_1_
  44.2 3.6 %shard_map.95 = (bf16[64,3584]{1,0:T(8,128)(2,1)}, bf16[64,3584]{1,0:T(8,128)(2,1)}) custom-call(s32[3]{0:T(128)S(1)} %pad_add_fusion.ids, bf16[2,64,512]{2,1,0:T(8,128)(2,1)S(1)} %collective-permute-done.13.refs_0_, bf16[2,64,512]{2,1,0:T(8,128)(2,1)S(1)} %collective-permute-done.14.refs_1_, bf16[512,1792]{1,0:T(8,128)(2,1)S(1)} %copy-done, ...), custom_call_target="tpu_custom_call" | custom-call | flops 939524096 | bytes 8519680 | tf_op jit(solution)/shard_map/pallas_call | solution.py:34
  47.8 3.0 %collective-permute-start.15 = (bf16[64,3584]{1,0:T(8,128)(2,1)}, bf16[64,3584]{1,0:T(8,128)(2,1)S(1)}, u32[]{:S(2)}, u32[]{:S(2)}) collective-permute-start(bf16[64,3584]{1,0:T(8,128)(2,1)} %get-tuple-element.36.refs_6_), channel_id=1, source_target_pairs={{0,8},{4,12},{8,0},{12,4},{16,24},{20,28},{24,16},{28,20},{1,9},{5... | collective-permute-start | bytes 1376264 | tf_op jit(solution)/shard_map/ppermute | solution.py:239
  50.8 1.1 collective-permute-start.16
  51.9 3.5 %shard_map.96 = (bf16[64,3584]{1,0:T(8,128)(2,1)}, bf16[64,3584]{1,0:T(8,128)(2,1)S(1)}) custom-call(s32[3]{0:T(128)S(1)} %pad_add_fusion.ids, bf16[2,64,512]{2,1,0:T(8,128)(2,1)S(1)} %collective-permute-done.12.refs_0_, bf16[2,64,512]{2,1,0:T(8,128)(2,1)S(1)} %get-tuple-element.33.refs_1_, bf16[512,1792]{1,0:T(8,128)(2,1)S(1)} %copy-done, ...), custom_call_target="tpu_custom_call" | custom-call | flops 939524096 | bytes 8519680 | tf_op jit(solution)/shard_map/pallas_call | solution.py:34
  55.3 0.8 copy-done.6
  56.7 2.1 %shard_map.97.refs_5_.refs_6_ = bf16[192,320]{1,0:T(8,128)(2,1)S(1)} custom-call(s32[3]{0:T(128)S(1)} %pad_add_fusion.ids, s32[192,1]{1,0:T(8,128)S(1)} %copy.10.refs_0_, bf16[192,1280]{1,0:T(8,128)(2,1)S(1)} %copy-done.4, bf16[32,1280]{1,0:T(8,128)(2,1)S(1)} %pad.4.refs_2_), custom_call_target="tpu_custom_call" | custom-call | bytes 697088 | tf_op jit(solution)/shard_map/pallas_call | solution.py:34
  58.7 3.1 %collective-permute-done.15.refs_2_ = bf16[64,3584]{1,0:T(8,128)(2,1)S(1)} collective-permute-done((bf16[64,3584]{1,0:T(8,128)(2,1)}, bf16[64,3584]{1,0:T(8,128)(2,1)S(1)}, u32[]{:S(2)}, u32[]{:S(2)}) %collective-permute-start.15) | collective-permute-done | bytes 458784 | tf_op jit(solution)/shard_map/ppermute | solution.py:239
  61.8 7.4 %collective-permute-done.16.refs_3_ = bf16[64,3584]{1,0:T(8,128)(2,1)S(1)} collective-permute-done((bf16[64,3584]{1,0:T(8,128)(2,1)}, bf16[64,3584]{1,0:T(8,128)(2,1)S(1)}, u32[]{:S(2)}, u32[]{:S(2)}) %collective-permute-start.16) | collective-permute-done | bytes 458784 | tf_op jit(solution)/shard_map/ppermute | solution.py:239
  69.2 1.0 copy-done.7
  70.2 1.0 shard_map.98.refs_0_
  71.7 0.9 collective-permute-start.20
  72.7 2.1 %collective-permute-start.21 = (bf16[64,1792]{1,0:T(8,128)(2,1)S(1)}, bf16[64,1792]{1,0:T(8,128)(2,1)S(1)}, u32[]{:S(2)}, u32[]{:S(2)}) collective-permute-start(bf16[64,1792]{1,0:T(8,128)(2,1)S(1)} %shard_map.98.refs_0_), channel_id=1, source_target_pairs={{0,24},{4,28},{8,16},{12,20},{16,8},{20,12},{24,0},{28,4},{1,25},{... | collective-permute-start | bytes 688136 | tf_op jit(solution)/shard_map/ppermute | solution.py:239
  74.8 2.5 %collective-permute-done.19.refs_0_ = bf16[64,1792]{1,0:T(8,128)(2,1)S(1)} collective-permute-done((bf16[64,1792]{1,0:T(8,128)(2,1)S(1)}, bf16[64,1792]{1,0:T(8,128)(2,1)S(1)}, u32[]{:S(2)}, u32[]{:S(2)}) %collective-permute-start.19) | collective-permute-done | bytes 229408 | tf_op jit(solution)/shard_map/ppermute | solution.py:239
  77.8 2.6 %collective-permute-done.21.refs_2_ = bf16[64,1792]{1,0:T(8,128)(2,1)S(1)} collective-permute-done((bf16[64,1792]{1,0:T(8,128)(2,1)S(1)}, bf16[64,1792]{1,0:T(8,128)(2,1)S(1)}, u32[]{:S(2)}, u32[]{:S(2)}) %collective-permute-start.21) | collective-permute-done | bytes 229408 | tf_op jit(solution)/shard_map/ppermute | solution.py:239
  80.4 2.9 %shard_map.100 = (bf16[2,64,512]{2,1,0:T(8,128)(2,1)S(1)}, bf16[2,64,512]{2,1,0:T(8,128)(2,1)S(1)}, bf16[2,64,512]{2,1,0:T(8,128)(2,1)S(1)}) custom-call(s32[3]{0:T(128)S(1)} %pad_add_fusion.ids, bf16[64,1792]{1,0:T(8,128)(2,1)S(1)} %collective-permute-done.19.refs_0_, bf16[64,1792]{1,0:T(8,128)(2,1)S(1)} %collective-permute-done.20.refs_1_, ...), custom_call_target="tpu_custom_call" | custom-call | flops 704643072 | bytes 4751360 | tf_op jit(solution)/shard_map/pallas_call | solution.py:34
  83.4 1.5 %collective-permute-start.22 = (bf16[2,64,512]{2,1,0:T(8,128)(2,1)S(1)}, bf16[2,64,512]{2,1,0:T(8,128)(2,1)S(1)}, u32[]{:S(2)}, u32[]{:S(2)}) collective-permute-start(bf16[2,64,512]{2,1,0:T(8,128)(2,1)S(1)} %get-tuple-element.41), channel_id=1, source_target_pairs={{0,8},{4,12},{8,0},{12,4},{16,24},{20,28},{24,16},{28,20},{1,9},{5... | collective-permute-start | bytes 393224 | tf_op jit(solution)/shard_map/ppermute | solution.py:239
  84.8 1.3 %collective-permute-start.23 = (bf16[2,64,512]{2,1,0:T(8,128)(2,1)S(1)}, bf16[2,64,512]{2,1,0:T(8,128)(2,1)S(1)}, u32[]{:S(2)}, u32[]{:S(2)}) collective-permute-start(bf16[2,64,512]{2,1,0:T(8,128)(2,1)S(1)} %get-tuple-element.42), channel_id=1, source_target_pairs={{0,16},{4,20},{8,24},{12,28},{16,0},{20,4},{24,8},{28,12},{1,17},{... | collective-permute-start | bytes 393224 | tf_op jit(solution)/shard_map/ppermute | solution.py:239
  86.2 0.7 collective-permute-start.24
  86.9 2.9 %shard_map.99.refs_0_ = bf16[2,64,512]{2,1,0:T(8,128)(2,1)S(1)} custom-call(s32[3]{0:T(128)S(1)} %pad_add_fusion.ids, bf16[64,1792]{1,0:T(8,128)(2,1)S(1)} %shard_map.98.refs_0_, bf16[1792,512]{1,0:T(8,128)(2,1)} %refs_3_.1, bf16[1792,512]{1,0:T(8,128)(2,1)} %collective-permute-done.18.refs_2_.refs_4_), custom_call_target="tpu_custom_call" | custom-call | flops 234881024 | bytes 4030464 | tf_op jit(solution)/shard_map/pallas_call | solution.py:34
  89.8 2.3 %collective-permute-done.24.refs_3_ = bf16[2,64,512]{2,1,0:T(8,128)(2,1)S(1)} collective-permute-done((bf16[2,64,512]{2,1,0:T(8,128)(2,1)S(1)}, bf16[2,64,512]{2,1,0:T(8,128)(2,1)S(1)}, u32[]{:S(2)}, u32[]{:S(2)}) %collective-permute-start.24) | collective-permute-done | bytes 131104 | tf_op jit(solution)/shard_map/ppermute | solution.py:239
  92.1 0.6 shard_map.101
  92.8 0.7 collective-permute-start.26
  93.4 3.7 %collective-permute-start.27 = (bf16[64,1024]{1,0:T(8,128)(2,1)S(1)}, bf16[64,1024]{1,0:T(8,128)(2,1)S(1)}, u32[]{:S(2)}, u32[]{:S(2)}) collective-permute-start(bf16[64,1024]{1,0:T(8,128)(2,1)S(1)} %get-tuple-element.47), channel_id=1, source_target_pairs={{0,3},{1,2},{2,1},{3,0},{4,7},{5,6},{6,5},{7,4},{8,11},{9,10},{10,... | collective-permute-start | bytes 393224 | tf_op jit(solution)/shard_map/ppermute | solution.py:254
  97.1 2.5 %collective-permute-done.25.refs_1_ = bf16[64,1024]{1,0:T(8,128)(2,1)S(1)} collective-permute-done((bf16[64,1024]{1,0:T(8,128)(2,1)S(1)}, bf16[64,1024]{1,0:T(8,128)(2,1)S(1)}, u32[]{:S(2)}, u32[]{:S(2)}) %collective-permute-start.25) | collective-permute-done | bytes 131104 | tf_op jit(solution)/shard_map/ppermute | solution.py:254
  99.6 3.3 %collective-permute-done.26.refs_2_ = bf16[64,1024]{1,0:T(8,128)(2,1)S(1)} collective-permute-done((bf16[64,1024]{1,0:T(8,128)(2,1)S(1)}, bf16[64,1024]{1,0:T(8,128)(2,1)S(1)}, u32[]{:S(2)}, u32[]{:S(2)}) %collective-permute-start.26) | collective-permute-done | bytes 131104 | tf_op jit(solution)/shard_map/ppermute | solution.py:254
  102.9 1.1 shard_map.102
  104.0 2.5 %collective-permute-start.28 = (bf16[16,1280]{1,0:T(8,128)(2,1)S(1)}, bf16[16,1280]{1,0:T(8,128)(2,1)S(1)}, u32[]{:S(2)}, u32[]{:S(2)}) collective-permute-start(bf16[16,1280]{1,0:T(8,128)(2,1)S(1)} %get-tuple-element.49), channel_id=1, source_target_pairs={{0,1},{1,0},{2,3},{3,2},{4,5},{5,4},{6,7},{7,6},{8,9},{9,8},{10,11... | collective-permute-start | bytes 122888 | tf_op jit(solution)/shard_map/ppermute | solution.py:242
  106.5 0.5 collective-permute-start.29
  107.0 1.9 %collective-permute-start.30 = (bf16[16,1280]{1,0:T(8,128)(2,1)S(1)}, bf16[16,1280]{1,0:T(8,128)(2,1)S(1)}, u32[]{:S(2)}, u32[]{:S(2)}) collective-permute-start(bf16[16,1280]{1,0:T(8,128)(2,1)S(1)} %get-tuple-element.51), channel_id=1, source_target_pairs={{0,3},{1,2},{2,1},{3,0},{4,7},{5,6},{6,5},{7,4},{8,11},{9,10},{10,... | collective-permute-start | bytes 122888 | tf_op jit(solution)/shard_map/ppermute | solution.py:242
  108.9 2.5 %collective-permute-done.29.refs_2_ = bf16[16,1280]{1,0:T(8,128)(2,1)S(1)} collective-permute-done((bf16[16,1280]{1,0:T(8,128)(2,1)S(1)}, bf16[16,1280]{1,0:T(8,128)(2,1)S(1)}, u32[]{:S(2)}, u32[]{:S(2)}) %collective-permute-start.29) | collective-permute-done | bytes 40992 | tf_op jit(solution)/shard_map/ppermute | solution.py:242
  111.4 1.5 %collective-permute-done.30.refs_3_ = bf16[16,1280]{1,0:T(8,128)(2,1)S(1)} collective-permute-done((bf16[16,1280]{1,0:T(8,128)(2,1)S(1)}, bf16[16,1280]{1,0:T(8,128)(2,1)S(1)}, u32[]{:S(2)}, u32[]{:S(2)}) %collective-permute-start.30) | collective-permute-done | bytes 40992 | tf_op jit(solution)/shard_map/ppermute | solution.py:242
  112.8 0.6 shard_map.103.refs_0_
  113.4 0.7 collective-permute-start.31
  114.1 0.9 collective-permute-start.32
  115.0 1.9 %collective-permute-start.33 = (bf16[16,1280]{1,0:T(8,128)(2,1)S(1)}, bf16[16,1280]{1,0:T(8,128)(2,1)S(1)}, u32[]{:S(2)}, u32[]{:S(2)}) collective-permute-start(bf16[16,1280]{1,0:T(8,128)(2,1)S(1)} %shard_map.103.refs_0_), channel_id=1, source_target_pairs={{0,24},{4,28},{8,16},{12,20},{16,8},{20,12},{24,0},{28,4},{1,25},{... | collective-permute-start | bytes 122888 | tf_op jit(solution)/shard_map/ppermute | solution.py:246
  117.5 0.6 collective-permute-done.32.refs_2_
  118.1 1.8 %collective-permute-done.33.refs_3_ = bf16[16,1280]{1,0:T(8,128)(2,1)S(1)} collective-permute-done((bf16[16,1280]{1,0:T(8,128)(2,1)S(1)}, bf16[16,1280]{1,0:T(8,128)(2,1)S(1)}, u32[]{:S(2)}, u32[]{:S(2)}) %collective-permute-start.33) | collective-permute-done | bytes 40992 | tf_op jit(solution)/shard_map/ppermute | solution.py:246
  120.0 1.4 %collective-permute-done.34.refs_4_ = bf16[4,16,1280]{2,1,0:T(8,128)(2,1)S(1)} collective-permute-done((bf16[4,16,1280]{2,1,0:T(8,128)(2,1)S(1)}, bf16[4,16,1280]{2,1,0:T(8,128)(2,1)S(1)}, u32[]{:S(2)}, u32[]{:S(2)}) %collective-permute-start.34) | collective-permute-done | bytes 163872 | tf_op jit(solution)/shard_map/ppermute | solution.py:236
  121.4 1.8 %shard_map.104 = bf16[192,1280]{1,0:T(8,128)(2,1)} custom-call(s32[3]{0:T(128)S(1)} %pad_add_fusion.ids, bf16[16,1280]{1,0:T(8,128)(2,1)S(1)} %shard_map.103.refs_0_, bf16[16,1280]{1,0:T(8,128)(2,1)S(1)} %collective-permute-done.31.refs_1_, bf16[16,1280]{1,0:T(8,128)(2,1)S(1)} %collective-permute-done.32.refs_2_, ...), custom_call_target="tpu_custom_call" | custom-call | bytes 1437696 | tf_op jit(solution)/shard_map/pallas_call | solution.py:34
  (47 shorter events, 3.4 us)
Async XLA Ops:
  0.0 14.6 %collective-permute-start.4 = (bf16[512,1792]{1,0:T(8,128)(2,1)}, bf16[512,1792]{1,0:T(8,128)(2,1)S(1)}, u32[]{:S(2)}, u32[]{:S(2)}) collective-permute-start(bf16[512,1792]{1,0:T(8,128)(2,1)} %refs_2_.3), channel_id=1, source_target_pairs={{0,4},{4,0},{8,12},{12,8},{16,20},{20,16},{24,28},{28,24},{1,5},{5... | collective-permute-start | bytes 5505032 | tf_op jit(solution)/shard_map/ppermute | solution.py:236
  0.5 14.2 %collective-permute-start.5 = (bf16[512,1792]{1,0:T(8,128)(2,1)}, bf16[512,1792]{1,0:T(8,128)(2,1)}, u32[]{:S(2)}, u32[]{:S(2)}) collective-permute-start(bf16[512,1792]{1,0:T(8,128)(2,1)} %refs_4_.5), channel_id=1, source_target_pairs={{0,4},{4,0},{8,12},{12,8},{16,20},{20,16},{24,28},{28,24},{1,5},{5... | collective-permute-start | bytes 5505032 | tf_op jit(solution)/shard_map/ppermute | solution.py:236
  0.6 1.0 copy-start.5
  1.6 0.7 copy-start.8
  3.1 5.5 %collective-permute-start = (bf16[32,1280]{1,0:T(8,128)(2,1)S(1)}, bf16[32,1280]{1,0:T(8,128)(2,1)S(1)}, u32[]{:S(2)}, u32[]{:S(2)}) collective-permute-start(bf16[32,1280]{1,0:T(8,128)(2,1)S(1)} %shard_map.91.refs_0_), channel_id=1, source_target_pairs={{0,8},{4,20},{8,0},{12,28},{16,24},{20,4},{24,16},{28,12},{1,9},{5... | collective-permute-start | bytes 245768 | tf_op jit(solution)/shard_map/ppermute | solution.py:246
  6.0 4.4 %collective-permute-start.1 = (bf16[32,1280]{1,0:T(8,128)(2,1)S(1)}, bf16[32,1280]{1,0:T(8,128)(2,1)S(1)}, u32[]{:S(2)}, u32[]{:S(2)}) collective-permute-start(bf16[32,1280]{1,0:T(8,128)(2,1)S(1)} %shard_map.91.refs_0_), channel_id=1, source_target_pairs={{0,16},{4,12},{8,24},{12,4},{16,0},{20,28},{24,8},{28,20},{1,17},{... | collective-permute-start | bytes 245768 | tf_op jit(solution)/shard_map/ppermute | solution.py:246
  7.6 5.3 %collective-permute-start.2 = (bf16[32,1280]{1,0:T(8,128)(2,1)S(1)}, bf16[32,1280]{1,0:T(8,128)(2,1)S(1)}, u32[]{:S(2)}, u32[]{:S(2)}) collective-permute-start(bf16[32,1280]{1,0:T(8,128)(2,1)S(1)} %shard_map.91.refs_0_), channel_id=1, source_target_pairs={{0,24},{4,28},{8,16},{12,20},{16,8},{20,12},{24,0},{28,4},{1,25},{... | collective-permute-start | bytes 245768 | tf_op jit(solution)/shard_map/ppermute | solution.py:246
  12.9 12.7 %copy-start.2 = (bf16[1280,1024]{1,0:T(8,128)(2,1)S(1)}, bf16[1280,1024]{1,0:T(8,128)(2,1)}, u32[]{:S(2)}) copy-start(bf16[1280,1024]{1,0:T(8,128)(2,1)} %refs_4_.3) | copy-start | bytes 7864324
  12.9 1.7 %collective-permute-start.3 = (bf16[128,1280]{1,0:T(8,128)(2,1)S(1)}, bf16[128,1280]{1,0:T(8,128)(2,1)S(1)}, u32[]{:S(2)}, u32[]{:S(2)}) collective-permute-start(bf16[128,1280]{1,0:T(8,128)(2,1)S(1)} %pad_maximum_fusion), channel_id=1, source_target_pairs={{0,4},{4,0},{8,12},{12,8},{16,20},{20,16},{24,28},{28,24},{1,5},{5... | collective-permute-start | bytes 983048 | tf_op jit(solution)/shard_map/ppermute | solution.py:236
  14.6 29.6 %copy-start.1 = (bf16[512,1792]{1,0:T(8,128)(2,1)S(1)}, bf16[512,1792]{1,0:T(8,128)(2,1)}, u32[]{:S(2)}) copy-start(bf16[512,1792]{1,0:T(8,128)(2,1)} %refs_4_.5) | copy-start | bytes 5505028
  15.4 28.8 %copy-start = (bf16[512,1792]{1,0:T(8,128)(2,1)S(1)}, bf16[512,1792]{1,0:T(8,128)(2,1)}, u32[]{:S(2)}) copy-start(bf16[512,1792]{1,0:T(8,128)(2,1)} %refs_2_.3) | copy-start | bytes 5505028
  15.4 65.0 %collective-permute-start.18 = (bf16[1792,512]{1,0:T(8,128)(2,1)}, bf16[1792,512]{1,0:T(8,128)(2,1)}, u32[]{:S(2)}, u32[]{:S(2)}) collective-permute-start(bf16[1792,512]{1,0:T(8,128)(2,1)} %refs_3_.1), channel_id=1, source_target_pairs={{0,4},{4,0},{8,12},{12,8},{16,20},{20,16},{24,28},{28,24},{1,5},{5... | collective-permute-start | bytes 5505032 | tf_op jit(solution)/shard_map/ppermute | solution.py:236
  15.6 4.4 %collective-permute-start.6 = (bf16[16,1280]{1,0:T(8,128)(2,1)S(1)}, bf16[16,1280]{1,0:T(8,128)(2,1)S(1)}, u32[]{:S(2)}, u32[]{:S(2)}) collective-permute-start(bf16[16,1280]{1,0:T(8,128)(2,1)S(1)} %get-tuple-element.30.refs_0_), channel_id=1, source_target_pairs={{0,1},{1,0},{2,3},{3,2},{4,5},{5,4},{6,7},{7,6},{8,9},{9,8},{10,11... | collective-permute-start | bytes 122888 | tf_op jit(solution)/shard_map/ppermute | solution.py:242
  17.2 5.7 %collective-permute-start.7 = (bf16[16,1280]{1,0:T(8,128)(2,1)S(1)}, bf16[16,1280]{1,0:T(8,128)(2,1)S(1)}, u32[]{:S(2)}, u32[]{:S(2)}) collective-permute-start(bf16[16,1280]{1,0:T(8,128)(2,1)S(1)} %get-tuple-element.30.refs_0_), channel_id=1, source_target_pairs={{0,2},{1,3},{2,0},{3,1},{4,6},{5,7},{6,4},{7,5},{8,10},{9,11},{10,... | collective-permute-start | bytes 122888 | tf_op jit(solution)/shard_map/ppermute | solution.py:242
  19.8 5.8 %collective-permute-start.8 = (bf16[16,1280]{1,0:T(8,128)(2,1)S(1)}, bf16[16,1280]{1,0:T(8,128)(2,1)S(1)}, u32[]{:S(2)}, u32[]{:S(2)}) collective-permute-start(bf16[16,1280]{1,0:T(8,128)(2,1)S(1)} %get-tuple-element.30.refs_0_), channel_id=1, source_target_pairs={{0,3},{1,2},{2,1},{3,0},{4,7},{5,6},{6,5},{7,4},{8,11},{9,10},{10,... | collective-permute-start | bytes 122888 | tf_op jit(solution)/shard_map/ppermute | solution.py:242
  26.7 7.2 %collective-permute-start.9 = (bf16[64,1024]{1,0:T(8,128)(2,1)S(1)}, bf16[64,1024]{1,0:T(8,128)(2,1)S(1)}, u32[]{:S(2)}, u32[]{:S(2)}) collective-permute-start(bf16[64,1024]{1,0:T(8,128)(2,1)S(1)} %shard_map.93.refs_0_.refs_4_), channel_id=1, source_target_pairs={{0,1},{1,0},{2,3},{3,2},{4,6},{5,7},{6,4},{7,5},{8,9},{9,8},{10,11... | collective-permute-start | bytes 393224 | tf_op jit(solution)/shard_map/ppermute | solution.py:254
  26.8 10.6 %collective-permute-start.10 = (bf16[64,1024]{1,0:T(8,128)(2,1)S(1)}, bf16[64,1024]{1,0:T(8,128)(2,1)S(1)}, u32[]{:S(2)}, u32[]{:S(2)}) collective-permute-start(bf16[64,1024]{1,0:T(8,128)(2,1)S(1)} %shard_map.93.refs_0_.refs_4_), channel_id=1, source_target_pairs={{0,2},{1,3},{2,0},{3,1},{4,5},{5,4},{6,7},{7,6},{8,10},{9,11},{10,... | collective-permute-start | bytes 393224 | tf_op jit(solution)/shard_map/ppermute | solution.py:254
  28.1 9.3 %collective-permute-start.11 = (bf16[64,1024]{1,0:T(8,128)(2,1)S(1)}, bf16[64,1024]{1,0:T(8,128)(2,1)S(1)}, u32[]{:S(2)}, u32[]{:S(2)}) collective-permute-start(bf16[64,1024]{1,0:T(8,128)(2,1)S(1)} %shard_map.93.refs_0_.refs_4_), channel_id=1, source_target_pairs={{0,3},{1,2},{2,1},{3,0},{4,7},{5,6},{6,5},{7,4},{8,11},{9,10},{10,... | collective-permute-start | bytes 393224 | tf_op jit(solution)/shard_map/ppermute | solution.py:254
  38.2 5.4 %collective-permute-start.13 = (bf16[2,64,512]{2,1,0:T(8,128)(2,1)S(1)}, bf16[2,64,512]{2,1,0:T(8,128)(2,1)S(1)}, u32[]{:S(2)}, u32[]{:S(2)}) collective-permute-start(bf16[2,64,512]{2,1,0:T(8,128)(2,1)S(1)} %get-tuple-element.34), channel_id=1, source_target_pairs={{0,8},{4,12},{8,0},{12,4},{16,24},{20,28},{24,16},{28,20},{1,9},{5... | collective-permute-start | bytes 393224 | tf_op jit(solution)/shard_map/ppermute | solution.py:239
  38.8 5.5 %collective-permute-start.14 = (bf16[2,64,512]{2,1,0:T(8,128)(2,1)S(1)}, bf16[2,64,512]{2,1,0:T(8,128)(2,1)S(1)}, u32[]{:S(2)}, u32[]{:S(2)}) collective-permute-start(bf16[2,64,512]{2,1,0:T(8,128)(2,1)S(1)} %get-tuple-element.35), channel_id=1, source_target_pairs={{0,16},{4,20},{8,24},{12,28},{16,0},{20,4},{24,8},{28,12},{1,17},{... | collective-permute-start | bytes 393224 | tf_op jit(solution)/shard_map/ppermute | solution.py:239
  39.9 12.0 %collective-permute-start.12 = (bf16[2,64,512]{2,1,0:T(8,128)(2,1)S(1)}, bf16[2,64,512]{2,1,0:T(8,128)(2,1)S(1)}, u32[]{:S(2)}, u32[]{:S(2)}) collective-permute-start(bf16[2,64,512]{2,1,0:T(8,128)(2,1)S(1)} %get-tuple-element.32), channel_id=1, source_target_pairs={{0,24},{4,28},{8,16},{12,20},{16,8},{20,12},{24,0},{28,4},{1,25},{... | collective-permute-start | bytes 393224 | tf_op jit(solution)/shard_map/ppermute | solution.py:239
  47.8 14.0 %collective-permute-start.15 = (bf16[64,3584]{1,0:T(8,128)(2,1)}, bf16[64,3584]{1,0:T(8,128)(2,1)S(1)}, u32[]{:S(2)}, u32[]{:S(2)}) collective-permute-start(bf16[64,3584]{1,0:T(8,128)(2,1)} %get-tuple-element.36.refs_6_), channel_id=1, source_target_pairs={{0,8},{4,12},{8,0},{12,4},{16,24},{20,28},{24,16},{28,20},{1,9},{5... | collective-permute-start | bytes 1376264 | tf_op jit(solution)/shard_map/ppermute | solution.py:239
  50.8 18.4 %collective-permute-start.16 = (bf16[64,3584]{1,0:T(8,128)(2,1)}, bf16[64,3584]{1,0:T(8,128)(2,1)S(1)}, u32[]{:S(2)}, u32[]{:S(2)}) collective-permute-start(bf16[64,3584]{1,0:T(8,128)(2,1)} %get-tuple-element.38), channel_id=1, source_target_pairs={{0,16},{4,20},{8,24},{12,28},{16,0},{20,4},{24,8},{28,12},{1,17},{... | collective-permute-start | bytes 1376264 | tf_op jit(solution)/shard_map/ppermute | solution.py:239
  51.9 4.6 %copy-start.9 = (s32[192]{0:T(256)S(1)}, s32[192]{0:T(256)}, u32[]{:S(2)}) copy-start(s32[192]{0:T(256)} %param.11) | copy-start | bytes 2308
  51.9 4.7 %copy-start.10 = (bf16[31,1280]{1,0:T(8,128)(2,1)S(1)}, bf16[31,1280]{1,0:T(8,128)(2,1)}, u32[]{:S(2)}) copy-start(bf16[31,1280]{1,0:T(8,128)(2,1)} %param.12) | copy-start | bytes 238084
  51.9 4.8 %copy-start.4 = (bf16[192,1280]{1,0:T(8,128)(2,1)S(1)}, bf16[192,1280]{1,0:T(8,128)(2,1)}, u32[]{:S(2)}) copy-start(bf16[192,1280]{1,0:T(8,128)(2,1)} %refs_7_.1) | copy-start | bytes 1474564
  55.3 0.8 copy-start.6
  56.1 13.1 %collective-permute-start.17 = (bf16[64,3584]{1,0:T(8,128)(2,1)}, bf16[64,3584]{1,0:T(8,128)(2,1)S(1)}, u32[]{:S(2)}, u32[]{:S(2)}) collective-permute-start(bf16[64,3584]{1,0:T(8,128)(2,1)} %get-tuple-element.39), channel_id=1, source_target_pairs={{0,24},{4,28},{8,16},{12,20},{16,8},{20,12},{24,0},{28,4},{1,25},{... | collective-permute-start | bytes 1376264 | tf_op jit(solution)/shard_map/ppermute | solution.py:239
  69.2 1.0 copy-start.7
  71.3 6.1 %collective-permute-start.19 = (bf16[64,1792]{1,0:T(8,128)(2,1)S(1)}, bf16[64,1792]{1,0:T(8,128)(2,1)S(1)}, u32[]{:S(2)}, u32[]{:S(2)}) collective-permute-start(bf16[64,1792]{1,0:T(8,128)(2,1)S(1)} %shard_map.98.refs_0_), channel_id=1, source_target_pairs={{0,8},{4,12},{8,0},{12,4},{16,24},{20,28},{24,16},{28,20},{1,9},{5... | collective-permute-start | bytes 688136 | tf_op jit(solution)/shard_map/ppermute | solution.py:239
  71.7 6.0 %collective-permute-start.20 = (bf16[64,1792]{1,0:T(8,128)(2,1)S(1)}, bf16[64,1792]{1,0:T(8,128)(2,1)S(1)}, u32[]{:S(2)}, u32[]{:S(2)}) collective-permute-start(bf16[64,1792]{1,0:T(8,128)(2,1)S(1)} %shard_map.98.refs_0_), channel_id=1, source_target_pairs={{0,16},{4,20},{8,24},{12,28},{16,0},{20,4},{24,8},{28,12},{1,17},{... | collective-permute-start | bytes 688136 | tf_op jit(solution)/shard_map/ppermute | solution.py:239
  72.7 7.7 %collective-permute-start.21 = (bf16[64,1792]{1,0:T(8,128)(2,1)S(1)}, bf16[64,1792]{1,0:T(8,128)(2,1)S(1)}, u32[]{:S(2)}, u32[]{:S(2)}) collective-permute-start(bf16[64,1792]{1,0:T(8,128)(2,1)S(1)} %shard_map.98.refs_0_), channel_id=1, source_target_pairs={{0,24},{4,28},{8,16},{12,20},{16,8},{20,12},{24,0},{28,4},{1,25},{... | collective-permute-start | bytes 688136 | tf_op jit(solution)/shard_map/ppermute | solution.py:239
  83.4 6.4 %collective-permute-start.22 = (bf16[2,64,512]{2,1,0:T(8,128)(2,1)S(1)}, bf16[2,64,512]{2,1,0:T(8,128)(2,1)S(1)}, u32[]{:S(2)}, u32[]{:S(2)}) collective-permute-start(bf16[2,64,512]{2,1,0:T(8,128)(2,1)S(1)} %get-tuple-element.41), channel_id=1, source_target_pairs={{0,8},{4,12},{8,0},{12,4},{16,24},{20,28},{24,16},{28,20},{1,9},{5... | collective-permute-start | bytes 393224 | tf_op jit(solution)/shard_map/ppermute | solution.py:239
  84.8 5.0 %collective-permute-start.23 = (bf16[2,64,512]{2,1,0:T(8,128)(2,1)S(1)}, bf16[2,64,512]{2,1,0:T(8,128)(2,1)S(1)}, u32[]{:S(2)}, u32[]{:S(2)}) collective-permute-start(bf16[2,64,512]{2,1,0:T(8,128)(2,1)S(1)} %get-tuple-element.42), channel_id=1, source_target_pairs={{0,16},{4,20},{8,24},{12,28},{16,0},{20,4},{24,8},{28,12},{1,17},{... | collective-permute-start | bytes 393224 | tf_op jit(solution)/shard_map/ppermute | solution.py:239
  86.2 16.7 %copy-start.3 = (bf16[1024,1280]{1,0:T(8,128)(2,1)S(1)}, bf16[1024,1280]{1,0:T(8,128)(2,1)}, u32[]{:S(2)}) copy-start(bf16[1024,1280]{1,0:T(8,128)(2,1)} %refs_5_.1) | copy-start | bytes 7864324
  86.2 5.9 %collective-permute-start.24 = (bf16[2,64,512]{2,1,0:T(8,128)(2,1)S(1)}, bf16[2,64,512]{2,1,0:T(8,128)(2,1)S(1)}, u32[]{:S(2)}, u32[]{:S(2)}) collective-permute-start(bf16[2,64,512]{2,1,0:T(8,128)(2,1)S(1)} %get-tuple-element.43), channel_id=1, source_target_pairs={{0,24},{4,28},{8,16},{12,20},{16,8},{20,12},{24,0},{28,4},{1,25},{... | collective-permute-start | bytes 393224 | tf_op jit(solution)/shard_map/ppermute | solution.py:239
  92.7 6.9 %collective-permute-start.25 = (bf16[64,1024]{1,0:T(8,128)(2,1)S(1)}, bf16[64,1024]{1,0:T(8,128)(2,1)S(1)}, u32[]{:S(2)}, u32[]{:S(2)}) collective-permute-start(bf16[64,1024]{1,0:T(8,128)(2,1)S(1)} %get-tuple-element.45), channel_id=1, source_target_pairs={{0,1},{1,0},{2,3},{3,2},{4,6},{5,7},{6,4},{7,5},{8,9},{9,8},{10,11... | collective-permute-start | bytes 393224 | tf_op jit(solution)/shard_map/ppermute | solution.py:254
  92.8 10.1 %collective-permute-start.26 = (bf16[64,1024]{1,0:T(8,128)(2,1)S(1)}, bf16[64,1024]{1,0:T(8,128)(2,1)S(1)}, u32[]{:S(2)}, u32[]{:S(2)}) collective-permute-start(bf16[64,1024]{1,0:T(8,128)(2,1)S(1)} %get-tuple-element.46), channel_id=1, source_target_pairs={{0,2},{1,3},{2,0},{3,1},{4,5},{5,4},{6,7},{7,6},{8,10},{9,11},{10,... | collective-permute-start | bytes 393224 | tf_op jit(solution)/shard_map/ppermute | solution.py:254
  93.4 9.4 %collective-permute-start.27 = (bf16[64,1024]{1,0:T(8,128)(2,1)S(1)}, bf16[64,1024]{1,0:T(8,128)(2,1)S(1)}, u32[]{:S(2)}, u32[]{:S(2)}) collective-permute-start(bf16[64,1024]{1,0:T(8,128)(2,1)S(1)} %get-tuple-element.47), channel_id=1, source_target_pairs={{0,3},{1,2},{2,1},{3,0},{4,7},{5,6},{6,5},{7,4},{8,11},{9,10},{10,... | collective-permute-start | bytes 393224 | tf_op jit(solution)/shard_map/ppermute | solution.py:254
  104.0 4.9 %collective-permute-start.28 = (bf16[16,1280]{1,0:T(8,128)(2,1)S(1)}, bf16[16,1280]{1,0:T(8,128)(2,1)S(1)}, u32[]{:S(2)}, u32[]{:S(2)}) collective-permute-start(bf16[16,1280]{1,0:T(8,128)(2,1)S(1)} %get-tuple-element.49), channel_id=1, source_target_pairs={{0,1},{1,0},{2,3},{3,2},{4,5},{5,4},{6,7},{7,6},{8,9},{9,8},{10,11... | collective-permute-start | bytes 122888 | tf_op jit(solution)/shard_map/ppermute | solution.py:242
  106.5 4.9 %collective-permute-start.29 = (bf16[16,1280]{1,0:T(8,128)(2,1)S(1)}, bf16[16,1280]{1,0:T(8,128)(2,1)S(1)}, u32[]{:S(2)}, u32[]{:S(2)}) collective-permute-start(bf16[16,1280]{1,0:T(8,128)(2,1)S(1)} %get-tuple-element.50), channel_id=1, source_target_pairs={{0,2},{1,3},{2,0},{3,1},{4,6},{5,7},{6,4},{7,5},{8,10},{9,11},{10,... | collective-permute-start | bytes 122888 | tf_op jit(solution)/shard_map/ppermute | solution.py:242
  107.0 5.8 %collective-permute-start.30 = (bf16[16,1280]{1,0:T(8,128)(2,1)S(1)}, bf16[16,1280]{1,0:T(8,128)(2,1)S(1)}, u32[]{:S(2)}, u32[]{:S(2)}) collective-permute-start(bf16[16,1280]{1,0:T(8,128)(2,1)S(1)} %get-tuple-element.51), channel_id=1, source_target_pairs={{0,3},{1,2},{2,1},{3,0},{4,7},{5,6},{6,5},{7,4},{8,11},{9,10},{10,... | collective-permute-start | bytes 122888 | tf_op jit(solution)/shard_map/ppermute | solution.py:242
  113.4 4.1 %collective-permute-start.31 = (bf16[16,1280]{1,0:T(8,128)(2,1)S(1)}, bf16[16,1280]{1,0:T(8,128)(2,1)S(1)}, u32[]{:S(2)}, u32[]{:S(2)}) collective-permute-start(bf16[16,1280]{1,0:T(8,128)(2,1)S(1)} %shard_map.103.refs_0_), channel_id=1, source_target_pairs={{0,8},{4,20},{8,0},{12,28},{16,24},{20,4},{24,16},{28,12},{1,9},{5... | collective-permute-start | bytes 122888 | tf_op jit(solution)/shard_map/ppermute | solution.py:246
  114.1 4.0 %collective-permute-start.32 = (bf16[16,1280]{1,0:T(8,128)(2,1)S(1)}, bf16[16,1280]{1,0:T(8,128)(2,1)S(1)}, u32[]{:S(2)}, u32[]{:S(2)}) collective-permute-start(bf16[16,1280]{1,0:T(8,128)(2,1)S(1)} %shard_map.103.refs_0_), channel_id=1, source_target_pairs={{0,16},{4,12},{8,24},{12,4},{16,0},{20,28},{24,8},{28,20},{1,17},{... | collective-permute-start | bytes 122888 | tf_op jit(solution)/shard_map/ppermute | solution.py:246
  115.0 4.9 %collective-permute-start.33 = (bf16[16,1280]{1,0:T(8,128)(2,1)S(1)}, bf16[16,1280]{1,0:T(8,128)(2,1)S(1)}, u32[]{:S(2)}, u32[]{:S(2)}) collective-permute-start(bf16[16,1280]{1,0:T(8,128)(2,1)S(1)} %shard_map.103.refs_0_), channel_id=1, source_target_pairs={{0,24},{4,28},{8,16},{12,20},{16,8},{20,12},{24,0},{28,4},{1,25},{... | collective-permute-start | bytes 122888 | tf_op jit(solution)/shard_map/ppermute | solution.py:246
  119.9 1.5 %collective-permute-start.34 = (bf16[4,16,1280]{2,1,0:T(8,128)(2,1)S(1)}, bf16[4,16,1280]{2,1,0:T(8,128)(2,1)S(1)}, u32[]{:S(2)}, u32[]{:S(2)}) collective-permute-start(bf16[4,16,1280]{2,1,0:T(8,128)(2,1)S(1)} %pad_maximum_fusion.1), channel_id=1, source_target_pairs={{0,4},{4,0},{8,12},{12,8},{16,20},{20,16},{24,28},{28,24},{1,5},{5... | collective-permute-start | bytes 491528 | tf_op jit(solution)/shard_map/ppermute | solution.py:236
